TPU v7x, 32 devices: a whole 2x2x4 slice. The times are simulated.
32 devices in a mesh: seq: 8 (over y, x, core), head: 4 (over z).
Axes of the slice: x: 2, y: 2, z: 4, core: 2. Of those that a mesh axis runs over, the one named last changes fastest.
Arguments:
- queries: bfloat16 [1024, 4096], P(('seq', 'head')), may hold values from -6 to 6
- keys: bfloat16 [1024, 8192], P(('seq', 'head')), may hold values from -6 to 6
- values: bfloat16 [1024, 8192], P(('seq', 'head')), may hold values from -6 to 6
- betas: bfloat16 [1024, 64], P(('seq', 'head')), may hold values from 0 to 2
- log_gates: bfloat16 [1024, 32], P(('seq', 'head')), may hold values from -3 to 0, as said below
- starts: int32 [1024], P('seq'), may hold values 0 or 1
Outputs:
- readout: bfloat16 [1024, 4096], P('seq', 'head')
Inputs may be any that keep to these rules, and one draw needn't show every extreme that they name: `log_gates`: log decays are negative.
All inputs are finite; a program needn't handle non-finite values. No bound on the sum of `starts` on one device may be relied on, other than what follows from the above.
Results may differ from a plain program's by a relative error of at most 0.001.
Values may be sent and summed in bfloat16 or wider, within the bound.
No kernel may reach another device: no remote copies, remote signals or barrier semaphores. Data moves between devices by JAX's collectives and lax.ppermute only.
A program may use at most 64 MiB of HBM per device.

v0:
```python
import math

import jax
import jax.numpy as jnp
from jax import lax
from jax.sharding import PartitionSpec as P

DK = 128
DV = 128
NH = 2
BLOCK = 64


EPSILON = 1e-06
PRECISE = lax.Precision.HIGHEST


def passed_along(value, axis, by):
    count = lax.axis_size(axis)
    pairs = [(i, i + by) for i in range(count) if 0 <= i + by < count]
    return lax.ppermute(value, axis, pairs)


def matmul_heads(left_side, right_side):
    return jnp.einsum("hde,hef->hdf", left_side, right_side, precision=PRECISE)


def batched_product(left_side, right_side):
    return jnp.einsum("hbnm,hbme->hbne", left_side, right_side, precision=PRECISE)


def unit_lower_solve(lower_part, targets):
    total_rows = lower_part.shape[-1]
    piece_rows = math.gcd(16, total_rows)
    piece_count = total_rows // piece_rows
    eye_piece = jnp.eye(piece_rows, dtype=jnp.float32)
    solved_pieces = []
    for index in range(piece_count):
        first_row = index * piece_rows
        last_row = first_row + piece_rows
        power = -lower_part[..., first_row:last_row, first_row:last_row]
        inverse = eye_piece + power
        for squaring in range(piece_rows.bit_length() - 2):
            power = batched_product(power, power)
            inverse = inverse + batched_product(inverse, power)
        remaining = targets[..., first_row:last_row, :]
        if index > 0:
            earlier = jnp.concatenate(solved_pieces, -2)
            remaining = remaining - batched_product(
                lower_part[..., first_row:last_row, :first_row], earlier
            )
        solved_pieces.append(batched_product(inverse, remaining))
    return jnp.concatenate(solved_pieces, -2)


def local(queries, keys, values, betas, log_gates, starts):
    queries, keys, values, betas, log_gates = (
        lax.all_to_all(queries, "head", split_axis=1, concat_axis=0, tiled=True),
        lax.all_to_all(keys, "head", split_axis=1, concat_axis=0, tiled=True),
        lax.all_to_all(values, "head", split_axis=1, concat_axis=0, tiled=True),
        lax.all_to_all(betas, "head", split_axis=1, concat_axis=0, tiled=True),
        lax.all_to_all(log_gates, "head", split_axis=1, concat_axis=0, tiled=True),
    )
    row_count = queries.shape[0]
    head_count = queries.shape[1] // DK
    blocks = row_count // BLOCK
    reflect_len = BLOCK * NH
    query_rows = jnp.transpose(
        queries.astype(jnp.float32).reshape(blocks, BLOCK, head_count, DK), (2, 0, 1, 3)
    )
    key_rows = jnp.transpose(
        keys.astype(jnp.float32).reshape(blocks, BLOCK, head_count, NH, DK), (2, 0, 1, 3, 4)
    )
    key_rows = key_rows.reshape(head_count, blocks, reflect_len, DK)
    key_rows = key_rows * lax.rsqrt(jnp.sum(key_rows * key_rows, -1, keepdims=True) + EPSILON)
    value_rows = jnp.transpose(
        values.astype(jnp.float32).reshape(blocks, BLOCK, head_count, NH, DV), (2, 0, 1, 3, 4)
    )
    value_rows = value_rows.reshape(head_count, blocks, reflect_len, DV)
    beta_rows = jnp.transpose(
        betas.astype(jnp.float32).reshape(blocks, BLOCK, head_count, NH), (2, 0, 1, 3)
    )
    beta_rows = beta_rows.reshape(head_count, blocks, reflect_len)
    gate_rows = jnp.transpose(
        log_gates.astype(jnp.float32).reshape(blocks, BLOCK, head_count), (2, 0, 1)
    )
    gate_rows = jnp.concatenate(
        [gate_rows[..., None], jnp.zeros(gate_rows.shape + (NH - 1,), jnp.float32)], -1
    )
    gate_rows = gate_rows.reshape(head_count, blocks, reflect_len)
    start_rows = starts.reshape(blocks, BLOCK)
    start_rows = jnp.concatenate(
        [start_rows[..., None], jnp.zeros(start_rows.shape + (NH - 1,), jnp.int32)], -1
    )
    start_rows = start_rows.reshape(blocks, reflect_len)
    log_decay = jnp.cumsum(gate_rows, -1)
    segment = jnp.cumsum(start_rows, -1)
    position = jnp.arange(reflect_len)
    causal = position[:, None] >= position[None, :]
    strict = position[:, None] > position[None, :]
    linked = (segment[:, :, None] == segment[:, None, :]) & causal
    log_ratio = log_decay[..., :, None] - log_decay[..., None, :]
    decay_ratio = jnp.where(linked, jnp.exp(jnp.where(linked, log_ratio, 0.0)), 0.0)
    carried = jnp.exp(log_decay) * (segment == 0).astype(jnp.float32)
    key_gram = jnp.einsum("hbnd,hbmd->hbnm", key_rows, key_rows, precision=PRECISE)
    strictly_below = jnp.where(strict, beta_rows[..., :, None] * decay_ratio * key_gram, 0.0)
    targets = jnp.concatenate(
        [beta_rows[..., None] * value_rows, (beta_rows * carried)[..., None] * key_rows], -1
    )
    solved = unit_lower_solve(strictly_below, targets)
    write_v = solved[..., :DV]
    write_k = solved[..., DV:]
    end_decay = decay_ratio[..., reflect_len - 1, :]
    end_keep = carried[..., reflect_len - 1]
    weighted = key_rows * end_decay[..., None]
    identity_block = jnp.eye(DK, dtype=jnp.float32)
    transition = end_keep[..., None, None] * identity_block - jnp.einsum(
        "hbmd,hbme->hbde", weighted, write_k, precision=PRECISE
    )
    inject = jnp.einsum("hbmd,hbme->hbde", weighted, write_v, precision=PRECISE)
    identity = jnp.broadcast_to(identity_block, (head_count, DK, DK))
    empty_state = jnp.zeros((head_count, DK, DV), jnp.float32)

    def compose(running, block_pair):
        step_transition, step_inject = block_pair
        advanced = (
            matmul_heads(step_transition, running[0]),
            matmul_heads(step_transition, running[1]) + step_inject,
        )
        return (advanced, running)

    (device_transition, device_inject), (prior_transition, prior_inject) = lax.scan(
        compose,
        (identity, empty_state),
        (jnp.moveaxis(transition, 1, 0), jnp.moveaxis(inject, 1, 0)),
    )

    def advance(round_index, incoming):
        return passed_along(matmul_heads(device_transition, incoming) + device_inject, "seq", 1)

    start_state = lax.fori_loop(0, lax.axis_size("seq") - 1, advance, empty_state)
    states = jnp.einsum(
        "bhde,hef->hbdf", prior_transition, start_state, precision=PRECISE
    ) + jnp.moveaxis(prior_inject, 0, 1)
    updates = write_v - jnp.einsum("hbmd,hbde->hbme", write_k, states, precision=PRECISE)
    decay_out = decay_ratio[..., NH - 1 :: NH, :]
    carried_out = carried[..., NH - 1 :: NH]
    scores = jnp.einsum("hbtd,hbmd->hbtm", query_rows, key_rows, precision=PRECISE) * decay_out
    result = carried_out[..., None] * jnp.einsum(
        "hbtd,hbde->hbte", query_rows, states, precision=PRECISE
    )
    result = result + jnp.einsum("hbtm,hbme->hbte", scores, updates, precision=PRECISE)
    return (
        jnp.transpose(result, (1, 2, 0, 3)).reshape(row_count, head_count * DV).astype(jnp.bfloat16)
    )


def solution(mesh):
    return jax.shard_map(
        local,
        mesh=mesh,
        in_specs=(
            P(("seq", "head"), None),
            P(("seq", "head"), None),
            P(("seq", "head"), None),
            P(("seq", "head"), None),
            P(("seq", "head"), None),
            P("seq"),
        ),
        out_specs=P("seq", "head"),
        check_vma=False,
    )
```

profile of v0, /device:TPU:12, one launch (start us, length us, event | category | flops | bytes accessed | tf_op | source)
XLA Modules:
  0.0 205.1 jit_solution(4649632174612987968)
XLA Ops:
  1.5 5.3 %all-to-all-start = ((bf16[4,2,128]{2,1,0:T(2,128)(2,1)}), bf16[4,2,128]{2,1,0:T(2,128)(2,1)S(1)}, u32[]{:S(2)}, u32[]{:S(2)}) async-start(bf16[4,2,128]{2,1,0:T(2,128)(2,1)} %reshape.142), calls=%async_computation | async-start | bytes 4096 | tf_op jit(solution)/shard_map/all_to_all | solution.py:62
  10.9 4.7 %all-to-all-start.2 = ((bf16[4,2,256]{2,1,0:T(2,128)(2,1)}), bf16[4,2,256]{2,1,0:T(2,128)(2,1)S(1)}, u32[]{:S(2)}, u32[]{:S(2)}) async-start(bf16[4,2,256]{2,1,0:T(2,128)(2,1)} %reshape.140), calls=%async_computation.2 | async-start | bytes 8192 | tf_op jit(solution)/shard_map/all_to_all | solution.py:61
  17.8 1.9 all-to-all-done.2
  19.7 4.8 %all-to-all-start.4 = ((bf16[32,4,1024]{2,0,1:T(8,128)(2,1)}), bf16[32,4,1024]{2,0,1:T(8,128)(2,1)S(1)}, u32[]{:S(2)}, u32[]{:S(2)}) async-start(bf16[32,4,1024]{2,0,1:T(8,128)(2,1)} %bitcast.208), calls=%async_computation.4 | async-start | bytes 524288 | tf_op jit(solution)/shard_map/all_to_all | solution.py:58
  27.2 3.5 %all-to-all-done.4 = bf16[32,4,1024]{2,0,1:T(8,128)(2,1)S(1)} async-done(((bf16[32,4,1024]{2,0,1:T(8,128)(2,1)}), bf16[32,4,1024]{2,0,1:T(8,128)(2,1)S(1)}, u32[]{:S(2)}, u32[]{:S(2)}) %all-to-all-start.4) | async-done | bytes 262176 | tf_op jit(solution)/shard_map/all_to_all | solution.py:58
  30.7 4.0 %all-to-all-start.1 = ((bf16[32,4,2048]{2,0,1:T(8,128)(2,1)}), bf16[32,4,2048]{2,0,1:T(8,128)(2,1)S(1)}, u32[]{:S(2)}, u32[]{:S(2)}) async-start(bf16[32,4,2048]{2,0,1:T(8,128)(2,1)} %bitcast.206), calls=%async_computation.1 | async-start | bytes 1048576 | tf_op jit(solution)/shard_map/all_to_all | solution.py:59
  35.7 2.6 %slice.115 = f32[8,2,64,128]{3,2,1,0:T(8,128)} slice(f32[8,2,128,128]{3,2,1,0:T(8,128)S(1)} %exponential_select_fusion), slice={[0:8:1], [0:2:1], [1:128:2], [0:128:1]} | slice | bytes 1048576 | tf_op jit(solution)/shard_map/slice | solution.py:146
  41.7 1.8 all-to-all-done.1
  43.5 6.5 %all-to-all-start.3 = ((bf16[32,4,2048]{2,0,1:T(8,128)(2,1)}), bf16[32,4,2048]{2,0,1:T(8,128)(2,1)S(1)}, u32[]{:S(2)}, u32[]{:S(2)}) async-start(bf16[32,4,2048]{2,0,1:T(8,128)(2,1)} %bitcast.205), calls=%async_computation.3 | async-start | bytes 1048576 | tf_op jit(solution)/shard_map/all_to_all | solution.py:60
  51.0 2.0 multiply_reduce_fusion
  55.0 3.4 %fusion.12 = f32[8,2,128,128]{3,2,1,0:T(8,128)S(1)} fusion(f32[8,2,128,128]{3,2,1,0:T(8,128)S(1)} %bitcast.224, f32[8,2,128]{2,1,0:T(2,128)} %copy.98, f32[8,2,128]{2,1,0:T(2,128)S(1)} %copy.92, pred[128,128]{1,0:T(8,128)(4,1)} %iota_compare_fusion, f32[8,2,128]{2,1,0:T(2,128)} %copy-done.28, pred[2,128,128]{2,1,0:T(8,128)(4,1)} %copy-done.26), kind=kOutput, calls=%fused_computation.35 | convolution fusion | flops 404488192 | bytes 2170880 | tf_op jit(solution)/shard_map/hbnd,hbmd->hbnm/dot_general | solution.py:105
  77.2 3.1 %reshape.134 = f32[2,64,8,2,128]{4,3,2,1,0:T(2,128)} reshape(f32[4,32,2048]{2,1,0:T(8,128)} %convert_bitcast_fusion) | data formatting | bytes 2097152 | tf_op jit(solution)/shard_map/reshape | solution.py:79
  80.3 1.8 copy.100
  98.7 3.7 %convolution_bitcast_fusion = f32[2,8,128,128]{3,2,0,1:T(8,128)} fusion(f32[8,2,128,256]{3,2,1,0:T(8,128)S(1)} %convolution_dynamic-update-slice_fusion, f32[8,2,128,128]{3,2,1,0:T(8,128)S(1)} %bitcast.226, f32[8,2,128]{2,1,0:T(2,128)S(1)} %bitcast.243, f32[8,2,128]{2,1,0:T(2,128)S(1)} %copy.92), kind=kOutput, calls=%fused_computation.31 | convolution fusion | flops 403177472 | bytes 3162112 | tf_op jit(solution)/shard_map/hbmd,hbme->hbde/dot_general | solution.py:120
  102.5 2.5 %fusion.11 = f32[2,8,128,128]{3,2,0,1:T(8,128)S(1)} fusion(f32[8,2,128,256]{3,2,1,0:T(8,128)S(1)} %convolution_dynamic-update-slice_fusion, f32[8,2,128,128]{3,2,1,0:T(8,128)S(1)} %bitcast.227, f32[8,2,128]{2,1,0:T(2,128)S(1)} %bitcast.244, f32[8,2,128]{2,1,0:T(2,128)S(1)} %copy.92, f32[128,128]{1,0:T(8,128)S(1)} %copy-done.14, f32[2,8]{0,1:T(8,128)S(1)} %copy-done.32), kind=kOutput, calls=%fused_computation.33 | convolution fusion | flops 403701760 | bytes 3231744 | tf_op jit(solution)/shard_map/hbmd,hbme->hbde/dot_general | solution.py:117
  105.0 7.3 %while.28 = (s32[]{:T(128)}, f32[8,128,128]{2,1,0:T(8,128)S(1)}, f32[8,128,128]{2,1,0:T(8,128)S(1)}, f32[2,8,128,128]{3,2,0,1:T(8,128)}, f32[2,8,128,128]{3,2,0,...) while((s32[]{:T(128)}, f32[8,128,128]{2,1,0:T(8,128)S(1)}, ...), condition=%wide.region_4.5_spmd.clone, body=%wide.region_3.4_spmd.clone.sunk | while | flops 403046400 | bytes 28837116 | solution.py:132
  112.3 84.4 %while.27 = (s32[]{:T(128)}, f32[8,128,128]{2,1,0:T(8,128)S(1)}, f32[8,128,128]{2,1,0:T(8,128)S(1)}, f32[8,128,128]{2,1,0:T(8,128)S(1)}, s32[]{:T(128)}) while((s32[]{:T(128)}, f32[8,128,128]{2,1,0:T(8,128)S(1)}, f32[8,128,128]{2,1,0:T(8,128)S(1)}, f32[8,128,128]{2,1,0:T(8,128)S(1)}, s32[]{:T(128)}) %tuple.69), condition=%wide.region_6.7_spmd, body=%wide.region_5.6_spmd.sunk | while | flops 201457664 | bytes 4194405 | solution.py:141
  113.0 1.9 collective-permute-start
  114.9 9.5 %collective-permute-done = f32[8,128,128]{2,1,0:T(8,128)S(1)} collective-permute-done((f32[8,128,128]{2,1,0:T(8,128)S(1)}, f32[8,128,128]{2,1,0:T(8,128)S(1)}, u32[]{:S(2)}, u32[]{:S(2)}) %collective-permute-start) | collective-permute-done | bytes 524320 | tf_op jit(solution)/shard_map/while/body/eval_jaxpr/ppermute | solution.py:21
  125.0 1.9 collective-permute-start
  127.0 9.5 %collective-permute-done = f32[8,128,128]{2,1,0:T(8,128)S(1)} collective-permute-done((f32[8,128,128]{2,1,0:T(8,128)S(1)}, f32[8,128,128]{2,1,0:T(8,128)S(1)}, u32[]{:S(2)}, u32[]{:S(2)}) %collective-permute-start) | collective-permute-done | bytes 524320 | tf_op jit(solution)/shard_map/while/body/eval_jaxpr/ppermute | solution.py:21
  137.1 1.9 collective-permute-start
  139.0 9.5 %collective-permute-done = f32[8,128,128]{2,1,0:T(8,128)S(1)} collective-permute-done((f32[8,128,128]{2,1,0:T(8,128)S(1)}, f32[8,128,128]{2,1,0:T(8,128)S(1)}, u32[]{:S(2)}, u32[]{:S(2)}) %collective-permute-start) | collective-permute-done | bytes 524320 | tf_op jit(solution)/shard_map/while/body/eval_jaxpr/ppermute | solution.py:21
  149.1 1.9 collective-permute-start
  151.1 9.5 %collective-permute-done = f32[8,128,128]{2,1,0:T(8,128)S(1)} collective-permute-done((f32[8,128,128]{2,1,0:T(8,128)S(1)}, f32[8,128,128]{2,1,0:T(8,128)S(1)}, u32[]{:S(2)}, u32[]{:S(2)}) %collective-permute-start) | collective-permute-done | bytes 524320 | tf_op jit(solution)/shard_map/while/body/eval_jaxpr/ppermute | solution.py:21
  161.2 1.9 collective-permute-start
  163.1 9.5 %collective-permute-done = f32[8,128,128]{2,1,0:T(8,128)S(1)} collective-permute-done((f32[8,128,128]{2,1,0:T(8,128)S(1)}, f32[8,128,128]{2,1,0:T(8,128)S(1)}, u32[]{:S(2)}, u32[]{:S(2)}) %collective-permute-start) | collective-permute-done | bytes 524320 | tf_op jit(solution)/shard_map/while/body/eval_jaxpr/ppermute | solution.py:21
  173.2 1.9 collective-permute-start
  175.2 9.5 %collective-permute-done = f32[8,128,128]{2,1,0:T(8,128)S(1)} collective-permute-done((f32[8,128,128]{2,1,0:T(8,128)S(1)}, f32[8,128,128]{2,1,0:T(8,128)S(1)}, u32[]{:S(2)}, u32[]{:S(2)}) %collective-permute-start) | collective-permute-done | bytes 524320 | tf_op jit(solution)/shard_map/while/body/eval_jaxpr/ppermute | solution.py:21
  185.3 1.9 collective-permute-start
  187.2 9.5 %collective-permute-done = f32[8,128,128]{2,1,0:T(8,128)S(1)} collective-permute-done((f32[8,128,128]{2,1,0:T(8,128)S(1)}, f32[8,128,128]{2,1,0:T(8,128)S(1)}, u32[]{:S(2)}, u32[]{:S(2)}) %collective-permute-start) | collective-permute-done | bytes 524320 | tf_op jit(solution)/shard_map/while/body/eval_jaxpr/ppermute | solution.py:21
  196.7 2.8 %convolution_add_fusion.2 = f32[8,2,128,128]{3,2,1,0:T(8,128)S(1)} fusion(f32[2,8,128,128]{3,2,0,1:T(8,128)} %get-tuple-element.67, f32[2,8,128,128]{3,2,0,1:T(8,128)} %get-tuple-element.71, f32[8,128,128]{2,1,0:T(8,128)S(1)} %get-tuple-element.70), kind=kOutput, calls=%fused_computation.30 | convolution fusion | flops 402915328 | bytes 3670016 | tf_op jit(solution)/shard_map/bhde,hef->hbdf/dot_general | solution.py:142
  (222 shorter events, 69.3 us)
Async XLA Ops:
  0.0 24.5 %copy-start.24 = (bf16[32,8192]{1,0:T(8,128)(2,1)S(1)}, bf16[32,8192]{1,0:T(8,128)(2,1)}, u32[]{:S(2)}) copy-start(bf16[32,8192]{1,0:T(8,128)(2,1)} %param.11) | copy-start | bytes 1572868
  0.0 25.4 %copy-start.25 = (bf16[32,8192]{1,0:T(8,128)(2,1)S(1)}, bf16[32,8192]{1,0:T(8,128)(2,1)}, u32[]{:S(2)}) copy-start(bf16[32,8192]{1,0:T(8,128)(2,1)} %param.12) | copy-start | bytes 1572868
  1.5 9.3 %all-to-all-start = ((bf16[4,2,128]{2,1,0:T(2,128)(2,1)}), bf16[4,2,128]{2,1,0:T(2,128)(2,1)S(1)}, u32[]{:S(2)}, u32[]{:S(2)}) async-start(bf16[4,2,128]{2,1,0:T(2,128)(2,1)} %reshape.142), calls=%async_computation | async-start | bytes 4096 | tf_op jit(solution)/shard_map/all_to_all | solution.py:62
  8.3 26.4 %copy-start.26 = (pred[2,128,128]{2,1,0:T(8,128)(4,1)}, pred[2,128,128]{2,1,0:T(8,128)(4,1)S(1)}, u32[]{:S(2)}) copy-start(pred[2,128,128]{2,1,0:T(8,128)(4,1)S(1)} %compare_and_fusion) | copy-start | bytes 98308
  10.9 8.8 %all-to-all-start.2 = ((bf16[4,2,256]{2,1,0:T(2,128)(2,1)}), bf16[4,2,256]{2,1,0:T(2,128)(2,1)S(1)}, u32[]{:S(2)}, u32[]{:S(2)}) async-start(bf16[4,2,256]{2,1,0:T(2,128)(2,1)} %reshape.140), calls=%async_computation.2 | async-start | bytes 8192 | tf_op jit(solution)/shard_map/all_to_all | solution.py:61
  19.7 11.0 %all-to-all-start.4 = ((bf16[32,4,1024]{2,0,1:T(8,128)(2,1)}), bf16[32,4,1024]{2,0,1:T(8,128)(2,1)S(1)}, u32[]{:S(2)}, u32[]{:S(2)}) async-start(bf16[32,4,1024]{2,0,1:T(8,128)(2,1)} %bitcast.208), calls=%async_computation.4 | async-start | bytes 524288 | tf_op jit(solution)/shard_map/all_to_all | solution.py:58
  27.2 12.1 %copy-start.28 = (f32[8,2,128]{2,1,0:T(2,128)}, f32[8,2,128]{2,1,0:T(2,128)S(1)}, u32[]{:S(2)}) copy-start(f32[8,2,128]{2,1,0:T(2,128)S(1)} %copy.93) | copy-start | bytes 24580
  30.7 12.8 %all-to-all-start.1 = ((bf16[32,4,2048]{2,0,1:T(8,128)(2,1)}), bf16[32,4,2048]{2,0,1:T(8,128)(2,1)S(1)}, u32[]{:S(2)}, u32[]{:S(2)}) async-start(bf16[32,4,2048]{2,0,1:T(8,128)(2,1)} %bitcast.206), calls=%async_computation.1 | async-start | bytes 1048576 | tf_op jit(solution)/shard_map/all_to_all | solution.py:59
  43.5 32.6 %all-to-all-start.3 = ((bf16[32,4,2048]{2,0,1:T(8,128)(2,1)}), bf16[32,4,2048]{2,0,1:T(8,128)(2,1)S(1)}, u32[]{:S(2)}, u32[]{:S(2)}) async-start(bf16[32,4,2048]{2,0,1:T(8,128)(2,1)} %bitcast.205), calls=%async_computation.3 | async-start | bytes 1048576 | tf_op jit(solution)/shard_map/all_to_all | solution.py:60
  77.2 4.9 %copy-start.22 = (f32[8,2,16,16]{3,2,1,0:T(8,128)S(1)}, f32[8,2,16,16]{3,2,1,0:T(8,128)}, u32[]{:S(2)}) copy-start(f32[8,2,16,16]{3,2,1,0:T(8,128)} %fusion.100) | copy-start | bytes 49156
  77.2 4.9 %copy-start.23 = (f32[8,2,16,16]{3,2,1,0:T(8,128)S(1)}, f32[8,2,16,16]{3,2,1,0:T(8,128)}, u32[]{:S(2)}) copy-start(f32[8,2,16,16]{3,2,1,0:T(8,128)} %convolution_add_fusion.25) | copy-start | bytes 49156
  77.2 5.2 %copy-start.29 = (f32[8,2,128]{2,1,0:T(2,128)S(1)}, f32[8,2,128]{2,1,0:T(2,128)}, u32[]{:S(2)}) copy-start(f32[8,2,128]{2,1,0:T(2,128)} %copy.98) | copy-start | bytes 24580
  77.2 5.2 %copy-start.31 = (f32[8,2,128]{2,1,0:T(2,128)S(1)}, f32[8,2,128]{2,1,0:T(2,128)}, u32[]{:S(2)}) copy-start(f32[8,2,128]{2,1,0:T(2,128)} %copy.102) | copy-start | bytes 24580
  96.5 1.3 copy-start.15
  98.3 4.1 %copy-start.14 = (f32[128,128]{1,0:T(8,128)S(1)}, f32[128,128]{1,0:T(8,128)}, u32[]{:S(2)}) copy-start(f32[128,128]{1,0:T(8,128)} %fusion.92) | copy-start | bytes 196612
  98.3 4.1 %copy-start.32 = (f32[2,8]{0,1:T(8,128)S(1)}, f32[2,8]{0,1:T(8,128)}, u32[]{:S(2)}) copy-start(f32[2,8]{0,1:T(8,128)} %copy.87) | copy-start | bytes 196
  98.7 6.2 %copy-start.1 = (f32[8,2,128,256]{3,2,1,0:T(8,128)}, f32[8,2,128,256]{3,2,1,0:T(8,128)S(1)}, u32[]{:S(2)}) copy-start(f32[8,2,128,256]{3,2,1,0:T(8,128)S(1)} %convolution_dynamic-update-slice_fusion) | copy-start | bytes 6291460
  105.0 1.5 copy-start.12
  105.1 1.8 copy-start
  106.7 1.3 copy-start.13
  108.7 1.5 copy-start.12
  108.7 1.8 copy-start
  110.3 1.3 copy-start.13
  113.0 11.4 %collective-permute-start = (f32[8,128,128]{2,1,0:T(8,128)S(1)}, f32[8,128,128]{2,1,0:T(8,128)S(1)}, u32[]{:S(2)}, u32[]{:S(2)}) collective-permute-start(f32[8,128,128]{2,1,0:T(8,128)S(1)} %convolution_add_fusion.29), channel_id=1, source_target_pairs={{0,4},{4,8},{8,12},{12,16},{16,20},{20,24},{24,28},{1,5},{5,9},{9,... | collective-permute-start | bytes 1572872 | tf_op jit(solution)/shard_map/while/body/eval_jaxpr/ppermute | solution.py:21
  125.0 11.4 %collective-permute-start = (f32[8,128,128]{2,1,0:T(8,128)S(1)}, f32[8,128,128]{2,1,0:T(8,128)S(1)}, u32[]{:S(2)}, u32[]{:S(2)}) collective-permute-start(f32[8,128,128]{2,1,0:T(8,128)S(1)} %convolution_add_fusion.29), channel_id=1, source_target_pairs={{0,4},{4,8},{8,12},{12,16},{16,20},{20,24},{24,28},{1,5},{5,9},{9,... | collective-permute-start | bytes 1572872 | tf_op jit(solution)/shard_map/while/body/eval_jaxpr/ppermute | solution.py:21
  137.1 11.4 %collective-permute-start = (f32[8,128,128]{2,1,0:T(8,128)S(1)}, f32[8,128,128]{2,1,0:T(8,128)S(1)}, u32[]{:S(2)}, u32[]{:S(2)}) collective-permute-start(f32[8,128,128]{2,1,0:T(8,128)S(1)} %convolution_add_fusion.29), channel_id=1, source_target_pairs={{0,4},{4,8},{8,12},{12,16},{16,20},{20,24},{24,28},{1,5},{5,9},{9,... | collective-permute-start | bytes 1572872 | tf_op jit(solution)/shard_map/while/body/eval_jaxpr/ppermute | solution.py:21
  149.1 11.4 %collective-permute-start = (f32[8,128,128]{2,1,0:T(8,128)S(1)}, f32[8,128,128]{2,1,0:T(8,128)S(1)}, u32[]{:S(2)}, u32[]{:S(2)}) collective-permute-start(f32[8,128,128]{2,1,0:T(8,128)S(1)} %convolution_add_fusion.29), channel_id=1, source_target_pairs={{0,4},{4,8},{8,12},{12,16},{16,20},{20,24},{24,28},{1,5},{5,9},{9,... | collective-permute-start | bytes 1572872 | tf_op jit(solution)/shard_map/while/body/eval_jaxpr/ppermute | solution.py:21
  161.2 11.4 %collective-permute-start = (f32[8,128,128]{2,1,0:T(8,128)S(1)}, f32[8,128,128]{2,1,0:T(8,128)S(1)}, u32[]{:S(2)}, u32[]{:S(2)}) collective-permute-start(f32[8,128,128]{2,1,0:T(8,128)S(1)} %convolution_add_fusion.29), channel_id=1, source_target_pairs={{0,4},{4,8},{8,12},{12,16},{16,20},{20,24},{24,28},{1,5},{5,9},{9,... | collective-permute-start | bytes 1572872 | tf_op jit(solution)/shard_map/while/body/eval_jaxpr/ppermute | solution.py:21
  173.2 11.4 %collective-permute-start = (f32[8,128,128]{2,1,0:T(8,128)S(1)}, f32[8,128,128]{2,1,0:T(8,128)S(1)}, u32[]{:S(2)}, u32[]{:S(2)}) collective-permute-start(f32[8,128,128]{2,1,0:T(8,128)S(1)} %convolution_add_fusion.29), channel_id=1, source_target_pairs={{0,4},{4,8},{8,12},{12,16},{16,20},{20,24},{24,28},{1,5},{5,9},{9,... | collective-permute-start | bytes 1572872 | tf_op jit(solution)/shard_map/while/body/eval_jaxpr/ppermute | solution.py:21
  185.3 11.4 %collective-permute-start = (f32[8,128,128]{2,1,0:T(8,128)S(1)}, f32[8,128,128]{2,1,0:T(8,128)S(1)}, u32[]{:S(2)}, u32[]{:S(2)}) collective-permute-start(f32[8,128,128]{2,1,0:T(8,128)S(1)} %convolution_add_fusion.29), channel_id=1, source_target_pairs={{0,4},{4,8},{8,12},{12,16},{16,20},{20,24},{24,28},{1,5},{5,9},{9,... | collective-permute-start | bytes 1572872 | tf_op jit(solution)/shard_map/while/body/eval_jaxpr/ppermute | solution.py:21
  196.7 2.8 %copy-start.2 = (f32[8,2,128,256]{3,2,1,0:T(8,128)S(1)}, f32[8,2,128,256]{3,2,1,0:T(8,128)}, u32[]{:S(2)}) copy-start(f32[8,2,128,256]{3,2,1,0:T(8,128)} %copy-done.1) | copy-start | bytes 6291460
  199.5 1.8 copy-start.9
  (18 other events, 19.2 us)
where the time goes:
time: 208 us; the launch traced here: 205 us
  waiting for transfers between devices  73.9 us (36%)
  matrix products  54.3 us (26%)
  starting transfers between devices  38.7 us (19%)
  local copies, waits for them, and re-layouts  29.2 us (14%)
  other arithmetic  7.22 us (3%)
    ppermute x7, waiting for transfers between devices, passed_along(): return lax.ppermute(value, axis, pairs)  66.3 us
    dot_general x63, matrix products, batched_product(): jnp.einsum('hbnm,hbme->hbne', left_side, right_side, precision=PRECISE)  30.6 us
    ppermute x7, starting transfers between devices, passed_along(): return lax.ppermute(value, axis, pairs)  13.4 us
    dot_general x11, matrix products, matmul_heads(): return jnp.einsum('hde,hef->hdf', left_side, right_side, precision=PRECISE)  7.09 us
    all_to_all x1, starting transfers between devices, local(): lax.all_to_all(values, 'head', split_axis=1, concat_axis=0, tiled=True)  6.47 us
    unnamed x65, local copies, waits for them, and re-layouts  5.84 us
    all_to_all x1, starting transfers between devices, local(): lax.all_to_all(log_gates, 'head', split_axis=1, concat_axis=0, tiled=True)  5.32 us
    reshape x2, local copies, waits for them, and re-layouts, local(): value_rows = value_rows.reshape(head_count, blocks, reflect_len, DV)  4.9 us
  transfers between devices with their start and end apart: 12, of which 11 were waited for; matrix products, arithmetic and copies ran while one was open for 20% of the time, Pallas kernels for 0%

commit v1 on v0

v1 whole, which is shorter than its diff:
```python
import jax
import jax.numpy as jnp
from jax import lax
from jax.experimental import pallas as pl
from jax.experimental.pallas import tpu as pltpu
from jax.sharding import Mesh
from jax.sharding import PartitionSpec as P

DK = 128
DV = 128
NH = 2
TOK = 32
CHUNK = 2 * TOK
REFL = CHUNK * NH
GROUP = 4
EPSILON = 1e-06

KEY_ROW = 0
VALUE_ROW = NH * TOK
QUERY_ROW = 2 * NH * TOK
SCALE_ROW = QUERY_ROW + TOK
SCALE_ROWS = 16
PACK_ROWS = SCALE_ROW + SCALE_ROWS

BF16 = jnp.bfloat16
F32 = jnp.float32
NT = (((1,), (1,)), ((), ()))


def iota(shape, axis):
    return lax.broadcasted_iota(jnp.int32, shape, axis)


def dot(left, right):
    return jnp.dot(left, right, preferred_element_type=F32)


def dot_nt(left, right):
    return lax.dot_general(left, right, NT, preferred_element_type=F32)


def split(value):
    high = value.astype(BF16)
    low = (value - high.astype(F32)).astype(BF16)
    return high, low


def beside(value):
    return jnp.concatenate(split(value), 1)


def twice(value):
    return jnp.concatenate([value, value], 0)


def factor(value):
    high, low = split(value)
    return jnp.concatenate(
        [jnp.concatenate([high, low], 1), jnp.concatenate([high, jnp.zeros_like(low)], 1)], 0
    )


def product(left_pair, right_factor):
    both = dot(left_pair, right_factor)
    half = both.shape[1] // 2
    return both[:, :half] + both[:, half:]


def pack_kernel(queries, keys, values, betas, log_gates, starts, out):
    heads = queries.shape[1] // DK
    for head in range(heads):
        for step in range(NH):
            column = (head * NH + step) * DK
            out[head, KEY_ROW + step * TOK : KEY_ROW + (step + 1) * TOK, :] = keys[
                :, column : column + DK
            ]
            out[head, VALUE_ROW + step * TOK : VALUE_ROW + (step + 1) * TOK, :] = values[
                :, column : column + DV
            ]
        out[head, QUERY_ROW : QUERY_ROW + TOK, :] = queries[:, head * DK : (head + 1) * DK]
    pieces = []
    for step in range(NH):
        pick = (iota((heads, heads * NH), 1) == iota((heads, heads * NH), 0) * NH + step).astype(
            BF16
        )
        pieces.append(dot_nt(pick, betas[...]))
    same = (iota((heads, heads), 0) == iota((heads, heads), 1)).astype(BF16)
    pieces.append(dot_nt(same, log_gates[...]))
    pieces.append(jnp.broadcast_to(starts[...].astype(F32), (heads, TOK)))
    scales = jnp.concatenate(pieces, 1).astype(BF16)
    for head in range(heads):
        out[head, SCALE_ROW:PACK_ROWS, :] = jnp.broadcast_to(
            scales[head : head + 1, :], (SCALE_ROWS, 4 * TOK)
        )


def pack(queries, keys, values, betas, log_gates, starts):
    heads = queries.shape[1] // DK
    return pl.pallas_call(
        pack_kernel,
        out_shape=jax.ShapeDtypeStruct((heads, PACK_ROWS, DK), BF16),
        compiler_params=pltpu.CompilerParams(vmem_limit_bytes=32 * 2**20),
        name="pack",
    )(queries, keys, values, betas, log_gates, starts)


def place(index):
    block = index // (NH * TOK)
    step = (index // TOK) % NH
    token = index % TOK
    return block, step, token, (block * TOK + token) * NH + step


def scale_maps():
    shape = (REFL, 8 * TOK)
    block, step, token, _ = place(iota(shape, 0))
    column = iota(shape, 1)
    source_block = column // (4 * TOK)
    kind = (column // TOK) % 4
    source = source_block * TOK + column % TOK
    now = block * TOK + token
    decay = (kind == NH) & (source <= now)
    segment = (kind == NH + 1) & (source <= now)
    beta = (kind == step) & (source == now)
    return jnp.concatenate([part.astype(F32) for part in (decay, segment, beta)], 0).astype(BF16)


def piece_rows(size):
    if size == TOK:
        return [slice(NH * TOK, 2 * NH * TOK)]
    return [
        slice(start, start + size)
        for part in range(2 * NH)
        for start in range(part * TOK + size, (part + 1) * TOK, 2 * size)
    ]


def taken(value, slices):
    return jnp.concatenate([value[each] for each in slices], 0) if len(slices) > 1 else value[slices[0]]


def put(base, rows, slices):
    pieces = []
    at = 0
    done = 0
    for each in slices:
        if each.start > at:
            pieces.append(base[at : each.start])
        size = each.stop - each.start
        pieces.append(base[each] + rows[done : done + size])
        done += size
        at = each.stop
    if at < REFL:
        pieces.append(base[at:])
    return jnp.concatenate(pieces, 0)


def inverses(lowers):
    small = 8
    count = len(lowers)
    lane = iota((small, REFL), 1)
    group_of = (lane // (NH * TOK)) * (TOK // small) + (lane % TOK) // small
    groups = [(block, piece) for block in range(2) for piece in range(TOK // small)]

    def start_row(block, step, piece):
        return block * NH * TOK + step * TOK + piece * small

    folded = []
    for lower in lowers:
        for step in range(NH):
            rows = jnp.zeros((small, REFL), F32)
            for number, (block, piece) in enumerate(groups):
                first = start_row(block, step, piece)
                rows = jnp.where(group_of == number, lower[first : first + small], rows)
            folded.append(rows)
    height = NH * small
    lower_fold = jnp.concatenate(folded, 0)
    wide = iota((count * height, REFL), 1)
    high = iota((count * height, REFL), 0) % height
    inverse = ((wide // TOK) % NH == high // small) & (wide % small == high % small)
    inverse = inverse.astype(F32).reshape(count, height, REFL)
    for token in range(small):
        for step in range(NH):
            if token == small - 1 and step == NH - 1:
                continue
            source = (wide // (NH * TOK)) * (NH * TOK) + step * TOK + (wide % TOK) // small * small + token
            column = jnp.take_along_axis(lower_fold, source, axis=1, mode="promise_in_bounds")
            row = step * small + token
            inverse = inverse - column.reshape(count, height, REFL) * inverse[:, row : row + 1, :]
    results = []
    for number in range(count):
        pieces = []
        for block in range(2):
            for step in range(NH):
                rows = inverse[number, step * small : (step + 1) * small]
                for piece in range(TOK // small):
                    mine = group_of == block * (TOK // small) + piece
                    pieces.append(jnp.where(mine, rows, 0.0))
        results.append(jnp.concatenate(pieces, 0))
    size = small
    zero = jnp.zeros((REFL, REFL), F32)
    while size < CHUNK:
        slices = piece_rows(size)
        row_block, _, row_token, _ = place(iota((REFL, REFL), 0))
        column_block, _, column_token, _ = place(iota((REFL, REFL), 1))
        row_piece = (row_block * TOK + row_token) // size
        column_piece = (column_block * TOK + column_token) // size
        linked = taken(row_piece, slices) == taken(column_piece, slices) + 1
        crossings = [
            product(beside(jnp.where(linked, taken(lower, slices), 0.0)), factor(result))
            for lower, result in zip(lowers, results)
        ]
        changes = [
            product(beside(taken(result, slices)), factor(put(zero, crossing, slices)))
            for crossing, result in zip(crossings, results)
        ]
        results = [put(result, -change, slices) for change, result in zip(changes, results)]
        size *= 2
    return results


def chunk_rows(packed, chunk, first, count):
    return jnp.concatenate(
        [packed[2 * chunk, first : first + count, :], packed[2 * chunk + 1, first : first + count, :]], 0
    )


def read_rows(value):
    return jnp.concatenate(
        [
            value[(NH - 1) * TOK : NH * TOK],
            value[(2 * NH - 1) * TOK : 2 * NH * TOK],
        ],
        0,
    )


def head_kernel(packed, *rest):
    entry, out, leave = rest if len(rest) == 3 else (None, rest[0], None)
    chunks = packed.shape[0] // 2
    scales = packed[:, SCALE_ROW:PACK_ROWS, :].reshape(2 * chunks * SCALE_ROWS, 4 * TOK)
    picks = []
    for block in range(2):
        shape = (chunks, 2 * chunks * SCALE_ROWS)
        pick = iota(shape, 1) == (2 * iota(shape, 0) + block) * SCALE_ROWS
        picks.append(dot(pick.astype(BF16), scales))
    by_chunk = jnp.concatenate(picks, 1).astype(BF16)
    maps = scale_maps()
    as_rows = dot_nt(by_chunk, maps)
    as_columns = dot_nt(maps, by_chunk)
    decay_row, segment_row, beta_row = (
        as_rows[:, number * REFL : (number + 1) * REFL] for number in range(3)
    )
    decay_column, segment_column, beta_column = (
        as_columns[number * REFL : (number + 1) * REFL] for number in range(3)
    )
    carried_row = jnp.exp(decay_row) * (segment_row == 0).astype(F32)
    carried_column = jnp.exp(decay_column) * (segment_column == 0).astype(F32)
    last = REFL - 1
    end_row = jnp.exp(decay_row[:, last:] - decay_row) * (segment_row[:, last:] == segment_row).astype(F32)
    square = (REFL, REFL)
    _, _, _, row_time = place(iota(square, 0))
    _, _, _, column_time = place(iota(square, 1))
    causal = row_time >= column_time
    strict = row_time > column_time
    diagonal = row_time == column_time
    state = jnp.zeros((DV, DK), F32) if entry is None else entry[...]
    for base in range(0, chunks, GROUP):
        members = range(base, min(base + GROUP, chunks))
        keys = [chunk_rows(packed, chunk, KEY_ROW, NH * TOK) for chunk in members]
        grams = [dot_nt(key, key) for key in keys]
        squares = [jnp.where(diagonal, gram, 0.0) for gram in grams]
        norm_rows = [lax.rsqrt(jnp.sum(each, 0, keepdims=True) + EPSILON) for each in squares]
        norm_columns = [lax.rsqrt(jnp.sum(each, 1, keepdims=True) + EPSILON) for each in squares]
        ratios = []
        lowers = []
        for number, chunk in enumerate(members):
            linked = causal & (segment_column[:, chunk : chunk + 1] == segment_row[chunk : chunk + 1])
            gap = decay_column[:, chunk : chunk + 1] - decay_row[chunk : chunk + 1]
            ratio = jnp.where(linked, jnp.exp(jnp.minimum(gap, 0.0)), 0.0) * norm_rows[number]
            ratios.append(read_rows(ratio))
            strengths = beta_column[:, chunk : chunk + 1] * norm_columns[number]
            lowers.append(jnp.where(strict, strengths * ratio * grams[number], 0.0))
        solved = inverses(lowers)
        factors = [factor(each) for each in solved]
        beta_rows = [beta_row[chunk : chunk + 1] for chunk in members]
        kept_rows = [
            beta_row[chunk : chunk + 1] * carried_row[chunk : chunk + 1] * norm
            for chunk, norm in zip(members, norm_rows)
        ]
        turned_keys = [key.T for key in keys]
        ends = [
            product(beside(turned.astype(F32) * (end_row[chunk : chunk + 1] * norm)), each)
            for chunk, turned, norm, each in zip(members, turned_keys, norm_rows, factors)
        ]
        same = (iota((DK, DK), 0) == iota((DK, DK), 1)).astype(F32)
        transitions = [
            carried_row[chunk : chunk + 1, last:] * same
            - dot_nt(jnp.concatenate([turned, turned], 1), beside(end * kept))
            for chunk, turned, end, kept in zip(members, turned_keys, ends, kept_rows)
        ]
        values = [chunk_rows(packed, chunk, VALUE_ROW, NH * TOK) for chunk in members]
        turned_values = [value.T for value in values]
        injects = [
            dot_nt(jnp.concatenate([turned, turned], 1), beside(end * beta))
            for turned, end, beta in zip(turned_values, ends, beta_rows)
        ]
        queries = [chunk_rows(packed, chunk, QUERY_ROW, TOK) for chunk in members]
        scores = [
            product(beside(dot_nt(query, key) * ratio), each)
            for query, key, ratio, each in zip(queries, keys, ratios, factors)
        ]
        inner = [
            dot(beside(score * beta), twice(value))
            for score, beta, value in zip(scores, beta_rows, values)
        ]
        readers = [
            read_rows(carried_column[:, chunk : chunk + 1]) * query.astype(F32)
            - dot(beside(score * kept), twice(key))
            for chunk, query, score, kept, key in zip(members, queries, scores, kept_rows, keys)
        ]
        for number, chunk in enumerate(members):
            high, low = split(state)
            turned = jnp.concatenate(
                [jnp.concatenate([high, high], 1), jnp.concatenate([low, jnp.zeros_like(low)], 1)], 0
            )
            both = dot_nt(beside(readers[number]), turned)
            result = inner[number] + both[:, :DV] + both[:, DV:]
            out[chunk * CHUNK : (chunk + 1) * CHUNK, :] = result.astype(BF16)
            state = product(jnp.concatenate([high, low], 1), factor(transitions[number])) + injects[number]
    if leave is not None:
        leave[...] = state


def head_recurrence(packed, entry=None):
    blocks = packed.shape[0]
    out = jax.ShapeDtypeStruct((blocks * TOK, DV), BF16)
    state = jax.ShapeDtypeStruct((DV, DK), F32)
    return pl.pallas_call(
        head_kernel,
        out_shape=out if entry is None else (out, state),
        compiler_params=pltpu.CompilerParams(vmem_limit_bytes=48 * 2**20),
        name="head_recurrence",
    )(*((packed,) if entry is None else (packed, entry)))


def local(queries, keys, values, betas, log_gates, starts):
    at = lax.axis_index("head") * TOK
    own_starts = lax.dynamic_slice(starts, (at,), (TOK,)).reshape(1, TOK)
    packed = pack(queries, keys, values, betas, log_gates, own_starts)
    groups = lax.axis_size("head")
    places = packed.shape[0] // groups
    packed = packed.reshape(groups, places, PACK_ROWS, DK).transpose(1, 0, 2, 3)
    packed = packed.reshape(groups * places, PACK_ROWS, DK)
    received = lax.all_to_all(packed, ("place", "head"), split_axis=0, concat_axis=0, tiled=True)
    spans = lax.axis_size("span")
    if spans == 1:
        out = head_recurrence(received)
    else:
        forward = [(index, index + 1) for index in range(spans - 1)]

        def advance(_, carry):
            entry, _ = carry
            out, leave = head_recurrence(received, entry)
            return lax.ppermute(leave, "span", forward), out

        nothing = jnp.zeros((received.shape[0] * TOK, DV), BF16)
        _, out = lax.fori_loop(0, spans, advance, (jnp.zeros((DV, DK), F32), nothing))
    out = out.reshape(places, out.shape[0] // places, DV)
    out = lax.all_to_all(out, "place", split_axis=0, concat_axis=0, tiled=True)
    return out.transpose(1, 0, 2).reshape(out.shape[1], places * DV)


def solution(mesh):
    groups = mesh.shape["head"]

    def run(queries, keys, values, betas, log_gates, starts):
        places = log_gates.shape[1] // groups
        spans = mesh.shape["seq"] // places
        split_mesh = Mesh(
            mesh.devices.reshape(spans, places, groups), ("span", "place", "head")
        )
        rows = P(("span", "place", "head"), None)
        return jax.shard_map(
            local,
            mesh=split_mesh,
            in_specs=(rows, rows, rows, rows, rows, P(("span", "place"))),
            out_specs=P(("span", "place"), "head"),
            check_vma=False,
        )(queries, keys, values, betas, log_gates, starts)

    return run
```

time: 208 us -> 69.4 us (0.33)
  the two profiles are of different devices: /device:TPU:12 before, /device:TPU:0 now
where the time goes in v1:
time: 69.4 us; the launch traced here: 69.1 us
  blocking collectives  51.5 us (74%)
  Pallas kernels  12.2 us (18%)
  local copies, waits for them, and re-layouts  5.36 us (8%)
    all_to_all x1, blocking collectives, local(): lax.all_to_all(packed, ('place', 'head'), split_axis=0, concat_axis=0, ti...  41.4 us
    pallas_call x1, Pallas kernels, head_recurrence(): pl.pallas_call(head_kernel, out_shape=out if entry is None else (out, sta...  11.7 us
    all_to_all x1, blocking collectives, local(): out = lax.all_to_all(out, 'place', split_axis=0, concat_axis=0, tiled=True)  10.1 us
    unnamed x12, local copies, waits for them, and re-layouts  4.43 us

profile of v1, /device:TPU:0, one launch (start us, length us, event | category | flops | bytes accessed | tf_op | source)
XLA Modules:
  0.0 69.1 jit_solution(16888684584810590403)
XLA Ops:
  0.0 0.0 copy-start
  0.0 0.0 copy-done
  0.0 0.1 dynamic-slice_bitcast_fusion.starts
  0.1 0.0 copy-start.1
  0.1 1.0 %copy-done.1 = bf16[32,8192]{1,0:T(8,128)(2,1)S(1)} copy-done((bf16[32,8192]{1,0:T(8,128)(2,1)S(1)}, bf16[32,8192]{1,0:T(8,128)(2,1)}, u32[]{:S(2)}) %copy-start.1) | copy-done | bytes 524312
  1.1 0.0 copy-start.2
  1.1 1.0 %copy-done.2 = bf16[32,8192]{1,0:T(8,128)(2,1)S(1)} copy-done((bf16[32,8192]{1,0:T(8,128)(2,1)S(1)}, bf16[32,8192]{1,0:T(8,128)(2,1)}, u32[]{:S(2)}) %copy-start.2) | copy-done | bytes 524312
  2.2 0.0 copy-start.3
  2.2 0.9 %copy-done.3 = bf16[32,4096]{1,0:T(8,128)(2,1)S(1)} copy-done((bf16[32,4096]{1,0:T(8,128)(2,1)S(1)}, bf16[32,4096]{1,0:T(8,128)(2,1)}, u32[]{:S(2)}) %copy-start.3) | copy-done | bytes 262168
  3.1 0.0 copy-start.4
  3.1 0.7 %copy-done.4 = bf16[32,64]{1,0:T(8,128)(2,1)S(1)} copy-done((bf16[32,64]{1,0:T(8,128)(2,1)S(1)}, bf16[32,64]{1,0:T(8,128)(2,1)}, u32[]{:S(2)}) %copy-start.4) | copy-done | bytes 4120
  3.8 0.0 copy-start.5
  3.8 0.7 %copy-done.5 = bf16[32,32]{1,0:T(8,128)(2,1)S(1)} copy-done((bf16[32,32]{1,0:T(8,128)(2,1)S(1)}, bf16[32,32]{1,0:T(8,128)(2,1)}, u32[]{:S(2)}) %copy-start.5) | copy-done | bytes 2072
  4.5 0.5 pack.1
  5.0 0.1 copy.7
  5.1 41.4 %all_to_all.10.packed = bf16[32,176,128]{2,1,0:T(8,128)(2,1)S(1)} all-to-all(bf16[32,176,128]{2,1,0:T(8,128)(2,1)S(1)} %bitcast.15), channel_id=1, replica_groups=mesh['seq'=8,'head'=4] {'seq','head'}, dimensions={0} | all-to-all | bytes 2883584 | tf_op jit(solution)/shard_map/all_to_all | solution.py:355
  46.5 11.7 %head_recurrence.1 = bf16[1024,128]{1,0:T(8,128)(2,1)S(1)} custom-call(bf16[32,176,128]{2,1,0:T(8,128)(2,1)S(1)} %all_to_all.10.packed), custom_call_target="tpu_custom_call" | custom-call | tf_op jit(solution)/shard_map/head_recurrence/pallas_call | solution.py:339
  58.2 10.1 %all_to_all.11 = bf16[8,128,128]{2,1,0:T(8,128)(2,1)S(1)} all-to-all(bf16[8,128,128]{2,1,0:T(8,128)(2,1)S(1)} %bitcast.14), channel_id=1, replica_groups=mesh['seq'=8,'head'=4] {'seq'}, dimensions={0} | all-to-all | bytes 524288 | tf_op jit(solution)/shard_map/all_to_all | solution.py:370
  68.3 0.7 %copy_bitcast_fusion = bf16[128,1024]{1,0:T(8,128)(2,1)} fusion(bf16[8,128,128]{2,1,0:T(8,128)(2,1)S(1)} %all_to_all.11), kind=kLoop, calls=%fused_computation | loop fusion | bytes 524288 | tf_op jit(solution)/shard_map/reshape | solution.py:371
Async XLA Ops:
  0.1 1.0 %copy-start.1 = (bf16[32,8192]{1,0:T(8,128)(2,1)S(1)}, bf16[32,8192]{1,0:T(8,128)(2,1)}, u32[]{:S(2)}) copy-start(bf16[32,8192]{1,0:T(8,128)(2,1)} %keys.1) | copy-start | bytes 1572868
  1.1 1.0 %copy-start.2 = (bf16[32,8192]{1,0:T(8,128)(2,1)S(1)}, bf16[32,8192]{1,0:T(8,128)(2,1)}, u32[]{:S(2)}) copy-start(bf16[32,8192]{1,0:T(8,128)(2,1)} %values.1) | copy-start | bytes 1572868
  2.2 0.9 %copy-start.3 = (bf16[32,4096]{1,0:T(8,128)(2,1)S(1)}, bf16[32,4096]{1,0:T(8,128)(2,1)}, u32[]{:S(2)}) copy-start(bf16[32,4096]{1,0:T(8,128)(2,1)} %queries.1) | copy-start | bytes 786436
  3.1 0.7 %copy-start.4 = (bf16[32,64]{1,0:T(8,128)(2,1)S(1)}, bf16[32,64]{1,0:T(8,128)(2,1)}, u32[]{:S(2)}) copy-start(bf16[32,64]{1,0:T(8,128)(2,1)} %betas.1) | copy-start | bytes 12292
  3.8 0.7 %copy-start.5 = (bf16[32,32]{1,0:T(8,128)(2,1)S(1)}, bf16[32,32]{1,0:T(8,128)(2,1)}, u32[]{:S(2)}) copy-start(bf16[32,32]{1,0:T(8,128)(2,1)} %log_gates.1) | copy-start | bytes 6148
  (1 other events, 0.0 us)

commit v2 on v1

v2 whole, which is shorter than its diff:
```python
import jax
import jax.numpy as jnp
from jax import lax
from jax.experimental import pallas as pl
from jax.experimental.pallas import tpu as pltpu
from jax.sharding import Mesh
from jax.sharding import PartitionSpec as P

DK = 128
DV = 128
NH = 2
TOK = 32
CHUNK = 2 * TOK
REFL = CHUNK * NH
GROUP = 8
EPSILON = 1e-06

KEY_ROWS = NH * TOK
SCALE_ROWS = 16

BF16 = jnp.bfloat16
F32 = jnp.float32
NT = (((1,), (1,)), ((), ()))


def iota(shape, axis):
    return lax.broadcasted_iota(jnp.int32, shape, axis)


def dot(left, right):
    return jnp.dot(left, right, preferred_element_type=F32)


def dot_nt(left, right):
    return lax.dot_general(left, right, NT, preferred_element_type=F32)


def split(value):
    high = value.astype(BF16)
    low = (value - high.astype(F32)).astype(BF16)
    return high, low


def beside(value):
    return jnp.concatenate(split(value), 1)


def twice(value):
    return jnp.concatenate([value, value], 0)


def factor(value):
    return factor_of(*split(value))


def factor_of(high, low):
    return jnp.concatenate(
        [jnp.concatenate([high, low], 1), jnp.concatenate([high, jnp.zeros_like(low)], 1)], 0
    )


def product(left_pair, right_factor):
    both = dot(left_pair, right_factor)
    half = both.shape[1] // 2
    return both[:, :half] + both[:, half:]


def place(index):
    block = index // (NH * TOK)
    step = (index // TOK) % NH
    token = index % TOK
    return block, step, token, (block * TOK + token) * NH + step


def scale_maps():
    shape = (REFL, 8 * TOK)
    block, step, token, _ = place(iota(shape, 0))
    column = iota(shape, 1)
    source_block = column // (4 * TOK)
    kind = (column // TOK) % 4
    source = source_block * TOK + column % TOK
    now = block * TOK + token
    decay = (kind == NH) & (source <= now)
    segment = (kind == NH + 1) & (source <= now)
    beta = (kind == step) & (source == now)
    return jnp.concatenate([part.astype(F32) for part in (decay, segment, beta)], 0).astype(BF16)


def piece_rows(size):
    if size == TOK:
        return [slice(NH * TOK, 2 * NH * TOK)]
    return [
        slice(start, start + size)
        for part in range(2 * NH)
        for start in range(part * TOK + size, (part + 1) * TOK, 2 * size)
    ]


def taken(value, slices):
    return jnp.concatenate([value[each] for each in slices], 0) if len(slices) > 1 else value[slices[0]]


def put(base, rows, slices):
    pieces = []
    at = 0
    done = 0
    for each in slices:
        if each.start > at:
            pieces.append(base[at : each.start])
        size = each.stop - each.start
        pieces.append(base[each] + rows[done : done + size])
        done += size
        at = each.stop
    if at < REFL:
        pieces.append(base[at:])
    return jnp.concatenate(pieces, 0)


def inverses(lowers):
    small = 8
    count = len(lowers)
    lane = iota((small, REFL), 1)
    group_of = (lane // (NH * TOK)) * (TOK // small) + (lane % TOK) // small
    groups = [(block, piece) for block in range(2) for piece in range(TOK // small)]

    def start_row(block, step, piece):
        return block * NH * TOK + step * TOK + piece * small

    folded = []
    for lower in lowers:
        for step in range(NH):
            rows = jnp.zeros((small, REFL), F32)
            for number, (block, piece) in enumerate(groups):
                first = start_row(block, step, piece)
                rows = jnp.where(group_of == number, lower[first : first + small], rows)
            folded.append(rows)
    height = NH * small
    lower_fold = jnp.concatenate(folded, 0)
    wide = iota((count * height, REFL), 1)
    high = iota((count * height, REFL), 0) % height
    inverse = ((wide // TOK) % NH == high // small) & (wide % small == high % small)
    inverse = inverse.astype(F32).reshape(count, height, REFL)
    for token in range(small):
        for step in range(NH):
            if token == small - 1 and step == NH - 1:
                continue
            source = (wide // (NH * TOK)) * (NH * TOK) + step * TOK + (wide % TOK) // small * small + token
            column = jnp.take_along_axis(lower_fold, source, axis=1, mode="promise_in_bounds")
            row = step * small + token
            inverse = inverse - column.reshape(count, height, REFL) * inverse[:, row : row + 1, :]
    results = []
    for number in range(count):
        pieces = []
        for block in range(2):
            for step in range(NH):
                rows = inverse[number, step * small : (step + 1) * small]
                for piece in range(TOK // small):
                    mine = group_of == block * (TOK // small) + piece
                    pieces.append(jnp.where(mine, rows, 0.0))
        results.append(jnp.concatenate(pieces, 0))
    size = small
    zero = jnp.zeros((REFL, REFL), F32)
    while size < CHUNK:
        slices = piece_rows(size)
        row_block, _, row_token, _ = place(iota((REFL, REFL), 0))
        column_block, _, column_token, _ = place(iota((REFL, REFL), 1))
        row_piece = (row_block * TOK + row_token) // size
        column_piece = (column_block * TOK + column_token) // size
        linked = taken(row_piece, slices) == taken(column_piece, slices) + 1
        crossings = [
            product(beside(jnp.where(linked, taken(lower, slices), 0.0)), factor(result))
            for lower, result in zip(lowers, results)
        ]
        changes = [
            product(beside(taken(result, slices)), factor(put(zero, crossing, slices)))
            for crossing, result in zip(crossings, results)
        ]
        results = [put(result, -change, slices) for change, result in zip(changes, results)]
        size *= 2
    return results


def read_rows(value):
    return jnp.concatenate(
        [
            value[(NH - 1) * TOK : NH * TOK],
            value[(2 * NH - 1) * TOK : 2 * NH * TOK],
        ],
        0,
    )


def call(kernel, outs, *args, scratch=(), flops=0, name=None):
    return pl.pallas_call(
        kernel,
        out_shape=outs,
        scratch_shapes=scratch,
        compiler_params=pltpu.CompilerParams(vmem_limit_bytes=24 * 2**20),
        cost_estimate=pl.CostEstimate(flops=flops, bytes_accessed=0, transcendentals=0),
        name=name,
    )(*args)


def shape(*sizes, dtype=BF16):
    return jax.ShapeDtypeStruct(sizes, dtype)


def axis_index(axis):
    return lax.axis_index(axis).astype(jnp.int32)


class Sizes:
    def __init__(self, groups, group_heads, chips):
        self.groups = groups
        self.group_heads = group_heads
        self.heads = group_heads // 2
        self.chips = chips
        self.units = self.heads * groups
        self.swapped = chips == self.heads and chips & (chips - 1) == 0

    def unit(self, number):
        return number // self.groups, number % self.groups


def shifted(index, by, size):
    moved = index + by
    return jnp.where(moved >= size, moved - size, moved)


def block_columns(source, first, count):
    return [
        source[:, pl.ds(pl.multiple_of(first + number * DK, DK), DK)] for number in range(count)
    ]


def pack_keys(sizes, keys, betas, log_gates, starts):
    rows = sizes.heads * KEY_ROWS
    count = sizes.heads * NH

    def kernel(keys, betas, log_gates, starts, *outs):
        z = axis_index("head")
        core = axis_index("core")
        heads = log_gates.shape[1]
        pieces = []
        for step in range(NH):
            extent = (heads, heads * NH)
            pick = iota(extent, 1) == iota(extent, 0) * NH + step
            pieces.append(dot_nt(pick.astype(BF16), betas[...]))
        same = iota((heads, heads), 0) == iota((heads, heads), 1)
        pieces.append(dot_nt(same.astype(BF16), log_gates[...]))
        pieces.append(jnp.broadcast_to(starts[...].astype(F32), (heads, TOK)))
        scales = jnp.concatenate(pieces, 1).astype(BF16)
        for ahead, out in enumerate(outs):
            target = shifted(z, ahead, sizes.groups)
            for side in range(2):
                owner = jnp.bitwise_xor(core, side)
                first = ((target * 2 + owner) * sizes.heads) * NH * DK
                for number, piece in enumerate(block_columns(keys, first, count)):
                    at = side * rows + number * TOK
                    out[at : at + TOK, :] = piece
            extent = (SCALE_ROWS, heads)
            pick = (iota(extent, 1) == target * sizes.group_heads + iota(extent, 0)) & (
                iota(extent, 0) < sizes.group_heads
            )
            out[2 * rows :, :] = dot(pick.astype(BF16), scales).astype(BF16)

    outs = [shape(2 * rows + SCALE_ROWS, DK)] * sizes.groups
    return call(kernel, outs, keys, betas, log_gates, starts, name="pack_keys")


def swap_keys(sizes, arrived):
    rows = sizes.heads * KEY_ROWS

    def kernel(*refs):
        out = refs[-1]
        z = axis_index("head")
        for behind, piece in enumerate(refs[:-1]):
            source = shifted(z, sizes.groups - behind, sizes.groups) if behind else z
            out[source] = piece[rows:, :]

    return call(kernel, shape(sizes.groups, rows + SCALE_ROWS, DK), *arrived, name="swap_keys")


def pack_reads(sizes, values, queries):
    value_rows = sizes.heads * KEY_ROWS
    rows = value_rows + sizes.heads * TOK

    def kernel(values, queries, kept, sent):
        z = axis_index("head")
        core = axis_index("core")
        for ahead in range(sizes.groups):
            target = shifted(z, ahead, sizes.groups)
            for side, out in enumerate((kept, sent)):
                first = (target * 2 + jnp.bitwise_xor(core, side)) * sizes.heads * DK
                pieces = block_columns(values, first * NH, sizes.heads * NH)
                pieces += block_columns(queries, first, sizes.heads)
                for number, piece in enumerate(pieces):
                    out[ahead, number * TOK : (number + 1) * TOK, :] = piece

    return call(
        kernel, [shape(sizes.groups, rows, DK)] * 2, values, queries, name="pack_reads"
    )


def merge_reads(sizes, kept, swapped):
    value_rows = sizes.heads * KEY_ROWS
    query_rows = sizes.heads * TOK

    def kernel(kept, swapped, *outs):
        for ahead in range(sizes.groups):
            for side, source in enumerate((kept, swapped)):
                outs[ahead][side] = source[ahead, :value_rows, :]
                outs[sizes.groups + ahead][side] = source[ahead, value_rows:, :]

    outs = [shape(2, value_rows, DK)] * sizes.groups + [shape(2, query_rows, DK)] * sizes.groups
    merged = call(kernel, outs, kept, swapped, name="merge_reads")
    return merged[: sizes.groups], merged[sizes.groups :]


def gather(sizes, pieces, scratch):
    z = axis_index("head")
    core = axis_index("core")
    for behind, piece in enumerate(pieces):
        source = shifted(z, sizes.groups - behind, sizes.groups) if behind else z
        for side in range(2):
            scratch[jnp.bitwise_xor(core, side) * sizes.groups + source] = piece[side]


def unit_rows(scratch, head, chunk, count):
    first = head * count
    return jnp.concatenate(
        [
            scratch[2 * chunk, first : first + count, :],
            scratch[2 * chunk + 1, first : first + count, :],
        ],
        0,
    )


def key_stage(sizes, arrived, swapped):
    rows = sizes.heads * KEY_ROWS
    units = sizes.units
    groups = sizes.groups

    def kernel(*refs):
        pieces = refs[:groups]
        swapped = refs[groups]
        keys_out, inverse_out, end_out, ratio_out, row_out, step_out, prefix_out = refs[
            groups + 1 : groups + 8
        ]
        totals = refs[groups + 8 : groups + 8 + sizes.heads]
        blocks, scales, every = refs[groups + 8 + sizes.heads :]
        z = axis_index("head")
        core = axis_index("core")
        for behind, piece in enumerate(pieces):
            source = shifted(z, groups - behind, groups) if behind else z
            blocks[core * groups + source] = piece[:rows, :]
            scales[core * groups + source] = piece[2 * rows :, :]
        other = (1 - core) * groups
        for source in range(groups):
            blocks[other + source] = swapped[source, :rows, :]
            scales[other + source] = swapped[source, rows:, :]
        flat = scales[...].reshape(2 * groups * SCALE_ROWS, 4 * TOK)
        picks = []
        for block in range(2):
            extent = (units, 2 * groups * SCALE_ROWS)
            unit = iota(extent, 0)
            row = (unit % groups * 2 + block) * SCALE_ROWS + unit // groups
            pick = iota(extent, 1) == row + core * sizes.heads
            picks.append(dot(pick.astype(BF16), flat))
        by_unit = jnp.concatenate(picks, 1).astype(BF16)
        maps = scale_maps()
        as_rows = dot_nt(by_unit, maps)
        as_columns = dot_nt(maps, by_unit)
        decay_row, segment_row, beta_row = (
            as_rows[:, number * REFL : (number + 1) * REFL] for number in range(3)
        )
        decay_column, segment_column, beta_column = (
            as_columns[number * REFL : (number + 1) * REFL] for number in range(3)
        )
        carried_row = jnp.exp(decay_row) * (segment_row == 0).astype(F32)
        last = REFL - 1
        end_row = jnp.exp(decay_row[:, last:] - decay_row)
        end_row = end_row * (segment_row[:, last:] == segment_row).astype(F32)
        square = (REFL, REFL)
        _, _, _, row_time = place(iota(square, 0))
        _, _, _, column_time = place(iota(square, 1))
        causal = row_time >= column_time
        strict = row_time > column_time
        diagonal = row_time == column_time
        same = (iota((DK, DK), 0) == iota((DK, DK), 1)).astype(F32)
        row_out[0] = beta_row
        row_out[2] = carried_row
        for base in range(0, units, GROUP):
            members = range(base, min(base + GROUP, units))
            keys = [unit_rows(blocks, *sizes.unit(unit), KEY_ROWS) for unit in members]
            grams = [dot_nt(key, key) for key in keys]
            squares = [jnp.where(diagonal, gram, 0.0) for gram in grams]
            norm_rows = [lax.rsqrt(jnp.sum(each, 0, keepdims=True) + EPSILON) for each in squares]
            norm_columns = [
                lax.rsqrt(jnp.sum(each, 1, keepdims=True) + EPSILON) for each in squares
            ]
            lowers = []
            for number, unit in enumerate(members):
                keys_out[unit] = keys[number]
                one = slice(unit, unit + 1)
                linked = causal & (segment_column[:, one] == segment_row[one])
                gap = decay_column[:, one] - decay_row[one]
                ratio = jnp.where(linked, jnp.exp(jnp.minimum(gap, 0.0)), 0.0) * norm_rows[number]
                ratio_out[unit] = read_rows(ratio)
                strengths = beta_column[:, one] * norm_columns[number]
                lowers.append(jnp.where(strict, strengths * ratio * grams[number], 0.0))
            solved = inverses(lowers)
            pairs = [split(each) for each in solved]
            kept_rows = [
                beta_row[unit : unit + 1] * carried_row[unit : unit + 1] * norm
                for unit, norm in zip(members, norm_rows)
            ]
            turned_keys = [key.T for key in keys]
            ends = []
            for number, unit in enumerate(members):
                high, low = pairs[number]
                inverse_out[unit] = jnp.concatenate([high, low], 1)
                row_out[1, unit : unit + 1, :] = kept_rows[number]
                weights = end_row[unit : unit + 1] * norm_rows[number]
                ends.append(
                    product(
                        beside(turned_keys[number].astype(F32) * weights), factor_of(high, low)
                    )
                )
            for number, unit in enumerate(members):
                turned = turned_keys[number]
                end_out[unit] = beside(ends[number] * beta_row[unit : unit + 1])
                every[unit] = carried_row[unit : unit + 1, last:] * same - dot_nt(
                    jnp.concatenate([turned, turned], 1), beside(ends[number] * kept_rows[number])
                )
        prefixes = [same] * sizes.heads
        for chunk in range(groups):
            for head in range(sizes.heads):
                unit = head * groups + chunk
                step = every[unit]
                high, low = split(step)
                step_out[unit] = jnp.concatenate([high, low], 1)
                prefix_out[unit] = prefixes[head]
                if chunk == 0:
                    prefixes[head] = step
                else:
                    prefixes[head] = product(beside(prefixes[head]), factor_of(high, low))
        if sizes.swapped:
            for head in range(sizes.heads):
                every[head] = prefixes[head]
            chip = axis_index("chip")
            for number in range(sizes.heads):
                totals[number][...] = every[jnp.bitwise_xor(chip, number)]
        else:
            for head in range(sizes.heads):
                totals[head][...] = prefixes[head]

    outs = [
        shape(units, REFL, DK),
        shape(units, REFL, 2 * REFL),
        shape(units, DK, 2 * REFL),
        shape(units, CHUNK, REFL, dtype=F32),
        shape(3, units, REFL, dtype=F32),
        shape(units, DK, 2 * DK),
        shape(units, DK, DK, dtype=F32),
    ] + [shape(DK, DK, dtype=F32)] * sizes.heads
    scratch = [
        pltpu.VMEM((2 * groups, rows, DK), BF16),
        pltpu.VMEM((2 * groups, SCALE_ROWS, DK), BF16),
        pltpu.VMEM((units, DK, DK), F32),
    ]
    results = call(
        kernel, outs, *arrived, swapped, scratch=scratch, flops=6_000_000_000, name="key_stage"
    )
    return results[:7], results[7:]


def value_stage(sizes, pieces, ends, steps):
    groups = sizes.groups

    def kernel(*refs):
        pieces = refs[:groups]
        ends, steps, values_out, before_out = refs[groups : groups + 4]
        totals = refs[groups + 4 : groups + 4 + sizes.heads]
        blocks, every = refs[groups + 4 + sizes.heads :]
        gather(sizes, pieces, blocks)
        injects = []
        for unit in range(sizes.units):
            value = unit_rows(blocks, *sizes.unit(unit), KEY_ROWS)
            values_out[unit] = value
            turned = value.T
            injects.append(dot_nt(jnp.concatenate([turned, turned], 1), ends[unit]))
        sums = [jnp.zeros((DV, DK), F32)] * sizes.heads
        for chunk in range(groups):
            for head in range(sizes.heads):
                unit = head * groups + chunk
                before_out[unit] = sums[head]
                if chunk == 0:
                    sums[head] = injects[unit]
                else:
                    step = steps[unit]
                    sums[head] = injects[unit] + product(
                        beside(sums[head]), factor_of(step[:, :DK], step[:, DK:])
                    )
        if sizes.swapped:
            for head in range(sizes.heads):
                every[head] = sums[head]
            chip = axis_index("chip")
            for number in range(sizes.heads):
                totals[number][...] = every[jnp.bitwise_xor(chip, number)]
        else:
            for head in range(sizes.heads):
                totals[head][...] = sums[head]

    outs = [shape(sizes.units, REFL, DV), shape(sizes.units, DV, DK, dtype=F32)]
    outs += [shape(DV, DK, dtype=F32)] * sizes.heads
    scratch = [
        pltpu.VMEM((2 * groups, sizes.heads * KEY_ROWS, DV), BF16),
        pltpu.VMEM((sizes.heads, DV, DK), F32),
    ]
    results = call(
        kernel, outs, *pieces, ends, steps, scratch=scratch, flops=2_000_000_000, name="value_stage"
    )
    return results[0], results[1], results[2:]


def scan_states(sizes, transitions, injects):
    chips = sizes.chips

    def kernel(*refs):
        transitions = refs[:chips]
        injects = refs[chips : 2 * chips]
        outs = refs[2 * chips : 3 * chips]
        step, inject, entry = refs[3 * chips :]
        chip = axis_index("chip")
        for number in range(chips):
            source = jnp.bitwise_xor(chip, number)
            step[source] = transitions[number][...]
            inject[source] = injects[number][...]
        state = jnp.zeros((DV, DK), F32)
        for index in range(chips):
            entry[index] = state
            if index == 0:
                state = inject[index]
            elif index < chips - 1:
                state = product(beside(state), factor(step[index])) + inject[index]
        for number in range(chips):
            outs[number][...] = entry[jnp.bitwise_xor(chip, number)]

    scratch = [pltpu.VMEM((chips, DV, DK), F32)] * 3
    return call(
        kernel,
        [shape(DV, DK, dtype=F32)] * chips,
        *transitions,
        *injects,
        scratch=scratch,
        name="scan_states",
    )


def exchanged(sizes, parts):
    return [parts[0]] + [
        lax.ppermute(part, "chip", [(chip, chip ^ number) for chip in range(sizes.chips)])
        for number, part in enumerate(parts)
        if number
    ]


def entry_states(sizes, transitions, injects):
    if sizes.swapped:
        arrived = exchanged(sizes, transitions), exchanged(sizes, injects)
        return exchanged(sizes, scan_states(sizes, *arrived))
    transition = jnp.stack(transitions)
    inject = jnp.stack(injects)
    forward = [(chip, chip + 1) for chip in range(sizes.chips - 1)]

    def advance(_, entry):
        left = jnp.einsum("hvd,hde->hve", entry, transition, precision=lax.Precision.HIGHEST)
        return lax.ppermute(left + inject, "chip", forward)

    entry = lax.fori_loop(0, sizes.chips - 1, advance, jnp.zeros_like(inject))
    return [entry[head] for head in range(sizes.heads)]


def query_stage(sizes, pieces, values, before, keys, inverses_, ratios, rows, prefixes):
    groups = sizes.groups

    def kernel(*refs):
        pieces = refs[:groups]
        values, before, keys, inverse, ratio, rows, prefix, reader_out, inner_out, blocks = refs[
            groups:
        ]
        gather(sizes, pieces, blocks)
        for base in range(0, sizes.units, GROUP):
            members = range(base, min(base + GROUP, sizes.units))
            queries = [unit_rows(blocks, *sizes.unit(unit), TOK) for unit in members]
            scores = []
            for number, unit in enumerate(members):
                pair = inverse[unit]
                score = dot_nt(queries[number], keys[unit]) * ratio[unit]
                scores.append(product(beside(score), factor_of(pair[:, :REFL], pair[:, REFL:])))
            for number, unit in enumerate(members):
                one = slice(unit, unit + 1)
                inner = dot(beside(scores[number] * rows[0, one, :]), twice(values[unit]))
                carried = read_rows(jnp.broadcast_to(rows[2, one, :], (DK, REFL)).T)
                reader = carried * queries[number].astype(F32) - dot(
                    beside(scores[number] * rows[1, one, :]), twice(keys[unit])
                )
                high, low = split(jnp.concatenate([prefix[unit], before[unit]], 0))
                pair = beside(reader)
                both = dot_nt(pair, jnp.concatenate([high, high], 1)) + dot_nt(pair[:, :DK], low)
                reader_out[unit] = beside(both[:, :DK])
                inner_out[unit] = inner + both[:, DK:]

    outs = [
        shape(sizes.units, CHUNK, 2 * DK),
        shape(sizes.units, CHUNK, DV, dtype=F32),
    ]
    scratch = [pltpu.VMEM((2 * groups, sizes.heads * TOK, DK), BF16)]
    return call(
        kernel,
        outs,
        *pieces,
        values,
        before,
        keys,
        inverses_,
        ratios,
        rows,
        prefixes,
        scratch=scratch,
        flops=3_000_000_000,
        name="query_stage",
    )


def read_states(sizes, states, readers, inners):
    groups = sizes.groups
    half = groups // 2

    def kernel(*refs):
        states = refs[: sizes.heads]
        readers, inners, own, other, entry = refs[sizes.heads :]
        core = axis_index("core")
        chip = axis_index("chip") if sizes.swapped else 0
        for number in range(sizes.heads):
            place_ = jnp.bitwise_xor(chip, number) if sizes.swapped else number
            entry[place_] = states[number][...]
        for head in range(sizes.heads):
            high, low = split(entry[head])
            stack = jnp.concatenate(
                [
                    jnp.concatenate([high, high], 1),
                    jnp.concatenate([low, jnp.zeros_like(low)], 1),
                ],
                0,
            )
            for side, out in enumerate((own, other)):
                first = head * groups + jnp.bitwise_xor(core, side) * half
                pair = readers[pl.ds(first, half)].reshape(half * CHUNK, 2 * DK)
                both = dot_nt(pair, stack)
                inner = inners[pl.ds(first, half)].reshape(half * CHUNK, DV)
                result = inner + both[:, :DV] + both[:, DV:]
                out[:, head * DV : (head + 1) * DV] = result.astype(BF16)

    outs = [shape(half * CHUNK, sizes.heads * DV)] * 2
    scratch = [pltpu.VMEM((sizes.heads, DV, DK), F32)]
    return call(kernel, outs, *states, readers, inners, scratch=scratch, name="read_states")


def join(sizes, own, other):
    width = sizes.heads * DV

    def kernel(own, other, out):
        first = axis_index("core") * width
        out[:, pl.ds(pl.multiple_of(first, width), width)] = own[...]
        out[:, pl.ds(pl.multiple_of(width - first, width), width)] = other[...]

    return call(kernel, shape(own.shape[0], 2 * width), own, other, name="join")


def local(queries, keys, values, betas, log_gates, starts):
    groups = lax.axis_size("head")
    sizes = Sizes(groups, log_gates.shape[1] // groups, lax.axis_size("chip"))
    own_starts = lax.dynamic_slice(starts, (axis_index("head") * TOK,), (TOK,)).reshape(1, TOK)

    def spread(parts):
        return [parts[0]] + [
            lax.ppermute(part, "head", [(z, (z + ahead) % groups) for z in range(groups)])
            for ahead, part in enumerate(parts)
            if ahead
        ]

    def swapped(part):
        return lax.ppermute(part, "core", [(0, 1), (1, 0)])

    arrived = spread(pack_keys(sizes, keys, betas, log_gates, own_starts))
    kept, sent = pack_reads(sizes, values, queries)
    value_parts, query_parts = merge_reads(sizes, kept, swapped(sent))
    value_parts = spread(value_parts)
    query_parts = spread(query_parts)
    other_keys = swapped(swap_keys(sizes, arrived))
    (unit_keys, inverse, ends, ratios, rows, steps, prefixes), transitions = key_stage(
        sizes, arrived, other_keys
    )
    unit_values, before, injects = value_stage(sizes, value_parts, ends, steps)
    states = entry_states(sizes, transitions, injects)
    readers, inners = query_stage(
        sizes, query_parts, unit_values, before, unit_keys, inverse, ratios, rows, prefixes
    )
    own, other = read_states(sizes, states, readers, inners)
    return join(sizes, own, swapped(other))


def solution(mesh):
    devices = mesh.devices
    rows = P(("chip", "core", "head"), None)
    return jax.shard_map(
        local,
        mesh=Mesh(
            devices.reshape(devices.shape[0] // 2, 2, devices.shape[1]), ("chip", "core", "head")
        ),
        in_specs=(rows, rows, rows, rows, rows, P(("chip", "core"))),
        out_specs=P(("chip", "core"), "head"),
        check_vma=False,
    )
```

time: 69.4 us -> 54.1 us (0.78)
  blocking collectives: 51.5 us -> 0 us
  starting transfers between devices: 0 us -> 28 us
  waiting for transfers between devices: 0 us -> 9.31 us
  local copies, waits for them, and re-layouts: 5.36 us -> 3.42 us
  Pallas kernels: 12.2 us -> 13 us
    all_to_all x2 -> x0, blocking collectives: 51.5 us -> none  [the longest x1 41.4 us: local(): lax.all_to_all(packed, ('place', 'head'), split_axis=0, concat_axis=0, ti...]
    ppermute x0 -> x21, starting transfers between devices: none -> 28 us  [the longest x9 17.2 us: spread(): lax.ppermute(part, 'head', [(z, (z + ahead) % groups) for z in range(grou...]
    ppermute x0 -> x21, waiting for transfers between devices: none -> 9.31 us  [the longest x9 6.3 us: spread(): lax.ppermute(part, 'head', [(z, (z + ahead) % groups) for z in range(grou...]
    unnamed x12, local copies, waits for them, and re-layouts: 4.43 us -> 3.35 us
    reshape x3 -> x1, local copies, waits for them, and re-layouts: 0.93 us -> 0.07 us  [local(): lax.dynamic_slice(starts, (axis_index('head') * TOK,), (TOK,))]
    pallas_call x2 -> x10, Pallas kernels: 12.2 us -> 13 us  [call(): pl.pallas_call(kernel, out_shape=outs, scratch_shapes=scratch, compiler_p...]
  transfers between devices with their start and end apart: 0 -> 21, of which waited for: 0 -> 5; matrix products, arithmetic and copies ran while one was open for 0% -> 0% of each run, Pallas kernels for 0% -> 21%
where the time goes in v2:
time: 54.1 us; the launch traced here: 53.9 us
  starting transfers between devices  28 us (52%)
  Pallas kernels  13 us (24%)
  waiting for transfers between devices  9.31 us (17%)
  local copies, waits for them, and re-layouts  3.42 us (6%)
    ppermute x9, starting transfers between devices, spread(): lax.ppermute(part, 'head', [(z, (z + ahead) % groups) for z in range(grou...  17.2 us
    pallas_call x10, Pallas kernels, call(): pl.pallas_call(kernel, out_shape=outs, scratch_shapes=scratch, compiler_p...  13 us
    ppermute x9, starting transfers between devices, exchanged(): lax.ppermute(part, 'chip', [(chip, chip ^ number) for chip in range(sizes...  10.7 us
    ppermute x9, waiting for transfers between devices, spread(): lax.ppermute(part, 'head', [(z, (z + ahead) % groups) for z in range(grou...  6.3 us
    unnamed x12, local copies, waits for them, and re-layouts  3.35 us
    ppermute x9, waiting for transfers between devices, exchanged(): lax.ppermute(part, 'chip', [(chip, chip ^ number) for chip in range(sizes...  1.66 us
    ppermute x3, waiting for transfers between devices, swapped(): return lax.ppermute(part, 'core', [(0, 1), (1, 0)])  1.34 us
  transfers between devices with their start and end apart: 21, of which 5 were waited for; matrix products, arithmetic and copies ran while one was open for 0% of the time, Pallas kernels for 21%

profile of v2, /device:TPU:0, one launch (start us, length us, event | category | flops | bytes accessed | tf_op | source)
XLA Modules:
  0.0 53.9 jit_solution(15032855759163638988)
XLA Ops:
  0.0 0.7 %copy-done = s32[128]{0:T(128)S(1)} copy-done((s32[128]{0:T(128)S(1)}, s32[128]{0:T(128)}, u32[]{:S(2)}) %copy-start) | copy-done | bytes 536
  0.7 1.0 %copy-done.1 = bf16[32,8192]{1,0:T(8,128)(2,1)S(1)} copy-done((bf16[32,8192]{1,0:T(8,128)(2,1)S(1)}, bf16[32,8192]{1,0:T(8,128)(2,1)}, u32[]{:S(2)}) %copy-start.1) | copy-done | bytes 524312
  1.8 0.7 %copy-done.5 = bf16[32,32]{1,0:T(8,128)(2,1)S(1)} copy-done((bf16[32,32]{1,0:T(8,128)(2,1)S(1)}, bf16[32,32]{1,0:T(8,128)(2,1)}, u32[]{:S(2)}) %copy-start.5) | copy-done | bytes 2072
  2.8 3.1 %collective-permute-start = (bf16[528,128]{1,0:T(8,128)(2,1)S(1)}, bf16[528,128]{1,0:T(8,128)(2,1)S(1)}, u32[]{:S(2)}, u32[]{:S(2)}) collective-permute-start(bf16[528,128]{1,0:T(8,128)(2,1)S(1)} %get-tuple-element.45), channel_id=1, source_target_pairs={{0,1},{1,2},{2,3},{3,0},{4,5},{5,6},{6,7},{7,4},{8,9},{9,10},{10,1... | collective-permute-start | bytes 405512 | tf_op jit(solution)/shard_map/ppermute | solution.py:690
  5.9 2.6 %collective-permute-start.1 = (bf16[528,128]{1,0:T(8,128)(2,1)S(1)}, bf16[528,128]{1,0:T(8,128)(2,1)S(1)}, u32[]{:S(2)}, u32[]{:S(2)}) collective-permute-start(bf16[528,128]{1,0:T(8,128)(2,1)S(1)} %get-tuple-element.46), channel_id=1, source_target_pairs={{0,2},{1,3},{2,0},{3,1},{4,6},{5,7},{6,4},{7,5},{8,10},{9,11},{10,... | collective-permute-start | bytes 405512 | tf_op jit(solution)/shard_map/ppermute | solution.py:690
  8.5 1.3 %collective-permute-start.2 = (bf16[528,128]{1,0:T(8,128)(2,1)S(1)}, bf16[528,128]{1,0:T(8,128)(2,1)S(1)}, u32[]{:S(2)}, u32[]{:S(2)}) collective-permute-start(bf16[528,128]{1,0:T(8,128)(2,1)S(1)} %get-tuple-element.47), channel_id=1, source_target_pairs={{0,3},{1,0},{2,1},{3,2},{4,7},{5,4},{6,5},{7,6},{8,11},{9,8},{10,9... | collective-permute-start | bytes 405512 | tf_op jit(solution)/shard_map/ppermute | solution.py:690
  9.8 0.9 %copy-done.3 = bf16[32,4096]{1,0:T(8,128)(2,1)S(1)} copy-done((bf16[32,4096]{1,0:T(8,128)(2,1)S(1)}, bf16[32,4096]{1,0:T(8,128)(2,1)}, u32[]{:S(2)}) %copy-start.3) | copy-done | bytes 262168
  11.1 1.4 %collective-permute-done.refs_1_ = bf16[528,128]{1,0:T(8,128)(2,1)S(1)} collective-permute-done((bf16[528,128]{1,0:T(8,128)(2,1)S(1)}, bf16[528,128]{1,0:T(8,128)(2,1)S(1)}, u32[]{:S(2)}, u32[]{:S(2)}) %collective-permute-start) | collective-permute-done | bytes 135200 | tf_op jit(solution)/shard_map/ppermute | solution.py:690
  12.4 4.9 %collective-permute-done.1.refs_2_ = bf16[528,128]{1,0:T(8,128)(2,1)S(1)} collective-permute-done((bf16[528,128]{1,0:T(8,128)(2,1)S(1)}, bf16[528,128]{1,0:T(8,128)(2,1)S(1)}, u32[]{:S(2)}, u32[]{:S(2)}) %collective-permute-start.1) | collective-permute-done | bytes 135200 | tf_op jit(solution)/shard_map/ppermute | solution.py:690
  17.5 3.4 %collective-permute-start.8 = (bf16[2,256,128]{2,1,0:T(8,128)(2,1)S(1)}, bf16[2,256,128]{2,1,0:T(8,128)(2,1)S(1)}, u32[]{:S(2)}, u32[]{:S(2)}) collective-permute-start(bf16[2,256,128]{2,1,0:T(8,128)(2,1)S(1)} %get-tuple-element.55), channel_id=1, source_target_pairs={{0,1},{1,2},{2,3},{3,0},{4,5},{5,6},{6,7},{7,4},{8,9},{9,10},{10,1... | collective-permute-start | bytes 393224 | tf_op jit(solution)/shard_map/ppermute | solution.py:690
  21.0 1.6 %collective-permute-start.9 = (bf16[2,256,128]{2,1,0:T(8,128)(2,1)S(1)}, bf16[2,256,128]{2,1,0:T(8,128)(2,1)S(1)}, u32[]{:S(2)}, u32[]{:S(2)}) collective-permute-start(bf16[2,256,128]{2,1,0:T(8,128)(2,1)S(1)} %get-tuple-element.56), channel_id=1, source_target_pairs={{0,2},{1,3},{2,0},{3,1},{4,6},{5,7},{6,4},{7,5},{8,10},{9,11},{10,... | collective-permute-start | bytes 393224 | tf_op jit(solution)/shard_map/ppermute | solution.py:690
  22.6 0.8 %collective-permute-start.10 = (bf16[2,256,128]{2,1,0:T(8,128)(2,1)S(1)}, bf16[2,256,128]{2,1,0:T(8,128)(2,1)S(1)}, u32[]{:S(2)}, u32[]{:S(2)}) collective-permute-start(bf16[2,256,128]{2,1,0:T(8,128)(2,1)S(1)} %get-tuple-element.57), channel_id=1, source_target_pairs={{0,3},{1,0},{2,1},{3,2},{4,7},{5,4},{6,5},{7,6},{8,11},{9,8},{10,9... | collective-permute-start | bytes 393224 | tf_op jit(solution)/shard_map/ppermute | solution.py:690
  23.4 7.1 %key_stage.1 = (bf16[16,128,128]{2,1,0:T(8,128)(2,1)S(1)}, bf16[16,128,256]{2,1,0:T(8,128)(2,1)S(1)}, bf16[16,128,256]{2,1,0:T(8,128)(2,1)S(1)}, f32[16,64,128]{...) custom-call(bf16[528,128]{1,0:T(8,128)(2,1)S(1)} %get-tuple-element., ...), custom_call_target="tpu_custom_call" | custom-call | flops 6000000000 | tf_op jit(solution)/shard_map/key_stage/pallas_call | solution.py:194
  30.5 1.6 %collective-permute-start.4 = (f32[128,128]{1,0:T(8,128)S(1)}, f32[128,128]{1,0:T(8,128)S(1)}, u32[]{:S(2)}, u32[]{:S(2)}) collective-permute-start(f32[128,128]{1,0:T(8,128)S(1)} %get-tuple-element.49), channel_id=1, source_target_pairs={{0,8},{8,0},{16,24},{24,16},{1,9},{9,1},{17,25},{25,17},{2,10},{10... | collective-permute-start | bytes 196616 | tf_op jit(solution)/shard_map/ppermute | solution.py:564
  32.1 1.5 %collective-permute-start.5 = (f32[128,128]{1,0:T(8,128)S(1)}, f32[128,128]{1,0:T(8,128)S(1)}, u32[]{:S(2)}, u32[]{:S(2)}) collective-permute-start(f32[128,128]{1,0:T(8,128)S(1)} %get-tuple-element.50), channel_id=1, source_target_pairs={{0,16},{8,24},{16,0},{24,8},{1,17},{9,25},{17,1},{25,9},{2,18},{10... | collective-permute-start | bytes 196616 | tf_op jit(solution)/shard_map/ppermute | solution.py:564
  33.6 0.5 collective-permute-start.6
  34.1 0.8 %value_stage.1 = (bf16[16,128,128]{2,1,0:T(8,128)(2,1)S(1)}, f32[16,128,128]{2,1,0:T(8,128)S(1)}, f32[128,128]{1,0:T(8,128)S(1)}, f32[128,128]{1,0:T(8,128)S(1)}...) custom-call(bf16[2,256,128]{2,1,0:T(8,128)(2,1)S(1)} %get-tuple-element.54.refs_0_, ...), custom_call_target="tpu_custom_call" | custom-call | flops 2000000000 | tf_op jit(solution)/shard_map/value_stage/pallas_call | solution.py:194
  34.9 1.6 %collective-permute-start.11 = (f32[128,128]{1,0:T(8,128)S(1)}, f32[128,128]{1,0:T(8,128)S(1)}, u32[]{:S(2)}, u32[]{:S(2)}) collective-permute-start(f32[128,128]{1,0:T(8,128)S(1)} %get-tuple-element.61), channel_id=1, source_target_pairs={{0,8},{8,0},{16,24},{24,16},{1,9},{9,1},{17,25},{25,17},{2,10},{10... | collective-permute-start | bytes 196616 | tf_op jit(solution)/shard_map/ppermute | solution.py:564
  36.5 1.5 %collective-permute-start.12 = (f32[128,128]{1,0:T(8,128)S(1)}, f32[128,128]{1,0:T(8,128)S(1)}, u32[]{:S(2)}, u32[]{:S(2)}) collective-permute-start(f32[128,128]{1,0:T(8,128)S(1)} %get-tuple-element.62), channel_id=1, source_target_pairs={{0,16},{8,24},{16,0},{24,8},{1,17},{9,25},{17,1},{25,9},{2,18},{10... | collective-permute-start | bytes 196616 | tf_op jit(solution)/shard_map/ppermute | solution.py:564
  38.0 0.4 collective-permute-start.13
  38.5 1.2 %collective-permute-start.17 = (bf16[2,128,128]{2,1,0:T(8,128)(2,1)S(1)}, bf16[2,128,128]{2,1,0:T(8,128)(2,1)S(1)}, u32[]{:S(2)}, u32[]{:S(2)}) collective-permute-start(bf16[2,128,128]{2,1,0:T(8,128)(2,1)S(1)} %get-tuple-element.69), channel_id=1, source_target_pairs={{0,1},{1,2},{2,3},{3,0},{4,5},{5,6},{6,7},{7,4},{8,9},{9,10},{10,1... | collective-permute-start | bytes 196616 | tf_op jit(solution)/shard_map/ppermute | solution.py:690
  39.7 1.3 %collective-permute-start.18 = (bf16[2,128,128]{2,1,0:T(8,128)(2,1)S(1)}, bf16[2,128,128]{2,1,0:T(8,128)(2,1)S(1)}, u32[]{:S(2)}, u32[]{:S(2)}) collective-permute-start(bf16[2,128,128]{2,1,0:T(8,128)(2,1)S(1)} %get-tuple-element.70), channel_id=1, source_target_pairs={{0,2},{1,3},{2,0},{3,1},{4,6},{5,7},{6,4},{7,5},{8,10},{9,11},{10,... | collective-permute-start | bytes 196616 | tf_op jit(solution)/shard_map/ppermute | solution.py:690
  41.0 1.8 %collective-permute-start.19 = (bf16[2,128,128]{2,1,0:T(8,128)(2,1)S(1)}, bf16[2,128,128]{2,1,0:T(8,128)(2,1)S(1)}, u32[]{:S(2)}, u32[]{:S(2)}) collective-permute-start(bf16[2,128,128]{2,1,0:T(8,128)(2,1)S(1)} %get-tuple-element.71), channel_id=1, source_target_pairs={{0,3},{1,0},{2,1},{3,2},{4,7},{5,4},{6,5},{7,6},{8,11},{9,8},{10,9... | collective-permute-start | bytes 196616 | tf_op jit(solution)/shard_map/ppermute | solution.py:690
  42.8 0.4 collective-permute-done.13.refs_7_
  43.6 1.0 %collective-permute-start.14 = (f32[128,128]{1,0:T(8,128)S(1)}, f32[128,128]{1,0:T(8,128)S(1)}, u32[]{:S(2)}, u32[]{:S(2)}) collective-permute-start(f32[128,128]{1,0:T(8,128)S(1)} %get-tuple-element.65), channel_id=1, source_target_pairs={{0,8},{8,0},{16,24},{24,16},{1,9},{9,1},{17,25},{25,17},{2,10},{10... | collective-permute-start | bytes 196616 | tf_op jit(solution)/shard_map/ppermute | solution.py:564
  44.5 1.5 %collective-permute-start.15 = (f32[128,128]{1,0:T(8,128)S(1)}, f32[128,128]{1,0:T(8,128)S(1)}, u32[]{:S(2)}, u32[]{:S(2)}) collective-permute-start(f32[128,128]{1,0:T(8,128)S(1)} %get-tuple-element.66), channel_id=1, source_target_pairs={{0,16},{8,24},{16,0},{24,8},{1,17},{9,25},{17,1},{25,9},{2,18},{10... | collective-permute-start | bytes 196616 | tf_op jit(solution)/shard_map/ppermute | solution.py:564
  46.0 1.1 %collective-permute-start.16 = (f32[128,128]{1,0:T(8,128)S(1)}, f32[128,128]{1,0:T(8,128)S(1)}, u32[]{:S(2)}, u32[]{:S(2)}) collective-permute-start(f32[128,128]{1,0:T(8,128)S(1)} %get-tuple-element.67), channel_id=1, source_target_pairs={{0,24},{8,16},{16,8},{24,0},{1,25},{9,17},{17,9},{25,1},{2,26},{10... | collective-permute-start | bytes 196616 | tf_op jit(solution)/shard_map/ppermute | solution.py:564
  47.1 2.8 %query_stage.1 = (bf16[16,64,256]{2,1,0:T(8,128)(2,1)S(1)}, f32[16,64,128]{2,1,0:T(8,128)S(1)}) custom-call(bf16[2,128,128]{2,1,0:T(8,128)(2,1)S(1)} %get-tuple-element.68.refs_0_, bf16[2,128,128]{2,1,0:T(8,128)(2,1)S(1)} %collective-permute-done.17.refs_1_, bf16[2,128,128]{2,1,0:T(8,128)(2,1)S(1)} %collective-permute-done.18.refs_2_, ...), custom_call_target="tpu_custom_call" | custom-call | flops 3000000000 | tf_op jit(solution)/shard_map/query_stage/pallas_call | solution.py:194
  50.0 1.2 %collective-permute-done.16.refs_3_ = f32[128,128]{1,0:T(8,128)S(1)} collective-permute-done((f32[128,128]{1,0:T(8,128)S(1)}, f32[128,128]{1,0:T(8,128)S(1)}, u32[]{:S(2)}, u32[]{:S(2)}) %collective-permute-start.16) | collective-permute-done | bytes 65568 | tf_op jit(solution)/shard_map/ppermute | solution.py:564
  51.2 0.5 read_states.1
  51.8 1.3 %collective-permute-done.20.other = bf16[128,512]{1,0:T(8,128)(2,1)S(1)} collective-permute-done((bf16[128,512]{1,0:T(8,128)(2,1)S(1)}, bf16[128,512]{1,0:T(8,128)(2,1)S(1)}, u32[]{:S(2)}, u32[]{:S(2)}) %collective-permute-start.20) | collective-permute-done | bytes 131104 | tf_op jit(solution)/shard_map/ppermute | solution.py:696
  53.1 0.7 %join.1 = bf16[128,1024]{1,0:T(8,128)(2,1)} custom-call(bf16[128,512]{1,0:T(8,128)(2,1)S(1)} %get-tuple-element.81.own, bf16[128,512]{1,0:T(8,128)(2,1)S(1)} %collective-permute-done.20.other), custom_call_target="tpu_custom_call" | custom-call | tf_op jit(solution)/shard_map/join/pallas_call | solution.py:194
  (33 shorter events, 1.3 us)
Async XLA Ops:
  0.0 0.7 %copy-start = (s32[128]{0:T(128)S(1)}, s32[128]{0:T(128)}, u32[]{:S(2)}) copy-start(s32[128]{0:T(128)} %param.11) | copy-start | bytes 1540
  0.0 0.7 %copy-start.4 = (bf16[32,64]{1,0:T(8,128)(2,1)S(1)}, bf16[32,64]{1,0:T(8,128)(2,1)}, u32[]{:S(2)}) copy-start(bf16[32,64]{1,0:T(8,128)(2,1)} %betas.1) | copy-start | bytes 12292
  0.7 1.0 %copy-start.1 = (bf16[32,8192]{1,0:T(8,128)(2,1)S(1)}, bf16[32,8192]{1,0:T(8,128)(2,1)}, u32[]{:S(2)}) copy-start(bf16[32,8192]{1,0:T(8,128)(2,1)} %keys.1) | copy-start | bytes 1572868
  1.8 0.7 %copy-start.5 = (bf16[32,32]{1,0:T(8,128)(2,1)S(1)}, bf16[32,32]{1,0:T(8,128)(2,1)}, u32[]{:S(2)}) copy-start(bf16[32,32]{1,0:T(8,128)(2,1)} %log_gates.1) | copy-start | bytes 6148
  2.5 7.4 %copy-start.2 = (bf16[32,8192]{1,0:T(8,128)(2,1)S(1)}, bf16[32,8192]{1,0:T(8,128)(2,1)}, u32[]{:S(2)}) copy-start(bf16[32,8192]{1,0:T(8,128)(2,1)} %values.1) | copy-start | bytes 1572868
  2.8 9.6 %collective-permute-start = (bf16[528,128]{1,0:T(8,128)(2,1)S(1)}, bf16[528,128]{1,0:T(8,128)(2,1)S(1)}, u32[]{:S(2)}, u32[]{:S(2)}) collective-permute-start(bf16[528,128]{1,0:T(8,128)(2,1)S(1)} %get-tuple-element.45), channel_id=1, source_target_pairs={{0,1},{1,2},{2,3},{3,0},{4,5},{5,6},{6,7},{7,4},{8,9},{9,10},{10,1... | collective-permute-start | bytes 405512 | tf_op jit(solution)/shard_map/ppermute | solution.py:690
  5.9 11.5 %collective-permute-start.1 = (bf16[528,128]{1,0:T(8,128)(2,1)S(1)}, bf16[528,128]{1,0:T(8,128)(2,1)S(1)}, u32[]{:S(2)}, u32[]{:S(2)}) collective-permute-start(bf16[528,128]{1,0:T(8,128)(2,1)S(1)} %get-tuple-element.46), channel_id=1, source_target_pairs={{0,2},{1,3},{2,0},{3,1},{4,6},{5,7},{6,4},{7,5},{8,10},{9,11},{10,... | collective-permute-start | bytes 405512 | tf_op jit(solution)/shard_map/ppermute | solution.py:690
  8.5 8.9 %collective-permute-start.2 = (bf16[528,128]{1,0:T(8,128)(2,1)S(1)}, bf16[528,128]{1,0:T(8,128)(2,1)S(1)}, u32[]{:S(2)}, u32[]{:S(2)}) collective-permute-start(bf16[528,128]{1,0:T(8,128)(2,1)S(1)} %get-tuple-element.47), channel_id=1, source_target_pairs={{0,3},{1,0},{2,1},{3,2},{4,7},{5,4},{6,5},{7,6},{8,11},{9,8},{10,9... | collective-permute-start | bytes 405512 | tf_op jit(solution)/shard_map/ppermute | solution.py:690
  9.8 1.0 %copy-start.3 = (bf16[32,4096]{1,0:T(8,128)(2,1)S(1)}, bf16[32,4096]{1,0:T(8,128)(2,1)}, u32[]{:S(2)}) copy-start(bf16[32,4096]{1,0:T(8,128)(2,1)} %queries.1) | copy-start | bytes 786436
  11.0 6.5 %collective-permute-start.7 = (bf16[4,384,128]{2,1,0:T(8,128)(2,1)S(1)}, bf16[4,384,128]{2,1,0:T(8,128)(2,1)S(1)}, u32[]{:S(2)}, u32[]{:S(2)}) collective-permute-start(bf16[4,384,128]{2,1,0:T(8,128)(2,1)S(1)} %get-tuple-element.53), channel_id=1, source_target_pairs={{0,4},{4,0},{1,5},{5,1},{2,6},{6,2},{3,7},{7,3},{8,12},{12,8},{9,1... | collective-permute-start | bytes 1179656 | tf_op jit(solution)/shard_map/ppermute | solution.py:696
  17.4 6.0 %collective-permute-start.3 = (bf16[4,272,128]{2,1,0:T(8,128)(2,1)S(1)}, bf16[4,272,128]{2,1,0:T(8,128)(2,1)S(1)}, u32[]{:S(2)}, u32[]{:S(2)}) collective-permute-start(bf16[4,272,128]{2,1,0:T(8,128)(2,1)S(1)} %swap_keys.1), channel_id=1, source_target_pairs={{0,4},{4,0},{1,5},{5,1},{2,6},{6,2},{3,7},{7,3},{8,12},{12,8},{9,1... | collective-permute-start | bytes 835592 | tf_op jit(solution)/shard_map/ppermute | solution.py:696
  17.5 16.1 %collective-permute-start.8 = (bf16[2,256,128]{2,1,0:T(8,128)(2,1)S(1)}, bf16[2,256,128]{2,1,0:T(8,128)(2,1)S(1)}, u32[]{:S(2)}, u32[]{:S(2)}) collective-permute-start(bf16[2,256,128]{2,1,0:T(8,128)(2,1)S(1)} %get-tuple-element.55), channel_id=1, source_target_pairs={{0,1},{1,2},{2,3},{3,0},{4,5},{5,6},{6,7},{7,4},{8,9},{9,10},{10,1... | collective-permute-start | bytes 393224 | tf_op jit(solution)/shard_map/ppermute | solution.py:690
  21.0 13.1 %collective-permute-start.9 = (bf16[2,256,128]{2,1,0:T(8,128)(2,1)S(1)}, bf16[2,256,128]{2,1,0:T(8,128)(2,1)S(1)}, u32[]{:S(2)}, u32[]{:S(2)}) collective-permute-start(bf16[2,256,128]{2,1,0:T(8,128)(2,1)S(1)} %get-tuple-element.56), channel_id=1, source_target_pairs={{0,2},{1,3},{2,0},{3,1},{4,6},{5,7},{6,4},{7,5},{8,10},{9,11},{10,... | collective-permute-start | bytes 393224 | tf_op jit(solution)/shard_map/ppermute | solution.py:690
  22.6 11.5 %collective-permute-start.10 = (bf16[2,256,128]{2,1,0:T(8,128)(2,1)S(1)}, bf16[2,256,128]{2,1,0:T(8,128)(2,1)S(1)}, u32[]{:S(2)}, u32[]{:S(2)}) collective-permute-start(bf16[2,256,128]{2,1,0:T(8,128)(2,1)S(1)} %get-tuple-element.57), channel_id=1, source_target_pairs={{0,3},{1,0},{2,1},{3,2},{4,7},{5,4},{6,5},{7,6},{8,11},{9,8},{10,9... | collective-permute-start | bytes 393224 | tf_op jit(solution)/shard_map/ppermute | solution.py:690
  30.5 7.5 %collective-permute-start.4 = (f32[128,128]{1,0:T(8,128)S(1)}, f32[128,128]{1,0:T(8,128)S(1)}, u32[]{:S(2)}, u32[]{:S(2)}) collective-permute-start(f32[128,128]{1,0:T(8,128)S(1)} %get-tuple-element.49), channel_id=1, source_target_pairs={{0,8},{8,0},{16,24},{24,16},{1,9},{9,1},{17,25},{25,17},{2,10},{10... | collective-permute-start | bytes 196616 | tf_op jit(solution)/shard_map/ppermute | solution.py:564
  32.1 6.3 %collective-permute-start.5 = (f32[128,128]{1,0:T(8,128)S(1)}, f32[128,128]{1,0:T(8,128)S(1)}, u32[]{:S(2)}, u32[]{:S(2)}) collective-permute-start(f32[128,128]{1,0:T(8,128)S(1)} %get-tuple-element.50), channel_id=1, source_target_pairs={{0,16},{8,24},{16,0},{24,8},{1,17},{9,25},{17,1},{25,9},{2,18},{10... | collective-permute-start | bytes 196616 | tf_op jit(solution)/shard_map/ppermute | solution.py:564
  33.6 6.0 %collective-permute-start.6 = (f32[128,128]{1,0:T(8,128)S(1)}, f32[128,128]{1,0:T(8,128)S(1)}, u32[]{:S(2)}, u32[]{:S(2)}) collective-permute-start(f32[128,128]{1,0:T(8,128)S(1)} %get-tuple-element.51), channel_id=1, source_target_pairs={{0,24},{8,16},{16,8},{24,0},{1,25},{9,17},{17,9},{25,1},{2,26},{10... | collective-permute-start | bytes 196616 | tf_op jit(solution)/shard_map/ppermute | solution.py:564
  34.9 6.1 %collective-permute-start.11 = (f32[128,128]{1,0:T(8,128)S(1)}, f32[128,128]{1,0:T(8,128)S(1)}, u32[]{:S(2)}, u32[]{:S(2)}) collective-permute-start(f32[128,128]{1,0:T(8,128)S(1)} %get-tuple-element.61), channel_id=1, source_target_pairs={{0,8},{8,0},{16,24},{24,16},{1,9},{9,1},{17,25},{25,17},{2,10},{10... | collective-permute-start | bytes 196616 | tf_op jit(solution)/shard_map/ppermute | solution.py:564
  36.5 6.3 %collective-permute-start.12 = (f32[128,128]{1,0:T(8,128)S(1)}, f32[128,128]{1,0:T(8,128)S(1)}, u32[]{:S(2)}, u32[]{:S(2)}) collective-permute-start(f32[128,128]{1,0:T(8,128)S(1)} %get-tuple-element.62), channel_id=1, source_target_pairs={{0,16},{8,24},{16,0},{24,8},{1,17},{9,25},{17,1},{25,9},{2,18},{10... | collective-permute-start | bytes 196616 | tf_op jit(solution)/shard_map/ppermute | solution.py:564
  38.0 5.2 %collective-permute-start.13 = (f32[128,128]{1,0:T(8,128)S(1)}, f32[128,128]{1,0:T(8,128)S(1)}, u32[]{:S(2)}, u32[]{:S(2)}) collective-permute-start(f32[128,128]{1,0:T(8,128)S(1)} %get-tuple-element.63), channel_id=1, source_target_pairs={{0,24},{8,16},{16,8},{24,0},{1,25},{9,17},{17,9},{25,1},{2,26},{10... | collective-permute-start | bytes 196616 | tf_op jit(solution)/shard_map/ppermute | solution.py:564
  38.5 7.6 %collective-permute-start.17 = (bf16[2,128,128]{2,1,0:T(8,128)(2,1)S(1)}, bf16[2,128,128]{2,1,0:T(8,128)(2,1)S(1)}, u32[]{:S(2)}, u32[]{:S(2)}) collective-permute-start(bf16[2,128,128]{2,1,0:T(8,128)(2,1)S(1)} %get-tuple-element.69), channel_id=1, source_target_pairs={{0,1},{1,2},{2,3},{3,0},{4,5},{5,6},{6,7},{7,4},{8,9},{9,10},{10,1... | collective-permute-start | bytes 196616 | tf_op jit(solution)/shard_map/ppermute | solution.py:690
  39.7 7.4 %collective-permute-start.18 = (bf16[2,128,128]{2,1,0:T(8,128)(2,1)S(1)}, bf16[2,128,128]{2,1,0:T(8,128)(2,1)S(1)}, u32[]{:S(2)}, u32[]{:S(2)}) collective-permute-start(bf16[2,128,128]{2,1,0:T(8,128)(2,1)S(1)} %get-tuple-element.70), channel_id=1, source_target_pairs={{0,2},{1,3},{2,0},{3,1},{4,6},{5,7},{6,4},{7,5},{8,10},{9,11},{10,... | collective-permute-start | bytes 196616 | tf_op jit(solution)/shard_map/ppermute | solution.py:690
  41.0 6.1 %collective-permute-start.19 = (bf16[2,128,128]{2,1,0:T(8,128)(2,1)S(1)}, bf16[2,128,128]{2,1,0:T(8,128)(2,1)S(1)}, u32[]{:S(2)}, u32[]{:S(2)}) collective-permute-start(bf16[2,128,128]{2,1,0:T(8,128)(2,1)S(1)} %get-tuple-element.71), channel_id=1, source_target_pairs={{0,3},{1,0},{2,1},{3,2},{4,7},{5,4},{6,5},{7,6},{8,11},{9,8},{10,9... | collective-permute-start | bytes 196616 | tf_op jit(solution)/shard_map/ppermute | solution.py:690
  43.6 6.4 %collective-permute-start.14 = (f32[128,128]{1,0:T(8,128)S(1)}, f32[128,128]{1,0:T(8,128)S(1)}, u32[]{:S(2)}, u32[]{:S(2)}) collective-permute-start(f32[128,128]{1,0:T(8,128)S(1)} %get-tuple-element.65), channel_id=1, source_target_pairs={{0,8},{8,0},{16,24},{24,16},{1,9},{9,1},{17,25},{25,17},{2,10},{10... | collective-permute-start | bytes 196616 | tf_op jit(solution)/shard_map/ppermute | solution.py:564
  44.5 5.5 %collective-permute-start.15 = (f32[128,128]{1,0:T(8,128)S(1)}, f32[128,128]{1,0:T(8,128)S(1)}, u32[]{:S(2)}, u32[]{:S(2)}) collective-permute-start(f32[128,128]{1,0:T(8,128)S(1)} %get-tuple-element.66), channel_id=1, source_target_pairs={{0,16},{8,24},{16,0},{24,8},{1,17},{9,25},{17,1},{25,9},{2,18},{10... | collective-permute-start | bytes 196616 | tf_op jit(solution)/shard_map/ppermute | solution.py:564
  46.0 5.2 %collective-permute-start.16 = (f32[128,128]{1,0:T(8,128)S(1)}, f32[128,128]{1,0:T(8,128)S(1)}, u32[]{:S(2)}, u32[]{:S(2)}) collective-permute-start(f32[128,128]{1,0:T(8,128)S(1)} %get-tuple-element.67), channel_id=1, source_target_pairs={{0,24},{8,16},{16,8},{24,0},{1,25},{9,17},{17,9},{25,1},{2,26},{10... | collective-permute-start | bytes 196616 | tf_op jit(solution)/shard_map/ppermute | solution.py:564
  51.7 1.4 %collective-permute-start.20 = (bf16[128,512]{1,0:T(8,128)(2,1)S(1)}, bf16[128,512]{1,0:T(8,128)(2,1)S(1)}, u32[]{:S(2)}, u32[]{:S(2)}) collective-permute-start(bf16[128,512]{1,0:T(8,128)(2,1)S(1)} %get-tuple-element.82), channel_id=1, source_target_pairs={{0,4},{4,0},{1,5},{5,1},{2,6},{6,2},{3,7},{7,3},{8,12},{12,8},{9,1... | collective-permute-start | bytes 393224 | tf_op jit(solution)/shard_map/ppermute | solution.py:696

commit v3 on v2

--- a/solution.py
+++ b/solution.py
@@ -190,15 +190,23 @@
     )
 
 
-def call(kernel, outs, *args, scratch=(), flops=0, name=None):
+def call(kernel, outs, *args, scratch=(), after=(), name=None):
+    count = len(args)
+
+    def body(*refs):
+        kernel(*refs[:count], *refs[count + len(after) :])
+
+    specs = [pl.BlockSpec(memory_space=pltpu.VMEM)] * count
+    specs += [pl.BlockSpec(memory_space=pl.ANY)] * len(after)
     return pl.pallas_call(
-        kernel,
+        body,
         out_shape=outs,
+        in_specs=specs,
         scratch_shapes=scratch,
         compiler_params=pltpu.CompilerParams(vmem_limit_bytes=24 * 2**20),
-        cost_estimate=pl.CostEstimate(flops=flops, bytes_accessed=0, transcendentals=0),
+        cost_estimate=pl.CostEstimate(flops=0, bytes_accessed=0, transcendentals=0),
         name=name,
-    )(*args)
+    )(*args, *after)
 
 
 def shape(*sizes, dtype=BF16):
@@ -237,7 +245,7 @@
     rows = sizes.heads * KEY_ROWS
     count = sizes.heads * NH
 
-    def kernel(keys, betas, log_gates, starts, *outs):
+    def kernel(keys, betas, log_gates, starts, kept, sent):
         z = axis_index("head")
         core = axis_index("core")
         heads = log_gates.shape[1]
@@ -250,38 +258,25 @@
         pieces.append(dot_nt(same.astype(BF16), log_gates[...]))
         pieces.append(jnp.broadcast_to(starts[...].astype(F32), (heads, TOK)))
         scales = jnp.concatenate(pieces, 1).astype(BF16)
-        for ahead, out in enumerate(outs):
+        for ahead in range(sizes.groups):
             target = shifted(z, ahead, sizes.groups)
-            for side in range(2):
-                owner = jnp.bitwise_xor(core, side)
-                first = ((target * 2 + owner) * sizes.heads) * NH * DK
-                for number, piece in enumerate(block_columns(keys, first, count)):
-                    at = side * rows + number * TOK
-                    out[at : at + TOK, :] = piece
             extent = (SCALE_ROWS, heads)
             pick = (iota(extent, 1) == target * sizes.group_heads + iota(extent, 0)) & (
                 iota(extent, 0) < sizes.group_heads
             )
-            out[2 * rows :, :] = dot(pick.astype(BF16), scales).astype(BF16)
-
-    outs = [shape(2 * rows + SCALE_ROWS, DK)] * sizes.groups
+            scale = dot(pick.astype(BF16), scales).astype(BF16)
+            for side, out in enumerate((kept, sent)):
+                owner = jnp.bitwise_xor(core, side)
+                first = ((target * 2 + owner) * sizes.heads) * NH * DK
+                for number, piece in enumerate(block_columns(keys, first, count)):
+                    out[ahead, number * TOK : (number + 1) * TOK, :] = piece
+                out[ahead, rows:, :] = scale
+
+    outs = [shape(sizes.groups, rows + SCALE_ROWS, DK)] * 2
     return call(kernel, outs, keys, betas, log_gates, starts, name="pack_keys")
 
 
-def swap_keys(sizes, arrived):
-    rows = sizes.heads * KEY_ROWS
-
-    def kernel(*refs):
-        out = refs[-1]
-        z = axis_index("head")
-        for behind, piece in enumerate(refs[:-1]):
-            source = shifted(z, sizes.groups - behind, sizes.groups) if behind else z
-            out[source] = piece[rows:, :]
-
-    return call(kernel, shape(sizes.groups, rows + SCALE_ROWS, DK), *arrived, name="swap_keys")
-
-
-def pack_reads(sizes, values, queries):
+def pack_reads(sizes, values, queries, after):
     value_rows = sizes.heads * KEY_ROWS
     rows = value_rows + sizes.heads * TOK
 
@@ -298,32 +293,34 @@
                     out[ahead, number * TOK : (number + 1) * TOK, :] = piece
 
     return call(
-        kernel, [shape(sizes.groups, rows, DK)] * 2, values, queries, name="pack_reads"
-    )
-
-
-def merge_reads(sizes, kept, swapped):
-    value_rows = sizes.heads * KEY_ROWS
-    query_rows = sizes.heads * TOK
-
+        kernel,
+        [shape(sizes.groups, rows, DK)] * 2,
+        values,
+        queries,
+        after=after,
+        name="pack_reads",
+    )
+
+
+def merge(sizes, kept, swapped, name):
     def kernel(kept, swapped, *outs):
         for ahead in range(sizes.groups):
             for side, source in enumerate((kept, swapped)):
-                outs[ahead][side] = source[ahead, :value_rows, :]
-                outs[sizes.groups + ahead][side] = source[ahead, value_rows:, :]
-
-    outs = [shape(2, value_rows, DK)] * sizes.groups + [shape(2, query_rows, DK)] * sizes.groups
-    merged = call(kernel, outs, kept, swapped, name="merge_reads")
-    return merged[: sizes.groups], merged[sizes.groups :]
-
-
-def gather(sizes, pieces, scratch):
+                outs[ahead][side] = source[ahead]
+
+    outs = [shape(2, *kept.shape[1:])] * sizes.groups
+    return call(kernel, outs, kept, swapped, name=name)
+
+
+def gather(sizes, pieces, first, count, scratch):
     z = axis_index("head")
     core = axis_index("core")
     for behind, piece in enumerate(pieces):
         source = shifted(z, sizes.groups - behind, sizes.groups) if behind else z
         for side in range(2):
-            scratch[jnp.bitwise_xor(core, side) * sizes.groups + source] = piece[side]
+            scratch[jnp.bitwise_xor(core, side) * sizes.groups + source] = piece[
+                side, first : first + count, :
+            ]
 
 
 def unit_rows(scratch, head, chunk, count):
@@ -337,29 +334,21 @@
     )
 
 
-def key_stage(sizes, arrived, swapped):
+def key_stage(sizes, pieces):
     rows = sizes.heads * KEY_ROWS
     units = sizes.units
     groups = sizes.groups
 
     def kernel(*refs):
         pieces = refs[:groups]
-        swapped = refs[groups]
         keys_out, inverse_out, end_out, ratio_out, row_out, step_out, prefix_out = refs[
-            groups + 1 : groups + 8
+            groups : groups + 7
         ]
-        totals = refs[groups + 8 : groups + 8 + sizes.heads]
-        blocks, scales, every = refs[groups + 8 + sizes.heads :]
-        z = axis_index("head")
+        totals = refs[groups + 7 : groups + 7 + sizes.heads]
+        blocks, scales, every = refs[groups + 7 + sizes.heads :]
         core = axis_index("core")
-        for behind, piece in enumerate(pieces):
-            source = shifted(z, groups - behind, groups) if behind else z
-            blocks[core * groups + source] = piece[:rows, :]
-            scales[core * groups + source] = piece[2 * rows :, :]
-        other = (1 - core) * groups
-        for source in range(groups):
-            blocks[other + source] = swapped[source, :rows, :]
-            scales[other + source] = swapped[source, rows:, :]
+        gather(sizes, pieces, 0, rows, blocks)
+        gather(sizes, pieces, rows, SCALE_ROWS, scales)
         flat = scales[...].reshape(2 * groups * SCALE_ROWS, 4 * TOK)
         picks = []
         for block in range(2):
@@ -471,7 +460,7 @@
         pltpu.VMEM((units, DK, DK), F32),
     ]
     results = call(
-        kernel, outs, *arrived, swapped, scratch=scratch, flops=6_000_000_000, name="key_stage"
+        kernel, outs, *pieces, scratch=scratch, name="key_stage"
     )
     return results[:7], results[7:]
 
@@ -484,7 +473,7 @@
         ends, steps, values_out, before_out = refs[groups : groups + 4]
         totals = refs[groups + 4 : groups + 4 + sizes.heads]
         blocks, every = refs[groups + 4 + sizes.heads :]
-        gather(sizes, pieces, blocks)
+        gather(sizes, pieces, 0, sizes.heads * KEY_ROWS, blocks)
         injects = []
         for unit in range(sizes.units):
             value = unit_rows(blocks, *sizes.unit(unit), KEY_ROWS)
@@ -520,7 +509,7 @@
         pltpu.VMEM((sizes.heads, DV, DK), F32),
     ]
     results = call(
-        kernel, outs, *pieces, ends, steps, scratch=scratch, flops=2_000_000_000, name="value_stage"
+        kernel, outs, *pieces, ends, steps, scratch=scratch, name="value_stage"
     )
     return results[0], results[1], results[2:]
 
@@ -591,7 +580,7 @@
         values, before, keys, inverse, ratio, rows, prefix, reader_out, inner_out, blocks = refs[
             groups:
         ]
-        gather(sizes, pieces, blocks)
+        gather(sizes, pieces, sizes.heads * KEY_ROWS, sizes.heads * TOK, blocks)
         for base in range(0, sizes.units, GROUP):
             members = range(base, min(base + GROUP, sizes.units))
             queries = [unit_rows(blocks, *sizes.unit(unit), TOK) for unit in members]
@@ -630,7 +619,6 @@
         rows,
         prefixes,
         scratch=scratch,
-        flops=3_000_000_000,
         name="query_stage",
     )
 
@@ -695,19 +683,17 @@
     def swapped(part):
         return lax.ppermute(part, "core", [(0, 1), (1, 0)])
 
-    arrived = spread(pack_keys(sizes, keys, betas, log_gates, own_starts))
-    kept, sent = pack_reads(sizes, values, queries)
-    value_parts, query_parts = merge_reads(sizes, kept, swapped(sent))
-    value_parts = spread(value_parts)
-    query_parts = spread(query_parts)
-    other_keys = swapped(swap_keys(sizes, arrived))
+    kept_keys, sent_keys = pack_keys(sizes, keys, betas, log_gates, own_starts)
+    key_parts = spread(merge(sizes, kept_keys, swapped(sent_keys), "merge_keys"))
+    kept, sent = pack_reads(sizes, values, queries, after=(kept_keys,))
+    reads = spread(merge(sizes, kept, swapped(sent), "merge_reads"))
     (unit_keys, inverse, ends, ratios, rows, steps, prefixes), transitions = key_stage(
-        sizes, arrived, other_keys
-    )
-    unit_values, before, injects = value_stage(sizes, value_parts, ends, steps)
+        sizes, key_parts
+    )
+    unit_values, before, injects = value_stage(sizes, reads, ends, steps)
     states = entry_states(sizes, transitions, injects)
     readers, inners = query_stage(
-        sizes, query_parts, unit_values, before, unit_keys, inverse, ratios, rows, prefixes
+        sizes, reads, unit_values, before, unit_keys, inverse, ratios, rows, prefixes
     )
     own, other = read_states(sizes, states, readers, inners)
     return join(sizes, own, swapped(other))

time: 54.1 us -> 59.1 us (1.092)
  the two profiles are of different devices: /device:TPU:0 before, /device:TPU:9 now
where the time goes in v3:
time: 59.1 us; the launch traced here: 58.8 us
  waiting for transfers between devices  21.4 us (36%)
  starting transfers between devices  21 us (36%)
  Pallas kernels  13 us (22%)
  local copies, waits for them, and re-layouts  3.39 us (6%)
    ppermute x6, waiting for transfers between devices, spread(): lax.ppermute(part, 'head', [(z, (z + ahead) % groups) for z in range(grou...  16.3 us
    pallas_call x10, Pallas kernels, call(): pl.pallas_call(body, out_shape=outs, in_specs=specs, scratch_shapes=scrat...  13 us
    ppermute x9, starting transfers between devices, exchanged(): lax.ppermute(part, 'chip', [(chip, chip ^ number) for chip in range(sizes...  8.14 us
    ppermute x6, starting transfers between devices, spread(): lax.ppermute(part, 'head', [(z, (z + ahead) % groups) for z in range(grou...  7.55 us
    ppermute x3, starting transfers between devices, swapped(): return lax.ppermute(part, 'core', [(0, 1), (1, 0)])  5.26 us
    ppermute x9, waiting for transfers between devices, exchanged(): lax.ppermute(part, 'chip', [(chip, chip ^ number) for chip in range(sizes...  4.05 us
    unnamed x12, local copies, waits for them, and re-layouts  3.31 us
  transfers between devices with their start and end apart: 18, of which 7 were waited for; matrix products, arithmetic and copies ran while one was open for 0% of the time, Pallas kernels for 19%

profile of v3, /device:TPU:9, one launch (start us, length us, event | category | flops | bytes accessed | tf_op | source)
XLA Modules:
  0.0 58.8 jit_solution(14119894917647364546)
XLA Ops:
  0.1 0.6 %copy-done.4 = bf16[32,64]{1,0:T(8,128)(2,1)S(1)} copy-done((bf16[32,64]{1,0:T(8,128)(2,1)S(1)}, bf16[32,64]{1,0:T(8,128)(2,1)}, u32[]{:S(2)}) %copy-start.4) | copy-done | bytes 4120
  0.7 1.0 %copy-done.1 = bf16[32,8192]{1,0:T(8,128)(2,1)S(1)} copy-done((bf16[32,8192]{1,0:T(8,128)(2,1)S(1)}, bf16[32,8192]{1,0:T(8,128)(2,1)}, u32[]{:S(2)}) %copy-start.1) | copy-done | bytes 524312
  1.7 0.7 %copy-done.5 = bf16[32,32]{1,0:T(8,128)(2,1)S(1)} copy-done((bf16[32,32]{1,0:T(8,128)(2,1)S(1)}, bf16[32,32]{1,0:T(8,128)(2,1)}, u32[]{:S(2)}) %copy-start.5) | copy-done | bytes 2072
  2.4 0.3 pack_keys.1
  2.8 0.7 %collective-permute-start = (bf16[4,272,128]{2,1,0:T(8,128)(2,1)S(1)}, bf16[4,272,128]{2,1,0:T(8,128)(2,1)S(1)}, u32[]{:S(2)}, u32[]{:S(2)}) collective-permute-start(bf16[4,272,128]{2,1,0:T(8,128)(2,1)S(1)} %get-tuple-element.43), channel_id=1, source_target_pairs={{0,4},{4,0},{1,5},{5,1},{2,6},{6,2},{3,7},{7,3},{8,12},{12,8},{9,1... | collective-permute-start | bytes 835592 | tf_op jit(solution)/shard_map/ppermute | solution.py:684
  3.5 0.9 %copy-done.3 = bf16[32,4096]{1,0:T(8,128)(2,1)S(1)} copy-done((bf16[32,4096]{1,0:T(8,128)(2,1)S(1)}, bf16[32,4096]{1,0:T(8,128)(2,1)}, u32[]{:S(2)}) %copy-start.3) | copy-done | bytes 262168
  4.6 0.7 %collective-permute-start.7 = (bf16[4,384,128]{2,1,0:T(8,128)(2,1)S(1)}, bf16[4,384,128]{2,1,0:T(8,128)(2,1)S(1)}, u32[]{:S(2)}, u32[]{:S(2)}) collective-permute-start(bf16[4,384,128]{2,1,0:T(8,128)(2,1)S(1)} %get-tuple-element.53), channel_id=1, source_target_pairs={{0,4},{4,0},{1,5},{5,1},{2,6},{6,2},{3,7},{7,3},{8,12},{12,8},{9,1... | collective-permute-start | bytes 1179656 | tf_op jit(solution)/shard_map/ppermute | solution.py:684
  5.4 1.3 %collective-permute-start.1 = (bf16[2,272,128]{2,1,0:T(8,128)(2,1)S(1)}, bf16[2,272,128]{2,1,0:T(8,128)(2,1)S(1)}, u32[]{:S(2)}, u32[]{:S(2)}) collective-permute-start(bf16[2,272,128]{2,1,0:T(8,128)(2,1)S(1)} %get-tuple-element.45), channel_id=1, source_target_pairs={{0,1},{1,2},{2,3},{3,0},{4,5},{5,6},{6,7},{7,4},{8,9},{9,10},{10,1... | collective-permute-start | bytes 417800 | tf_op jit(solution)/shard_map/ppermute | solution.py:678
  6.8 1.1 %collective-permute-start.2 = (bf16[2,272,128]{2,1,0:T(8,128)(2,1)S(1)}, bf16[2,272,128]{2,1,0:T(8,128)(2,1)S(1)}, u32[]{:S(2)}, u32[]{:S(2)}) collective-permute-start(bf16[2,272,128]{2,1,0:T(8,128)(2,1)S(1)} %get-tuple-element.46), channel_id=1, source_target_pairs={{0,2},{1,3},{2,0},{3,1},{4,6},{5,7},{6,4},{7,5},{8,10},{9,11},{10,... | collective-permute-start | bytes 417800 | tf_op jit(solution)/shard_map/ppermute | solution.py:678
  7.9 1.4 %collective-permute-start.3 = (bf16[2,272,128]{2,1,0:T(8,128)(2,1)S(1)}, bf16[2,272,128]{2,1,0:T(8,128)(2,1)S(1)}, u32[]{:S(2)}, u32[]{:S(2)}) collective-permute-start(bf16[2,272,128]{2,1,0:T(8,128)(2,1)S(1)} %get-tuple-element.47), channel_id=1, source_target_pairs={{0,3},{1,0},{2,1},{3,2},{4,7},{5,4},{6,5},{7,6},{8,11},{9,8},{10,9... | collective-permute-start | bytes 417800 | tf_op jit(solution)/shard_map/ppermute | solution.py:678
  9.4 3.1 %collective-permute-start.9 = (bf16[2,384,128]{2,1,0:T(8,128)(2,1)S(1)}, bf16[2,384,128]{2,1,0:T(8,128)(2,1)S(1)}, u32[]{:S(2)}, u32[]{:S(2)}) collective-permute-start(bf16[2,384,128]{2,1,0:T(8,128)(2,1)S(1)} %get-tuple-element.56), channel_id=1, source_target_pairs={{0,2},{1,3},{2,0},{3,1},{4,6},{5,7},{6,4},{7,5},{8,10},{9,11},{10,... | collective-permute-start | bytes 589832 | tf_op jit(solution)/shard_map/ppermute | solution.py:678
  12.5 0.5 collective-permute-start.10
  13.0 5.8 %collective-permute-done.2.refs_2_ = bf16[2,272,128]{2,1,0:T(8,128)(2,1)S(1)} collective-permute-done((bf16[2,272,128]{2,1,0:T(8,128)(2,1)S(1)}, bf16[2,272,128]{2,1,0:T(8,128)(2,1)S(1)}, u32[]{:S(2)}, u32[]{:S(2)}) %collective-permute-start.2) | collective-permute-done | bytes 139296 | tf_op jit(solution)/shard_map/ppermute | solution.py:678
  18.9 10.5 %collective-permute-done.3.refs_3_ = bf16[2,272,128]{2,1,0:T(8,128)(2,1)S(1)} collective-permute-done((bf16[2,272,128]{2,1,0:T(8,128)(2,1)S(1)}, bf16[2,272,128]{2,1,0:T(8,128)(2,1)S(1)}, u32[]{:S(2)}, u32[]{:S(2)}) %collective-permute-start.3) | collective-permute-done | bytes 139296 | tf_op jit(solution)/shard_map/ppermute | solution.py:678
  29.4 7.1 %key_stage.1 = (bf16[16,128,128]{2,1,0:T(8,128)(2,1)S(1)}, bf16[16,128,256]{2,1,0:T(8,128)(2,1)S(1)}, bf16[16,128,256]{2,1,0:T(8,128)(2,1)S(1)}, f32[16,64,128]{...) custom-call(bf16[2,272,128]{2,1,0:T(8,128)(2,1)S(1)} %get-tuple-elem, ...), custom_call_target="tpu_custom_call" | custom-call | tf_op jit(solution)/shard_map/key_stage/pallas_call | solution.py:201
  36.5 1.3 %collective-permute-start.4 = (f32[128,128]{1,0:T(8,128)S(1)}, f32[128,128]{1,0:T(8,128)S(1)}, u32[]{:S(2)}, u32[]{:S(2)}) collective-permute-start(f32[128,128]{1,0:T(8,128)S(1)} %get-tuple-element.49), channel_id=1, source_target_pairs={{0,8},{8,0},{16,24},{24,16},{1,9},{9,1},{17,25},{25,17},{2,10},{10... | collective-permute-start | bytes 196616 | tf_op jit(solution)/shard_map/ppermute | solution.py:553
  37.8 1.3 %collective-permute-start.5 = (f32[128,128]{1,0:T(8,128)S(1)}, f32[128,128]{1,0:T(8,128)S(1)}, u32[]{:S(2)}, u32[]{:S(2)}) collective-permute-start(f32[128,128]{1,0:T(8,128)S(1)} %get-tuple-element.50), channel_id=1, source_target_pairs={{0,16},{8,24},{16,0},{24,8},{1,17},{9,25},{17,1},{25,9},{2,18},{10... | collective-permute-start | bytes 196616 | tf_op jit(solution)/shard_map/ppermute | solution.py:553
  39.2 0.8 %value_stage.1 = (bf16[16,128,128]{2,1,0:T(8,128)(2,1)S(1)}, f32[16,128,128]{2,1,0:T(8,128)S(1)}, f32[128,128]{1,0:T(8,128)S(1)}, f32[128,128]{1,0:T(8,128)S(1)}...) custom-call(bf16[2,384,128]{2,1,0:T(8,128)(2,1)S(1)} %get-tuple-element.54.refs_0_, ...), custom_call_target="tpu_custom_call" | custom-call | tf_op jit(solution)/shard_map/value_stage/pallas_call | solution.py:201
  40.0 1.3 %collective-permute-start.11 = (f32[128,128]{1,0:T(8,128)S(1)}, f32[128,128]{1,0:T(8,128)S(1)}, u32[]{:S(2)}, u32[]{:S(2)}) collective-permute-start(f32[128,128]{1,0:T(8,128)S(1)} %get-tuple-element.61), channel_id=1, source_target_pairs={{0,8},{8,0},{16,24},{24,16},{1,9},{9,1},{17,25},{25,17},{2,10},{10... | collective-permute-start | bytes 196616 | tf_op jit(solution)/shard_map/ppermute | solution.py:553
  41.3 1.3 %collective-permute-start.12 = (f32[128,128]{1,0:T(8,128)S(1)}, f32[128,128]{1,0:T(8,128)S(1)}, u32[]{:S(2)}, u32[]{:S(2)}) collective-permute-start(f32[128,128]{1,0:T(8,128)S(1)} %get-tuple-element.62), channel_id=1, source_target_pairs={{0,16},{8,24},{16,0},{24,8},{1,17},{9,25},{17,1},{25,9},{2,18},{10... | collective-permute-start | bytes 196616 | tf_op jit(solution)/shard_map/ppermute | solution.py:553
  42.7 0.3 collective-permute-done.6.refs_3_
  43.1 0.5 collective-permute-done.11.refs_5_
  43.6 1.8 %collective-permute-done.12.refs_6_ = f32[128,128]{1,0:T(8,128)S(1)} collective-permute-done((f32[128,128]{1,0:T(8,128)S(1)}, f32[128,128]{1,0:T(8,128)S(1)}, u32[]{:S(2)}, u32[]{:S(2)}) %collective-permute-start.12) | collective-permute-done | bytes 65568 | tf_op jit(solution)/shard_map/ppermute | solution.py:553
  45.4 1.4 %collective-permute-done.13.refs_7_ = f32[128,128]{1,0:T(8,128)S(1)} collective-permute-done((f32[128,128]{1,0:T(8,128)S(1)}, f32[128,128]{1,0:T(8,128)S(1)}, u32[]{:S(2)}, u32[]{:S(2)}) %collective-permute-start.13) | collective-permute-done | bytes 65568 | tf_op jit(solution)/shard_map/ppermute | solution.py:553
  46.8 0.4 scan_states.1
  47.1 0.5 collective-permute-start.14
  47.9 2.0 %collective-permute-start.16 = (f32[128,128]{1,0:T(8,128)S(1)}, f32[128,128]{1,0:T(8,128)S(1)}, u32[]{:S(2)}, u32[]{:S(2)}) collective-permute-start(f32[128,128]{1,0:T(8,128)S(1)} %get-tuple-element.67), channel_id=1, source_target_pairs={{0,24},{8,16},{16,8},{24,0},{1,25},{9,17},{17,9},{25,1},{2,26},{10... | collective-permute-start | bytes 196616 | tf_op jit(solution)/shard_map/ppermute | solution.py:553
  49.9 2.8 %query_stage.1 = (bf16[16,64,256]{2,1,0:T(8,128)(2,1)S(1)}, f32[16,64,128]{2,1,0:T(8,128)S(1)}) custom-call(bf16[2,384,128]{2,1,0:T(8,128)(2,1)S(1)} %get-tuple-element.54.refs_0_, bf16[2,384,128]{2,1,0:T(8,128)(2,1)S(1)} %collective-permute-done.8.refs_1_, bf16[2,384,128]{2,1,0:T(8,128)(2,1)S(1)} %collective-permute-done.9.refs_2_, ...), custom_call_target="tpu_custom_call" | custom-call | tf_op jit(solution)/shard_map/query_stage/pallas_call | solution.py:201
  52.7 0.5 read_states.1
  53.2 3.8 %collective-permute-start.17 = (bf16[128,512]{1,0:T(8,128)(2,1)S(1)}, bf16[128,512]{1,0:T(8,128)(2,1)S(1)}, u32[]{:S(2)}, u32[]{:S(2)}) collective-permute-start(bf16[128,512]{1,0:T(8,128)(2,1)S(1)} %get-tuple-element.78), channel_id=1, source_target_pairs={{0,4},{4,0},{1,5},{5,1},{2,6},{6,2},{3,7},{7,3},{8,12},{12,8},{9,1... | collective-permute-start | bytes 393224 | tf_op jit(solution)/shard_map/ppermute | solution.py:684
  57.1 1.0 %collective-permute-done.17.refs_1_ = bf16[128,512]{1,0:T(8,128)(2,1)S(1)} collective-permute-done((bf16[128,512]{1,0:T(8,128)(2,1)S(1)}, bf16[128,512]{1,0:T(8,128)(2,1)S(1)}, u32[]{:S(2)}, u32[]{:S(2)}) %collective-permute-start.17) | collective-permute-done | bytes 131104 | tf_op jit(solution)/shard_map/ppermute | solution.py:684
  58.1 0.7 %join.1 = bf16[128,1024]{1,0:T(8,128)(2,1)} custom-call(bf16[128,512]{1,0:T(8,128)(2,1)S(1)} %get-tuple-element.77.refs_0_, bf16[128,512]{1,0:T(8,128)(2,1)S(1)} %collective-permute-done.17.refs_1_), custom_call_target="tpu_custom_call" | custom-call | tf_op jit(solution)/shard_map/join/pallas_call | solution.py:201
  (27 shorter events, 1.1 us)
Async XLA Ops:
  0.0 0.7 %copy-start.4 = (bf16[32,64]{1,0:T(8,128)(2,1)S(1)}, bf16[32,64]{1,0:T(8,128)(2,1)}, u32[]{:S(2)}) copy-start(bf16[32,64]{1,0:T(8,128)(2,1)} %refs_1_.2) | copy-start | bytes 12292
  0.7 1.0 %copy-start.1 = (bf16[32,8192]{1,0:T(8,128)(2,1)S(1)}, bf16[32,8192]{1,0:T(8,128)(2,1)}, u32[]{:S(2)}) copy-start(bf16[32,8192]{1,0:T(8,128)(2,1)} %refs_0_.2) | copy-start | bytes 1572868
  1.7 0.7 %copy-start.5 = (bf16[32,32]{1,0:T(8,128)(2,1)S(1)}, bf16[32,32]{1,0:T(8,128)(2,1)}, u32[]{:S(2)}) copy-start(bf16[32,32]{1,0:T(8,128)(2,1)} %refs_2_.1) | copy-start | bytes 6148
  2.4 1.0 %copy-start.2 = (bf16[32,8192]{1,0:T(8,128)(2,1)S(1)}, bf16[32,8192]{1,0:T(8,128)(2,1)}, u32[]{:S(2)}) copy-start(bf16[32,8192]{1,0:T(8,128)(2,1)} %refs_0_.3) | copy-start | bytes 1572868
  2.8 2.6 %collective-permute-start = (bf16[4,272,128]{2,1,0:T(8,128)(2,1)S(1)}, bf16[4,272,128]{2,1,0:T(8,128)(2,1)S(1)}, u32[]{:S(2)}, u32[]{:S(2)}) collective-permute-start(bf16[4,272,128]{2,1,0:T(8,128)(2,1)S(1)} %get-tuple-element.43), channel_id=1, source_target_pairs={{0,4},{4,0},{1,5},{5,1},{2,6},{6,2},{3,7},{7,3},{8,12},{12,8},{9,1... | collective-permute-start | bytes 835592 | tf_op jit(solution)/shard_map/ppermute | solution.py:684
  3.5 1.0 %copy-start.3 = (bf16[32,4096]{1,0:T(8,128)(2,1)S(1)}, bf16[32,4096]{1,0:T(8,128)(2,1)}, u32[]{:S(2)}) copy-start(bf16[32,4096]{1,0:T(8,128)(2,1)} %refs_1_.3) | copy-start | bytes 786436
  4.6 4.6 %collective-permute-start.7 = (bf16[4,384,128]{2,1,0:T(8,128)(2,1)S(1)}, bf16[4,384,128]{2,1,0:T(8,128)(2,1)S(1)}, u32[]{:S(2)}, u32[]{:S(2)}) collective-permute-start(bf16[4,384,128]{2,1,0:T(8,128)(2,1)S(1)} %get-tuple-element.53), channel_id=1, source_target_pairs={{0,4},{4,0},{1,5},{5,1},{2,6},{6,2},{3,7},{7,3},{8,12},{12,8},{9,1... | collective-permute-start | bytes 1179656 | tf_op jit(solution)/shard_map/ppermute | solution.py:684
  5.4 7.1 %collective-permute-start.1 = (bf16[2,272,128]{2,1,0:T(8,128)(2,1)S(1)}, bf16[2,272,128]{2,1,0:T(8,128)(2,1)S(1)}, u32[]{:S(2)}, u32[]{:S(2)}) collective-permute-start(bf16[2,272,128]{2,1,0:T(8,128)(2,1)S(1)} %get-tuple-element.45), channel_id=1, source_target_pairs={{0,1},{1,2},{2,3},{3,0},{4,5},{5,6},{6,7},{7,4},{8,9},{9,10},{10,1... | collective-permute-start | bytes 417800 | tf_op jit(solution)/shard_map/ppermute | solution.py:678
  6.8 12.1 %collective-permute-start.2 = (bf16[2,272,128]{2,1,0:T(8,128)(2,1)S(1)}, bf16[2,272,128]{2,1,0:T(8,128)(2,1)S(1)}, u32[]{:S(2)}, u32[]{:S(2)}) collective-permute-start(bf16[2,272,128]{2,1,0:T(8,128)(2,1)S(1)} %get-tuple-element.46), channel_id=1, source_target_pairs={{0,2},{1,3},{2,0},{3,1},{4,6},{5,7},{6,4},{7,5},{8,10},{9,11},{10,... | collective-permute-start | bytes 417800 | tf_op jit(solution)/shard_map/ppermute | solution.py:678
  7.9 21.5 %collective-permute-start.3 = (bf16[2,272,128]{2,1,0:T(8,128)(2,1)S(1)}, bf16[2,272,128]{2,1,0:T(8,128)(2,1)S(1)}, u32[]{:S(2)}, u32[]{:S(2)}) collective-permute-start(bf16[2,272,128]{2,1,0:T(8,128)(2,1)S(1)} %get-tuple-element.47), channel_id=1, source_target_pairs={{0,3},{1,0},{2,1},{3,2},{4,7},{5,4},{6,5},{7,6},{8,11},{9,8},{10,9... | collective-permute-start | bytes 417800 | tf_op jit(solution)/shard_map/ppermute | solution.py:678
  9.3 29.7 %collective-permute-start.8 = (bf16[2,384,128]{2,1,0:T(8,128)(2,1)S(1)}, bf16[2,384,128]{2,1,0:T(8,128)(2,1)S(1)}, u32[]{:S(2)}, u32[]{:S(2)}) collective-permute-start(bf16[2,384,128]{2,1,0:T(8,128)(2,1)S(1)} %get-tuple-element.55), channel_id=1, source_target_pairs={{0,1},{1,2},{2,3},{3,0},{4,5},{5,6},{6,7},{7,4},{8,9},{9,10},{10,1... | collective-permute-start | bytes 589832 | tf_op jit(solution)/shard_map/ppermute | solution.py:678
  9.4 29.8 %collective-permute-start.9 = (bf16[2,384,128]{2,1,0:T(8,128)(2,1)S(1)}, bf16[2,384,128]{2,1,0:T(8,128)(2,1)S(1)}, u32[]{:S(2)}, u32[]{:S(2)}) collective-permute-start(bf16[2,384,128]{2,1,0:T(8,128)(2,1)S(1)} %get-tuple-element.56), channel_id=1, source_target_pairs={{0,2},{1,3},{2,0},{3,1},{4,6},{5,7},{6,4},{7,5},{8,10},{9,11},{10,... | collective-permute-start | bytes 589832 | tf_op jit(solution)/shard_map/ppermute | solution.py:678
  12.5 26.7 %collective-permute-start.10 = (bf16[2,384,128]{2,1,0:T(8,128)(2,1)S(1)}, bf16[2,384,128]{2,1,0:T(8,128)(2,1)S(1)}, u32[]{:S(2)}, u32[]{:S(2)}) collective-permute-start(bf16[2,384,128]{2,1,0:T(8,128)(2,1)S(1)} %get-tuple-element.57), channel_id=1, source_target_pairs={{0,3},{1,0},{2,1},{3,2},{4,7},{5,4},{6,5},{7,6},{8,11},{9,8},{10,9... | collective-permute-start | bytes 589832 | tf_op jit(solution)/shard_map/ppermute | solution.py:678
  36.5 6.1 %collective-permute-start.4 = (f32[128,128]{1,0:T(8,128)S(1)}, f32[128,128]{1,0:T(8,128)S(1)}, u32[]{:S(2)}, u32[]{:S(2)}) collective-permute-start(f32[128,128]{1,0:T(8,128)S(1)} %get-tuple-element.49), channel_id=1, source_target_pairs={{0,8},{8,0},{16,24},{24,16},{1,9},{9,1},{17,25},{25,17},{2,10},{10... | collective-permute-start | bytes 196616 | tf_op jit(solution)/shard_map/ppermute | solution.py:553
  37.8 5.0 %collective-permute-start.5 = (f32[128,128]{1,0:T(8,128)S(1)}, f32[128,128]{1,0:T(8,128)S(1)}, u32[]{:S(2)}, u32[]{:S(2)}) collective-permute-start(f32[128,128]{1,0:T(8,128)S(1)} %get-tuple-element.50), channel_id=1, source_target_pairs={{0,16},{8,24},{16,0},{24,8},{1,17},{9,25},{17,1},{25,9},{2,18},{10... | collective-permute-start | bytes 196616 | tf_op jit(solution)/shard_map/ppermute | solution.py:553
  39.1 4.0 %collective-permute-start.6 = (f32[128,128]{1,0:T(8,128)S(1)}, f32[128,128]{1,0:T(8,128)S(1)}, u32[]{:S(2)}, u32[]{:S(2)}) collective-permute-start(f32[128,128]{1,0:T(8,128)S(1)} %get-tuple-element.51), channel_id=1, source_target_pairs={{0,24},{8,16},{16,8},{24,0},{1,25},{9,17},{17,9},{25,1},{2,26},{10... | collective-permute-start | bytes 196616 | tf_op jit(solution)/shard_map/ppermute | solution.py:553
  40.0 3.5 %collective-permute-start.11 = (f32[128,128]{1,0:T(8,128)S(1)}, f32[128,128]{1,0:T(8,128)S(1)}, u32[]{:S(2)}, u32[]{:S(2)}) collective-permute-start(f32[128,128]{1,0:T(8,128)S(1)} %get-tuple-element.61), channel_id=1, source_target_pairs={{0,8},{8,0},{16,24},{24,16},{1,9},{9,1},{17,25},{25,17},{2,10},{10... | collective-permute-start | bytes 196616 | tf_op jit(solution)/shard_map/ppermute | solution.py:553
  41.3 4.1 %collective-permute-start.12 = (f32[128,128]{1,0:T(8,128)S(1)}, f32[128,128]{1,0:T(8,128)S(1)}, u32[]{:S(2)}, u32[]{:S(2)}) collective-permute-start(f32[128,128]{1,0:T(8,128)S(1)} %get-tuple-element.62), channel_id=1, source_target_pairs={{0,16},{8,24},{16,0},{24,8},{1,17},{9,25},{17,1},{25,9},{2,18},{10... | collective-permute-start | bytes 196616 | tf_op jit(solution)/shard_map/ppermute | solution.py:553
  42.6 4.2 %collective-permute-start.13 = (f32[128,128]{1,0:T(8,128)S(1)}, f32[128,128]{1,0:T(8,128)S(1)}, u32[]{:S(2)}, u32[]{:S(2)}) collective-permute-start(f32[128,128]{1,0:T(8,128)S(1)} %get-tuple-element.63), channel_id=1, source_target_pairs={{0,24},{8,16},{16,8},{24,0},{1,25},{9,17},{17,9},{25,1},{2,26},{10... | collective-permute-start | bytes 196616 | tf_op jit(solution)/shard_map/ppermute | solution.py:553
  47.1 5.6 %collective-permute-start.14 = (f32[128,128]{1,0:T(8,128)S(1)}, f32[128,128]{1,0:T(8,128)S(1)}, u32[]{:S(2)}, u32[]{:S(2)}) collective-permute-start(f32[128,128]{1,0:T(8,128)S(1)} %get-tuple-element.65), channel_id=1, source_target_pairs={{0,8},{8,0},{16,24},{24,16},{1,9},{9,1},{17,25},{25,17},{2,10},{10... | collective-permute-start | bytes 196616 | tf_op jit(solution)/shard_map/ppermute | solution.py:553
  47.6 5.1 %collective-permute-start.15 = (f32[128,128]{1,0:T(8,128)S(1)}, f32[128,128]{1,0:T(8,128)S(1)}, u32[]{:S(2)}, u32[]{:S(2)}) collective-permute-start(f32[128,128]{1,0:T(8,128)S(1)} %get-tuple-element.66), channel_id=1, source_target_pairs={{0,16},{8,24},{16,0},{24,8},{1,17},{9,25},{17,1},{25,9},{2,18},{10... | collective-permute-start | bytes 196616 | tf_op jit(solution)/shard_map/ppermute | solution.py:553
  47.9 4.8 %collective-permute-start.16 = (f32[128,128]{1,0:T(8,128)S(1)}, f32[128,128]{1,0:T(8,128)S(1)}, u32[]{:S(2)}, u32[]{:S(2)}) collective-permute-start(f32[128,128]{1,0:T(8,128)S(1)} %get-tuple-element.67), channel_id=1, source_target_pairs={{0,24},{8,16},{16,8},{24,0},{1,25},{9,17},{17,9},{25,1},{2,26},{10... | collective-permute-start | bytes 196616 | tf_op jit(solution)/shard_map/ppermute | solution.py:553
  53.2 4.8 %collective-permute-start.17 = (bf16[128,512]{1,0:T(8,128)(2,1)S(1)}, bf16[128,512]{1,0:T(8,128)(2,1)S(1)}, u32[]{:S(2)}, u32[]{:S(2)}) collective-permute-start(bf16[128,512]{1,0:T(8,128)(2,1)S(1)} %get-tuple-element.78), channel_id=1, source_target_pairs={{0,4},{4,0},{1,5},{5,1},{2,6},{6,2},{3,7},{7,3},{8,12},{12,8},{9,1... | collective-permute-start | bytes 393224 | tf_op jit(solution)/shard_map/ppermute | solution.py:684
  (1 other events, 0.0 us)

commit v4 on v3

--- a/solution.py
+++ b/solution.py
@@ -310,6 +310,21 @@
 
     outs = [shape(2, *kept.shape[1:])] * sizes.groups
     return call(kernel, outs, kept, swapped, name=name)
+
+
+def merge_reads(sizes, kept, swapped):
+    value_rows = sizes.heads * KEY_ROWS
+    query_rows = sizes.heads * TOK
+
+    def kernel(kept, swapped, *outs):
+        for ahead in range(sizes.groups):
+            for side, source in enumerate((kept, swapped)):
+                outs[ahead][side] = source[ahead, :value_rows, :]
+                outs[sizes.groups + ahead][side] = source[ahead, value_rows:, :]
+
+    outs = [shape(2, value_rows, DK)] * sizes.groups + [shape(2, query_rows, DK)] * sizes.groups
+    merged = call(kernel, outs, kept, swapped, name="merge_reads")
+    return merged[: sizes.groups], merged[sizes.groups :]
 
 
 def gather(sizes, pieces, first, count, scratch):
@@ -580,7 +595,7 @@
         values, before, keys, inverse, ratio, rows, prefix, reader_out, inner_out, blocks = refs[
             groups:
         ]
-        gather(sizes, pieces, sizes.heads * KEY_ROWS, sizes.heads * TOK, blocks)
+        gather(sizes, pieces, 0, sizes.heads * TOK, blocks)
         for base in range(0, sizes.units, GROUP):
             members = range(base, min(base + GROUP, sizes.units))
             queries = [unit_rows(blocks, *sizes.unit(unit), TOK) for unit in members]
@@ -686,14 +701,16 @@
     kept_keys, sent_keys = pack_keys(sizes, keys, betas, log_gates, own_starts)
     key_parts = spread(merge(sizes, kept_keys, swapped(sent_keys), "merge_keys"))
     kept, sent = pack_reads(sizes, values, queries, after=(kept_keys,))
-    reads = spread(merge(sizes, kept, swapped(sent), "merge_reads"))
+    value_parts, query_parts = merge_reads(sizes, kept, swapped(sent))
+    value_parts = spread(value_parts)
+    query_parts = spread(query_parts)
     (unit_keys, inverse, ends, ratios, rows, steps, prefixes), transitions = key_stage(
         sizes, key_parts
     )
-    unit_values, before, injects = value_stage(sizes, reads, ends, steps)
+    unit_values, before, injects = value_stage(sizes, value_parts, ends, steps)
     states = entry_states(sizes, transitions, injects)
     readers, inners = query_stage(
-        sizes, reads, unit_values, before, unit_keys, inverse, ratios, rows, prefixes
+        sizes, query_parts, unit_values, before, unit_keys, inverse, ratios, rows, prefixes
     )
     own, other = read_states(sizes, states, readers, inners)
     return join(sizes, own, swapped(other))

time: 59.1 us -> 58.6 us (level)
  the two profiles are of different devices: /device:TPU:9 before, /device:TPU:0 now
where the time goes in v4:
time: 58.6 us; the launch traced here: 58.2 us
  starting transfers between devices  32.8 us (56%)
  Pallas kernels  12.9 us (22%)
  waiting for transfers between devices  8.73 us (15%)
  local copies, waits for them, and re-layouts  3.68 us (6%)
    ppermute x9, starting transfers between devices, spread(): lax.ppermute(part, 'head', [(z, (z + ahead) % groups) for z in range(grou...  21.1 us
    pallas_call x10, Pallas kernels, call(): pl.pallas_call(body, out_shape=outs, in_specs=specs, scratch_shapes=scrat...  12.9 us
    ppermute x9, starting transfers between devices, exchanged(): lax.ppermute(part, 'chip', [(chip, chip ^ number) for chip in range(sizes...  10.7 us
    ppermute x9, waiting for transfers between devices, spread(): lax.ppermute(part, 'head', [(z, (z + ahead) % groups) for z in range(grou...  6.07 us
    unnamed x12, local copies, waits for them, and re-layouts  3.6 us
    ppermute x3, waiting for transfers between devices, swapped(): return lax.ppermute(part, 'core', [(0, 1), (1, 0)])  1.34 us
    ppermute x9, waiting for transfers between devices, exchanged(): lax.ppermute(part, 'chip', [(chip, chip ^ number) for chip in range(sizes...  1.32 us
  transfers between devices with their start and end apart: 21, of which 5 were waited for; matrix products, arithmetic and copies ran while one was open for 0% of the time, Pallas kernels for 20%

profile of v4, /device:TPU:0, one launch (start us, length us, event | category | flops | bytes accessed | tf_op | source)
XLA Modules:
  0.0 58.2 jit_solution(18429898706869331347)
XLA Ops:
  0.0 0.7 %copy-done = s32[128]{0:T(128)S(1)} copy-done((s32[128]{0:T(128)S(1)}, s32[128]{0:T(128)}, u32[]{:S(2)}) %copy-start) | copy-done | bytes 536
  0.7 1.0 %copy-done.1 = bf16[32,8192]{1,0:T(8,128)(2,1)S(1)} copy-done((bf16[32,8192]{1,0:T(8,128)(2,1)S(1)}, bf16[32,8192]{1,0:T(8,128)(2,1)}, u32[]{:S(2)}) %copy-start.1) | copy-done | bytes 524312
  1.8 0.7 %copy-done.5 = bf16[32,32]{1,0:T(8,128)(2,1)S(1)} copy-done((bf16[32,32]{1,0:T(8,128)(2,1)S(1)}, bf16[32,32]{1,0:T(8,128)(2,1)}, u32[]{:S(2)}) %copy-start.5) | copy-done | bytes 2072
  2.8 0.4 collective-permute-start
  3.5 0.9 %copy-done.3 = bf16[32,4096]{1,0:T(8,128)(2,1)S(1)} copy-done((bf16[32,4096]{1,0:T(8,128)(2,1)S(1)}, bf16[32,4096]{1,0:T(8,128)(2,1)}, u32[]{:S(2)}) %copy-start.3) | copy-done | bytes 262168
  4.7 0.5 collective-permute-start.7
  5.2 2.7 %collective-permute-start.1 = (bf16[2,272,128]{2,1,0:T(8,128)(2,1)S(1)}, bf16[2,272,128]{2,1,0:T(8,128)(2,1)S(1)}, u32[]{:S(2)}, u32[]{:S(2)}) collective-permute-start(bf16[2,272,128]{2,1,0:T(8,128)(2,1)S(1)} %get-tuple-element.49), channel_id=1, source_target_pairs={{0,1},{1,2},{2,3},{3,0},{4,5},{5,6},{6,7},{7,4},{8,9},{9,10},{10,1... | collective-permute-start | bytes 417800 | tf_op jit(solution)/shard_map/ppermute | solution.py:693
  7.9 2.6 %collective-permute-start.2 = (bf16[2,272,128]{2,1,0:T(8,128)(2,1)S(1)}, bf16[2,272,128]{2,1,0:T(8,128)(2,1)S(1)}, u32[]{:S(2)}, u32[]{:S(2)}) collective-permute-start(bf16[2,272,128]{2,1,0:T(8,128)(2,1)S(1)} %get-tuple-element.50), channel_id=1, source_target_pairs={{0,2},{1,3},{2,0},{3,1},{4,6},{5,7},{6,4},{7,5},{8,10},{9,11},{10,... | collective-permute-start | bytes 417800 | tf_op jit(solution)/shard_map/ppermute | solution.py:693
  10.5 1.3 %collective-permute-start.3 = (bf16[2,272,128]{2,1,0:T(8,128)(2,1)S(1)}, bf16[2,272,128]{2,1,0:T(8,128)(2,1)S(1)}, u32[]{:S(2)}, u32[]{:S(2)}) collective-permute-start(bf16[2,272,128]{2,1,0:T(8,128)(2,1)S(1)} %get-tuple-element.51), channel_id=1, source_target_pairs={{0,3},{1,0},{2,1},{3,2},{4,7},{5,4},{6,5},{7,6},{8,11},{9,8},{10,9... | collective-permute-start | bytes 417800 | tf_op jit(solution)/shard_map/ppermute | solution.py:693
  11.9 0.7 %collective-permute-start.8 = (bf16[2,256,128]{2,1,0:T(8,128)(2,1)S(1)}, bf16[2,256,128]{2,1,0:T(8,128)(2,1)S(1)}, u32[]{:S(2)}, u32[]{:S(2)}) collective-permute-start(bf16[2,256,128]{2,1,0:T(8,128)(2,1)S(1)} %get-tuple-element.59), channel_id=1, source_target_pairs={{0,1},{1,2},{2,3},{3,0},{4,5},{5,6},{6,7},{7,4},{8,9},{9,10},{10,1... | collective-permute-start | bytes 393224 | tf_op jit(solution)/shard_map/ppermute | solution.py:693
  13.0 1.6 %collective-permute-done.1.refs_1_ = bf16[2,272,128]{2,1,0:T(8,128)(2,1)S(1)} collective-permute-done((bf16[2,272,128]{2,1,0:T(8,128)(2,1)S(1)}, bf16[2,272,128]{2,1,0:T(8,128)(2,1)S(1)}, u32[]{:S(2)}, u32[]{:S(2)}) %collective-permute-start.1) | collective-permute-done | bytes 139296 | tf_op jit(solution)/shard_map/ppermute | solution.py:693
  14.5 2.0 %collective-permute-start.10 = (bf16[2,256,128]{2,1,0:T(8,128)(2,1)S(1)}, bf16[2,256,128]{2,1,0:T(8,128)(2,1)S(1)}, u32[]{:S(2)}, u32[]{:S(2)}) collective-permute-start(bf16[2,256,128]{2,1,0:T(8,128)(2,1)S(1)} %get-tuple-element.61), channel_id=1, source_target_pairs={{0,3},{1,0},{2,1},{3,2},{4,7},{5,4},{6,5},{7,6},{8,11},{9,8},{10,9... | collective-permute-start | bytes 393224 | tf_op jit(solution)/shard_map/ppermute | solution.py:693
  16.6 4.0 %collective-permute-done.2.refs_2_ = bf16[2,272,128]{2,1,0:T(8,128)(2,1)S(1)} collective-permute-done((bf16[2,272,128]{2,1,0:T(8,128)(2,1)S(1)}, bf16[2,272,128]{2,1,0:T(8,128)(2,1)S(1)}, u32[]{:S(2)}, u32[]{:S(2)}) %collective-permute-start.2) | collective-permute-done | bytes 139296 | tf_op jit(solution)/shard_map/ppermute | solution.py:693
  20.5 7.1 %key_stage.1 = (bf16[16,128,128]{2,1,0:T(8,128)(2,1)S(1)}, bf16[16,128,256]{2,1,0:T(8,128)(2,1)S(1)}, bf16[16,128,256]{2,1,0:T(8,128)(2,1)S(1)}, f32[16,64,128]{...) custom-call(bf16[2,272,128]{2,1,0:T(8,128)(2,1)S(1)} %get-tuple-elem, ...), custom_call_target="tpu_custom_call" | custom-call | tf_op jit(solution)/shard_map/key_stage/pallas_call | solution.py:201
  27.6 1.7 %collective-permute-start.4 = (f32[128,128]{1,0:T(8,128)S(1)}, f32[128,128]{1,0:T(8,128)S(1)}, u32[]{:S(2)}, u32[]{:S(2)}) collective-permute-start(f32[128,128]{1,0:T(8,128)S(1)} %get-tuple-element.53), channel_id=1, source_target_pairs={{0,8},{8,0},{16,24},{24,16},{1,9},{9,1},{17,25},{25,17},{2,10},{10... | collective-permute-start | bytes 196616 | tf_op jit(solution)/shard_map/ppermute | solution.py:568
  29.3 1.5 %collective-permute-start.5 = (f32[128,128]{1,0:T(8,128)S(1)}, f32[128,128]{1,0:T(8,128)S(1)}, u32[]{:S(2)}, u32[]{:S(2)}) collective-permute-start(f32[128,128]{1,0:T(8,128)S(1)} %get-tuple-element.54), channel_id=1, source_target_pairs={{0,16},{8,24},{16,0},{24,8},{1,17},{9,25},{17,1},{25,9},{2,18},{10... | collective-permute-start | bytes 196616 | tf_op jit(solution)/shard_map/ppermute | solution.py:568
  31.2 0.5 collective-permute-done.9.refs_2_
  31.7 0.8 %value_stage.1 = (bf16[16,128,128]{2,1,0:T(8,128)(2,1)S(1)}, f32[16,128,128]{2,1,0:T(8,128)S(1)}, f32[128,128]{1,0:T(8,128)S(1)}, f32[128,128]{1,0:T(8,128)S(1)}...) custom-call(bf16[2,256,128]{2,1,0:T(8,128)(2,1)S(1)} %get-tuple-element.58.refs_0_, ...), custom_call_target="tpu_custom_call" | custom-call | tf_op jit(solution)/shard_map/value_stage/pallas_call | solution.py:201
  32.5 1.5 %collective-permute-start.11 = (f32[128,128]{1,0:T(8,128)S(1)}, f32[128,128]{1,0:T(8,128)S(1)}, u32[]{:S(2)}, u32[]{:S(2)}) collective-permute-start(f32[128,128]{1,0:T(8,128)S(1)} %get-tuple-element.65), channel_id=1, source_target_pairs={{0,8},{8,0},{16,24},{24,16},{1,9},{9,1},{17,25},{25,17},{2,10},{10... | collective-permute-start | bytes 196616 | tf_op jit(solution)/shard_map/ppermute | solution.py:568
  34.1 1.5 %collective-permute-start.12 = (f32[128,128]{1,0:T(8,128)S(1)}, f32[128,128]{1,0:T(8,128)S(1)}, u32[]{:S(2)}, u32[]{:S(2)}) collective-permute-start(f32[128,128]{1,0:T(8,128)S(1)} %get-tuple-element.66), channel_id=1, source_target_pairs={{0,16},{8,24},{16,0},{24,8},{1,17},{9,25},{17,1},{25,9},{2,18},{10... | collective-permute-start | bytes 196616 | tf_op jit(solution)/shard_map/ppermute | solution.py:568
  35.6 0.5 collective-permute-start.13
  36.1 8.4 %collective-permute-start.17 = (bf16[2,128,128]{2,1,0:T(8,128)(2,1)S(1)}, bf16[2,128,128]{2,1,0:T(8,128)(2,1)S(1)}, u32[]{:S(2)}, u32[]{:S(2)}) collective-permute-start(bf16[2,128,128]{2,1,0:T(8,128)(2,1)S(1)} %get-tuple-element.73), channel_id=1, source_target_pairs={{0,1},{1,2},{2,3},{3,0},{4,5},{5,6},{6,7},{7,4},{8,9},{9,10},{10,1... | collective-permute-start | bytes 196616 | tf_op jit(solution)/shard_map/ppermute | solution.py:693
  44.5 2.0 %collective-permute-start.18 = (bf16[2,128,128]{2,1,0:T(8,128)(2,1)S(1)}, bf16[2,128,128]{2,1,0:T(8,128)(2,1)S(1)}, u32[]{:S(2)}, u32[]{:S(2)}) collective-permute-start(bf16[2,128,128]{2,1,0:T(8,128)(2,1)S(1)} %get-tuple-element.74), channel_id=1, source_target_pairs={{0,2},{1,3},{2,0},{3,1},{4,6},{5,7},{6,4},{7,5},{8,10},{9,11},{10,... | collective-permute-start | bytes 196616 | tf_op jit(solution)/shard_map/ppermute | solution.py:693
  46.5 1.0 %collective-permute-start.19 = (bf16[2,128,128]{2,1,0:T(8,128)(2,1)S(1)}, bf16[2,128,128]{2,1,0:T(8,128)(2,1)S(1)}, u32[]{:S(2)}, u32[]{:S(2)}) collective-permute-start(bf16[2,128,128]{2,1,0:T(8,128)(2,1)S(1)} %get-tuple-element.75), channel_id=1, source_target_pairs={{0,3},{1,0},{2,1},{3,2},{4,7},{5,4},{6,5},{7,6},{8,11},{9,8},{10,9... | collective-permute-start | bytes 196616 | tf_op jit(solution)/shard_map/ppermute | solution.py:693
  47.9 1.0 %collective-permute-start.14 = (f32[128,128]{1,0:T(8,128)S(1)}, f32[128,128]{1,0:T(8,128)S(1)}, u32[]{:S(2)}, u32[]{:S(2)}) collective-permute-start(f32[128,128]{1,0:T(8,128)S(1)} %get-tuple-element.69), channel_id=1, source_target_pairs={{0,8},{8,0},{16,24},{24,16},{1,9},{9,1},{17,25},{25,17},{2,10},{10... | collective-permute-start | bytes 196616 | tf_op jit(solution)/shard_map/ppermute | solution.py:568
  48.9 1.6 %collective-permute-start.15 = (f32[128,128]{1,0:T(8,128)S(1)}, f32[128,128]{1,0:T(8,128)S(1)}, u32[]{:S(2)}, u32[]{:S(2)}) collective-permute-start(f32[128,128]{1,0:T(8,128)S(1)} %get-tuple-element.70), channel_id=1, source_target_pairs={{0,16},{8,24},{16,0},{24,8},{1,17},{9,25},{17,1},{25,9},{2,18},{10... | collective-permute-start | bytes 196616 | tf_op jit(solution)/shard_map/ppermute | solution.py:568
  50.4 1.0 %collective-permute-start.16 = (f32[128,128]{1,0:T(8,128)S(1)}, f32[128,128]{1,0:T(8,128)S(1)}, u32[]{:S(2)}, u32[]{:S(2)}) collective-permute-start(f32[128,128]{1,0:T(8,128)S(1)} %get-tuple-element.71), channel_id=1, source_target_pairs={{0,24},{8,16},{16,8},{24,0},{1,25},{9,17},{17,9},{25,1},{2,26},{10... | collective-permute-start | bytes 196616 | tf_op jit(solution)/shard_map/ppermute | solution.py:568
  51.4 2.8 %query_stage.1 = (bf16[16,64,256]{2,1,0:T(8,128)(2,1)S(1)}, f32[16,64,128]{2,1,0:T(8,128)S(1)}) custom-call(bf16[2,128,128]{2,1,0:T(8,128)(2,1)S(1)} %get-tuple-element.72.refs_0_, bf16[2,128,128]{2,1,0:T(8,128)(2,1)S(1)} %collective-permute-done.17.refs_1_, bf16[2,128,128]{2,1,0:T(8,128)(2,1)S(1)} %collective-permute-done.18.refs_2_, ...), custom_call_target="tpu_custom_call" | custom-call | tf_op jit(solution)/shard_map/query_stage/pallas_call | solution.py:201
  54.3 1.3 %collective-permute-done.16.refs_3_ = f32[128,128]{1,0:T(8,128)S(1)} collective-permute-done((f32[128,128]{1,0:T(8,128)S(1)}, f32[128,128]{1,0:T(8,128)S(1)}, u32[]{:S(2)}, u32[]{:S(2)}) %collective-permute-start.16) | collective-permute-done | bytes 65568 | tf_op jit(solution)/shard_map/ppermute | solution.py:568
  55.6 0.5 read_states.1
  56.2 1.3 %collective-permute-done.20.refs_1_ = bf16[128,512]{1,0:T(8,128)(2,1)S(1)} collective-permute-done((bf16[128,512]{1,0:T(8,128)(2,1)S(1)}, bf16[128,512]{1,0:T(8,128)(2,1)S(1)}, u32[]{:S(2)}, u32[]{:S(2)}) %collective-permute-start.20) | collective-permute-done | bytes 131104 | tf_op jit(solution)/shard_map/ppermute | solution.py:699
  57.5 0.7 %join.1 = bf16[128,1024]{1,0:T(8,128)(2,1)} custom-call(bf16[128,512]{1,0:T(8,128)(2,1)S(1)} %get-tuple-element.85.refs_0_, bf16[128,512]{1,0:T(8,128)(2,1)S(1)} %collective-permute-done.20.refs_1_), custom_call_target="tpu_custom_call" | custom-call | tf_op jit(solution)/shard_map/join/pallas_call | solution.py:201
  (33 shorter events, 2.1 us)
Async XLA Ops:
  0.0 0.7 %copy-start = (s32[128]{0:T(128)S(1)}, s32[128]{0:T(128)}, u32[]{:S(2)}) copy-start(s32[128]{0:T(128)} %param.11) | copy-start | bytes 1540
  0.0 0.7 %copy-start.4 = (bf16[32,64]{1,0:T(8,128)(2,1)S(1)}, bf16[32,64]{1,0:T(8,128)(2,1)}, u32[]{:S(2)}) copy-start(bf16[32,64]{1,0:T(8,128)(2,1)} %refs_1_.2) | copy-start | bytes 12292
  0.7 1.0 %copy-start.1 = (bf16[32,8192]{1,0:T(8,128)(2,1)S(1)}, bf16[32,8192]{1,0:T(8,128)(2,1)}, u32[]{:S(2)}) copy-start(bf16[32,8192]{1,0:T(8,128)(2,1)} %refs_0_.2) | copy-start | bytes 1572868
  1.8 0.7 %copy-start.5 = (bf16[32,32]{1,0:T(8,128)(2,1)S(1)}, bf16[32,32]{1,0:T(8,128)(2,1)}, u32[]{:S(2)}) copy-start(bf16[32,32]{1,0:T(8,128)(2,1)} %refs_2_.1) | copy-start | bytes 6148
  2.5 1.0 %copy-start.2 = (bf16[32,8192]{1,0:T(8,128)(2,1)S(1)}, bf16[32,8192]{1,0:T(8,128)(2,1)}, u32[]{:S(2)}) copy-start(bf16[32,8192]{1,0:T(8,128)(2,1)} %refs_0_.3) | copy-start | bytes 1572868
  2.8 2.4 %collective-permute-start = (bf16[4,272,128]{2,1,0:T(8,128)(2,1)S(1)}, bf16[4,272,128]{2,1,0:T(8,128)(2,1)S(1)}, u32[]{:S(2)}, u32[]{:S(2)}) collective-permute-start(bf16[4,272,128]{2,1,0:T(8,128)(2,1)S(1)} %get-tuple-element.47), channel_id=1, source_target_pairs={{0,4},{4,0},{1,5},{5,1},{2,6},{6,2},{3,7},{7,3},{8,12},{12,8},{9,1... | collective-permute-start | bytes 835592 | tf_op jit(solution)/shard_map/ppermute | solution.py:699
  3.5 0.9 %copy-start.3 = (bf16[32,4096]{1,0:T(8,128)(2,1)S(1)}, bf16[32,4096]{1,0:T(8,128)(2,1)}, u32[]{:S(2)}) copy-start(bf16[32,4096]{1,0:T(8,128)(2,1)} %refs_1_.3) | copy-start | bytes 786436
  4.7 7.2 %collective-permute-start.7 = (bf16[4,384,128]{2,1,0:T(8,128)(2,1)S(1)}, bf16[4,384,128]{2,1,0:T(8,128)(2,1)S(1)}, u32[]{:S(2)}, u32[]{:S(2)}) collective-permute-start(bf16[4,384,128]{2,1,0:T(8,128)(2,1)S(1)} %get-tuple-element.57), channel_id=1, source_target_pairs={{0,4},{4,0},{1,5},{5,1},{2,6},{6,2},{3,7},{7,3},{8,12},{12,8},{9,1... | collective-permute-start | bytes 1179656 | tf_op jit(solution)/shard_map/ppermute | solution.py:699
  5.2 9.3 %collective-permute-start.1 = (bf16[2,272,128]{2,1,0:T(8,128)(2,1)S(1)}, bf16[2,272,128]{2,1,0:T(8,128)(2,1)S(1)}, u32[]{:S(2)}, u32[]{:S(2)}) collective-permute-start(bf16[2,272,128]{2,1,0:T(8,128)(2,1)S(1)} %get-tuple-element.49), channel_id=1, source_target_pairs={{0,1},{1,2},{2,3},{3,0},{4,5},{5,6},{6,7},{7,4},{8,9},{9,10},{10,1... | collective-permute-start | bytes 417800 | tf_op jit(solution)/shard_map/ppermute | solution.py:693
  7.9 12.6 %collective-permute-start.2 = (bf16[2,272,128]{2,1,0:T(8,128)(2,1)S(1)}, bf16[2,272,128]{2,1,0:T(8,128)(2,1)S(1)}, u32[]{:S(2)}, u32[]{:S(2)}) collective-permute-start(bf16[2,272,128]{2,1,0:T(8,128)(2,1)S(1)} %get-tuple-element.50), channel_id=1, source_target_pairs={{0,2},{1,3},{2,0},{3,1},{4,6},{5,7},{6,4},{7,5},{8,10},{9,11},{10,... | collective-permute-start | bytes 417800 | tf_op jit(solution)/shard_map/ppermute | solution.py:693
  10.5 10.1 %collective-permute-start.3 = (bf16[2,272,128]{2,1,0:T(8,128)(2,1)S(1)}, bf16[2,272,128]{2,1,0:T(8,128)(2,1)S(1)}, u32[]{:S(2)}, u32[]{:S(2)}) collective-permute-start(bf16[2,272,128]{2,1,0:T(8,128)(2,1)S(1)} %get-tuple-element.51), channel_id=1, source_target_pairs={{0,3},{1,0},{2,1},{3,2},{4,7},{5,4},{6,5},{7,6},{8,11},{9,8},{10,9... | collective-permute-start | bytes 417800 | tf_op jit(solution)/shard_map/ppermute | solution.py:693
  11.9 19.0 %collective-permute-start.8 = (bf16[2,256,128]{2,1,0:T(8,128)(2,1)S(1)}, bf16[2,256,128]{2,1,0:T(8,128)(2,1)S(1)}, u32[]{:S(2)}, u32[]{:S(2)}) collective-permute-start(bf16[2,256,128]{2,1,0:T(8,128)(2,1)S(1)} %get-tuple-element.59), channel_id=1, source_target_pairs={{0,1},{1,2},{2,3},{3,0},{4,5},{5,6},{6,7},{7,4},{8,9},{9,10},{10,1... | collective-permute-start | bytes 393224 | tf_op jit(solution)/shard_map/ppermute | solution.py:693
  12.6 19.1 %collective-permute-start.9 = (bf16[2,256,128]{2,1,0:T(8,128)(2,1)S(1)}, bf16[2,256,128]{2,1,0:T(8,128)(2,1)S(1)}, u32[]{:S(2)}, u32[]{:S(2)}) collective-permute-start(bf16[2,256,128]{2,1,0:T(8,128)(2,1)S(1)} %get-tuple-element.60), channel_id=1, source_target_pairs={{0,2},{1,3},{2,0},{3,1},{4,6},{5,7},{6,4},{7,5},{8,10},{9,11},{10,... | collective-permute-start | bytes 393224 | tf_op jit(solution)/shard_map/ppermute | solution.py:693
  14.5 17.2 %collective-permute-start.10 = (bf16[2,256,128]{2,1,0:T(8,128)(2,1)S(1)}, bf16[2,256,128]{2,1,0:T(8,128)(2,1)S(1)}, u32[]{:S(2)}, u32[]{:S(2)}) collective-permute-start(bf16[2,256,128]{2,1,0:T(8,128)(2,1)S(1)} %get-tuple-element.61), channel_id=1, source_target_pairs={{0,3},{1,0},{2,1},{3,2},{4,7},{5,4},{6,5},{7,6},{8,11},{9,8},{10,9... | collective-permute-start | bytes 393224 | tf_op jit(solution)/shard_map/ppermute | solution.py:693
  27.6 7.9 %collective-permute-start.4 = (f32[128,128]{1,0:T(8,128)S(1)}, f32[128,128]{1,0:T(8,128)S(1)}, u32[]{:S(2)}, u32[]{:S(2)}) collective-permute-start(f32[128,128]{1,0:T(8,128)S(1)} %get-tuple-element.53), channel_id=1, source_target_pairs={{0,8},{8,0},{16,24},{24,16},{1,9},{9,1},{17,25},{25,17},{2,10},{10... | collective-permute-start | bytes 196616 | tf_op jit(solution)/shard_map/ppermute | solution.py:568
  29.3 6.8 %collective-permute-start.5 = (f32[128,128]{1,0:T(8,128)S(1)}, f32[128,128]{1,0:T(8,128)S(1)}, u32[]{:S(2)}, u32[]{:S(2)}) collective-permute-start(f32[128,128]{1,0:T(8,128)S(1)} %get-tuple-element.54), channel_id=1, source_target_pairs={{0,16},{8,24},{16,0},{24,8},{1,17},{9,25},{17,1},{25,9},{2,18},{10... | collective-permute-start | bytes 196616 | tf_op jit(solution)/shard_map/ppermute | solution.py:568
  30.9 13.7 %collective-permute-start.6 = (f32[128,128]{1,0:T(8,128)S(1)}, f32[128,128]{1,0:T(8,128)S(1)}, u32[]{:S(2)}, u32[]{:S(2)}) collective-permute-start(f32[128,128]{1,0:T(8,128)S(1)} %get-tuple-element.55), channel_id=1, source_target_pairs={{0,24},{8,16},{16,8},{24,0},{1,25},{9,17},{17,9},{25,1},{2,26},{10... | collective-permute-start | bytes 196616 | tf_op jit(solution)/shard_map/ppermute | solution.py:568
  32.5 14.0 %collective-permute-start.11 = (f32[128,128]{1,0:T(8,128)S(1)}, f32[128,128]{1,0:T(8,128)S(1)}, u32[]{:S(2)}, u32[]{:S(2)}) collective-permute-start(f32[128,128]{1,0:T(8,128)S(1)} %get-tuple-element.65), channel_id=1, source_target_pairs={{0,8},{8,0},{16,24},{24,16},{1,9},{9,1},{17,25},{25,17},{2,10},{10... | collective-permute-start | bytes 196616 | tf_op jit(solution)/shard_map/ppermute | solution.py:568
  34.1 13.4 %collective-permute-start.12 = (f32[128,128]{1,0:T(8,128)S(1)}, f32[128,128]{1,0:T(8,128)S(1)}, u32[]{:S(2)}, u32[]{:S(2)}) collective-permute-start(f32[128,128]{1,0:T(8,128)S(1)} %get-tuple-element.66), channel_id=1, source_target_pairs={{0,16},{8,24},{16,0},{24,8},{1,17},{9,25},{17,1},{25,9},{2,18},{10... | collective-permute-start | bytes 196616 | tf_op jit(solution)/shard_map/ppermute | solution.py:568
  35.6 11.9 %collective-permute-start.13 = (f32[128,128]{1,0:T(8,128)S(1)}, f32[128,128]{1,0:T(8,128)S(1)}, u32[]{:S(2)}, u32[]{:S(2)}) collective-permute-start(f32[128,128]{1,0:T(8,128)S(1)} %get-tuple-element.67), channel_id=1, source_target_pairs={{0,24},{8,16},{16,8},{24,0},{1,25},{9,17},{17,9},{25,1},{2,26},{10... | collective-permute-start | bytes 196616 | tf_op jit(solution)/shard_map/ppermute | solution.py:568
  36.1 14.3 %collective-permute-start.17 = (bf16[2,128,128]{2,1,0:T(8,128)(2,1)S(1)}, bf16[2,128,128]{2,1,0:T(8,128)(2,1)S(1)}, u32[]{:S(2)}, u32[]{:S(2)}) collective-permute-start(bf16[2,128,128]{2,1,0:T(8,128)(2,1)S(1)} %get-tuple-element.73), channel_id=1, source_target_pairs={{0,1},{1,2},{2,3},{3,0},{4,5},{5,6},{6,7},{7,4},{8,9},{9,10},{10,1... | collective-permute-start | bytes 196616 | tf_op jit(solution)/shard_map/ppermute | solution.py:693
  44.5 6.9 %collective-permute-start.18 = (bf16[2,128,128]{2,1,0:T(8,128)(2,1)S(1)}, bf16[2,128,128]{2,1,0:T(8,128)(2,1)S(1)}, u32[]{:S(2)}, u32[]{:S(2)}) collective-permute-start(bf16[2,128,128]{2,1,0:T(8,128)(2,1)S(1)} %get-tuple-element.74), channel_id=1, source_target_pairs={{0,2},{1,3},{2,0},{3,1},{4,6},{5,7},{6,4},{7,5},{8,10},{9,11},{10,... | collective-permute-start | bytes 196616 | tf_op jit(solution)/shard_map/ppermute | solution.py:693
  46.5 4.9 %collective-permute-start.19 = (bf16[2,128,128]{2,1,0:T(8,128)(2,1)S(1)}, bf16[2,128,128]{2,1,0:T(8,128)(2,1)S(1)}, u32[]{:S(2)}, u32[]{:S(2)}) collective-permute-start(bf16[2,128,128]{2,1,0:T(8,128)(2,1)S(1)} %get-tuple-element.75), channel_id=1, source_target_pairs={{0,3},{1,0},{2,1},{3,2},{4,7},{5,4},{6,5},{7,6},{8,11},{9,8},{10,9... | collective-permute-start | bytes 196616 | tf_op jit(solution)/shard_map/ppermute | solution.py:693
  47.9 6.4 %collective-permute-start.14 = (f32[128,128]{1,0:T(8,128)S(1)}, f32[128,128]{1,0:T(8,128)S(1)}, u32[]{:S(2)}, u32[]{:S(2)}) collective-permute-start(f32[128,128]{1,0:T(8,128)S(1)} %get-tuple-element.69), channel_id=1, source_target_pairs={{0,8},{8,0},{16,24},{24,16},{1,9},{9,1},{17,25},{25,17},{2,10},{10... | collective-permute-start | bytes 196616 | tf_op jit(solution)/shard_map/ppermute | solution.py:568
  48.9 5.4 %collective-permute-start.15 = (f32[128,128]{1,0:T(8,128)S(1)}, f32[128,128]{1,0:T(8,128)S(1)}, u32[]{:S(2)}, u32[]{:S(2)}) collective-permute-start(f32[128,128]{1,0:T(8,128)S(1)} %get-tuple-element.70), channel_id=1, source_target_pairs={{0,16},{8,24},{16,0},{24,8},{1,17},{9,25},{17,1},{25,9},{2,18},{10... | collective-permute-start | bytes 196616 | tf_op jit(solution)/shard_map/ppermute | solution.py:568
  50.4 5.2 %collective-permute-start.16 = (f32[128,128]{1,0:T(8,128)S(1)}, f32[128,128]{1,0:T(8,128)S(1)}, u32[]{:S(2)}, u32[]{:S(2)}) collective-permute-start(f32[128,128]{1,0:T(8,128)S(1)} %get-tuple-element.71), channel_id=1, source_target_pairs={{0,24},{8,16},{16,8},{24,0},{1,25},{9,17},{17,9},{25,1},{2,26},{10... | collective-permute-start | bytes 196616 | tf_op jit(solution)/shard_map/ppermute | solution.py:568
  56.1 1.4 %collective-permute-start.20 = (bf16[128,512]{1,0:T(8,128)(2,1)S(1)}, bf16[128,512]{1,0:T(8,128)(2,1)S(1)}, u32[]{:S(2)}, u32[]{:S(2)}) collective-permute-start(bf16[128,512]{1,0:T(8,128)(2,1)S(1)} %get-tuple-element.86), channel_id=1, source_target_pairs={{0,4},{4,0},{1,5},{5,1},{2,6},{6,2},{3,7},{7,3},{8,12},{12,8},{9,1... | collective-permute-start | bytes 393224 | tf_op jit(solution)/shard_map/ppermute | solution.py:699

commit v5 on v2

--- a/solution.py
+++ b/solution.py
@@ -233,21 +233,22 @@
     ]
 
 
-def pack_keys(sizes, keys, betas, log_gates, starts):
+def pack_keys(sizes, keys, scalars, starts):
     rows = sizes.heads * KEY_ROWS
     count = sizes.heads * NH
 
-    def kernel(keys, betas, log_gates, starts, *outs):
+    def kernel(keys, scalars, starts, *outs):
         z = axis_index("head")
         core = axis_index("core")
-        heads = log_gates.shape[1]
+        width = scalars.shape[1]
+        heads = width // (NH + 1)
+        extent = (heads, width)
         pieces = []
         for step in range(NH):
-            extent = (heads, heads * NH)
             pick = iota(extent, 1) == iota(extent, 0) * NH + step
-            pieces.append(dot_nt(pick.astype(BF16), betas[...]))
-        same = iota((heads, heads), 0) == iota((heads, heads), 1)
-        pieces.append(dot_nt(same.astype(BF16), log_gates[...]))
+            pieces.append(dot_nt(pick.astype(BF16), scalars[...]))
+        pick = iota(extent, 1) == iota(extent, 0) + heads * NH
+        pieces.append(dot_nt(pick.astype(BF16), scalars[...]))
         pieces.append(jnp.broadcast_to(starts[...].astype(F32), (heads, TOK)))
         scales = jnp.concatenate(pieces, 1).astype(BF16)
         for ahead, out in enumerate(outs):
@@ -265,7 +266,7 @@
             out[2 * rows :, :] = dot(pick.astype(BF16), scales).astype(BF16)
 
     outs = [shape(2 * rows + SCALE_ROWS, DK)] * sizes.groups
-    return call(kernel, outs, keys, betas, log_gates, starts, name="pack_keys")
+    return call(kernel, outs, keys, scalars, starts, name="pack_keys")
 
 
 def swap_keys(sizes, arrived):
@@ -592,6 +593,9 @@
             groups:
         ]
         gather(sizes, pieces, blocks)
+        extent = (CHUNK, REFL)
+        block, step, token, _ = place(iota(extent, 1))
+        read_places = (step == NH - 1) & (block * TOK + token == iota(extent, 0))
         for base in range(0, sizes.units, GROUP):
             members = range(base, min(base + GROUP, sizes.units))
             queries = [unit_rows(blocks, *sizes.unit(unit), TOK) for unit in members]
@@ -603,9 +607,14 @@
             for number, unit in enumerate(members):
                 one = slice(unit, unit + 1)
                 inner = dot(beside(scores[number] * rows[0, one, :]), twice(values[unit]))
-                carried = read_rows(jnp.broadcast_to(rows[2, one, :], (DK, REFL)).T)
-                reader = carried * queries[number].astype(F32) - dot(
-                    beside(scores[number] * rows[1, one, :]), twice(keys[unit])
+                query = queries[number]
+                halves = [query[:TOK]] * NH + [query[TOK:]] * NH
+                carried = jnp.where(read_places, rows[2, one, :], 0.0)
+                reader = dot(
+                    jnp.concatenate(
+                        [beside(carried), beside(scores[number] * -rows[1, one, :])], 1
+                    ),
+                    jnp.concatenate([twice(jnp.concatenate(halves, 0)), twice(keys[unit])], 0),
                 )
                 high, low = split(jnp.concatenate([prefix[unit], before[unit]], 0))
                 pair = beside(reader)
@@ -695,7 +704,7 @@
     def swapped(part):
         return lax.ppermute(part, "core", [(0, 1), (1, 0)])
 
-    arrived = spread(pack_keys(sizes, keys, betas, log_gates, own_starts))
+    arrived = spread(pack_keys(sizes, keys, jnp.concatenate([betas, log_gates], 1), own_starts))
     kept, sent = pack_reads(sizes, values, queries)
     value_parts, query_parts = merge_reads(sizes, kept, swapped(sent))
     value_parts = spread(value_parts)

time: 54.1 us -> 54.2 us (level)
  other arithmetic: 0 us -> 0.77 us
  local copies, waits for them, and re-layouts: 3.42 us -> 2.69 us
    concatenate x0 -> x1, other arithmetic: none -> 0.77 us  [local(): jnp.concatenate([betas, log_gates], 1)]
    unnamed x12 -> x10, local copies, waits for them, and re-layouts: 3.35 us -> 2.62 us
where the time goes in v5:
time: 54.2 us; the launch traced here: 53.9 us
  starting transfers between devices  28.1 us (52%)
  Pallas kernels  13 us (24%)
  waiting for transfers between devices  9.31 us (17%)
  local copies, waits for them, and re-layouts  2.69 us (5%)
  other arithmetic  0.77 us (1%)
    ppermute x9, starting transfers between devices, spread(): lax.ppermute(part, 'head', [(z, (z + ahead) % groups) for z in range(grou...  17.2 us
    pallas_call x10, Pallas kernels, call(): pl.pallas_call(kernel, out_shape=outs, scratch_shapes=scratch, compiler_p...  13 us
    ppermute x9, starting transfers between devices, exchanged(): lax.ppermute(part, 'chip', [(chip, chip ^ number) for chip in range(sizes...  10.7 us
    ppermute x9, waiting for transfers between devices, spread(): lax.ppermute(part, 'head', [(z, (z + ahead) % groups) for z in range(grou...  6.33 us
    unnamed x10, local copies, waits for them, and re-layouts  2.62 us
    ppermute x9, waiting for transfers between devices, exchanged(): lax.ppermute(part, 'chip', [(chip, chip ^ number) for chip in range(sizes...  1.64 us
    ppermute x3, waiting for transfers between devices, swapped(): return lax.ppermute(part, 'core', [(0, 1), (1, 0)])  1.34 us
  transfers between devices with their start and end apart: 21, of which 5 were waited for; matrix products, arithmetic and copies ran while one was open for 0% of the time, Pallas kernels for 21%

profile of v5, /device:TPU:0, one launch (start us, length us, event | category | flops | bytes accessed | tf_op | source)
XLA Modules:
  0.0 53.9 jit_solution(11129290192349930)
XLA Ops:
  0.1 0.6 %copy-done.4 = bf16[32,32]{1,0:T(8,128)(2,1)S(1)} copy-done((bf16[32,32]{1,0:T(8,128)(2,1)S(1)}, bf16[32,32]{1,0:T(8,128)(2,1)}, u32[]{:S(2)}) %copy-start.4) | copy-done | bytes 2072
  0.7 0.8 %pad_maximum_fusion.scalars = bf16[32,96]{1,0:T(8,128)(2,1)S(1)} fusion(bf16[32,32]{1,0:T(8,128)(2,1)S(1)} %copy-done.4, bf16[32,64]{1,0:T(8,128)(2,1)} %param.9), kind=kLoop, calls=%fused_computation | loop fusion | flops 12288 | bytes 12288 | tf_op jit(solution)/shard_map/concatenate | solution.py:707
  1.5 1.0 %copy-done.1 = bf16[32,8192]{1,0:T(8,128)(2,1)S(1)} copy-done((bf16[32,8192]{1,0:T(8,128)(2,1)S(1)}, bf16[32,8192]{1,0:T(8,128)(2,1)}, u32[]{:S(2)}) %copy-start.1) | copy-done | bytes 524312
  2.9 3.1 %collective-permute-start = (bf16[528,128]{1,0:T(8,128)(2,1)S(1)}, bf16[528,128]{1,0:T(8,128)(2,1)S(1)}, u32[]{:S(2)}, u32[]{:S(2)}) collective-permute-start(bf16[528,128]{1,0:T(8,128)(2,1)S(1)} %get-tuple-element.45), channel_id=1, source_target_pairs={{0,1},{1,2},{2,3},{3,0},{4,5},{5,6},{6,7},{7,4},{8,9},{9,10},{10,1... | collective-permute-start | bytes 405512 | tf_op jit(solution)/shard_map/ppermute | solution.py:699
  5.9 2.6 %collective-permute-start.1 = (bf16[528,128]{1,0:T(8,128)(2,1)S(1)}, bf16[528,128]{1,0:T(8,128)(2,1)S(1)}, u32[]{:S(2)}, u32[]{:S(2)}) collective-permute-start(bf16[528,128]{1,0:T(8,128)(2,1)S(1)} %get-tuple-element.46), channel_id=1, source_target_pairs={{0,2},{1,3},{2,0},{3,1},{4,6},{5,7},{6,4},{7,5},{8,10},{9,11},{10,... | collective-permute-start | bytes 405512 | tf_op jit(solution)/shard_map/ppermute | solution.py:699
  8.5 1.3 %collective-permute-start.2 = (bf16[528,128]{1,0:T(8,128)(2,1)S(1)}, bf16[528,128]{1,0:T(8,128)(2,1)S(1)}, u32[]{:S(2)}, u32[]{:S(2)}) collective-permute-start(bf16[528,128]{1,0:T(8,128)(2,1)S(1)} %get-tuple-element.47), channel_id=1, source_target_pairs={{0,3},{1,0},{2,1},{3,2},{4,7},{5,4},{6,5},{7,6},{8,11},{9,8},{10,9... | collective-permute-start | bytes 405512 | tf_op jit(solution)/shard_map/ppermute | solution.py:699
  9.9 0.9 %copy-done.3 = bf16[32,4096]{1,0:T(8,128)(2,1)S(1)} copy-done((bf16[32,4096]{1,0:T(8,128)(2,1)S(1)}, bf16[32,4096]{1,0:T(8,128)(2,1)}, u32[]{:S(2)}) %copy-start.3) | copy-done | bytes 262168
  11.1 1.4 %collective-permute-done.refs_1_ = bf16[528,128]{1,0:T(8,128)(2,1)S(1)} collective-permute-done((bf16[528,128]{1,0:T(8,128)(2,1)S(1)}, bf16[528,128]{1,0:T(8,128)(2,1)S(1)}, u32[]{:S(2)}, u32[]{:S(2)}) %collective-permute-start) | collective-permute-done | bytes 135200 | tf_op jit(solution)/shard_map/ppermute | solution.py:699
  12.5 5.0 %collective-permute-done.1.refs_2_ = bf16[528,128]{1,0:T(8,128)(2,1)S(1)} collective-permute-done((bf16[528,128]{1,0:T(8,128)(2,1)S(1)}, bf16[528,128]{1,0:T(8,128)(2,1)S(1)}, u32[]{:S(2)}, u32[]{:S(2)}) %collective-permute-start.1) | collective-permute-done | bytes 135200 | tf_op jit(solution)/shard_map/ppermute | solution.py:699
  17.6 3.4 %collective-permute-start.8 = (bf16[2,256,128]{2,1,0:T(8,128)(2,1)S(1)}, bf16[2,256,128]{2,1,0:T(8,128)(2,1)S(1)}, u32[]{:S(2)}, u32[]{:S(2)}) collective-permute-start(bf16[2,256,128]{2,1,0:T(8,128)(2,1)S(1)} %get-tuple-element.55), channel_id=1, source_target_pairs={{0,1},{1,2},{2,3},{3,0},{4,5},{5,6},{6,7},{7,4},{8,9},{9,10},{10,1... | collective-permute-start | bytes 393224 | tf_op jit(solution)/shard_map/ppermute | solution.py:699
  21.0 1.6 %collective-permute-start.9 = (bf16[2,256,128]{2,1,0:T(8,128)(2,1)S(1)}, bf16[2,256,128]{2,1,0:T(8,128)(2,1)S(1)}, u32[]{:S(2)}, u32[]{:S(2)}) collective-permute-start(bf16[2,256,128]{2,1,0:T(8,128)(2,1)S(1)} %get-tuple-element.56), channel_id=1, source_target_pairs={{0,2},{1,3},{2,0},{3,1},{4,6},{5,7},{6,4},{7,5},{8,10},{9,11},{10,... | collective-permute-start | bytes 393224 | tf_op jit(solution)/shard_map/ppermute | solution.py:699
  22.7 0.8 %collective-permute-start.10 = (bf16[2,256,128]{2,1,0:T(8,128)(2,1)S(1)}, bf16[2,256,128]{2,1,0:T(8,128)(2,1)S(1)}, u32[]{:S(2)}, u32[]{:S(2)}) collective-permute-start(bf16[2,256,128]{2,1,0:T(8,128)(2,1)S(1)} %get-tuple-element.57), channel_id=1, source_target_pairs={{0,3},{1,0},{2,1},{3,2},{4,7},{5,4},{6,5},{7,6},{8,11},{9,8},{10,9... | collective-permute-start | bytes 393224 | tf_op jit(solution)/shard_map/ppermute | solution.py:699
  23.5 7.1 %key_stage.1 = (bf16[16,128,128]{2,1,0:T(8,128)(2,1)S(1)}, bf16[16,128,256]{2,1,0:T(8,128)(2,1)S(1)}, bf16[16,128,256]{2,1,0:T(8,128)(2,1)S(1)}, f32[16,64,128]{...) custom-call(bf16[528,128]{1,0:T(8,128)(2,1)S(1)} %get-tuple-element., ...), custom_call_target="tpu_custom_call" | custom-call | flops 6000000000 | tf_op jit(solution)/shard_map/key_stage/pallas_call | solution.py:194
  30.6 1.6 %collective-permute-start.4 = (f32[128,128]{1,0:T(8,128)S(1)}, f32[128,128]{1,0:T(8,128)S(1)}, u32[]{:S(2)}, u32[]{:S(2)}) collective-permute-start(f32[128,128]{1,0:T(8,128)S(1)} %get-tuple-element.49), channel_id=1, source_target_pairs={{0,8},{8,0},{16,24},{24,16},{1,9},{9,1},{17,25},{25,17},{2,10},{10... | collective-permute-start | bytes 196616 | tf_op jit(solution)/shard_map/ppermute | solution.py:565
  32.2 1.5 %collective-permute-start.5 = (f32[128,128]{1,0:T(8,128)S(1)}, f32[128,128]{1,0:T(8,128)S(1)}, u32[]{:S(2)}, u32[]{:S(2)}) collective-permute-start(f32[128,128]{1,0:T(8,128)S(1)} %get-tuple-element.50), channel_id=1, source_target_pairs={{0,16},{8,24},{16,0},{24,8},{1,17},{9,25},{17,1},{25,9},{2,18},{10... | collective-permute-start | bytes 196616 | tf_op jit(solution)/shard_map/ppermute | solution.py:565
  33.7 0.5 collective-permute-start.6
  34.2 0.8 %value_stage.1 = (bf16[16,128,128]{2,1,0:T(8,128)(2,1)S(1)}, f32[16,128,128]{2,1,0:T(8,128)S(1)}, f32[128,128]{1,0:T(8,128)S(1)}, f32[128,128]{1,0:T(8,128)S(1)}...) custom-call(bf16[2,256,128]{2,1,0:T(8,128)(2,1)S(1)} %get-tuple-element.54.refs_0_, ...), custom_call_target="tpu_custom_call" | custom-call | flops 2000000000 | tf_op jit(solution)/shard_map/value_stage/pallas_call | solution.py:194
  35.0 1.6 %collective-permute-start.11 = (f32[128,128]{1,0:T(8,128)S(1)}, f32[128,128]{1,0:T(8,128)S(1)}, u32[]{:S(2)}, u32[]{:S(2)}) collective-permute-start(f32[128,128]{1,0:T(8,128)S(1)} %get-tuple-element.61), channel_id=1, source_target_pairs={{0,8},{8,0},{16,24},{24,16},{1,9},{9,1},{17,25},{25,17},{2,10},{10... | collective-permute-start | bytes 196616 | tf_op jit(solution)/shard_map/ppermute | solution.py:565
  36.6 1.5 %collective-permute-start.12 = (f32[128,128]{1,0:T(8,128)S(1)}, f32[128,128]{1,0:T(8,128)S(1)}, u32[]{:S(2)}, u32[]{:S(2)}) collective-permute-start(f32[128,128]{1,0:T(8,128)S(1)} %get-tuple-element.62), channel_id=1, source_target_pairs={{0,16},{8,24},{16,0},{24,8},{1,17},{9,25},{17,1},{25,9},{2,18},{10... | collective-permute-start | bytes 196616 | tf_op jit(solution)/shard_map/ppermute | solution.py:565
  38.1 0.4 collective-permute-start.13
  38.5 1.2 %collective-permute-start.17 = (bf16[2,128,128]{2,1,0:T(8,128)(2,1)S(1)}, bf16[2,128,128]{2,1,0:T(8,128)(2,1)S(1)}, u32[]{:S(2)}, u32[]{:S(2)}) collective-permute-start(bf16[2,128,128]{2,1,0:T(8,128)(2,1)S(1)} %get-tuple-element.69), channel_id=1, source_target_pairs={{0,1},{1,2},{2,3},{3,0},{4,5},{5,6},{6,7},{7,4},{8,9},{9,10},{10,1... | collective-permute-start | bytes 196616 | tf_op jit(solution)/shard_map/ppermute | solution.py:699
  39.8 1.3 %collective-permute-start.18 = (bf16[2,128,128]{2,1,0:T(8,128)(2,1)S(1)}, bf16[2,128,128]{2,1,0:T(8,128)(2,1)S(1)}, u32[]{:S(2)}, u32[]{:S(2)}) collective-permute-start(bf16[2,128,128]{2,1,0:T(8,128)(2,1)S(1)} %get-tuple-element.70), channel_id=1, source_target_pairs={{0,2},{1,3},{2,0},{3,1},{4,6},{5,7},{6,4},{7,5},{8,10},{9,11},{10,... | collective-permute-start | bytes 196616 | tf_op jit(solution)/shard_map/ppermute | solution.py:699
  41.1 1.8 %collective-permute-start.19 = (bf16[2,128,128]{2,1,0:T(8,128)(2,1)S(1)}, bf16[2,128,128]{2,1,0:T(8,128)(2,1)S(1)}, u32[]{:S(2)}, u32[]{:S(2)}) collective-permute-start(bf16[2,128,128]{2,1,0:T(8,128)(2,1)S(1)} %get-tuple-element.71), channel_id=1, source_target_pairs={{0,3},{1,0},{2,1},{3,2},{4,7},{5,4},{6,5},{7,6},{8,11},{9,8},{10,9... | collective-permute-start | bytes 196616 | tf_op jit(solution)/shard_map/ppermute | solution.py:699
  42.9 0.4 collective-permute-done.13.refs_7_
  43.6 1.0 %collective-permute-start.14 = (f32[128,128]{1,0:T(8,128)S(1)}, f32[128,128]{1,0:T(8,128)S(1)}, u32[]{:S(2)}, u32[]{:S(2)}) collective-permute-start(f32[128,128]{1,0:T(8,128)S(1)} %get-tuple-element.65), channel_id=1, source_target_pairs={{0,8},{8,0},{16,24},{24,16},{1,9},{9,1},{17,25},{25,17},{2,10},{10... | collective-permute-start | bytes 196616 | tf_op jit(solution)/shard_map/ppermute | solution.py:565
  44.6 1.5 %collective-permute-start.15 = (f32[128,128]{1,0:T(8,128)S(1)}, f32[128,128]{1,0:T(8,128)S(1)}, u32[]{:S(2)}, u32[]{:S(2)}) collective-permute-start(f32[128,128]{1,0:T(8,128)S(1)} %get-tuple-element.66), channel_id=1, source_target_pairs={{0,16},{8,24},{16,0},{24,8},{1,17},{9,25},{17,1},{25,9},{2,18},{10... | collective-permute-start | bytes 196616 | tf_op jit(solution)/shard_map/ppermute | solution.py:565
  46.1 1.1 %collective-permute-start.16 = (f32[128,128]{1,0:T(8,128)S(1)}, f32[128,128]{1,0:T(8,128)S(1)}, u32[]{:S(2)}, u32[]{:S(2)}) collective-permute-start(f32[128,128]{1,0:T(8,128)S(1)} %get-tuple-element.67), channel_id=1, source_target_pairs={{0,24},{8,16},{16,8},{24,0},{1,25},{9,17},{17,9},{25,1},{2,26},{10... | collective-permute-start | bytes 196616 | tf_op jit(solution)/shard_map/ppermute | solution.py:565
  47.2 2.8 %query_stage.1 = (bf16[16,64,256]{2,1,0:T(8,128)(2,1)S(1)}, f32[16,64,128]{2,1,0:T(8,128)S(1)}) custom-call(bf16[2,128,128]{2,1,0:T(8,128)(2,1)S(1)} %get-tuple-element.68.refs_0_, bf16[2,128,128]{2,1,0:T(8,128)(2,1)S(1)} %collective-permute-done.17.refs_1_, bf16[2,128,128]{2,1,0:T(8,128)(2,1)S(1)} %collective-permute-done.18.refs_2_, ...), custom_call_target="tpu_custom_call" | custom-call | flops 3000000000 | tf_op jit(solution)/shard_map/query_stage/pallas_call | solution.py:194
  50.1 1.2 %collective-permute-done.16.refs_3_ = f32[128,128]{1,0:T(8,128)S(1)} collective-permute-done((f32[128,128]{1,0:T(8,128)S(1)}, f32[128,128]{1,0:T(8,128)S(1)}, u32[]{:S(2)}, u32[]{:S(2)}) %collective-permute-start.16) | collective-permute-done | bytes 65568 | tf_op jit(solution)/shard_map/ppermute | solution.py:565
  51.3 0.5 read_states.1
  51.9 1.3 %collective-permute-done.20.other = bf16[128,512]{1,0:T(8,128)(2,1)S(1)} collective-permute-done((bf16[128,512]{1,0:T(8,128)(2,1)S(1)}, bf16[128,512]{1,0:T(8,128)(2,1)S(1)}, u32[]{:S(2)}, u32[]{:S(2)}) %collective-permute-start.20) | collective-permute-done | bytes 131104 | tf_op jit(solution)/shard_map/ppermute | solution.py:705
  53.2 0.7 %join.1 = bf16[128,1024]{1,0:T(8,128)(2,1)} custom-call(bf16[128,512]{1,0:T(8,128)(2,1)S(1)} %get-tuple-element.81.own, bf16[128,512]{1,0:T(8,128)(2,1)S(1)} %collective-permute-done.20.other), custom_call_target="tpu_custom_call" | custom-call | tf_op jit(solution)/shard_map/join/pallas_call | solution.py:194
  (32 shorter events, 1.3 us)
Async XLA Ops:
  0.0 0.7 %copy-start.4 = (bf16[32,32]{1,0:T(8,128)(2,1)S(1)}, bf16[32,32]{1,0:T(8,128)(2,1)}, u32[]{:S(2)}) copy-start(bf16[32,32]{1,0:T(8,128)(2,1)} %param.10) | copy-start | bytes 6148
  1.5 1.0 %copy-start.1 = (bf16[32,8192]{1,0:T(8,128)(2,1)S(1)}, bf16[32,8192]{1,0:T(8,128)(2,1)}, u32[]{:S(2)}) copy-start(bf16[32,8192]{1,0:T(8,128)(2,1)} %keys.1) | copy-start | bytes 1572868
  2.5 7.4 %copy-start.2 = (bf16[32,8192]{1,0:T(8,128)(2,1)S(1)}, bf16[32,8192]{1,0:T(8,128)(2,1)}, u32[]{:S(2)}) copy-start(bf16[32,8192]{1,0:T(8,128)(2,1)} %values.1) | copy-start | bytes 1572868
  2.9 9.6 %collective-permute-start = (bf16[528,128]{1,0:T(8,128)(2,1)S(1)}, bf16[528,128]{1,0:T(8,128)(2,1)S(1)}, u32[]{:S(2)}, u32[]{:S(2)}) collective-permute-start(bf16[528,128]{1,0:T(8,128)(2,1)S(1)} %get-tuple-element.45), channel_id=1, source_target_pairs={{0,1},{1,2},{2,3},{3,0},{4,5},{5,6},{6,7},{7,4},{8,9},{9,10},{10,1... | collective-permute-start | bytes 405512 | tf_op jit(solution)/shard_map/ppermute | solution.py:699
  5.9 11.5 %collective-permute-start.1 = (bf16[528,128]{1,0:T(8,128)(2,1)S(1)}, bf16[528,128]{1,0:T(8,128)(2,1)S(1)}, u32[]{:S(2)}, u32[]{:S(2)}) collective-permute-start(bf16[528,128]{1,0:T(8,128)(2,1)S(1)} %get-tuple-element.46), channel_id=1, source_target_pairs={{0,2},{1,3},{2,0},{3,1},{4,6},{5,7},{6,4},{7,5},{8,10},{9,11},{10,... | collective-permute-start | bytes 405512 | tf_op jit(solution)/shard_map/ppermute | solution.py:699
  8.5 8.9 %collective-permute-start.2 = (bf16[528,128]{1,0:T(8,128)(2,1)S(1)}, bf16[528,128]{1,0:T(8,128)(2,1)S(1)}, u32[]{:S(2)}, u32[]{:S(2)}) collective-permute-start(bf16[528,128]{1,0:T(8,128)(2,1)S(1)} %get-tuple-element.47), channel_id=1, source_target_pairs={{0,3},{1,0},{2,1},{3,2},{4,7},{5,4},{6,5},{7,6},{8,11},{9,8},{10,9... | collective-permute-start | bytes 405512 | tf_op jit(solution)/shard_map/ppermute | solution.py:699
  9.9 1.0 %copy-start.3 = (bf16[32,4096]{1,0:T(8,128)(2,1)S(1)}, bf16[32,4096]{1,0:T(8,128)(2,1)}, u32[]{:S(2)}) copy-start(bf16[32,4096]{1,0:T(8,128)(2,1)} %queries.1) | copy-start | bytes 786436
  11.0 6.5 %collective-permute-start.7 = (bf16[4,384,128]{2,1,0:T(8,128)(2,1)S(1)}, bf16[4,384,128]{2,1,0:T(8,128)(2,1)S(1)}, u32[]{:S(2)}, u32[]{:S(2)}) collective-permute-start(bf16[4,384,128]{2,1,0:T(8,128)(2,1)S(1)} %get-tuple-element.53), channel_id=1, source_target_pairs={{0,4},{4,0},{1,5},{5,1},{2,6},{6,2},{3,7},{7,3},{8,12},{12,8},{9,1... | collective-permute-start | bytes 1179656 | tf_op jit(solution)/shard_map/ppermute | solution.py:705
  17.5 6.0 %collective-permute-start.3 = (bf16[4,272,128]{2,1,0:T(8,128)(2,1)S(1)}, bf16[4,272,128]{2,1,0:T(8,128)(2,1)S(1)}, u32[]{:S(2)}, u32[]{:S(2)}) collective-permute-start(bf16[4,272,128]{2,1,0:T(8,128)(2,1)S(1)} %swap_keys.1), channel_id=1, source_target_pairs={{0,4},{4,0},{1,5},{5,1},{2,6},{6,2},{3,7},{7,3},{8,12},{12,8},{9,1... | collective-permute-start | bytes 835592 | tf_op jit(solution)/shard_map/ppermute | solution.py:705
  17.6 16.1 %collective-permute-start.8 = (bf16[2,256,128]{2,1,0:T(8,128)(2,1)S(1)}, bf16[2,256,128]{2,1,0:T(8,128)(2,1)S(1)}, u32[]{:S(2)}, u32[]{:S(2)}) collective-permute-start(bf16[2,256,128]{2,1,0:T(8,128)(2,1)S(1)} %get-tuple-element.55), channel_id=1, source_target_pairs={{0,1},{1,2},{2,3},{3,0},{4,5},{5,6},{6,7},{7,4},{8,9},{9,10},{10,1... | collective-permute-start | bytes 393224 | tf_op jit(solution)/shard_map/ppermute | solution.py:699
  21.0 13.2 %collective-permute-start.9 = (bf16[2,256,128]{2,1,0:T(8,128)(2,1)S(1)}, bf16[2,256,128]{2,1,0:T(8,128)(2,1)S(1)}, u32[]{:S(2)}, u32[]{:S(2)}) collective-permute-start(bf16[2,256,128]{2,1,0:T(8,128)(2,1)S(1)} %get-tuple-element.56), channel_id=1, source_target_pairs={{0,2},{1,3},{2,0},{3,1},{4,6},{5,7},{6,4},{7,5},{8,10},{9,11},{10,... | collective-permute-start | bytes 393224 | tf_op jit(solution)/shard_map/ppermute | solution.py:699
  22.7 11.5 %collective-permute-start.10 = (bf16[2,256,128]{2,1,0:T(8,128)(2,1)S(1)}, bf16[2,256,128]{2,1,0:T(8,128)(2,1)S(1)}, u32[]{:S(2)}, u32[]{:S(2)}) collective-permute-start(bf16[2,256,128]{2,1,0:T(8,128)(2,1)S(1)} %get-tuple-element.57), channel_id=1, source_target_pairs={{0,3},{1,0},{2,1},{3,2},{4,7},{5,4},{6,5},{7,6},{8,11},{9,8},{10,9... | collective-permute-start | bytes 393224 | tf_op jit(solution)/shard_map/ppermute | solution.py:699
  30.6 7.5 %collective-permute-start.4 = (f32[128,128]{1,0:T(8,128)S(1)}, f32[128,128]{1,0:T(8,128)S(1)}, u32[]{:S(2)}, u32[]{:S(2)}) collective-permute-start(f32[128,128]{1,0:T(8,128)S(1)} %get-tuple-element.49), channel_id=1, source_target_pairs={{0,8},{8,0},{16,24},{24,16},{1,9},{9,1},{17,25},{25,17},{2,10},{10... | collective-permute-start | bytes 196616 | tf_op jit(solution)/shard_map/ppermute | solution.py:565
  32.2 6.3 %collective-permute-start.5 = (f32[128,128]{1,0:T(8,128)S(1)}, f32[128,128]{1,0:T(8,128)S(1)}, u32[]{:S(2)}, u32[]{:S(2)}) collective-permute-start(f32[128,128]{1,0:T(8,128)S(1)} %get-tuple-element.50), channel_id=1, source_target_pairs={{0,16},{8,24},{16,0},{24,8},{1,17},{9,25},{17,1},{25,9},{2,18},{10... | collective-permute-start | bytes 196616 | tf_op jit(solution)/shard_map/ppermute | solution.py:565
  33.7 6.0 %collective-permute-start.6 = (f32[128,128]{1,0:T(8,128)S(1)}, f32[128,128]{1,0:T(8,128)S(1)}, u32[]{:S(2)}, u32[]{:S(2)}) collective-permute-start(f32[128,128]{1,0:T(8,128)S(1)} %get-tuple-element.51), channel_id=1, source_target_pairs={{0,24},{8,16},{16,8},{24,0},{1,25},{9,17},{17,9},{25,1},{2,26},{10... | collective-permute-start | bytes 196616 | tf_op jit(solution)/shard_map/ppermute | solution.py:565
  35.0 6.1 %collective-permute-start.11 = (f32[128,128]{1,0:T(8,128)S(1)}, f32[128,128]{1,0:T(8,128)S(1)}, u32[]{:S(2)}, u32[]{:S(2)}) collective-permute-start(f32[128,128]{1,0:T(8,128)S(1)} %get-tuple-element.61), channel_id=1, source_target_pairs={{0,8},{8,0},{16,24},{24,16},{1,9},{9,1},{17,25},{25,17},{2,10},{10... | collective-permute-start | bytes 196616 | tf_op jit(solution)/shard_map/ppermute | solution.py:565
  36.6 6.3 %collective-permute-start.12 = (f32[128,128]{1,0:T(8,128)S(1)}, f32[128,128]{1,0:T(8,128)S(1)}, u32[]{:S(2)}, u32[]{:S(2)}) collective-permute-start(f32[128,128]{1,0:T(8,128)S(1)} %get-tuple-element.62), channel_id=1, source_target_pairs={{0,16},{8,24},{16,0},{24,8},{1,17},{9,25},{17,1},{25,9},{2,18},{10... | collective-permute-start | bytes 196616 | tf_op jit(solution)/shard_map/ppermute | solution.py:565
  38.1 5.2 %collective-permute-start.13 = (f32[128,128]{1,0:T(8,128)S(1)}, f32[128,128]{1,0:T(8,128)S(1)}, u32[]{:S(2)}, u32[]{:S(2)}) collective-permute-start(f32[128,128]{1,0:T(8,128)S(1)} %get-tuple-element.63), channel_id=1, source_target_pairs={{0,24},{8,16},{16,8},{24,0},{1,25},{9,17},{17,9},{25,1},{2,26},{10... | collective-permute-start | bytes 196616 | tf_op jit(solution)/shard_map/ppermute | solution.py:565
  38.5 7.6 %collective-permute-start.17 = (bf16[2,128,128]{2,1,0:T(8,128)(2,1)S(1)}, bf16[2,128,128]{2,1,0:T(8,128)(2,1)S(1)}, u32[]{:S(2)}, u32[]{:S(2)}) collective-permute-start(bf16[2,128,128]{2,1,0:T(8,128)(2,1)S(1)} %get-tuple-element.69), channel_id=1, source_target_pairs={{0,1},{1,2},{2,3},{3,0},{4,5},{5,6},{6,7},{7,4},{8,9},{9,10},{10,1... | collective-permute-start | bytes 196616 | tf_op jit(solution)/shard_map/ppermute | solution.py:699
  39.8 7.4 %collective-permute-start.18 = (bf16[2,128,128]{2,1,0:T(8,128)(2,1)S(1)}, bf16[2,128,128]{2,1,0:T(8,128)(2,1)S(1)}, u32[]{:S(2)}, u32[]{:S(2)}) collective-permute-start(bf16[2,128,128]{2,1,0:T(8,128)(2,1)S(1)} %get-tuple-element.70), channel_id=1, source_target_pairs={{0,2},{1,3},{2,0},{3,1},{4,6},{5,7},{6,4},{7,5},{8,10},{9,11},{10,... | collective-permute-start | bytes 196616 | tf_op jit(solution)/shard_map/ppermute | solution.py:699
  41.1 6.1 %collective-permute-start.19 = (bf16[2,128,128]{2,1,0:T(8,128)(2,1)S(1)}, bf16[2,128,128]{2,1,0:T(8,128)(2,1)S(1)}, u32[]{:S(2)}, u32[]{:S(2)}) collective-permute-start(bf16[2,128,128]{2,1,0:T(8,128)(2,1)S(1)} %get-tuple-element.71), channel_id=1, source_target_pairs={{0,3},{1,0},{2,1},{3,2},{4,7},{5,4},{6,5},{7,6},{8,11},{9,8},{10,9... | collective-permute-start | bytes 196616 | tf_op jit(solution)/shard_map/ppermute | solution.py:699
  43.6 6.4 %collective-permute-start.14 = (f32[128,128]{1,0:T(8,128)S(1)}, f32[128,128]{1,0:T(8,128)S(1)}, u32[]{:S(2)}, u32[]{:S(2)}) collective-permute-start(f32[128,128]{1,0:T(8,128)S(1)} %get-tuple-element.65), channel_id=1, source_target_pairs={{0,8},{8,0},{16,24},{24,16},{1,9},{9,1},{17,25},{25,17},{2,10},{10... | collective-permute-start | bytes 196616 | tf_op jit(solution)/shard_map/ppermute | solution.py:565
  44.6 5.5 %collective-permute-start.15 = (f32[128,128]{1,0:T(8,128)S(1)}, f32[128,128]{1,0:T(8,128)S(1)}, u32[]{:S(2)}, u32[]{:S(2)}) collective-permute-start(f32[128,128]{1,0:T(8,128)S(1)} %get-tuple-element.66), channel_id=1, source_target_pairs={{0,16},{8,24},{16,0},{24,8},{1,17},{9,25},{17,1},{25,9},{2,18},{10... | collective-permute-start | bytes 196616 | tf_op jit(solution)/shard_map/ppermute | solution.py:565
  46.1 5.2 %collective-permute-start.16 = (f32[128,128]{1,0:T(8,128)S(1)}, f32[128,128]{1,0:T(8,128)S(1)}, u32[]{:S(2)}, u32[]{:S(2)}) collective-permute-start(f32[128,128]{1,0:T(8,128)S(1)} %get-tuple-element.67), channel_id=1, source_target_pairs={{0,24},{8,16},{16,8},{24,0},{1,25},{9,17},{17,9},{25,1},{2,26},{10... | collective-permute-start | bytes 196616 | tf_op jit(solution)/shard_map/ppermute | solution.py:565
  51.8 1.4 %collective-permute-start.20 = (bf16[128,512]{1,0:T(8,128)(2,1)S(1)}, bf16[128,512]{1,0:T(8,128)(2,1)S(1)}, u32[]{:S(2)}, u32[]{:S(2)}) collective-permute-start(bf16[128,512]{1,0:T(8,128)(2,1)S(1)} %get-tuple-element.82), channel_id=1, source_target_pairs={{0,4},{4,0},{1,5},{5,1},{2,6},{6,2},{3,7},{7,3},{8,12},{12,8},{9,1... | collective-permute-start | bytes 393224 | tf_op jit(solution)/shard_map/ppermute | solution.py:705
  (1 other events, 0.0 us)

commit v6 on v5

--- a/solution.py
+++ b/solution.py
@@ -216,7 +216,7 @@
         self.heads = group_heads // 2
         self.chips = chips
         self.units = self.heads * groups
-        self.swapped = chips == self.heads and chips & (chips - 1) == 0
+        self.paired = chips == 4
 
     def unit(self, number):
         return number // self.groups, number % self.groups
@@ -349,8 +349,7 @@
         keys_out, inverse_out, end_out, ratio_out, row_out, step_out, prefix_out = refs[
             groups + 1 : groups + 8
         ]
-        totals = refs[groups + 8 : groups + 8 + sizes.heads]
-        blocks, scales, every = refs[groups + 8 + sizes.heads :]
+        total_out, blocks, scales, every = refs[groups + 8 :]
         z = axis_index("head")
         core = axis_index("core")
         for behind, piece in enumerate(pieces):
@@ -447,15 +446,8 @@
                     prefixes[head] = step
                 else:
                     prefixes[head] = product(beside(prefixes[head]), factor_of(high, low))
-        if sizes.swapped:
-            for head in range(sizes.heads):
-                every[head] = prefixes[head]
-            chip = axis_index("chip")
-            for number in range(sizes.heads):
-                totals[number][...] = every[jnp.bitwise_xor(chip, number)]
-        else:
-            for head in range(sizes.heads):
-                totals[head][...] = prefixes[head]
+        for head in range(sizes.heads):
+            total_out[head] = prefixes[head]
 
     outs = [
         shape(units, REFL, DK),
@@ -465,7 +457,8 @@
         shape(3, units, REFL, dtype=F32),
         shape(units, DK, 2 * DK),
         shape(units, DK, DK, dtype=F32),
-    ] + [shape(DK, DK, dtype=F32)] * sizes.heads
+        shape(sizes.heads, DK, DK, dtype=F32),
+    ]
     scratch = [
         pltpu.VMEM((2 * groups, rows, DK), BF16),
         pltpu.VMEM((2 * groups, SCALE_ROWS, DK), BF16),
@@ -474,7 +467,7 @@
     results = call(
         kernel, outs, *arrived, swapped, scratch=scratch, flops=6_000_000_000, name="key_stage"
     )
-    return results[:7], results[7:]
+    return results[:7], results[7]
 
 
 def value_stage(sizes, pieces, ends, steps):
@@ -482,9 +475,7 @@
 
     def kernel(*refs):
         pieces = refs[:groups]
-        ends, steps, values_out, before_out = refs[groups : groups + 4]
-        totals = refs[groups + 4 : groups + 4 + sizes.heads]
-        blocks, every = refs[groups + 4 + sizes.heads :]
+        ends, steps, values_out, before_out, total_out, blocks = refs[groups:]
         gather(sizes, pieces, blocks)
         injects = []
         for unit in range(sizes.units):
@@ -504,84 +495,48 @@
                     sums[head] = injects[unit] + product(
                         beside(sums[head]), factor_of(step[:, :DK], step[:, DK:])
                     )
-        if sizes.swapped:
-            for head in range(sizes.heads):
-                every[head] = sums[head]
-            chip = axis_index("chip")
-            for number in range(sizes.heads):
-                totals[number][...] = every[jnp.bitwise_xor(chip, number)]
-        else:
-            for head in range(sizes.heads):
-                totals[head][...] = sums[head]
+        for head in range(sizes.heads):
+            total_out[head] = sums[head]
 
     outs = [shape(sizes.units, REFL, DV), shape(sizes.units, DV, DK, dtype=F32)]
-    outs += [shape(DV, DK, dtype=F32)] * sizes.heads
-    scratch = [
-        pltpu.VMEM((2 * groups, sizes.heads * KEY_ROWS, DV), BF16),
-        pltpu.VMEM((sizes.heads, DV, DK), F32),
-    ]
-    results = call(
+    outs += [shape(sizes.heads, DV, DK, dtype=F32)]
+    scratch = [pltpu.VMEM((2 * groups, sizes.heads * KEY_ROWS, DV), BF16)]
+    return call(
         kernel, outs, *pieces, ends, steps, scratch=scratch, flops=2_000_000_000, name="value_stage"
     )
-    return results[0], results[1], results[2:]
-
-
-def scan_states(sizes, transitions, injects):
-    chips = sizes.chips
-
-    def kernel(*refs):
-        transitions = refs[:chips]
-        injects = refs[chips : 2 * chips]
-        outs = refs[2 * chips : 3 * chips]
-        step, inject, entry = refs[3 * chips :]
-        chip = axis_index("chip")
-        for number in range(chips):
-            source = jnp.bitwise_xor(chip, number)
-            step[source] = transitions[number][...]
-            inject[source] = injects[number][...]
-        state = jnp.zeros((DV, DK), F32)
-        for index in range(chips):
-            entry[index] = state
-            if index == 0:
-                state = inject[index]
-            elif index < chips - 1:
-                state = product(beside(state), factor(step[index])) + inject[index]
-        for number in range(chips):
-            outs[number][...] = entry[jnp.bitwise_xor(chip, number)]
-
-    scratch = [pltpu.VMEM((chips, DV, DK), F32)] * 3
+
+
+def pair_injects(sizes, transitions, injects):
+    def kernel(own_step, step, own, other, out):
+        first = axis_index("chip") % 2 == 0
+        for head in range(sizes.heads):
+            later_step = jnp.where(first, step[head], own_step[head])
+            earlier = jnp.where(first, own[head], other[head])
+            later = jnp.where(first, other[head], own[head])
+            out[head] = product(beside(earlier), factor(later_step)) + later
+
     return call(
-        kernel,
-        [shape(DV, DK, dtype=F32)] * chips,
-        *transitions,
-        *injects,
-        scratch=scratch,
-        name="scan_states",
-    )
-
-
-def exchanged(sizes, parts):
-    return [parts[0]] + [
-        lax.ppermute(part, "chip", [(chip, chip ^ number) for chip in range(sizes.chips)])
-        for number, part in enumerate(parts)
-        if number
-    ]
+        kernel, shape(sizes.heads, DV, DK, dtype=F32), *transitions, *injects, name="pair_injects"
+    )
+
+
+def partnered(sizes, part, bit):
+    return lax.ppermute(part, "chip", [(chip, chip ^ bit) for chip in range(sizes.chips)])
 
 
 def entry_states(sizes, transitions, injects):
-    if sizes.swapped:
-        arrived = exchanged(sizes, transitions), exchanged(sizes, injects)
-        return exchanged(sizes, scan_states(sizes, *arrived))
-    transition = jnp.stack(transitions)
-    inject = jnp.stack(injects)
+    if sizes.paired:
+        step = partnered(sizes, transitions, 1)
+        inject = partnered(sizes, injects, 1)
+        pair = pair_injects(sizes, (transitions, step), (injects, inject))
+        return partnered(sizes, pair, 2), step, inject
     forward = [(chip, chip + 1) for chip in range(sizes.chips - 1)]
 
     def advance(_, entry):
-        left = jnp.einsum("hvd,hde->hve", entry, transition, precision=lax.Precision.HIGHEST)
-        return lax.ppermute(left + inject, "chip", forward)
-
-    entry = lax.fori_loop(0, sizes.chips - 1, advance, jnp.zeros_like(inject))
-    return [entry[head] for head in range(sizes.heads)]
+        left = jnp.einsum("hvd,hde->hve", entry, transitions, precision=lax.Precision.HIGHEST)
+        return lax.ppermute(left + injects, "chip", forward)
+
+    return (lax.fori_loop(0, sizes.chips - 1, advance, jnp.zeros_like(injects)),)
 
 
 def query_stage(sizes, pieces, values, before, keys, inverses_, ratios, rows, prefixes):
@@ -644,20 +599,22 @@
     )
 
 
-def read_states(sizes, states, readers, inners):
+def read_states(sizes, states_, readers, inners):
     groups = sizes.groups
     half = groups // 2
 
     def kernel(*refs):
-        states = refs[: sizes.heads]
-        readers, inners, own, other, entry = refs[sizes.heads :]
+        states = refs[: len(states_)]
+        readers, inners, own, other = refs[len(states_) :]
         core = axis_index("core")
-        chip = axis_index("chip") if sizes.swapped else 0
-        for number in range(sizes.heads):
-            place_ = jnp.bitwise_xor(chip, number) if sizes.swapped else number
-            entry[place_] = states[number][...]
+        chip = axis_index("chip")
         for head in range(sizes.heads):
-            high, low = split(entry[head])
+            entry = states[0][head]
+            if sizes.paired:
+                entry = jnp.where(chip >= 2, entry, 0.0)
+                further = product(beside(entry), factor(states[1][head])) + states[2][head]
+                entry = jnp.where(chip % 2 == 0, entry, further)
+            high, low = split(entry)
             stack = jnp.concatenate(
                 [
                     jnp.concatenate([high, high], 1),
@@ -674,8 +631,7 @@
                 out[:, head * DV : (head + 1) * DV] = result.astype(BF16)
 
     outs = [shape(half * CHUNK, sizes.heads * DV)] * 2
-    scratch = [pltpu.VMEM((sizes.heads, DV, DK), F32)]
-    return call(kernel, outs, *states, readers, inners, scratch=scratch, name="read_states")
+    return call(kernel, outs, *states_, readers, inners, name="read_states")
 
 
 def join(sizes, own, other):

time: 54.2 us -> 55.6 us (1.026)
  waiting for transfers between devices: 9.31 us -> 15.1 us
  starting transfers between devices: 28.1 us -> 23.3 us
    ppermute x9 -> x3, starting transfers between devices: 10.7 us -> 4.51 us  [partnered(): lax.ppermute(part, 'chip', [(chip, chip ^ bit) for chip in range(sizes.ch...]
    ppermute x9 -> x3, waiting for transfers between devices: 1.64 us -> 7.46 us  [partnered(): lax.ppermute(part, 'chip', [(chip, chip ^ bit) for chip in range(sizes.ch...]
    ppermute x9, starting transfers between devices: 17.2 us -> 18.5 us  [spread(): lax.ppermute(part, 'head', [(z, (z + ahead) % groups) for z in range(grou...]
  transfers between devices with their start and end apart: 21 -> 15, of which waited for: 5 -> 5; matrix products, arithmetic and copies ran while one was open for 0% -> 0% of each run, Pallas kernels for 21% -> 20%
where the time goes in v6:
time: 55.6 us; the launch traced here: 55.3 us
  starting transfers between devices  23.3 us (42%)
  waiting for transfers between devices  15.1 us (27%)
  Pallas kernels  13.4 us (24%)
  local copies, waits for them, and re-layouts  2.69 us (5%)
  other arithmetic  0.77 us (1%)
    ppermute x9, starting transfers between devices, spread(): lax.ppermute(part, 'head', [(z, (z + ahead) % groups) for z in range(grou...  18.5 us
    pallas_call x10, Pallas kernels, call(): pl.pallas_call(kernel, out_shape=outs, scratch_shapes=scratch, compiler_p...  13.4 us
    ppermute x3, waiting for transfers between devices, partnered(): lax.ppermute(part, 'chip', [(chip, chip ^ bit) for chip in range(sizes.ch...  7.46 us
    ppermute x9, waiting for transfers between devices, spread(): lax.ppermute(part, 'head', [(z, (z + ahead) % groups) for z in range(grou...  6.33 us
    ppermute x3, starting transfers between devices, partnered(): lax.ppermute(part, 'chip', [(chip, chip ^ bit) for chip in range(sizes.ch...  4.51 us
    unnamed x10, local copies, waits for them, and re-layouts  2.62 us
    ppermute x3, waiting for transfers between devices, swapped(): return lax.ppermute(part, 'core', [(0, 1), (1, 0)])  1.34 us
  transfers between devices with their start and end apart: 15, of which 5 were waited for; matrix products, arithmetic and copies ran while one was open for 0% of the time, Pallas kernels for 20%

profile of v6, /device:TPU:0, one launch (start us, length us, event | category | flops | bytes accessed | tf_op | source)
XLA Modules:
  0.0 55.3 jit_solution(18313259991275155089)
XLA Ops:
  0.0 0.1 dynamic-slice_bitcast_fusion.starts
  0.1 0.6 %copy-done.4 = bf16[32,32]{1,0:T(8,128)(2,1)S(1)} copy-done((bf16[32,32]{1,0:T(8,128)(2,1)S(1)}, bf16[32,32]{1,0:T(8,128)(2,1)}, u32[]{:S(2)}) %copy-start.4) | copy-done | bytes 2072
  0.7 0.8 %pad_maximum_fusion.scalars = bf16[32,96]{1,0:T(8,128)(2,1)S(1)} fusion(bf16[32,32]{1,0:T(8,128)(2,1)S(1)} %copy-done.4, bf16[32,64]{1,0:T(8,128)(2,1)} %param.9), kind=kLoop, calls=%fused_computation | loop fusion | flops 12288 | bytes 12288 | tf_op jit(solution)/shard_map/concatenate | solution.py:663
  1.5 1.0 %copy-done.1 = bf16[32,8192]{1,0:T(8,128)(2,1)S(1)} copy-done((bf16[32,8192]{1,0:T(8,128)(2,1)S(1)}, bf16[32,8192]{1,0:T(8,128)(2,1)}, u32[]{:S(2)}) %copy-start.1) | copy-done | bytes 524312
  2.5 0.3 pack_keys.1
  2.9 3.1 %collective-permute-start = (bf16[528,128]{1,0:T(8,128)(2,1)S(1)}, bf16[528,128]{1,0:T(8,128)(2,1)S(1)}, u32[]{:S(2)}, u32[]{:S(2)}) collective-permute-start(bf16[528,128]{1,0:T(8,128)(2,1)S(1)} %get-tuple-element.35), channel_id=1, source_target_pairs={{0,1},{1,2},{2,3},{3,0},{4,5},{5,6},{6,7},{7,4},{8,9},{9,10},{10,1... | collective-permute-start | bytes 405512 | tf_op jit(solution)/shard_map/ppermute | solution.py:655
  5.9 2.6 %collective-permute-start.1 = (bf16[528,128]{1,0:T(8,128)(2,1)S(1)}, bf16[528,128]{1,0:T(8,128)(2,1)S(1)}, u32[]{:S(2)}, u32[]{:S(2)}) collective-permute-start(bf16[528,128]{1,0:T(8,128)(2,1)S(1)} %get-tuple-element.36), channel_id=1, source_target_pairs={{0,2},{1,3},{2,0},{3,1},{4,6},{5,7},{6,4},{7,5},{8,10},{9,11},{10,... | collective-permute-start | bytes 405512 | tf_op jit(solution)/shard_map/ppermute | solution.py:655
  8.5 1.3 %collective-permute-start.2 = (bf16[528,128]{1,0:T(8,128)(2,1)S(1)}, bf16[528,128]{1,0:T(8,128)(2,1)S(1)}, u32[]{:S(2)}, u32[]{:S(2)}) collective-permute-start(bf16[528,128]{1,0:T(8,128)(2,1)S(1)} %get-tuple-element.37), channel_id=1, source_target_pairs={{0,3},{1,0},{2,1},{3,2},{4,7},{5,4},{6,5},{7,6},{8,11},{9,8},{10,9... | collective-permute-start | bytes 405512 | tf_op jit(solution)/shard_map/ppermute | solution.py:655
  9.9 0.9 %copy-done.3 = bf16[32,4096]{1,0:T(8,128)(2,1)S(1)} copy-done((bf16[32,4096]{1,0:T(8,128)(2,1)S(1)}, bf16[32,4096]{1,0:T(8,128)(2,1)}, u32[]{:S(2)}) %copy-start.3) | copy-done | bytes 262168
  10.8 0.2 pack_reads.1
  11.1 1.4 %collective-permute-done.refs_1_ = bf16[528,128]{1,0:T(8,128)(2,1)S(1)} collective-permute-done((bf16[528,128]{1,0:T(8,128)(2,1)S(1)}, bf16[528,128]{1,0:T(8,128)(2,1)S(1)}, u32[]{:S(2)}, u32[]{:S(2)}) %collective-permute-start) | collective-permute-done | bytes 135200 | tf_op jit(solution)/shard_map/ppermute | solution.py:655
  12.5 5.0 %collective-permute-done.1.refs_2_ = bf16[528,128]{1,0:T(8,128)(2,1)S(1)} collective-permute-done((bf16[528,128]{1,0:T(8,128)(2,1)S(1)}, bf16[528,128]{1,0:T(8,128)(2,1)S(1)}, u32[]{:S(2)}, u32[]{:S(2)}) %collective-permute-start.1) | collective-permute-done | bytes 135200 | tf_op jit(solution)/shard_map/ppermute | solution.py:655
  17.5 0.1 collective-permute-start.3
  17.6 3.4 %collective-permute-start.6 = (bf16[2,256,128]{2,1,0:T(8,128)(2,1)S(1)}, bf16[2,256,128]{2,1,0:T(8,128)(2,1)S(1)}, u32[]{:S(2)}, u32[]{:S(2)}) collective-permute-start(bf16[2,256,128]{2,1,0:T(8,128)(2,1)S(1)} %get-tuple-element.42), channel_id=1, source_target_pairs={{0,1},{1,2},{2,3},{3,0},{4,5},{5,6},{6,7},{7,4},{8,9},{9,10},{10,1... | collective-permute-start | bytes 393224 | tf_op jit(solution)/shard_map/ppermute | solution.py:655
  21.0 1.6 %collective-permute-start.7 = (bf16[2,256,128]{2,1,0:T(8,128)(2,1)S(1)}, bf16[2,256,128]{2,1,0:T(8,128)(2,1)S(1)}, u32[]{:S(2)}, u32[]{:S(2)}) collective-permute-start(bf16[2,256,128]{2,1,0:T(8,128)(2,1)S(1)} %get-tuple-element.43), channel_id=1, source_target_pairs={{0,2},{1,3},{2,0},{3,1},{4,6},{5,7},{6,4},{7,5},{8,10},{9,11},{10,... | collective-permute-start | bytes 393224 | tf_op jit(solution)/shard_map/ppermute | solution.py:655
  22.7 0.8 %collective-permute-start.8 = (bf16[2,256,128]{2,1,0:T(8,128)(2,1)S(1)}, bf16[2,256,128]{2,1,0:T(8,128)(2,1)S(1)}, u32[]{:S(2)}, u32[]{:S(2)}) collective-permute-start(bf16[2,256,128]{2,1,0:T(8,128)(2,1)S(1)} %get-tuple-element.44), channel_id=1, source_target_pairs={{0,3},{1,0},{2,1},{3,2},{4,7},{5,4},{6,5},{7,6},{8,11},{9,8},{10,9... | collective-permute-start | bytes 393224 | tf_op jit(solution)/shard_map/ppermute | solution.py:655
  23.5 7.1 %key_stage.1 = (bf16[16,128,128]{2,1,0:T(8,128)(2,1)S(1)}, bf16[16,128,256]{2,1,0:T(8,128)(2,1)S(1)}, bf16[16,128,256]{2,1,0:T(8,128)(2,1)S(1)}, f32[16,64,128]{...) custom-call(bf16[528,128]{1,0:T(8,128)(2,1)S(1)} %get-tuple-element., ...), custom_call_target="tpu_custom_call" | custom-call | flops 6000000000 | tf_op jit(solution)/shard_map/key_stage/pallas_call | solution.py:194
  30.6 1.6 %collective-permute-start.4 = (f32[4,128,128]{2,1,0:T(8,128)S(1)}, f32[4,128,128]{2,1,0:T(8,128)S(1)}, u32[]{:S(2)}, u32[]{:S(2)}) collective-permute-start(f32[4,128,128]{2,1,0:T(8,128)S(1)} %get-tuple-element.38.own_step), channel_id=1, source_target_pairs={{0,8},{8,0},{16,24},{24,16},{1,9},{9,1},{17,25},{25,17},{2,10},{10... | collective-permute-start | bytes 786440 | tf_op jit(solution)/shard_map/ppermute | solution.py:524
  32.1 0.8 %value_stage.1 = (bf16[16,128,128]{2,1,0:T(8,128)(2,1)S(1)}, f32[16,128,128]{2,1,0:T(8,128)S(1)}, f32[4,128,128]{2,1,0:T(8,128)S(1)}) custom-call(bf16[2,256,128]{2,1,0:T(8,128)(2,1)S(1)} %get-tuple-element.41.refs_0_, bf16[2,256,128]{2,1,0:T(8,128)(2,1)S(1)} %collective-permute-done.6.refs_1_, bf16[2,256,128]{2,1,0:T(8,128)(2,1)S(1)} %collective-permute-done.7.refs_2_, ...), custom_call_target="tpu_custom_call" | custom-call | flops 2000000000 | tf_op jit(solution)/shard_map/value_stage/pallas_call | solution.py:194
  32.9 1.3 %collective-permute-start.9 = (f32[4,128,128]{2,1,0:T(8,128)S(1)}, f32[4,128,128]{2,1,0:T(8,128)S(1)}, u32[]{:S(2)}, u32[]{:S(2)}) collective-permute-start(f32[4,128,128]{2,1,0:T(8,128)S(1)} %get-tuple-element.47.own), channel_id=1, source_target_pairs={{0,8},{8,0},{16,24},{24,16},{1,9},{9,1},{17,25},{25,17},{2,10},{10... | collective-permute-start | bytes 786440 | tf_op jit(solution)/shard_map/ppermute | solution.py:524
  34.3 3.3 %collective-permute-start.11 = (bf16[2,128,128]{2,1,0:T(8,128)(2,1)S(1)}, bf16[2,128,128]{2,1,0:T(8,128)(2,1)S(1)}, u32[]{:S(2)}, u32[]{:S(2)}) collective-permute-start(bf16[2,128,128]{2,1,0:T(8,128)(2,1)S(1)} %get-tuple-element.49), channel_id=1, source_target_pairs={{0,1},{1,2},{2,3},{3,0},{4,5},{5,6},{6,7},{7,4},{8,9},{9,10},{10,1... | collective-permute-start | bytes 196616 | tf_op jit(solution)/shard_map/ppermute | solution.py:655
  37.6 1.3 %collective-permute-start.12 = (bf16[2,128,128]{2,1,0:T(8,128)(2,1)S(1)}, bf16[2,128,128]{2,1,0:T(8,128)(2,1)S(1)}, u32[]{:S(2)}, u32[]{:S(2)}) collective-permute-start(bf16[2,128,128]{2,1,0:T(8,128)(2,1)S(1)} %get-tuple-element.50), channel_id=1, source_target_pairs={{0,2},{1,3},{2,0},{3,1},{4,6},{5,7},{6,4},{7,5},{8,10},{9,11},{10,... | collective-permute-start | bytes 196616 | tf_op jit(solution)/shard_map/ppermute | solution.py:655
  38.9 1.1 %collective-permute-start.13 = (bf16[2,128,128]{2,1,0:T(8,128)(2,1)S(1)}, bf16[2,128,128]{2,1,0:T(8,128)(2,1)S(1)}, u32[]{:S(2)}, u32[]{:S(2)}) collective-permute-start(bf16[2,128,128]{2,1,0:T(8,128)(2,1)S(1)} %get-tuple-element.51), channel_id=1, source_target_pairs={{0,3},{1,0},{2,1},{3,2},{4,7},{5,4},{6,5},{7,6},{8,11},{9,8},{10,9... | collective-permute-start | bytes 196616 | tf_op jit(solution)/shard_map/ppermute | solution.py:655
  39.9 4.5 %collective-permute-done.9.other.refs_2_ = f32[4,128,128]{2,1,0:T(8,128)S(1)} collective-permute-done((f32[4,128,128]{2,1,0:T(8,128)S(1)}, f32[4,128,128]{2,1,0:T(8,128)S(1)}, u32[]{:S(2)}, u32[]{:S(2)}) %collective-permute-start.9) | collective-permute-done | bytes 262176 | tf_op jit(solution)/shard_map/ppermute | solution.py:524
  44.5 0.2 pair_injects.1
  44.7 1.6 %collective-permute-start.10 = (f32[4,128,128]{2,1,0:T(8,128)S(1)}, f32[4,128,128]{2,1,0:T(8,128)S(1)}, u32[]{:S(2)}, u32[]{:S(2)}) collective-permute-start(f32[4,128,128]{2,1,0:T(8,128)S(1)} %pair_injects.1), channel_id=1, source_target_pairs={{0,16},{8,24},{16,0},{24,8},{1,17},{9,25},{17,1},{25,9},{2,18},{10... | collective-permute-start | bytes 786440 | tf_op jit(solution)/shard_map/ppermute | solution.py:524
  46.4 2.8 %query_stage.1 = (bf16[16,64,256]{2,1,0:T(8,128)(2,1)S(1)}, f32[16,64,128]{2,1,0:T(8,128)S(1)}) custom-call(bf16[2,128,128]{2,1,0:T(8,128)(2,1)S(1)} %get-tuple-element.48.refs_0_, bf16[2,128,128]{2,1,0:T(8,128)(2,1)S(1)} %collective-permute-done.11.refs_1_, bf16[2,128,128]{2,1,0:T(8,128)(2,1)S(1)} %collective-permute-done.12.refs_2_, ...), custom_call_target="tpu_custom_call" | custom-call | flops 3000000000 | tf_op jit(solution)/shard_map/query_stage/pallas_call | solution.py:194
  49.2 2.9 %collective-permute-done.10.refs_0_ = f32[4,128,128]{2,1,0:T(8,128)S(1)} collective-permute-done((f32[4,128,128]{2,1,0:T(8,128)S(1)}, f32[4,128,128]{2,1,0:T(8,128)S(1)}, u32[]{:S(2)}, u32[]{:S(2)}) %collective-permute-start.10) | collective-permute-done | bytes 262176 | tf_op jit(solution)/shard_map/ppermute | solution.py:524
  52.1 1.1 %read_states.1 = (bf16[128,512]{1,0:T(8,128)(2,1)S(1)}, bf16[128,512]{1,0:T(8,128)(2,1)S(1)}) custom-call(f32[4,128,128]{2,1,0:T(8,128)S(1)} %collective-permute-done.10.refs_0_, f32[4,128,128]{2,1,0:T(8,128)S(1)} %collective-permute-done.4.step.refs_1_, f32[4,128,128]{2,1,0:T(8,128)S(1)} %collective-permute-done.9.other.refs_2_, ...), custom_call_target="tpu_custom_call" | custom-call | tf_op jit(solution)/shard_map/read_states/pallas_call | solution.py:194
  53.2 0.1 collective-permute-start.14
  53.3 1.3 %collective-permute-done.14.other = bf16[128,512]{1,0:T(8,128)(2,1)S(1)} collective-permute-done((bf16[128,512]{1,0:T(8,128)(2,1)S(1)}, bf16[128,512]{1,0:T(8,128)(2,1)S(1)}, u32[]{:S(2)}, u32[]{:S(2)}) %collective-permute-start.14) | collective-permute-done | bytes 131104 | tf_op jit(solution)/shard_map/ppermute | solution.py:661
  54.6 0.7 %join.1 = bf16[128,1024]{1,0:T(8,128)(2,1)} custom-call(bf16[128,512]{1,0:T(8,128)(2,1)S(1)} %get-tuple-element.61.own, bf16[128,512]{1,0:T(8,128)(2,1)S(1)} %collective-permute-done.14.other), custom_call_target="tpu_custom_call" | custom-call | tf_op jit(solution)/shard_map/join/pallas_call | solution.py:194
  (20 shorter events, 0.2 us)
Async XLA Ops:
  0.0 0.7 %copy-start.4 = (bf16[32,32]{1,0:T(8,128)(2,1)S(1)}, bf16[32,32]{1,0:T(8,128)(2,1)}, u32[]{:S(2)}) copy-start(bf16[32,32]{1,0:T(8,128)(2,1)} %param.10) | copy-start | bytes 6148
  1.5 1.0 %copy-start.1 = (bf16[32,8192]{1,0:T(8,128)(2,1)S(1)}, bf16[32,8192]{1,0:T(8,128)(2,1)}, u32[]{:S(2)}) copy-start(bf16[32,8192]{1,0:T(8,128)(2,1)} %keys.1) | copy-start | bytes 1572868
  2.5 7.4 %copy-start.2 = (bf16[32,8192]{1,0:T(8,128)(2,1)S(1)}, bf16[32,8192]{1,0:T(8,128)(2,1)}, u32[]{:S(2)}) copy-start(bf16[32,8192]{1,0:T(8,128)(2,1)} %values.1) | copy-start | bytes 1572868
  2.9 9.6 %collective-permute-start = (bf16[528,128]{1,0:T(8,128)(2,1)S(1)}, bf16[528,128]{1,0:T(8,128)(2,1)S(1)}, u32[]{:S(2)}, u32[]{:S(2)}) collective-permute-start(bf16[528,128]{1,0:T(8,128)(2,1)S(1)} %get-tuple-element.35), channel_id=1, source_target_pairs={{0,1},{1,2},{2,3},{3,0},{4,5},{5,6},{6,7},{7,4},{8,9},{9,10},{10,1... | collective-permute-start | bytes 405512 | tf_op jit(solution)/shard_map/ppermute | solution.py:655
  5.9 11.5 %collective-permute-start.1 = (bf16[528,128]{1,0:T(8,128)(2,1)S(1)}, bf16[528,128]{1,0:T(8,128)(2,1)S(1)}, u32[]{:S(2)}, u32[]{:S(2)}) collective-permute-start(bf16[528,128]{1,0:T(8,128)(2,1)S(1)} %get-tuple-element.36), channel_id=1, source_target_pairs={{0,2},{1,3},{2,0},{3,1},{4,6},{5,7},{6,4},{7,5},{8,10},{9,11},{10,... | collective-permute-start | bytes 405512 | tf_op jit(solution)/shard_map/ppermute | solution.py:655
  8.5 8.9 %collective-permute-start.2 = (bf16[528,128]{1,0:T(8,128)(2,1)S(1)}, bf16[528,128]{1,0:T(8,128)(2,1)S(1)}, u32[]{:S(2)}, u32[]{:S(2)}) collective-permute-start(bf16[528,128]{1,0:T(8,128)(2,1)S(1)} %get-tuple-element.37), channel_id=1, source_target_pairs={{0,3},{1,0},{2,1},{3,2},{4,7},{5,4},{6,5},{7,6},{8,11},{9,8},{10,9... | collective-permute-start | bytes 405512 | tf_op jit(solution)/shard_map/ppermute | solution.py:655
  9.9 1.0 %copy-start.3 = (bf16[32,4096]{1,0:T(8,128)(2,1)S(1)}, bf16[32,4096]{1,0:T(8,128)(2,1)}, u32[]{:S(2)}) copy-start(bf16[32,4096]{1,0:T(8,128)(2,1)} %queries.1) | copy-start | bytes 786436
  11.0 6.5 %collective-permute-start.5 = (bf16[4,384,128]{2,1,0:T(8,128)(2,1)S(1)}, bf16[4,384,128]{2,1,0:T(8,128)(2,1)S(1)}, u32[]{:S(2)}, u32[]{:S(2)}) collective-permute-start(bf16[4,384,128]{2,1,0:T(8,128)(2,1)S(1)} %get-tuple-element.40), channel_id=1, source_target_pairs={{0,4},{4,0},{1,5},{5,1},{2,6},{6,2},{3,7},{7,3},{8,12},{12,8},{9,1... | collective-permute-start | bytes 1179656 | tf_op jit(solution)/shard_map/ppermute | solution.py:661
  17.5 6.0 %collective-permute-start.3 = (bf16[4,272,128]{2,1,0:T(8,128)(2,1)S(1)}, bf16[4,272,128]{2,1,0:T(8,128)(2,1)S(1)}, u32[]{:S(2)}, u32[]{:S(2)}) collective-permute-start(bf16[4,272,128]{2,1,0:T(8,128)(2,1)S(1)} %swap_keys.1), channel_id=1, source_target_pairs={{0,4},{4,0},{1,5},{5,1},{2,6},{6,2},{3,7},{7,3},{8,12},{12,8},{9,1... | collective-permute-start | bytes 835592 | tf_op jit(solution)/shard_map/ppermute | solution.py:661
  17.6 14.5 %collective-permute-start.6 = (bf16[2,256,128]{2,1,0:T(8,128)(2,1)S(1)}, bf16[2,256,128]{2,1,0:T(8,128)(2,1)S(1)}, u32[]{:S(2)}, u32[]{:S(2)}) collective-permute-start(bf16[2,256,128]{2,1,0:T(8,128)(2,1)S(1)} %get-tuple-element.42), channel_id=1, source_target_pairs={{0,1},{1,2},{2,3},{3,0},{4,5},{5,6},{6,7},{7,4},{8,9},{9,10},{10,1... | collective-permute-start | bytes 393224 | tf_op jit(solution)/shard_map/ppermute | solution.py:655
  21.0 11.1 %collective-permute-start.7 = (bf16[2,256,128]{2,1,0:T(8,128)(2,1)S(1)}, bf16[2,256,128]{2,1,0:T(8,128)(2,1)S(1)}, u32[]{:S(2)}, u32[]{:S(2)}) collective-permute-start(bf16[2,256,128]{2,1,0:T(8,128)(2,1)S(1)} %get-tuple-element.43), channel_id=1, source_target_pairs={{0,2},{1,3},{2,0},{3,1},{4,6},{5,7},{6,4},{7,5},{8,10},{9,11},{10,... | collective-permute-start | bytes 393224 | tf_op jit(solution)/shard_map/ppermute | solution.py:655
  22.7 9.5 %collective-permute-start.8 = (bf16[2,256,128]{2,1,0:T(8,128)(2,1)S(1)}, bf16[2,256,128]{2,1,0:T(8,128)(2,1)S(1)}, u32[]{:S(2)}, u32[]{:S(2)}) collective-permute-start(bf16[2,256,128]{2,1,0:T(8,128)(2,1)S(1)} %get-tuple-element.44), channel_id=1, source_target_pairs={{0,3},{1,0},{2,1},{3,2},{4,7},{5,4},{6,5},{7,6},{8,11},{9,8},{10,9... | collective-permute-start | bytes 393224 | tf_op jit(solution)/shard_map/ppermute | solution.py:655
  30.6 9.4 %collective-permute-start.4 = (f32[4,128,128]{2,1,0:T(8,128)S(1)}, f32[4,128,128]{2,1,0:T(8,128)S(1)}, u32[]{:S(2)}, u32[]{:S(2)}) collective-permute-start(f32[4,128,128]{2,1,0:T(8,128)S(1)} %get-tuple-element.38.own_step), channel_id=1, source_target_pairs={{0,8},{8,0},{16,24},{24,16},{1,9},{9,1},{17,25},{25,17},{2,10},{10... | collective-permute-start | bytes 786440 | tf_op jit(solution)/shard_map/ppermute | solution.py:524
  32.9 11.5 %collective-permute-start.9 = (f32[4,128,128]{2,1,0:T(8,128)S(1)}, f32[4,128,128]{2,1,0:T(8,128)S(1)}, u32[]{:S(2)}, u32[]{:S(2)}) collective-permute-start(f32[4,128,128]{2,1,0:T(8,128)S(1)} %get-tuple-element.47.own), channel_id=1, source_target_pairs={{0,8},{8,0},{16,24},{24,16},{1,9},{9,1},{17,25},{25,17},{2,10},{10... | collective-permute-start | bytes 786440 | tf_op jit(solution)/shard_map/ppermute | solution.py:524
  34.3 12.1 %collective-permute-start.11 = (bf16[2,128,128]{2,1,0:T(8,128)(2,1)S(1)}, bf16[2,128,128]{2,1,0:T(8,128)(2,1)S(1)}, u32[]{:S(2)}, u32[]{:S(2)}) collective-permute-start(bf16[2,128,128]{2,1,0:T(8,128)(2,1)S(1)} %get-tuple-element.49), channel_id=1, source_target_pairs={{0,1},{1,2},{2,3},{3,0},{4,5},{5,6},{6,7},{7,4},{8,9},{9,10},{10,1... | collective-permute-start | bytes 196616 | tf_op jit(solution)/shard_map/ppermute | solution.py:655
  37.6 8.8 %collective-permute-start.12 = (bf16[2,128,128]{2,1,0:T(8,128)(2,1)S(1)}, bf16[2,128,128]{2,1,0:T(8,128)(2,1)S(1)}, u32[]{:S(2)}, u32[]{:S(2)}) collective-permute-start(bf16[2,128,128]{2,1,0:T(8,128)(2,1)S(1)} %get-tuple-element.50), channel_id=1, source_target_pairs={{0,2},{1,3},{2,0},{3,1},{4,6},{5,7},{6,4},{7,5},{8,10},{9,11},{10,... | collective-permute-start | bytes 196616 | tf_op jit(solution)/shard_map/ppermute | solution.py:655
  38.9 7.5 %collective-permute-start.13 = (bf16[2,128,128]{2,1,0:T(8,128)(2,1)S(1)}, bf16[2,128,128]{2,1,0:T(8,128)(2,1)S(1)}, u32[]{:S(2)}, u32[]{:S(2)}) collective-permute-start(bf16[2,128,128]{2,1,0:T(8,128)(2,1)S(1)} %get-tuple-element.51), channel_id=1, source_target_pairs={{0,3},{1,0},{2,1},{3,2},{4,7},{5,4},{6,5},{7,6},{8,11},{9,8},{10,9... | collective-permute-start | bytes 196616 | tf_op jit(solution)/shard_map/ppermute | solution.py:655
  44.7 7.4 %collective-permute-start.10 = (f32[4,128,128]{2,1,0:T(8,128)S(1)}, f32[4,128,128]{2,1,0:T(8,128)S(1)}, u32[]{:S(2)}, u32[]{:S(2)}) collective-permute-start(f32[4,128,128]{2,1,0:T(8,128)S(1)} %pair_injects.1), channel_id=1, source_target_pairs={{0,16},{8,24},{16,0},{24,8},{1,17},{9,25},{17,1},{25,9},{2,18},{10... | collective-permute-start | bytes 786440 | tf_op jit(solution)/shard_map/ppermute | solution.py:524
  53.2 1.4 %collective-permute-start.14 = (bf16[128,512]{1,0:T(8,128)(2,1)S(1)}, bf16[128,512]{1,0:T(8,128)(2,1)S(1)}, u32[]{:S(2)}, u32[]{:S(2)}) collective-permute-start(bf16[128,512]{1,0:T(8,128)(2,1)S(1)} %get-tuple-element.62), channel_id=1, source_target_pairs={{0,4},{4,0},{1,5},{5,1},{2,6},{6,2},{3,7},{7,3},{8,12},{12,8},{9,1... | collective-permute-start | bytes 393224 | tf_op jit(solution)/shard_map/ppermute | solution.py:661
  (1 other events, 0.0 us)

commit v7 on v2

--- a/solution.py
+++ b/solution.py
@@ -190,10 +190,13 @@
     )
 
 
-def call(kernel, outs, *args, scratch=(), flops=0, name=None):
+def call(kernel, outs, *args, scratch=(), flops=0, far=0, name=None):
+    specs = [pl.BlockSpec(memory_space=pltpu.HBM)] * far
+    specs += [pl.BlockSpec(memory_space=pltpu.VMEM)] * (len(args) - far)
     return pl.pallas_call(
         kernel,
         out_shape=outs,
+        in_specs=specs,
         scratch_shapes=scratch,
         compiler_params=pltpu.CompilerParams(vmem_limit_bytes=24 * 2**20),
         cost_estimate=pl.CostEstimate(flops=flops, bytes_accessed=0, transcendentals=0),
@@ -237,7 +240,22 @@
     rows = sizes.heads * KEY_ROWS
     count = sizes.heads * NH
 
-    def kernel(keys, betas, log_gates, starts, *outs):
+    def kernel(far_keys, far_betas, far_gates, far_starts, *refs):
+        outs = refs[: sizes.groups]
+        keys, betas, log_gates, starts, done = refs[sizes.groups :]
+        width = sizes.group_heads * NH * DK
+        pairs = [(far_betas, betas), (far_gates, log_gates), (far_starts, starts)]
+        for group in range(sizes.groups):
+            part = slice(group * width, (group + 1) * width)
+            pairs.append((far_keys.at[:, part], keys.at[:, part]))
+        copies = [
+            pltpu.make_async_copy(far, near, done.at[number])
+            for number, (far, near) in enumerate(pairs)
+        ]
+        for copy in copies:
+            copy.start()
+        for copy in copies:
+            copy.wait()
         z = axis_index("head")
         core = axis_index("core")
         heads = log_gates.shape[1]
@@ -248,7 +266,10 @@
             pieces.append(dot_nt(pick.astype(BF16), betas[...]))
         same = iota((heads, heads), 0) == iota((heads, heads), 1)
         pieces.append(dot_nt(same.astype(BF16), log_gates[...]))
-        pieces.append(jnp.broadcast_to(starts[...].astype(F32), (heads, TOK)))
+        length = sizes.groups * TOK
+        own = iota((length, TOK), 0) == z * TOK + iota((length, TOK), 1)
+        own_starts = jnp.broadcast_to(starts[...].astype(F32), (heads, length)).astype(BF16)
+        pieces.append(dot(own_starts, own.astype(BF16)))
         scales = jnp.concatenate(pieces, 1).astype(BF16)
         for ahead, out in enumerate(outs):
             target = shifted(z, ahead, sizes.groups)
@@ -265,7 +286,16 @@
             out[2 * rows :, :] = dot(pick.astype(BF16), scales).astype(BF16)
 
     outs = [shape(2 * rows + SCALE_ROWS, DK)] * sizes.groups
-    return call(kernel, outs, keys, betas, log_gates, starts, name="pack_keys")
+    loaded = (keys, betas, log_gates, starts)
+    scratch = [pltpu.VMEM(each.shape, each.dtype) for each in loaded]
+    return call(
+        kernel,
+        outs,
+        *[pltpu.with_memory_space_constraint(each, pltpu.HBM) for each in loaded],
+        scratch=scratch + [pltpu.SemaphoreType.DMA((3 + sizes.groups,))],
+        far=4,
+        name="pack_keys",
+    )
 
 
 def swap_keys(sizes, arrived):
@@ -683,7 +713,6 @@
 def local(queries, keys, values, betas, log_gates, starts):
     groups = lax.axis_size("head")
     sizes = Sizes(groups, log_gates.shape[1] // groups, lax.axis_size("chip"))
-    own_starts = lax.dynamic_slice(starts, (axis_index("head") * TOK,), (TOK,)).reshape(1, TOK)
 
     def spread(parts):
         return [parts[0]] + [
@@ -695,7 +724,7 @@
     def swapped(part):
         return lax.ppermute(part, "core", [(0, 1), (1, 0)])
 
-    arrived = spread(pack_keys(sizes, keys, betas, log_gates, own_starts))
+    arrived = spread(pack_keys(sizes, keys, betas, log_gates, starts.reshape(1, -1)))
     kept, sent = pack_reads(sizes, values, queries)
     value_parts, query_parts = merge_reads(sizes, kept, swapped(sent))
     value_parts = spread(value_parts)

time: 54.1 us -> 52.9 us (0.978)
  local copies, waits for them, and re-layouts: 3.42 us -> 0.95 us
  Pallas kernels: 13 us -> 14.3 us
    unnamed x12 -> x4, local copies, waits for them, and re-layouts: 3.35 us -> 0.95 us
    pallas_call x10, Pallas kernels: 13 us -> 14.3 us  [call(): pl.pallas_call(kernel, out_shape=outs, in_specs=specs, scratch_shapes=scr...]
  transfers between devices with their start and end apart: 21 -> 21, of which waited for: 5 -> 5; matrix products, arithmetic and copies ran while one was open for 0% -> 0% of each run, Pallas kernels for 21% -> 22%
where the time goes in v7:
time: 52.9 us; the launch traced here: 52.7 us
  starting transfers between devices  28.1 us (53%)
  Pallas kernels  14.3 us (27%)
  waiting for transfers between devices  9.3 us (18%)
  local copies, waits for them, and re-layouts  0.95 us (2%)
    ppermute x9, starting transfers between devices, spread(): lax.ppermute(part, 'head', [(z, (z + ahead) % groups) for z in range(grou...  17.2 us
    pallas_call x10, Pallas kernels, call(): pl.pallas_call(kernel, out_shape=outs, in_specs=specs, scratch_shapes=scr...  14.3 us
    ppermute x9, starting transfers between devices, exchanged(): lax.ppermute(part, 'chip', [(chip, chip ^ number) for chip in range(sizes...  10.7 us
    ppermute x9, waiting for transfers between devices, spread(): lax.ppermute(part, 'head', [(z, (z + ahead) % groups) for z in range(grou...  6.33 us
    ppermute x9, waiting for transfers between devices, exchanged(): lax.ppermute(part, 'chip', [(chip, chip ^ number) for chip in range(sizes...  1.63 us
    ppermute x3, waiting for transfers between devices, swapped(): return lax.ppermute(part, 'core', [(0, 1), (1, 0)])  1.34 us
  transfers between devices with their start and end apart: 21, of which 5 were waited for; matrix products, arithmetic and copies ran while one was open for 0% of the time, Pallas kernels for 22%

profile of v7, /device:TPU:0, one launch (start us, length us, event | category | flops | bytes accessed | tf_op | source)
XLA Modules:
  0.0 52.7 jit_solution(14418063740312966622)
XLA Ops:
  0.0 1.6 %pack_keys.1 = (bf16[528,128]{1,0:T(8,128)(2,1)S(1)}, bf16[528,128]{1,0:T(8,128)(2,1)S(1)}, bf16[528,128]{1,0:T(8,128)(2,1)S(1)}, bf16[528,128]{1,0:T(8,128)(2,1)S(1)}) custom-call(bf16[32,8192]{1,0:T(8,128)(2,1)} %far_keys.1, bf16[32,64]{1,0:T(8,128)(2,1)} %far_betas.1, bf16[32,32]{1,0:T(8,128)(2,1)} %far_gates.1, s32[1,128]{1,0:T(1,128)} %bitcast.1), custom_call_target="tpu_custom_call" | custom-call | tf_op jit(solution)/shard_map/pack_keys/pallas_call | solution.py:196
  1.6 3.1 %collective-permute-start = (bf16[528,128]{1,0:T(8,128)(2,1)S(1)}, bf16[528,128]{1,0:T(8,128)(2,1)S(1)}, u32[]{:S(2)}, u32[]{:S(2)}) collective-permute-start(bf16[528,128]{1,0:T(8,128)(2,1)S(1)} %get-tuple-element.45), channel_id=1, source_target_pairs={{0,1},{1,2},{2,3},{3,0},{4,5},{5,6},{6,7},{7,4},{8,9},{9,10},{10,1... | collective-permute-start | bytes 405512 | tf_op jit(solution)/shard_map/ppermute | solution.py:719
  4.7 2.6 %collective-permute-start.1 = (bf16[528,128]{1,0:T(8,128)(2,1)S(1)}, bf16[528,128]{1,0:T(8,128)(2,1)S(1)}, u32[]{:S(2)}, u32[]{:S(2)}) collective-permute-start(bf16[528,128]{1,0:T(8,128)(2,1)S(1)} %get-tuple-element.46), channel_id=1, source_target_pairs={{0,2},{1,3},{2,0},{3,1},{4,6},{5,7},{6,4},{7,5},{8,10},{9,11},{10,... | collective-permute-start | bytes 405512 | tf_op jit(solution)/shard_map/ppermute | solution.py:719
  7.3 1.3 %collective-permute-start.2 = (bf16[528,128]{1,0:T(8,128)(2,1)S(1)}, bf16[528,128]{1,0:T(8,128)(2,1)S(1)}, u32[]{:S(2)}, u32[]{:S(2)}) collective-permute-start(bf16[528,128]{1,0:T(8,128)(2,1)S(1)} %get-tuple-element.47), channel_id=1, source_target_pairs={{0,3},{1,0},{2,1},{3,2},{4,7},{5,4},{6,5},{7,6},{8,11},{9,8},{10,9... | collective-permute-start | bytes 405512 | tf_op jit(solution)/shard_map/ppermute | solution.py:719
  8.7 0.9 %copy-done.1 = bf16[32,4096]{1,0:T(8,128)(2,1)S(1)} copy-done((bf16[32,4096]{1,0:T(8,128)(2,1)S(1)}, bf16[32,4096]{1,0:T(8,128)(2,1)}, u32[]{:S(2)}) %copy-start.1) | copy-done | bytes 262168
  9.6 0.2 pack_reads.1
  9.9 1.4 %collective-permute-done.refs_1_ = bf16[528,128]{1,0:T(8,128)(2,1)S(1)} collective-permute-done((bf16[528,128]{1,0:T(8,128)(2,1)S(1)}, bf16[528,128]{1,0:T(8,128)(2,1)S(1)}, u32[]{:S(2)}, u32[]{:S(2)}) %collective-permute-start) | collective-permute-done | bytes 135200 | tf_op jit(solution)/shard_map/ppermute | solution.py:719
  11.2 5.0 %collective-permute-done.1.refs_2_ = bf16[528,128]{1,0:T(8,128)(2,1)S(1)} collective-permute-done((bf16[528,128]{1,0:T(8,128)(2,1)S(1)}, bf16[528,128]{1,0:T(8,128)(2,1)S(1)}, u32[]{:S(2)}, u32[]{:S(2)}) %collective-permute-start.1) | collective-permute-done | bytes 135200 | tf_op jit(solution)/shard_map/ppermute | solution.py:719
  16.4 3.4 %collective-permute-start.8 = (bf16[2,256,128]{2,1,0:T(8,128)(2,1)S(1)}, bf16[2,256,128]{2,1,0:T(8,128)(2,1)S(1)}, u32[]{:S(2)}, u32[]{:S(2)}) collective-permute-start(bf16[2,256,128]{2,1,0:T(8,128)(2,1)S(1)} %get-tuple-element.55), channel_id=1, source_target_pairs={{0,1},{1,2},{2,3},{3,0},{4,5},{5,6},{6,7},{7,4},{8,9},{9,10},{10,1... | collective-permute-start | bytes 393224 | tf_op jit(solution)/shard_map/ppermute | solution.py:719
  19.8 1.6 %collective-permute-start.9 = (bf16[2,256,128]{2,1,0:T(8,128)(2,1)S(1)}, bf16[2,256,128]{2,1,0:T(8,128)(2,1)S(1)}, u32[]{:S(2)}, u32[]{:S(2)}) collective-permute-start(bf16[2,256,128]{2,1,0:T(8,128)(2,1)S(1)} %get-tuple-element.56), channel_id=1, source_target_pairs={{0,2},{1,3},{2,0},{3,1},{4,6},{5,7},{6,4},{7,5},{8,10},{9,11},{10,... | collective-permute-start | bytes 393224 | tf_op jit(solution)/shard_map/ppermute | solution.py:719
  21.4 0.8 %collective-permute-start.10 = (bf16[2,256,128]{2,1,0:T(8,128)(2,1)S(1)}, bf16[2,256,128]{2,1,0:T(8,128)(2,1)S(1)}, u32[]{:S(2)}, u32[]{:S(2)}) collective-permute-start(bf16[2,256,128]{2,1,0:T(8,128)(2,1)S(1)} %get-tuple-element.57), channel_id=1, source_target_pairs={{0,3},{1,0},{2,1},{3,2},{4,7},{5,4},{6,5},{7,6},{8,11},{9,8},{10,9... | collective-permute-start | bytes 393224 | tf_op jit(solution)/shard_map/ppermute | solution.py:719
  22.3 7.1 %key_stage.1 = (bf16[16,128,128]{2,1,0:T(8,128)(2,1)S(1)}, bf16[16,128,256]{2,1,0:T(8,128)(2,1)S(1)}, bf16[16,128,256]{2,1,0:T(8,128)(2,1)S(1)}, f32[16,64,128]{...) custom-call(bf16[528,128]{1,0:T(8,128)(2,1)S(1)} %get-tuple-element., ...), custom_call_target="tpu_custom_call" | custom-call | flops 6000000000 | tf_op jit(solution)/shard_map/key_stage/pallas_call | solution.py:196
  29.4 1.6 %collective-permute-start.4 = (f32[128,128]{1,0:T(8,128)S(1)}, f32[128,128]{1,0:T(8,128)S(1)}, u32[]{:S(2)}, u32[]{:S(2)}) collective-permute-start(f32[128,128]{1,0:T(8,128)S(1)} %get-tuple-element.49), channel_id=1, source_target_pairs={{0,8},{8,0},{16,24},{24,16},{1,9},{9,1},{17,25},{25,17},{2,10},{10... | collective-permute-start | bytes 196616 | tf_op jit(solution)/shard_map/ppermute | solution.py:594
  31.0 1.5 %collective-permute-start.5 = (f32[128,128]{1,0:T(8,128)S(1)}, f32[128,128]{1,0:T(8,128)S(1)}, u32[]{:S(2)}, u32[]{:S(2)}) collective-permute-start(f32[128,128]{1,0:T(8,128)S(1)} %get-tuple-element.50), channel_id=1, source_target_pairs={{0,16},{8,24},{16,0},{24,8},{1,17},{9,25},{17,1},{25,9},{2,18},{10... | collective-permute-start | bytes 196616 | tf_op jit(solution)/shard_map/ppermute | solution.py:594
  32.5 0.5 collective-permute-start.6
  33.0 0.8 %value_stage.1 = (bf16[16,128,128]{2,1,0:T(8,128)(2,1)S(1)}, f32[16,128,128]{2,1,0:T(8,128)S(1)}, f32[128,128]{1,0:T(8,128)S(1)}, f32[128,128]{1,0:T(8,128)S(1)}...) custom-call(bf16[2,256,128]{2,1,0:T(8,128)(2,1)S(1)} %get-tuple-element.54.refs_0_, ...), custom_call_target="tpu_custom_call" | custom-call | flops 2000000000 | tf_op jit(solution)/shard_map/value_stage/pallas_call | solution.py:196
  33.8 1.6 %collective-permute-start.11 = (f32[128,128]{1,0:T(8,128)S(1)}, f32[128,128]{1,0:T(8,128)S(1)}, u32[]{:S(2)}, u32[]{:S(2)}) collective-permute-start(f32[128,128]{1,0:T(8,128)S(1)} %get-tuple-element.61), channel_id=1, source_target_pairs={{0,8},{8,0},{16,24},{24,16},{1,9},{9,1},{17,25},{25,17},{2,10},{10... | collective-permute-start | bytes 196616 | tf_op jit(solution)/shard_map/ppermute | solution.py:594
  35.3 1.6 %collective-permute-start.12 = (f32[128,128]{1,0:T(8,128)S(1)}, f32[128,128]{1,0:T(8,128)S(1)}, u32[]{:S(2)}, u32[]{:S(2)}) collective-permute-start(f32[128,128]{1,0:T(8,128)S(1)} %get-tuple-element.62), channel_id=1, source_target_pairs={{0,16},{8,24},{16,0},{24,8},{1,17},{9,25},{17,1},{25,9},{2,18},{10... | collective-permute-start | bytes 196616 | tf_op jit(solution)/shard_map/ppermute | solution.py:594
  36.9 0.4 collective-permute-start.13
  37.3 1.2 %collective-permute-start.17 = (bf16[2,128,128]{2,1,0:T(8,128)(2,1)S(1)}, bf16[2,128,128]{2,1,0:T(8,128)(2,1)S(1)}, u32[]{:S(2)}, u32[]{:S(2)}) collective-permute-start(bf16[2,128,128]{2,1,0:T(8,128)(2,1)S(1)} %get-tuple-element.69), channel_id=1, source_target_pairs={{0,1},{1,2},{2,3},{3,0},{4,5},{5,6},{6,7},{7,4},{8,9},{9,10},{10,1... | collective-permute-start | bytes 196616 | tf_op jit(solution)/shard_map/ppermute | solution.py:719
  38.5 1.3 %collective-permute-start.18 = (bf16[2,128,128]{2,1,0:T(8,128)(2,1)S(1)}, bf16[2,128,128]{2,1,0:T(8,128)(2,1)S(1)}, u32[]{:S(2)}, u32[]{:S(2)}) collective-permute-start(bf16[2,128,128]{2,1,0:T(8,128)(2,1)S(1)} %get-tuple-element.70), channel_id=1, source_target_pairs={{0,2},{1,3},{2,0},{3,1},{4,6},{5,7},{6,4},{7,5},{8,10},{9,11},{10,... | collective-permute-start | bytes 196616 | tf_op jit(solution)/shard_map/ppermute | solution.py:719
  39.8 1.8 %collective-permute-start.19 = (bf16[2,128,128]{2,1,0:T(8,128)(2,1)S(1)}, bf16[2,128,128]{2,1,0:T(8,128)(2,1)S(1)}, u32[]{:S(2)}, u32[]{:S(2)}) collective-permute-start(bf16[2,128,128]{2,1,0:T(8,128)(2,1)S(1)} %get-tuple-element.71), channel_id=1, source_target_pairs={{0,3},{1,0},{2,1},{3,2},{4,7},{5,4},{6,5},{7,6},{8,11},{9,8},{10,9... | collective-permute-start | bytes 196616 | tf_op jit(solution)/shard_map/ppermute | solution.py:719
  41.7 0.4 collective-permute-done.13.refs_7_
  42.0 0.4 scan_states.1
  42.4 0.9 %collective-permute-start.14 = (f32[128,128]{1,0:T(8,128)S(1)}, f32[128,128]{1,0:T(8,128)S(1)}, u32[]{:S(2)}, u32[]{:S(2)}) collective-permute-start(f32[128,128]{1,0:T(8,128)S(1)} %get-tuple-element.65), channel_id=1, source_target_pairs={{0,8},{8,0},{16,24},{24,16},{1,9},{9,1},{17,25},{25,17},{2,10},{10... | collective-permute-start | bytes 196616 | tf_op jit(solution)/shard_map/ppermute | solution.py:594
  43.3 1.6 %collective-permute-start.15 = (f32[128,128]{1,0:T(8,128)S(1)}, f32[128,128]{1,0:T(8,128)S(1)}, u32[]{:S(2)}, u32[]{:S(2)}) collective-permute-start(f32[128,128]{1,0:T(8,128)S(1)} %get-tuple-element.66), channel_id=1, source_target_pairs={{0,16},{8,24},{16,0},{24,8},{1,17},{9,25},{17,1},{25,9},{2,18},{10... | collective-permute-start | bytes 196616 | tf_op jit(solution)/shard_map/ppermute | solution.py:594
  44.9 1.1 %collective-permute-start.16 = (f32[128,128]{1,0:T(8,128)S(1)}, f32[128,128]{1,0:T(8,128)S(1)}, u32[]{:S(2)}, u32[]{:S(2)}) collective-permute-start(f32[128,128]{1,0:T(8,128)S(1)} %get-tuple-element.67), channel_id=1, source_target_pairs={{0,24},{8,16},{16,8},{24,0},{1,25},{9,17},{17,9},{25,1},{2,26},{10... | collective-permute-start | bytes 196616 | tf_op jit(solution)/shard_map/ppermute | solution.py:594
  46.0 2.8 %query_stage.1 = (bf16[16,64,256]{2,1,0:T(8,128)(2,1)S(1)}, f32[16,64,128]{2,1,0:T(8,128)S(1)}) custom-call(bf16[2,128,128]{2,1,0:T(8,128)(2,1)S(1)} %get-tuple-element.68.refs_0_, bf16[2,128,128]{2,1,0:T(8,128)(2,1)S(1)} %collective-permute-done.17.refs_1_, bf16[2,128,128]{2,1,0:T(8,128)(2,1)S(1)} %collective-permute-done.18.refs_2_, ...), custom_call_target="tpu_custom_call" | custom-call | flops 3000000000 | tf_op jit(solution)/shard_map/query_stage/pallas_call | solution.py:196
  48.8 1.2 %collective-permute-done.16.refs_3_ = f32[128,128]{1,0:T(8,128)S(1)} collective-permute-done((f32[128,128]{1,0:T(8,128)S(1)}, f32[128,128]{1,0:T(8,128)S(1)}, u32[]{:S(2)}, u32[]{:S(2)}) %collective-permute-start.16) | collective-permute-done | bytes 65568 | tf_op jit(solution)/shard_map/ppermute | solution.py:594
  50.1 0.5 read_states.1
  50.7 1.3 %collective-permute-done.20.other = bf16[128,512]{1,0:T(8,128)(2,1)S(1)} collective-permute-done((bf16[128,512]{1,0:T(8,128)(2,1)S(1)}, bf16[128,512]{1,0:T(8,128)(2,1)S(1)}, u32[]{:S(2)}, u32[]{:S(2)}) %collective-permute-start.20) | collective-permute-done | bytes 131104 | tf_op jit(solution)/shard_map/ppermute | solution.py:725
  52.0 0.7 %join.1 = bf16[128,1024]{1,0:T(8,128)(2,1)} custom-call(bf16[128,512]{1,0:T(8,128)(2,1)S(1)} %get-tuple-element.81.own, bf16[128,512]{1,0:T(8,128)(2,1)S(1)} %collective-permute-done.20.other), custom_call_target="tpu_custom_call" | custom-call | tf_op jit(solution)/shard_map/join/pallas_call | solution.py:196
  (24 shorter events, 0.3 us)
Async XLA Ops:
  0.0 8.6 %copy-start = (bf16[32,8192]{1,0:T(8,128)(2,1)S(1)}, bf16[32,8192]{1,0:T(8,128)(2,1)}, u32[]{:S(2)}) copy-start(bf16[32,8192]{1,0:T(8,128)(2,1)} %values.1) | copy-start | bytes 1572868
  1.6 9.6 %collective-permute-start = (bf16[528,128]{1,0:T(8,128)(2,1)S(1)}, bf16[528,128]{1,0:T(8,128)(2,1)S(1)}, u32[]{:S(2)}, u32[]{:S(2)}) collective-permute-start(bf16[528,128]{1,0:T(8,128)(2,1)S(1)} %get-tuple-element.45), channel_id=1, source_target_pairs={{0,1},{1,2},{2,3},{3,0},{4,5},{5,6},{6,7},{7,4},{8,9},{9,10},{10,1... | collective-permute-start | bytes 405512 | tf_op jit(solution)/shard_map/ppermute | solution.py:719
  4.7 11.5 %collective-permute-start.1 = (bf16[528,128]{1,0:T(8,128)(2,1)S(1)}, bf16[528,128]{1,0:T(8,128)(2,1)S(1)}, u32[]{:S(2)}, u32[]{:S(2)}) collective-permute-start(bf16[528,128]{1,0:T(8,128)(2,1)S(1)} %get-tuple-element.46), channel_id=1, source_target_pairs={{0,2},{1,3},{2,0},{3,1},{4,6},{5,7},{6,4},{7,5},{8,10},{9,11},{10,... | collective-permute-start | bytes 405512 | tf_op jit(solution)/shard_map/ppermute | solution.py:719
  7.3 8.9 %collective-permute-start.2 = (bf16[528,128]{1,0:T(8,128)(2,1)S(1)}, bf16[528,128]{1,0:T(8,128)(2,1)S(1)}, u32[]{:S(2)}, u32[]{:S(2)}) collective-permute-start(bf16[528,128]{1,0:T(8,128)(2,1)S(1)} %get-tuple-element.47), channel_id=1, source_target_pairs={{0,3},{1,0},{2,1},{3,2},{4,7},{5,4},{6,5},{7,6},{8,11},{9,8},{10,9... | collective-permute-start | bytes 405512 | tf_op jit(solution)/shard_map/ppermute | solution.py:719
  8.7 1.0 %copy-start.1 = (bf16[32,4096]{1,0:T(8,128)(2,1)S(1)}, bf16[32,4096]{1,0:T(8,128)(2,1)}, u32[]{:S(2)}) copy-start(bf16[32,4096]{1,0:T(8,128)(2,1)} %queries.1) | copy-start | bytes 786436
  9.8 6.5 %collective-permute-start.7 = (bf16[4,384,128]{2,1,0:T(8,128)(2,1)S(1)}, bf16[4,384,128]{2,1,0:T(8,128)(2,1)S(1)}, u32[]{:S(2)}, u32[]{:S(2)}) collective-permute-start(bf16[4,384,128]{2,1,0:T(8,128)(2,1)S(1)} %get-tuple-element.53), channel_id=1, source_target_pairs={{0,4},{4,0},{1,5},{5,1},{2,6},{6,2},{3,7},{7,3},{8,12},{12,8},{9,1... | collective-permute-start | bytes 1179656 | tf_op jit(solution)/shard_map/ppermute | solution.py:725
  16.2 6.0 %collective-permute-start.3 = (bf16[4,272,128]{2,1,0:T(8,128)(2,1)S(1)}, bf16[4,272,128]{2,1,0:T(8,128)(2,1)S(1)}, u32[]{:S(2)}, u32[]{:S(2)}) collective-permute-start(bf16[4,272,128]{2,1,0:T(8,128)(2,1)S(1)} %swap_keys.1), channel_id=1, source_target_pairs={{0,4},{4,0},{1,5},{5,1},{2,6},{6,2},{3,7},{7,3},{8,12},{12,8},{9,1... | collective-permute-start | bytes 835592 | tf_op jit(solution)/shard_map/ppermute | solution.py:725
  16.4 16.1 %collective-permute-start.8 = (bf16[2,256,128]{2,1,0:T(8,128)(2,1)S(1)}, bf16[2,256,128]{2,1,0:T(8,128)(2,1)S(1)}, u32[]{:S(2)}, u32[]{:S(2)}) collective-permute-start(bf16[2,256,128]{2,1,0:T(8,128)(2,1)S(1)} %get-tuple-element.55), channel_id=1, source_target_pairs={{0,1},{1,2},{2,3},{3,0},{4,5},{5,6},{6,7},{7,4},{8,9},{9,10},{10,1... | collective-permute-start | bytes 393224 | tf_op jit(solution)/shard_map/ppermute | solution.py:719
  19.8 13.1 %collective-permute-start.9 = (bf16[2,256,128]{2,1,0:T(8,128)(2,1)S(1)}, bf16[2,256,128]{2,1,0:T(8,128)(2,1)S(1)}, u32[]{:S(2)}, u32[]{:S(2)}) collective-permute-start(bf16[2,256,128]{2,1,0:T(8,128)(2,1)S(1)} %get-tuple-element.56), channel_id=1, source_target_pairs={{0,2},{1,3},{2,0},{3,1},{4,6},{5,7},{6,4},{7,5},{8,10},{9,11},{10,... | collective-permute-start | bytes 393224 | tf_op jit(solution)/shard_map/ppermute | solution.py:719
  21.4 11.5 %collective-permute-start.10 = (bf16[2,256,128]{2,1,0:T(8,128)(2,1)S(1)}, bf16[2,256,128]{2,1,0:T(8,128)(2,1)S(1)}, u32[]{:S(2)}, u32[]{:S(2)}) collective-permute-start(bf16[2,256,128]{2,1,0:T(8,128)(2,1)S(1)} %get-tuple-element.57), channel_id=1, source_target_pairs={{0,3},{1,0},{2,1},{3,2},{4,7},{5,4},{6,5},{7,6},{8,11},{9,8},{10,9... | collective-permute-start | bytes 393224 | tf_op jit(solution)/shard_map/ppermute | solution.py:719
  29.4 7.5 %collective-permute-start.4 = (f32[128,128]{1,0:T(8,128)S(1)}, f32[128,128]{1,0:T(8,128)S(1)}, u32[]{:S(2)}, u32[]{:S(2)}) collective-permute-start(f32[128,128]{1,0:T(8,128)S(1)} %get-tuple-element.49), channel_id=1, source_target_pairs={{0,8},{8,0},{16,24},{24,16},{1,9},{9,1},{17,25},{25,17},{2,10},{10... | collective-permute-start | bytes 196616 | tf_op jit(solution)/shard_map/ppermute | solution.py:594
  31.0 6.4 %collective-permute-start.5 = (f32[128,128]{1,0:T(8,128)S(1)}, f32[128,128]{1,0:T(8,128)S(1)}, u32[]{:S(2)}, u32[]{:S(2)}) collective-permute-start(f32[128,128]{1,0:T(8,128)S(1)} %get-tuple-element.50), channel_id=1, source_target_pairs={{0,16},{8,24},{16,0},{24,8},{1,17},{9,25},{17,1},{25,9},{2,18},{10... | collective-permute-start | bytes 196616 | tf_op jit(solution)/shard_map/ppermute | solution.py:594
  32.5 6.1 %collective-permute-start.6 = (f32[128,128]{1,0:T(8,128)S(1)}, f32[128,128]{1,0:T(8,128)S(1)}, u32[]{:S(2)}, u32[]{:S(2)}) collective-permute-start(f32[128,128]{1,0:T(8,128)S(1)} %get-tuple-element.51), channel_id=1, source_target_pairs={{0,24},{8,16},{16,8},{24,0},{1,25},{9,17},{17,9},{25,1},{2,26},{10... | collective-permute-start | bytes 196616 | tf_op jit(solution)/shard_map/ppermute | solution.py:594
  33.8 6.1 %collective-permute-start.11 = (f32[128,128]{1,0:T(8,128)S(1)}, f32[128,128]{1,0:T(8,128)S(1)}, u32[]{:S(2)}, u32[]{:S(2)}) collective-permute-start(f32[128,128]{1,0:T(8,128)S(1)} %get-tuple-element.61), channel_id=1, source_target_pairs={{0,8},{8,0},{16,24},{24,16},{1,9},{9,1},{17,25},{25,17},{2,10},{10... | collective-permute-start | bytes 196616 | tf_op jit(solution)/shard_map/ppermute | solution.py:594
  35.3 6.3 %collective-permute-start.12 = (f32[128,128]{1,0:T(8,128)S(1)}, f32[128,128]{1,0:T(8,128)S(1)}, u32[]{:S(2)}, u32[]{:S(2)}) collective-permute-start(f32[128,128]{1,0:T(8,128)S(1)} %get-tuple-element.62), channel_id=1, source_target_pairs={{0,16},{8,24},{16,0},{24,8},{1,17},{9,25},{17,1},{25,9},{2,18},{10... | collective-permute-start | bytes 196616 | tf_op jit(solution)/shard_map/ppermute | solution.py:594
  36.9 5.2 %collective-permute-start.13 = (f32[128,128]{1,0:T(8,128)S(1)}, f32[128,128]{1,0:T(8,128)S(1)}, u32[]{:S(2)}, u32[]{:S(2)}) collective-permute-start(f32[128,128]{1,0:T(8,128)S(1)} %get-tuple-element.63), channel_id=1, source_target_pairs={{0,24},{8,16},{16,8},{24,0},{1,25},{9,17},{17,9},{25,1},{2,26},{10... | collective-permute-start | bytes 196616 | tf_op jit(solution)/shard_map/ppermute | solution.py:594
  37.3 7.6 %collective-permute-start.17 = (bf16[2,128,128]{2,1,0:T(8,128)(2,1)S(1)}, bf16[2,128,128]{2,1,0:T(8,128)(2,1)S(1)}, u32[]{:S(2)}, u32[]{:S(2)}) collective-permute-start(bf16[2,128,128]{2,1,0:T(8,128)(2,1)S(1)} %get-tuple-element.69), channel_id=1, source_target_pairs={{0,1},{1,2},{2,3},{3,0},{4,5},{5,6},{6,7},{7,4},{8,9},{9,10},{10,1... | collective-permute-start | bytes 196616 | tf_op jit(solution)/shard_map/ppermute | solution.py:719
  38.5 7.4 %collective-permute-start.18 = (bf16[2,128,128]{2,1,0:T(8,128)(2,1)S(1)}, bf16[2,128,128]{2,1,0:T(8,128)(2,1)S(1)}, u32[]{:S(2)}, u32[]{:S(2)}) collective-permute-start(bf16[2,128,128]{2,1,0:T(8,128)(2,1)S(1)} %get-tuple-element.70), channel_id=1, source_target_pairs={{0,2},{1,3},{2,0},{3,1},{4,6},{5,7},{6,4},{7,5},{8,10},{9,11},{10,... | collective-permute-start | bytes 196616 | tf_op jit(solution)/shard_map/ppermute | solution.py:719
  39.8 6.1 %collective-permute-start.19 = (bf16[2,128,128]{2,1,0:T(8,128)(2,1)S(1)}, bf16[2,128,128]{2,1,0:T(8,128)(2,1)S(1)}, u32[]{:S(2)}, u32[]{:S(2)}) collective-permute-start(bf16[2,128,128]{2,1,0:T(8,128)(2,1)S(1)} %get-tuple-element.71), channel_id=1, source_target_pairs={{0,3},{1,0},{2,1},{3,2},{4,7},{5,4},{6,5},{7,6},{8,11},{9,8},{10,9... | collective-permute-start | bytes 196616 | tf_op jit(solution)/shard_map/ppermute | solution.py:719
  42.4 6.4 %collective-permute-start.14 = (f32[128,128]{1,0:T(8,128)S(1)}, f32[128,128]{1,0:T(8,128)S(1)}, u32[]{:S(2)}, u32[]{:S(2)}) collective-permute-start(f32[128,128]{1,0:T(8,128)S(1)} %get-tuple-element.65), channel_id=1, source_target_pairs={{0,8},{8,0},{16,24},{24,16},{1,9},{9,1},{17,25},{25,17},{2,10},{10... | collective-permute-start | bytes 196616 | tf_op jit(solution)/shard_map/ppermute | solution.py:594
  43.3 5.5 %collective-permute-start.15 = (f32[128,128]{1,0:T(8,128)S(1)}, f32[128,128]{1,0:T(8,128)S(1)}, u32[]{:S(2)}, u32[]{:S(2)}) collective-permute-start(f32[128,128]{1,0:T(8,128)S(1)} %get-tuple-element.66), channel_id=1, source_target_pairs={{0,16},{8,24},{16,0},{24,8},{1,17},{9,25},{17,1},{25,9},{2,18},{10... | collective-permute-start | bytes 196616 | tf_op jit(solution)/shard_map/ppermute | solution.py:594
  44.9 5.2 %collective-permute-start.16 = (f32[128,128]{1,0:T(8,128)S(1)}, f32[128,128]{1,0:T(8,128)S(1)}, u32[]{:S(2)}, u32[]{:S(2)}) collective-permute-start(f32[128,128]{1,0:T(8,128)S(1)} %get-tuple-element.67), channel_id=1, source_target_pairs={{0,24},{8,16},{16,8},{24,0},{1,25},{9,17},{17,9},{25,1},{2,26},{10... | collective-permute-start | bytes 196616 | tf_op jit(solution)/shard_map/ppermute | solution.py:594
  50.6 1.4 %collective-permute-start.20 = (bf16[128,512]{1,0:T(8,128)(2,1)S(1)}, bf16[128,512]{1,0:T(8,128)(2,1)S(1)}, u32[]{:S(2)}, u32[]{:S(2)}) collective-permute-start(bf16[128,512]{1,0:T(8,128)(2,1)S(1)} %get-tuple-element.82), channel_id=1, source_target_pairs={{0,4},{4,0},{1,5},{5,1},{2,6},{6,2},{3,7},{7,3},{8,12},{12,8},{9,1... | collective-permute-start | bytes 393224 | tf_op jit(solution)/shard_map/ppermute | solution.py:725

commit v8 on v7

--- a/solution.py
+++ b/solution.py
@@ -190,18 +190,24 @@
     )
 
 
-def call(kernel, outs, *args, scratch=(), flops=0, far=0, name=None):
+def call(kernel, outs, *args, scratch=(), flops=0, far=0, after=(), name=None):
+    count = len(args)
+
+    def body(*refs):
+        kernel(*refs[:count], *refs[count + len(after) :])
+
     specs = [pl.BlockSpec(memory_space=pltpu.HBM)] * far
-    specs += [pl.BlockSpec(memory_space=pltpu.VMEM)] * (len(args) - far)
+    specs += [pl.BlockSpec(memory_space=pltpu.VMEM)] * (count - far)
+    specs += [pl.BlockSpec(memory_space=pl.ANY)] * len(after)
     return pl.pallas_call(
-        kernel,
+        body,
         out_shape=outs,
         in_specs=specs,
         scratch_shapes=scratch,
         compiler_params=pltpu.CompilerParams(vmem_limit_bytes=24 * 2**20),
         cost_estimate=pl.CostEstimate(flops=flops, bytes_accessed=0, transcendentals=0),
         name=name,
-    )(*args)
+    )(*args, *after)
 
 
 def shape(*sizes, dtype=BF16):
@@ -210,6 +216,18 @@
 
 def axis_index(axis):
     return lax.axis_index(axis).astype(jnp.int32)
+
+
+def held(value, after):
+    return pl.pallas_call(
+        lambda *refs: None,
+        out_shape=shape(*value.shape, dtype=value.dtype),
+        in_specs=[pl.BlockSpec(memory_space=pl.ANY)] * (1 + len(after)),
+        out_specs=pl.BlockSpec(memory_space=pl.ANY),
+        input_output_aliases={0: 0},
+        compiler_params=pltpu.CompilerParams(vmem_limit_bytes=2**20),
+        name="held",
+    )(value, *after)
 
 
 class Sizes:
@@ -328,7 +346,11 @@
                     out[ahead, number * TOK : (number + 1) * TOK, :] = piece
 
     return call(
-        kernel, [shape(sizes.groups, rows, DK)] * 2, values, queries, name="pack_reads"
+        kernel,
+        [shape(sizes.groups, rows, DK)] * 2,
+        values,
+        queries,
+        name="pack_reads",
     )
 
 
@@ -726,6 +748,7 @@
 
     arrived = spread(pack_keys(sizes, keys, betas, log_gates, starts.reshape(1, -1)))
     kept, sent = pack_reads(sizes, values, queries)
+    sent = held(sent, after=arrived[1:])
     value_parts, query_parts = merge_reads(sizes, kept, swapped(sent))
     value_parts = spread(value_parts)
     query_parts = spread(query_parts)

time: 52.9 us -> 54.5 us (1.030)
  waiting for transfers between devices: 9.3 us -> 10.2 us
  starting transfers between devices: 28.1 us -> 28.8 us
    ppermute x3, waiting for transfers between devices: 1.34 us -> 2.45 us  [swapped(): return lax.ppermute(part, 'core', [(0, 1), (1, 0)])]
    pallas_call x10 -> x11, Pallas kernels: 14.3 us -> 14.3 us  [the longest x10 14.3 us: call(): pl.pallas_call(body, out_shape=outs, in_specs=specs, scratch_shapes=scrat...]
  transfers between devices with their start and end apart: 21 -> 21, of which waited for: 5 -> 6; matrix products, arithmetic and copies ran while one was open for 0% -> 0% of each run, Pallas kernels for 22% -> 21%
where the time goes in v8:
time: 54.5 us; the launch traced here: 54.3 us
  starting transfers between devices  28.8 us (53%)
  Pallas kernels  14.3 us (26%)
  waiting for transfers between devices  10.2 us (19%)
  local copies, waits for them, and re-layouts  0.95 us (2%)
    ppermute x9, starting transfers between devices, spread(): lax.ppermute(part, 'head', [(z, (z + ahead) % groups) for z in range(grou...  17.5 us
    pallas_call x10, Pallas kernels, call(): pl.pallas_call(body, out_shape=outs, in_specs=specs, scratch_shapes=scrat...  14.3 us
    ppermute x9, starting transfers between devices, exchanged(): lax.ppermute(part, 'chip', [(chip, chip ^ number) for chip in range(sizes...  10.7 us
    ppermute x9, waiting for transfers between devices, spread(): lax.ppermute(part, 'head', [(z, (z + ahead) % groups) for z in range(grou...  6.41 us
    ppermute x3, waiting for transfers between devices, swapped(): return lax.ppermute(part, 'core', [(0, 1), (1, 0)])  2.45 us
    ppermute x9, waiting for transfers between devices, exchanged(): lax.ppermute(part, 'chip', [(chip, chip ^ number) for chip in range(sizes...  1.3 us
  transfers between devices with their start and end apart: 21, of which 6 were waited for; matrix products, arithmetic and copies ran while one was open for 0% of the time, Pallas kernels for 21%

profile of v8, /device:TPU:0, one launch (start us, length us, event | category | flops | bytes accessed | tf_op | source)
XLA Modules:
  0.0 54.3 jit_solution(9705001770902563018)
XLA Ops:
  0.0 1.6 %pack_keys.1 = (bf16[528,128]{1,0:T(8,128)(2,1)S(1)}, bf16[528,128]{1,0:T(8,128)(2,1)S(1)}, bf16[528,128]{1,0:T(8,128)(2,1)S(1)}, bf16[528,128]{1,0:T(8,128)(2,1)S(1)}) custom-call(bf16[32,8192]{1,0:T(8,128)(2,1)} %refs_0_.2, bf16[32,64]{1,0:T(8,128)(2,1)} %refs_1_.2, bf16[32,32]{1,0:T(8,128)(2,1)} %refs_2_.1, s32[1,128]{1,0:T(1,128)} %bitcast.1), custom_call_target="tpu_custom_call" | custom-call | tf_op jit(solution)/shard_map/pack_keys/pallas_call | solution.py:202
  1.6 3.1 %collective-permute-start = (bf16[528,128]{1,0:T(8,128)(2,1)S(1)}, bf16[528,128]{1,0:T(8,128)(2,1)S(1)}, u32[]{:S(2)}, u32[]{:S(2)}) collective-permute-start(bf16[528,128]{1,0:T(8,128)(2,1)S(1)} %get-tuple-element.45), channel_id=1, source_target_pairs={{0,1},{1,2},{2,3},{3,0},{4,5},{5,6},{6,7},{7,4},{8,9},{9,10},{10,1... | collective-permute-start | bytes 405512 | tf_op jit(solution)/shard_map/ppermute | solution.py:741
  4.7 2.6 %collective-permute-start.1 = (bf16[528,128]{1,0:T(8,128)(2,1)S(1)}, bf16[528,128]{1,0:T(8,128)(2,1)S(1)}, u32[]{:S(2)}, u32[]{:S(2)}) collective-permute-start(bf16[528,128]{1,0:T(8,128)(2,1)S(1)} %get-tuple-element.46), channel_id=1, source_target_pairs={{0,2},{1,3},{2,0},{3,1},{4,6},{5,7},{6,4},{7,5},{8,10},{9,11},{10,... | collective-permute-start | bytes 405512 | tf_op jit(solution)/shard_map/ppermute | solution.py:741
  7.3 1.3 %collective-permute-start.2 = (bf16[528,128]{1,0:T(8,128)(2,1)S(1)}, bf16[528,128]{1,0:T(8,128)(2,1)S(1)}, u32[]{:S(2)}, u32[]{:S(2)}) collective-permute-start(bf16[528,128]{1,0:T(8,128)(2,1)S(1)} %get-tuple-element.47), channel_id=1, source_target_pairs={{0,3},{1,0},{2,1},{3,2},{4,7},{5,4},{6,5},{7,6},{8,11},{9,8},{10,9... | collective-permute-start | bytes 405512 | tf_op jit(solution)/shard_map/ppermute | solution.py:741
  8.7 0.9 %copy-done.1 = bf16[32,4096]{1,0:T(8,128)(2,1)S(1)} copy-done((bf16[32,4096]{1,0:T(8,128)(2,1)S(1)}, bf16[32,4096]{1,0:T(8,128)(2,1)}, u32[]{:S(2)}) %copy-start.1) | copy-done | bytes 262168
  9.8 1.4 %collective-permute-done.refs_1_ = bf16[528,128]{1,0:T(8,128)(2,1)S(1)} collective-permute-done((bf16[528,128]{1,0:T(8,128)(2,1)S(1)}, bf16[528,128]{1,0:T(8,128)(2,1)S(1)}, u32[]{:S(2)}, u32[]{:S(2)}) %collective-permute-start) | collective-permute-done | bytes 135200 | tf_op jit(solution)/shard_map/ppermute | solution.py:741
  11.2 5.0 %collective-permute-done.1.refs_2_ = bf16[528,128]{1,0:T(8,128)(2,1)S(1)} collective-permute-done((bf16[528,128]{1,0:T(8,128)(2,1)S(1)}, bf16[528,128]{1,0:T(8,128)(2,1)S(1)}, u32[]{:S(2)}, u32[]{:S(2)}) %collective-permute-start.1) | collective-permute-done | bytes 135200 | tf_op jit(solution)/shard_map/ppermute | solution.py:741
  16.2 0.6 %collective-permute-start.3 = (bf16[4,272,128]{2,1,0:T(8,128)(2,1)S(1)}, bf16[4,272,128]{2,1,0:T(8,128)(2,1)S(1)}, u32[]{:S(2)}, u32[]{:S(2)}) collective-permute-start(bf16[4,272,128]{2,1,0:T(8,128)(2,1)S(1)} %swap_keys.1), channel_id=1, source_target_pairs={{0,4},{4,0},{1,5},{5,1},{2,6},{6,2},{3,7},{7,3},{8,12},{12,8},{9,1... | collective-permute-start | bytes 835592 | tf_op jit(solution)/shard_map/ppermute | solution.py:747
  16.8 1.1 %collective-permute-done.7.refs_1_ = bf16[4,384,128]{2,1,0:T(8,128)(2,1)S(1)} collective-permute-done((bf16[4,384,128]{2,1,0:T(8,128)(2,1)S(1)}, bf16[4,384,128]{2,1,0:T(8,128)(2,1)S(1)}, u32[]{:S(2)}, u32[]{:S(2)}) %collective-permute-start.7) | collective-permute-done | bytes 393248 | tf_op jit(solution)/shard_map/ppermute | solution.py:747
  18.0 3.4 %collective-permute-start.8 = (bf16[2,256,128]{2,1,0:T(8,128)(2,1)S(1)}, bf16[2,256,128]{2,1,0:T(8,128)(2,1)S(1)}, u32[]{:S(2)}, u32[]{:S(2)}) collective-permute-start(bf16[2,256,128]{2,1,0:T(8,128)(2,1)S(1)} %get-tuple-element.55), channel_id=1, source_target_pairs={{0,1},{1,2},{2,3},{3,0},{4,5},{5,6},{6,7},{7,4},{8,9},{9,10},{10,1... | collective-permute-start | bytes 393224 | tf_op jit(solution)/shard_map/ppermute | solution.py:741
  21.4 1.6 %collective-permute-start.9 = (bf16[2,256,128]{2,1,0:T(8,128)(2,1)S(1)}, bf16[2,256,128]{2,1,0:T(8,128)(2,1)S(1)}, u32[]{:S(2)}, u32[]{:S(2)}) collective-permute-start(bf16[2,256,128]{2,1,0:T(8,128)(2,1)S(1)} %get-tuple-element.56), channel_id=1, source_target_pairs={{0,2},{1,3},{2,0},{3,1},{4,6},{5,7},{6,4},{7,5},{8,10},{9,11},{10,... | collective-permute-start | bytes 393224 | tf_op jit(solution)/shard_map/ppermute | solution.py:741
  23.0 0.8 %collective-permute-start.10 = (bf16[2,256,128]{2,1,0:T(8,128)(2,1)S(1)}, bf16[2,256,128]{2,1,0:T(8,128)(2,1)S(1)}, u32[]{:S(2)}, u32[]{:S(2)}) collective-permute-start(bf16[2,256,128]{2,1,0:T(8,128)(2,1)S(1)} %get-tuple-element.57), channel_id=1, source_target_pairs={{0,3},{1,0},{2,1},{3,2},{4,7},{5,4},{6,5},{7,6},{8,11},{9,8},{10,9... | collective-permute-start | bytes 393224 | tf_op jit(solution)/shard_map/ppermute | solution.py:741
  23.8 7.1 %key_stage.1 = (bf16[16,128,128]{2,1,0:T(8,128)(2,1)S(1)}, bf16[16,128,256]{2,1,0:T(8,128)(2,1)S(1)}, bf16[16,128,256]{2,1,0:T(8,128)(2,1)S(1)}, f32[16,64,128]{...) custom-call(bf16[528,128]{1,0:T(8,128)(2,1)S(1)} %get-tuple-element., ...), custom_call_target="tpu_custom_call" | custom-call | flops 6000000000 | tf_op jit(solution)/shard_map/key_stage/pallas_call | solution.py:202
  31.0 1.6 %collective-permute-start.4 = (f32[128,128]{1,0:T(8,128)S(1)}, f32[128,128]{1,0:T(8,128)S(1)}, u32[]{:S(2)}, u32[]{:S(2)}) collective-permute-start(f32[128,128]{1,0:T(8,128)S(1)} %get-tuple-element.49), channel_id=1, source_target_pairs={{0,8},{8,0},{16,24},{24,16},{1,9},{9,1},{17,25},{25,17},{2,10},{10... | collective-permute-start | bytes 196616 | tf_op jit(solution)/shard_map/ppermute | solution.py:616
  32.6 1.5 %collective-permute-start.5 = (f32[128,128]{1,0:T(8,128)S(1)}, f32[128,128]{1,0:T(8,128)S(1)}, u32[]{:S(2)}, u32[]{:S(2)}) collective-permute-start(f32[128,128]{1,0:T(8,128)S(1)} %get-tuple-element.50), channel_id=1, source_target_pairs={{0,16},{8,24},{16,0},{24,8},{1,17},{9,25},{17,1},{25,9},{2,18},{10... | collective-permute-start | bytes 196616 | tf_op jit(solution)/shard_map/ppermute | solution.py:616
  34.1 0.5 collective-permute-start.6
  34.6 0.8 %value_stage.1 = (bf16[16,128,128]{2,1,0:T(8,128)(2,1)S(1)}, f32[16,128,128]{2,1,0:T(8,128)S(1)}, f32[128,128]{1,0:T(8,128)S(1)}, f32[128,128]{1,0:T(8,128)S(1)}...) custom-call(bf16[2,256,128]{2,1,0:T(8,128)(2,1)S(1)} %get-tuple-element.54.refs_0_, ...), custom_call_target="tpu_custom_call" | custom-call | flops 2000000000 | tf_op jit(solution)/shard_map/value_stage/pallas_call | solution.py:202
  35.4 1.6 %collective-permute-start.11 = (f32[128,128]{1,0:T(8,128)S(1)}, f32[128,128]{1,0:T(8,128)S(1)}, u32[]{:S(2)}, u32[]{:S(2)}) collective-permute-start(f32[128,128]{1,0:T(8,128)S(1)} %get-tuple-element.61), channel_id=1, source_target_pairs={{0,8},{8,0},{16,24},{24,16},{1,9},{9,1},{17,25},{25,17},{2,10},{10... | collective-permute-start | bytes 196616 | tf_op jit(solution)/shard_map/ppermute | solution.py:616
  36.9 1.6 %collective-permute-start.12 = (f32[128,128]{1,0:T(8,128)S(1)}, f32[128,128]{1,0:T(8,128)S(1)}, u32[]{:S(2)}, u32[]{:S(2)}) collective-permute-start(f32[128,128]{1,0:T(8,128)S(1)} %get-tuple-element.62), channel_id=1, source_target_pairs={{0,16},{8,24},{16,0},{24,8},{1,17},{9,25},{17,1},{25,9},{2,18},{10... | collective-permute-start | bytes 196616 | tf_op jit(solution)/shard_map/ppermute | solution.py:616
  38.5 0.4 collective-permute-start.13
  38.9 1.2 %collective-permute-start.17 = (bf16[2,128,128]{2,1,0:T(8,128)(2,1)S(1)}, bf16[2,128,128]{2,1,0:T(8,128)(2,1)S(1)}, u32[]{:S(2)}, u32[]{:S(2)}) collective-permute-start(bf16[2,128,128]{2,1,0:T(8,128)(2,1)S(1)} %get-tuple-element.69), channel_id=1, source_target_pairs={{0,1},{1,2},{2,3},{3,0},{4,5},{5,6},{6,7},{7,4},{8,9},{9,10},{10,1... | collective-permute-start | bytes 196616 | tf_op jit(solution)/shard_map/ppermute | solution.py:741
  40.1 1.3 %collective-permute-start.18 = (bf16[2,128,128]{2,1,0:T(8,128)(2,1)S(1)}, bf16[2,128,128]{2,1,0:T(8,128)(2,1)S(1)}, u32[]{:S(2)}, u32[]{:S(2)}) collective-permute-start(bf16[2,128,128]{2,1,0:T(8,128)(2,1)S(1)} %get-tuple-element.70), channel_id=1, source_target_pairs={{0,2},{1,3},{2,0},{3,1},{4,6},{5,7},{6,4},{7,5},{8,10},{9,11},{10,... | collective-permute-start | bytes 196616 | tf_op jit(solution)/shard_map/ppermute | solution.py:741
  41.4 2.1 %collective-permute-start.19 = (bf16[2,128,128]{2,1,0:T(8,128)(2,1)S(1)}, bf16[2,128,128]{2,1,0:T(8,128)(2,1)S(1)}, u32[]{:S(2)}, u32[]{:S(2)}) collective-permute-start(bf16[2,128,128]{2,1,0:T(8,128)(2,1)S(1)} %get-tuple-element.71), channel_id=1, source_target_pairs={{0,3},{1,0},{2,1},{3,2},{4,7},{5,4},{6,5},{7,6},{8,11},{9,8},{10,9... | collective-permute-start | bytes 196616 | tf_op jit(solution)/shard_map/ppermute | solution.py:741
  43.6 0.4 scan_states.1
  44.0 0.9 %collective-permute-start.14 = (f32[128,128]{1,0:T(8,128)S(1)}, f32[128,128]{1,0:T(8,128)S(1)}, u32[]{:S(2)}, u32[]{:S(2)}) collective-permute-start(f32[128,128]{1,0:T(8,128)S(1)} %get-tuple-element.65), channel_id=1, source_target_pairs={{0,8},{8,0},{16,24},{24,16},{1,9},{9,1},{17,25},{25,17},{2,10},{10... | collective-permute-start | bytes 196616 | tf_op jit(solution)/shard_map/ppermute | solution.py:616
  44.9 1.6 %collective-permute-start.15 = (f32[128,128]{1,0:T(8,128)S(1)}, f32[128,128]{1,0:T(8,128)S(1)}, u32[]{:S(2)}, u32[]{:S(2)}) collective-permute-start(f32[128,128]{1,0:T(8,128)S(1)} %get-tuple-element.66), channel_id=1, source_target_pairs={{0,16},{8,24},{16,0},{24,8},{1,17},{9,25},{17,1},{25,9},{2,18},{10... | collective-permute-start | bytes 196616 | tf_op jit(solution)/shard_map/ppermute | solution.py:616
  46.5 1.1 %collective-permute-start.16 = (f32[128,128]{1,0:T(8,128)S(1)}, f32[128,128]{1,0:T(8,128)S(1)}, u32[]{:S(2)}, u32[]{:S(2)}) collective-permute-start(f32[128,128]{1,0:T(8,128)S(1)} %get-tuple-element.67), channel_id=1, source_target_pairs={{0,24},{8,16},{16,8},{24,0},{1,25},{9,17},{17,9},{25,1},{2,26},{10... | collective-permute-start | bytes 196616 | tf_op jit(solution)/shard_map/ppermute | solution.py:616
  47.6 2.8 %query_stage.1 = (bf16[16,64,256]{2,1,0:T(8,128)(2,1)S(1)}, f32[16,64,128]{2,1,0:T(8,128)S(1)}) custom-call(bf16[2,128,128]{2,1,0:T(8,128)(2,1)S(1)} %get-tuple-element.68.refs_0_, bf16[2,128,128]{2,1,0:T(8,128)(2,1)S(1)} %collective-permute-done.17.refs_1_, bf16[2,128,128]{2,1,0:T(8,128)(2,1)S(1)} %collective-permute-done.18.refs_2_, ...), custom_call_target="tpu_custom_call" | custom-call | flops 3000000000 | tf_op jit(solution)/shard_map/query_stage/pallas_call | solution.py:202
  50.4 1.2 %collective-permute-done.16.refs_3_ = f32[128,128]{1,0:T(8,128)S(1)} collective-permute-done((f32[128,128]{1,0:T(8,128)S(1)}, f32[128,128]{1,0:T(8,128)S(1)}, u32[]{:S(2)}, u32[]{:S(2)}) %collective-permute-start.16) | collective-permute-done | bytes 65568 | tf_op jit(solution)/shard_map/ppermute | solution.py:616
  51.7 0.5 read_states.1
  52.3 1.3 %collective-permute-done.20.refs_1_ = bf16[128,512]{1,0:T(8,128)(2,1)S(1)} collective-permute-done((bf16[128,512]{1,0:T(8,128)(2,1)S(1)}, bf16[128,512]{1,0:T(8,128)(2,1)S(1)}, u32[]{:S(2)}, u32[]{:S(2)}) %collective-permute-start.20) | collective-permute-done | bytes 131104 | tf_op jit(solution)/shard_map/ppermute | solution.py:747
  53.6 0.7 %join.1 = bf16[128,1024]{1,0:T(8,128)(2,1)} custom-call(bf16[128,512]{1,0:T(8,128)(2,1)S(1)} %get-tuple-element.81.refs_0_, bf16[128,512]{1,0:T(8,128)(2,1)S(1)} %collective-permute-done.20.refs_1_), custom_call_target="tpu_custom_call" | custom-call | tf_op jit(solution)/shard_map/join/pallas_call | solution.py:202
  (25 shorter events, 0.5 us)
Async XLA Ops:
  0.0 8.6 %copy-start = (bf16[32,8192]{1,0:T(8,128)(2,1)S(1)}, bf16[32,8192]{1,0:T(8,128)(2,1)}, u32[]{:S(2)}) copy-start(bf16[32,8192]{1,0:T(8,128)(2,1)} %refs_0_.3) | copy-start | bytes 1572868
  1.6 9.6 %collective-permute-start = (bf16[528,128]{1,0:T(8,128)(2,1)S(1)}, bf16[528,128]{1,0:T(8,128)(2,1)S(1)}, u32[]{:S(2)}, u32[]{:S(2)}) collective-permute-start(bf16[528,128]{1,0:T(8,128)(2,1)S(1)} %get-tuple-element.45), channel_id=1, source_target_pairs={{0,1},{1,2},{2,3},{3,0},{4,5},{5,6},{6,7},{7,4},{8,9},{9,10},{10,1... | collective-permute-start | bytes 405512 | tf_op jit(solution)/shard_map/ppermute | solution.py:741
  4.7 11.5 %collective-permute-start.1 = (bf16[528,128]{1,0:T(8,128)(2,1)S(1)}, bf16[528,128]{1,0:T(8,128)(2,1)S(1)}, u32[]{:S(2)}, u32[]{:S(2)}) collective-permute-start(bf16[528,128]{1,0:T(8,128)(2,1)S(1)} %get-tuple-element.46), channel_id=1, source_target_pairs={{0,2},{1,3},{2,0},{3,1},{4,6},{5,7},{6,4},{7,5},{8,10},{9,11},{10,... | collective-permute-start | bytes 405512 | tf_op jit(solution)/shard_map/ppermute | solution.py:741
  7.3 8.9 %collective-permute-start.2 = (bf16[528,128]{1,0:T(8,128)(2,1)S(1)}, bf16[528,128]{1,0:T(8,128)(2,1)S(1)}, u32[]{:S(2)}, u32[]{:S(2)}) collective-permute-start(bf16[528,128]{1,0:T(8,128)(2,1)S(1)} %get-tuple-element.47), channel_id=1, source_target_pairs={{0,3},{1,0},{2,1},{3,2},{4,7},{5,4},{6,5},{7,6},{8,11},{9,8},{10,9... | collective-permute-start | bytes 405512 | tf_op jit(solution)/shard_map/ppermute | solution.py:741
  8.7 1.0 %copy-start.1 = (bf16[32,4096]{1,0:T(8,128)(2,1)S(1)}, bf16[32,4096]{1,0:T(8,128)(2,1)}, u32[]{:S(2)}) copy-start(bf16[32,4096]{1,0:T(8,128)(2,1)} %refs_1_.3) | copy-start | bytes 786436
  16.2 1.7 %collective-permute-start.7 = (bf16[4,384,128]{2,1,0:T(8,128)(2,1)S(1)}, bf16[4,384,128]{2,1,0:T(8,128)(2,1)S(1)}, u32[]{:S(2)}, u32[]{:S(2)}) collective-permute-start(bf16[4,384,128]{2,1,0:T(8,128)(2,1)S(1)} %held.1), channel_id=1, source_target_pairs={{0,4},{4,0},{1,5},{5,1},{2,6},{6,2},{3,7},{7,3},{8,12},{12,8},{9,1... | collective-permute-start | bytes 1179656 | tf_op jit(solution)/shard_map/ppermute | solution.py:747
  16.2 7.6 %collective-permute-start.3 = (bf16[4,272,128]{2,1,0:T(8,128)(2,1)S(1)}, bf16[4,272,128]{2,1,0:T(8,128)(2,1)S(1)}, u32[]{:S(2)}, u32[]{:S(2)}) collective-permute-start(bf16[4,272,128]{2,1,0:T(8,128)(2,1)S(1)} %swap_keys.1), channel_id=1, source_target_pairs={{0,4},{4,0},{1,5},{5,1},{2,6},{6,2},{3,7},{7,3},{8,12},{12,8},{9,1... | collective-permute-start | bytes 835592 | tf_op jit(solution)/shard_map/ppermute | solution.py:747
  18.0 16.1 %collective-permute-start.8 = (bf16[2,256,128]{2,1,0:T(8,128)(2,1)S(1)}, bf16[2,256,128]{2,1,0:T(8,128)(2,1)S(1)}, u32[]{:S(2)}, u32[]{:S(2)}) collective-permute-start(bf16[2,256,128]{2,1,0:T(8,128)(2,1)S(1)} %get-tuple-element.55), channel_id=1, source_target_pairs={{0,1},{1,2},{2,3},{3,0},{4,5},{5,6},{6,7},{7,4},{8,9},{9,10},{10,1... | collective-permute-start | bytes 393224 | tf_op jit(solution)/shard_map/ppermute | solution.py:741
  21.4 13.2 %collective-permute-start.9 = (bf16[2,256,128]{2,1,0:T(8,128)(2,1)S(1)}, bf16[2,256,128]{2,1,0:T(8,128)(2,1)S(1)}, u32[]{:S(2)}, u32[]{:S(2)}) collective-permute-start(bf16[2,256,128]{2,1,0:T(8,128)(2,1)S(1)} %get-tuple-element.56), channel_id=1, source_target_pairs={{0,2},{1,3},{2,0},{3,1},{4,6},{5,7},{6,4},{7,5},{8,10},{9,11},{10,... | collective-permute-start | bytes 393224 | tf_op jit(solution)/shard_map/ppermute | solution.py:741
  23.0 11.5 %collective-permute-start.10 = (bf16[2,256,128]{2,1,0:T(8,128)(2,1)S(1)}, bf16[2,256,128]{2,1,0:T(8,128)(2,1)S(1)}, u32[]{:S(2)}, u32[]{:S(2)}) collective-permute-start(bf16[2,256,128]{2,1,0:T(8,128)(2,1)S(1)} %get-tuple-element.57), channel_id=1, source_target_pairs={{0,3},{1,0},{2,1},{3,2},{4,7},{5,4},{6,5},{7,6},{8,11},{9,8},{10,9... | collective-permute-start | bytes 393224 | tf_op jit(solution)/shard_map/ppermute | solution.py:741
  31.0 7.5 %collective-permute-start.4 = (f32[128,128]{1,0:T(8,128)S(1)}, f32[128,128]{1,0:T(8,128)S(1)}, u32[]{:S(2)}, u32[]{:S(2)}) collective-permute-start(f32[128,128]{1,0:T(8,128)S(1)} %get-tuple-element.49), channel_id=1, source_target_pairs={{0,8},{8,0},{16,24},{24,16},{1,9},{9,1},{17,25},{25,17},{2,10},{10... | collective-permute-start | bytes 196616 | tf_op jit(solution)/shard_map/ppermute | solution.py:616
  32.6 6.4 %collective-permute-start.5 = (f32[128,128]{1,0:T(8,128)S(1)}, f32[128,128]{1,0:T(8,128)S(1)}, u32[]{:S(2)}, u32[]{:S(2)}) collective-permute-start(f32[128,128]{1,0:T(8,128)S(1)} %get-tuple-element.50), channel_id=1, source_target_pairs={{0,16},{8,24},{16,0},{24,8},{1,17},{9,25},{17,1},{25,9},{2,18},{10... | collective-permute-start | bytes 196616 | tf_op jit(solution)/shard_map/ppermute | solution.py:616
  34.1 6.1 %collective-permute-start.6 = (f32[128,128]{1,0:T(8,128)S(1)}, f32[128,128]{1,0:T(8,128)S(1)}, u32[]{:S(2)}, u32[]{:S(2)}) collective-permute-start(f32[128,128]{1,0:T(8,128)S(1)} %get-tuple-element.51), channel_id=1, source_target_pairs={{0,24},{8,16},{16,8},{24,0},{1,25},{9,17},{17,9},{25,1},{2,26},{10... | collective-permute-start | bytes 196616 | tf_op jit(solution)/shard_map/ppermute | solution.py:616
  35.4 6.1 %collective-permute-start.11 = (f32[128,128]{1,0:T(8,128)S(1)}, f32[128,128]{1,0:T(8,128)S(1)}, u32[]{:S(2)}, u32[]{:S(2)}) collective-permute-start(f32[128,128]{1,0:T(8,128)S(1)} %get-tuple-element.61), channel_id=1, source_target_pairs={{0,8},{8,0},{16,24},{24,16},{1,9},{9,1},{17,25},{25,17},{2,10},{10... | collective-permute-start | bytes 196616 | tf_op jit(solution)/shard_map/ppermute | solution.py:616
  36.9 6.7 %collective-permute-start.12 = (f32[128,128]{1,0:T(8,128)S(1)}, f32[128,128]{1,0:T(8,128)S(1)}, u32[]{:S(2)}, u32[]{:S(2)}) collective-permute-start(f32[128,128]{1,0:T(8,128)S(1)} %get-tuple-element.62), channel_id=1, source_target_pairs={{0,16},{8,24},{16,0},{24,8},{1,17},{9,25},{17,1},{25,9},{2,18},{10... | collective-permute-start | bytes 196616 | tf_op jit(solution)/shard_map/ppermute | solution.py:616
  38.5 5.2 %collective-permute-start.13 = (f32[128,128]{1,0:T(8,128)S(1)}, f32[128,128]{1,0:T(8,128)S(1)}, u32[]{:S(2)}, u32[]{:S(2)}) collective-permute-start(f32[128,128]{1,0:T(8,128)S(1)} %get-tuple-element.63), channel_id=1, source_target_pairs={{0,24},{8,16},{16,8},{24,0},{1,25},{9,17},{17,9},{25,1},{2,26},{10... | collective-permute-start | bytes 196616 | tf_op jit(solution)/shard_map/ppermute | solution.py:616
  38.9 7.6 %collective-permute-start.17 = (bf16[2,128,128]{2,1,0:T(8,128)(2,1)S(1)}, bf16[2,128,128]{2,1,0:T(8,128)(2,1)S(1)}, u32[]{:S(2)}, u32[]{:S(2)}) collective-permute-start(bf16[2,128,128]{2,1,0:T(8,128)(2,1)S(1)} %get-tuple-element.69), channel_id=1, source_target_pairs={{0,1},{1,2},{2,3},{3,0},{4,5},{5,6},{6,7},{7,4},{8,9},{9,10},{10,1... | collective-permute-start | bytes 196616 | tf_op jit(solution)/shard_map/ppermute | solution.py:741
  40.1 7.4 %collective-permute-start.18 = (bf16[2,128,128]{2,1,0:T(8,128)(2,1)S(1)}, bf16[2,128,128]{2,1,0:T(8,128)(2,1)S(1)}, u32[]{:S(2)}, u32[]{:S(2)}) collective-permute-start(bf16[2,128,128]{2,1,0:T(8,128)(2,1)S(1)} %get-tuple-element.70), channel_id=1, source_target_pairs={{0,2},{1,3},{2,0},{3,1},{4,6},{5,7},{6,4},{7,5},{8,10},{9,11},{10,... | collective-permute-start | bytes 196616 | tf_op jit(solution)/shard_map/ppermute | solution.py:741
  41.4 6.1 %collective-permute-start.19 = (bf16[2,128,128]{2,1,0:T(8,128)(2,1)S(1)}, bf16[2,128,128]{2,1,0:T(8,128)(2,1)S(1)}, u32[]{:S(2)}, u32[]{:S(2)}) collective-permute-start(bf16[2,128,128]{2,1,0:T(8,128)(2,1)S(1)} %get-tuple-element.71), channel_id=1, source_target_pairs={{0,3},{1,0},{2,1},{3,2},{4,7},{5,4},{6,5},{7,6},{8,11},{9,8},{10,9... | collective-permute-start | bytes 196616 | tf_op jit(solution)/shard_map/ppermute | solution.py:741
  44.0 6.4 %collective-permute-start.14 = (f32[128,128]{1,0:T(8,128)S(1)}, f32[128,128]{1,0:T(8,128)S(1)}, u32[]{:S(2)}, u32[]{:S(2)}) collective-permute-start(f32[128,128]{1,0:T(8,128)S(1)} %get-tuple-element.65), channel_id=1, source_target_pairs={{0,8},{8,0},{16,24},{24,16},{1,9},{9,1},{17,25},{25,17},{2,10},{10... | collective-permute-start | bytes 196616 | tf_op jit(solution)/shard_map/ppermute | solution.py:616
  44.9 5.5 %collective-permute-start.15 = (f32[128,128]{1,0:T(8,128)S(1)}, f32[128,128]{1,0:T(8,128)S(1)}, u32[]{:S(2)}, u32[]{:S(2)}) collective-permute-start(f32[128,128]{1,0:T(8,128)S(1)} %get-tuple-element.66), channel_id=1, source_target_pairs={{0,16},{8,24},{16,0},{24,8},{1,17},{9,25},{17,1},{25,9},{2,18},{10... | collective-permute-start | bytes 196616 | tf_op jit(solution)/shard_map/ppermute | solution.py:616
  46.5 5.2 %collective-permute-start.16 = (f32[128,128]{1,0:T(8,128)S(1)}, f32[128,128]{1,0:T(8,128)S(1)}, u32[]{:S(2)}, u32[]{:S(2)}) collective-permute-start(f32[128,128]{1,0:T(8,128)S(1)} %get-tuple-element.67), channel_id=1, source_target_pairs={{0,24},{8,16},{16,8},{24,0},{1,25},{9,17},{17,9},{25,1},{2,26},{10... | collective-permute-start | bytes 196616 | tf_op jit(solution)/shard_map/ppermute | solution.py:616
  52.2 1.4 %collective-permute-start.20 = (bf16[128,512]{1,0:T(8,128)(2,1)S(1)}, bf16[128,512]{1,0:T(8,128)(2,1)S(1)}, u32[]{:S(2)}, u32[]{:S(2)}) collective-permute-start(bf16[128,512]{1,0:T(8,128)(2,1)S(1)} %get-tuple-element.82), channel_id=1, source_target_pairs={{0,4},{4,0},{1,5},{5,1},{2,6},{6,2},{3,7},{7,3},{8,12},{12,8},{9,1... | collective-permute-start | bytes 393224 | tf_op jit(solution)/shard_map/ppermute | solution.py:747

commit v9 on v7

--- a/solution.py
+++ b/solution.py
@@ -219,6 +219,7 @@
         self.heads = group_heads // 2
         self.chips = chips
         self.units = self.heads * groups
+        self.distances = [0] + sorted(range(1, groups), key=lambda ahead: abs(2 * ahead - groups))
         self.swapped = chips == self.heads and chips & (chips - 1) == 0
 
     def unit(self, number):
@@ -271,7 +272,7 @@
         own_starts = jnp.broadcast_to(starts[...].astype(F32), (heads, length)).astype(BF16)
         pieces.append(dot(own_starts, own.astype(BF16)))
         scales = jnp.concatenate(pieces, 1).astype(BF16)
-        for ahead, out in enumerate(outs):
+        for ahead, out in zip(sizes.distances, outs):
             target = shifted(z, ahead, sizes.groups)
             for side in range(2):
                 owner = jnp.bitwise_xor(core, side)
@@ -304,7 +305,7 @@
     def kernel(*refs):
         out = refs[-1]
         z = axis_index("head")
-        for behind, piece in enumerate(refs[:-1]):
+        for behind, piece in zip(sizes.distances, refs[:-1]):
             source = shifted(z, sizes.groups - behind, sizes.groups) if behind else z
             out[source] = piece[rows:, :]
 
@@ -337,10 +338,10 @@
     query_rows = sizes.heads * TOK
 
     def kernel(kept, swapped, *outs):
-        for ahead in range(sizes.groups):
+        for number, ahead in enumerate(sizes.distances):
             for side, source in enumerate((kept, swapped)):
-                outs[ahead][side] = source[ahead, :value_rows, :]
-                outs[sizes.groups + ahead][side] = source[ahead, value_rows:, :]
+                outs[number][side] = source[ahead, :value_rows, :]
+                outs[sizes.groups + number][side] = source[ahead, value_rows:, :]
 
     outs = [shape(2, value_rows, DK)] * sizes.groups + [shape(2, query_rows, DK)] * sizes.groups
     merged = call(kernel, outs, kept, swapped, name="merge_reads")
@@ -350,7 +351,7 @@
 def gather(sizes, pieces, scratch):
     z = axis_index("head")
     core = axis_index("core")
-    for behind, piece in enumerate(pieces):
+    for behind, piece in zip(sizes.distances, pieces):
         source = shifted(z, sizes.groups - behind, sizes.groups) if behind else z
         for side in range(2):
             scratch[jnp.bitwise_xor(core, side) * sizes.groups + source] = piece[side]
@@ -382,7 +383,7 @@
         blocks, scales, every = refs[groups + 8 + sizes.heads :]
         z = axis_index("head")
         core = axis_index("core")
-        for behind, piece in enumerate(pieces):
+        for behind, piece in zip(sizes.distances, pieces):
             source = shifted(z, groups - behind, groups) if behind else z
             blocks[core * groups + source] = piece[:rows, :]
             scales[core * groups + source] = piece[2 * rows :, :]
@@ -717,8 +718,7 @@
     def spread(parts):
         return [parts[0]] + [
             lax.ppermute(part, "head", [(z, (z + ahead) % groups) for z in range(groups)])
-            for ahead, part in enumerate(parts)
-            if ahead
+            for ahead, part in zip(sizes.distances[1:], parts[1:])
         ]
 
     def swapped(part):

time: 52.9 us -> 55.2 us (1.043)
  starting transfers between devices: 28.1 us -> 29.9 us
    ppermute x9, starting transfers between devices: 17.2 us -> 19 us  [spread(): lax.ppermute(part, 'head', [(z, (z + ahead) % groups) for z in range(grou...]
    ppermute x9, waiting for transfers between devices: 1.63 us -> 2.55 us  [exchanged(): lax.ppermute(part, 'chip', [(chip, chip ^ number) for chip in range(sizes...]
  transfers between devices with their start and end apart: 21 -> 21, of which waited for: 5 -> 7; matrix products, arithmetic and copies ran while one was open for 0% -> 0% of each run, Pallas kernels for 22% -> 21%
where the time goes in v9:
time: 55.2 us; the launch traced here: 55 us
  starting transfers between devices  29.9 us (54%)
  Pallas kernels  14.3 us (26%)
  waiting for transfers between devices  9.81 us (18%)
  local copies, waits for them, and re-layouts  0.95 us (2%)
    ppermute x9, starting transfers between devices, spread(): lax.ppermute(part, 'head', [(z, (z + ahead) % groups) for z in range(grou...  19 us
    pallas_call x10, Pallas kernels, call(): pl.pallas_call(kernel, out_shape=outs, in_specs=specs, scratch_shapes=scr...  14.3 us
    ppermute x9, starting transfers between devices, exchanged(): lax.ppermute(part, 'chip', [(chip, chip ^ number) for chip in range(sizes...  10.7 us
    ppermute x9, waiting for transfers between devices, spread(): lax.ppermute(part, 'head', [(z, (z + ahead) % groups) for z in range(grou...  5.92 us
    ppermute x9, waiting for transfers between devices, exchanged(): lax.ppermute(part, 'chip', [(chip, chip ^ number) for chip in range(sizes...  2.55 us
    ppermute x3, waiting for transfers between devices, swapped(): return lax.ppermute(part, 'core', [(0, 1), (1, 0)])  1.34 us
  transfers between devices with their start and end apart: 21, of which 7 were waited for; matrix products, arithmetic and copies ran while one was open for 0% of the time, Pallas kernels for 21%

profile of v9, /device:TPU:0, one launch (start us, length us, event | category | flops | bytes accessed | tf_op | source)
XLA Modules:
  0.0 55.0 jit_solution(6036847022485338273)
XLA Ops:
  0.0 1.6 %pack_keys.1 = (bf16[528,128]{1,0:T(8,128)(2,1)S(1)}, bf16[528,128]{1,0:T(8,128)(2,1)S(1)}, bf16[528,128]{1,0:T(8,128)(2,1)S(1)}, bf16[528,128]{1,0:T(8,128)(2,1)S(1)}) custom-call(bf16[32,8192]{1,0:T(8,128)(2,1)} %far_keys.1, bf16[32,64]{1,0:T(8,128)(2,1)} %far_betas.1, bf16[32,32]{1,0:T(8,128)(2,1)} %far_gates.1, s32[1,128]{1,0:T(1,128)} %bitcast.1), custom_call_target="tpu_custom_call" | custom-call | tf_op jit(solution)/shard_map/pack_keys/pallas_call | solution.py:196
  1.6 4.1 %collective-permute-start = (bf16[528,128]{1,0:T(8,128)(2,1)S(1)}, bf16[528,128]{1,0:T(8,128)(2,1)S(1)}, u32[]{:S(2)}, u32[]{:S(2)}) collective-permute-start(bf16[528,128]{1,0:T(8,128)(2,1)S(1)} %get-tuple-element.45), channel_id=1, source_target_pairs={{0,2},{1,3},{2,0},{3,1},{4,6},{5,7},{6,4},{7,5},{8,10},{9,11},{10,... | collective-permute-start | bytes 405512 | tf_op jit(solution)/shard_map/ppermute | solution.py:720
  5.7 1.6 %collective-permute-start.1 = (bf16[528,128]{1,0:T(8,128)(2,1)S(1)}, bf16[528,128]{1,0:T(8,128)(2,1)S(1)}, u32[]{:S(2)}, u32[]{:S(2)}) collective-permute-start(bf16[528,128]{1,0:T(8,128)(2,1)S(1)} %get-tuple-element.46), channel_id=1, source_target_pairs={{0,1},{1,2},{2,3},{3,0},{4,5},{5,6},{6,7},{7,4},{8,9},{9,10},{10,1... | collective-permute-start | bytes 405512 | tf_op jit(solution)/shard_map/ppermute | solution.py:720
  7.3 2.2 %collective-permute-start.2 = (bf16[528,128]{1,0:T(8,128)(2,1)S(1)}, bf16[528,128]{1,0:T(8,128)(2,1)S(1)}, u32[]{:S(2)}, u32[]{:S(2)}) collective-permute-start(bf16[528,128]{1,0:T(8,128)(2,1)S(1)} %get-tuple-element.47), channel_id=1, source_target_pairs={{0,3},{1,0},{2,1},{3,2},{4,7},{5,4},{6,5},{7,6},{8,11},{9,8},{10,9... | collective-permute-start | bytes 405512 | tf_op jit(solution)/shard_map/ppermute | solution.py:720
  9.6 0.9 %copy-done.1 = bf16[32,4096]{1,0:T(8,128)(2,1)S(1)} copy-done((bf16[32,4096]{1,0:T(8,128)(2,1)S(1)}, bf16[32,4096]{1,0:T(8,128)(2,1)}, u32[]{:S(2)}) %copy-start.1) | copy-done | bytes 262168
  10.5 0.2 pack_reads.1
  10.8 5.2 %collective-permute-done.refs_1_ = bf16[528,128]{1,0:T(8,128)(2,1)S(1)} collective-permute-done((bf16[528,128]{1,0:T(8,128)(2,1)S(1)}, bf16[528,128]{1,0:T(8,128)(2,1)S(1)}, u32[]{:S(2)}, u32[]{:S(2)}) %collective-permute-start) | collective-permute-done | bytes 135200 | tf_op jit(solution)/shard_map/ppermute | solution.py:720
  16.0 0.7 %collective-permute-done.2.refs_3_ = bf16[528,128]{1,0:T(8,128)(2,1)S(1)} collective-permute-done((bf16[528,128]{1,0:T(8,128)(2,1)S(1)}, bf16[528,128]{1,0:T(8,128)(2,1)S(1)}, u32[]{:S(2)}, u32[]{:S(2)}) %collective-permute-start.2) | collective-permute-done | bytes 135200 | tf_op jit(solution)/shard_map/ppermute | solution.py:720
  16.9 4.0 %collective-permute-start.8 = (bf16[2,256,128]{2,1,0:T(8,128)(2,1)S(1)}, bf16[2,256,128]{2,1,0:T(8,128)(2,1)S(1)}, u32[]{:S(2)}, u32[]{:S(2)}) collective-permute-start(bf16[2,256,128]{2,1,0:T(8,128)(2,1)S(1)} %get-tuple-element.55), channel_id=1, source_target_pairs={{0,2},{1,3},{2,0},{3,1},{4,6},{5,7},{6,4},{7,5},{8,10},{9,11},{10,... | collective-permute-start | bytes 393224 | tf_op jit(solution)/shard_map/ppermute | solution.py:720
  20.9 3.8 %collective-permute-start.10 = (bf16[2,256,128]{2,1,0:T(8,128)(2,1)S(1)}, bf16[2,256,128]{2,1,0:T(8,128)(2,1)S(1)}, u32[]{:S(2)}, u32[]{:S(2)}) collective-permute-start(bf16[2,256,128]{2,1,0:T(8,128)(2,1)S(1)} %get-tuple-element.57), channel_id=1, source_target_pairs={{0,3},{1,0},{2,1},{3,2},{4,7},{5,4},{6,5},{7,6},{8,11},{9,8},{10,9... | collective-permute-start | bytes 393224 | tf_op jit(solution)/shard_map/ppermute | solution.py:720
  24.7 7.1 %key_stage.1 = (bf16[16,128,128]{2,1,0:T(8,128)(2,1)S(1)}, bf16[16,128,256]{2,1,0:T(8,128)(2,1)S(1)}, bf16[16,128,256]{2,1,0:T(8,128)(2,1)S(1)}, f32[16,64,128]{...) custom-call(bf16[528,128]{1,0:T(8,128)(2,1)S(1)} %get-tuple-element., ...), custom_call_target="tpu_custom_call" | custom-call | flops 6000000000 | tf_op jit(solution)/shard_map/key_stage/pallas_call | solution.py:196
  31.9 1.6 %collective-permute-start.4 = (f32[128,128]{1,0:T(8,128)S(1)}, f32[128,128]{1,0:T(8,128)S(1)}, u32[]{:S(2)}, u32[]{:S(2)}) collective-permute-start(f32[128,128]{1,0:T(8,128)S(1)} %get-tuple-element.49), channel_id=1, source_target_pairs={{0,8},{8,0},{16,24},{24,16},{1,9},{9,1},{17,25},{25,17},{2,10},{10... | collective-permute-start | bytes 196616 | tf_op jit(solution)/shard_map/ppermute | solution.py:595
  33.4 1.5 %collective-permute-start.5 = (f32[128,128]{1,0:T(8,128)S(1)}, f32[128,128]{1,0:T(8,128)S(1)}, u32[]{:S(2)}, u32[]{:S(2)}) collective-permute-start(f32[128,128]{1,0:T(8,128)S(1)} %get-tuple-element.50), channel_id=1, source_target_pairs={{0,16},{8,24},{16,0},{24,8},{1,17},{9,25},{17,1},{25,9},{2,18},{10... | collective-permute-start | bytes 196616 | tf_op jit(solution)/shard_map/ppermute | solution.py:595
  35.0 0.5 collective-permute-start.6
  35.4 0.8 %value_stage.1 = (bf16[16,128,128]{2,1,0:T(8,128)(2,1)S(1)}, f32[16,128,128]{2,1,0:T(8,128)S(1)}, f32[128,128]{1,0:T(8,128)S(1)}, f32[128,128]{1,0:T(8,128)S(1)}...) custom-call(bf16[2,256,128]{2,1,0:T(8,128)(2,1)S(1)} %get-tuple-element.54.refs_0_, ...), custom_call_target="tpu_custom_call" | custom-call | flops 2000000000 | tf_op jit(solution)/shard_map/value_stage/pallas_call | solution.py:196
  36.2 1.6 %collective-permute-start.11 = (f32[128,128]{1,0:T(8,128)S(1)}, f32[128,128]{1,0:T(8,128)S(1)}, u32[]{:S(2)}, u32[]{:S(2)}) collective-permute-start(f32[128,128]{1,0:T(8,128)S(1)} %get-tuple-element.61), channel_id=1, source_target_pairs={{0,8},{8,0},{16,24},{24,16},{1,9},{9,1},{17,25},{25,17},{2,10},{10... | collective-permute-start | bytes 196616 | tf_op jit(solution)/shard_map/ppermute | solution.py:595
  37.8 1.6 %collective-permute-start.12 = (f32[128,128]{1,0:T(8,128)S(1)}, f32[128,128]{1,0:T(8,128)S(1)}, u32[]{:S(2)}, u32[]{:S(2)}) collective-permute-start(f32[128,128]{1,0:T(8,128)S(1)} %get-tuple-element.62), channel_id=1, source_target_pairs={{0,16},{8,24},{16,0},{24,8},{1,17},{9,25},{17,1},{25,9},{2,18},{10... | collective-permute-start | bytes 196616 | tf_op jit(solution)/shard_map/ppermute | solution.py:595
  39.3 0.4 collective-permute-start.13
  39.8 0.4 collective-permute-done.6.refs_3_
  40.2 0.1 collective-permute-start.18
  40.4 0.6 %collective-permute-done.11.refs_5_ = f32[128,128]{1,0:T(8,128)S(1)} collective-permute-done((f32[128,128]{1,0:T(8,128)S(1)}, f32[128,128]{1,0:T(8,128)S(1)}, u32[]{:S(2)}, u32[]{:S(2)}) %collective-permute-start.11) | collective-permute-done | bytes 65568 | tf_op jit(solution)/shard_map/ppermute | solution.py:595
  41.0 3.1 %collective-permute-start.19 = (bf16[2,128,128]{2,1,0:T(8,128)(2,1)S(1)}, bf16[2,128,128]{2,1,0:T(8,128)(2,1)S(1)}, u32[]{:S(2)}, u32[]{:S(2)}) collective-permute-start(bf16[2,128,128]{2,1,0:T(8,128)(2,1)S(1)} %get-tuple-element.71), channel_id=1, source_target_pairs={{0,3},{1,0},{2,1},{3,2},{4,7},{5,4},{6,5},{7,6},{8,11},{9,8},{10,9... | collective-permute-start | bytes 196616 | tf_op jit(solution)/shard_map/ppermute | solution.py:720
  44.1 0.4 collective-permute-done.13.refs_7_
  44.5 0.4 scan_states.1
  44.9 0.7 %collective-permute-start.14 = (f32[128,128]{1,0:T(8,128)S(1)}, f32[128,128]{1,0:T(8,128)S(1)}, u32[]{:S(2)}, u32[]{:S(2)}) collective-permute-start(f32[128,128]{1,0:T(8,128)S(1)} %get-tuple-element.65), channel_id=1, source_target_pairs={{0,8},{8,0},{16,24},{24,16},{1,9},{9,1},{17,25},{25,17},{2,10},{10... | collective-permute-start | bytes 196616 | tf_op jit(solution)/shard_map/ppermute | solution.py:595
  45.6 1.6 %collective-permute-start.15 = (f32[128,128]{1,0:T(8,128)S(1)}, f32[128,128]{1,0:T(8,128)S(1)}, u32[]{:S(2)}, u32[]{:S(2)}) collective-permute-start(f32[128,128]{1,0:T(8,128)S(1)} %get-tuple-element.66), channel_id=1, source_target_pairs={{0,16},{8,24},{16,0},{24,8},{1,17},{9,25},{17,1},{25,9},{2,18},{10... | collective-permute-start | bytes 196616 | tf_op jit(solution)/shard_map/ppermute | solution.py:595
  47.2 1.2 %collective-permute-start.16 = (f32[128,128]{1,0:T(8,128)S(1)}, f32[128,128]{1,0:T(8,128)S(1)}, u32[]{:S(2)}, u32[]{:S(2)}) collective-permute-start(f32[128,128]{1,0:T(8,128)S(1)} %get-tuple-element.67), channel_id=1, source_target_pairs={{0,24},{8,16},{16,8},{24,0},{1,25},{9,17},{17,9},{25,1},{2,26},{10... | collective-permute-start | bytes 196616 | tf_op jit(solution)/shard_map/ppermute | solution.py:595
  48.4 2.8 %query_stage.1 = (bf16[16,64,256]{2,1,0:T(8,128)(2,1)S(1)}, f32[16,64,128]{2,1,0:T(8,128)S(1)}) custom-call(bf16[2,128,128]{2,1,0:T(8,128)(2,1)S(1)} %get-tuple-element.68.refs_0_, bf16[2,128,128]{2,1,0:T(8,128)(2,1)S(1)} %collective-permute-done.17.refs_1_, bf16[2,128,128]{2,1,0:T(8,128)(2,1)S(1)} %collective-permute-done.18.refs_2_, ...), custom_call_target="tpu_custom_call" | custom-call | flops 3000000000 | tf_op jit(solution)/shard_map/query_stage/pallas_call | solution.py:196
  51.3 1.1 %collective-permute-done.16.refs_3_ = f32[128,128]{1,0:T(8,128)S(1)} collective-permute-done((f32[128,128]{1,0:T(8,128)S(1)}, f32[128,128]{1,0:T(8,128)S(1)}, u32[]{:S(2)}, u32[]{:S(2)}) %collective-permute-start.16) | collective-permute-done | bytes 65568 | tf_op jit(solution)/shard_map/ppermute | solution.py:595
  52.4 0.5 read_states.1
  52.9 1.3 %collective-permute-done.20.other = bf16[128,512]{1,0:T(8,128)(2,1)S(1)} collective-permute-done((bf16[128,512]{1,0:T(8,128)(2,1)S(1)}, bf16[128,512]{1,0:T(8,128)(2,1)S(1)}, u32[]{:S(2)}, u32[]{:S(2)}) %collective-permute-start.20) | collective-permute-done | bytes 131104 | tf_op jit(solution)/shard_map/ppermute | solution.py:725
  54.3 0.7 %join.1 = bf16[128,1024]{1,0:T(8,128)(2,1)} custom-call(bf16[128,512]{1,0:T(8,128)(2,1)S(1)} %get-tuple-element.81.own, bf16[128,512]{1,0:T(8,128)(2,1)S(1)} %collective-permute-done.20.other), custom_call_target="tpu_custom_call" | custom-call | tf_op jit(solution)/shard_map/join/pallas_call | solution.py:196
  (24 shorter events, 0.3 us)
Async XLA Ops:
  0.0 9.6 %copy-start = (bf16[32,8192]{1,0:T(8,128)(2,1)S(1)}, bf16[32,8192]{1,0:T(8,128)(2,1)}, u32[]{:S(2)}) copy-start(bf16[32,8192]{1,0:T(8,128)(2,1)} %values.1) | copy-start | bytes 1572868
  1.6 14.4 %collective-permute-start = (bf16[528,128]{1,0:T(8,128)(2,1)S(1)}, bf16[528,128]{1,0:T(8,128)(2,1)S(1)}, u32[]{:S(2)}, u32[]{:S(2)}) collective-permute-start(bf16[528,128]{1,0:T(8,128)(2,1)S(1)} %get-tuple-element.45), channel_id=1, source_target_pairs={{0,2},{1,3},{2,0},{3,1},{4,6},{5,7},{6,4},{7,5},{8,10},{9,11},{10,... | collective-permute-start | bytes 405512 | tf_op jit(solution)/shard_map/ppermute | solution.py:720
  5.7 10.3 %collective-permute-start.1 = (bf16[528,128]{1,0:T(8,128)(2,1)S(1)}, bf16[528,128]{1,0:T(8,128)(2,1)S(1)}, u32[]{:S(2)}, u32[]{:S(2)}) collective-permute-start(bf16[528,128]{1,0:T(8,128)(2,1)S(1)} %get-tuple-element.46), channel_id=1, source_target_pairs={{0,1},{1,2},{2,3},{3,0},{4,5},{5,6},{6,7},{7,4},{8,9},{9,10},{10,1... | collective-permute-start | bytes 405512 | tf_op jit(solution)/shard_map/ppermute | solution.py:720
  7.3 9.4 %collective-permute-start.2 = (bf16[528,128]{1,0:T(8,128)(2,1)S(1)}, bf16[528,128]{1,0:T(8,128)(2,1)S(1)}, u32[]{:S(2)}, u32[]{:S(2)}) collective-permute-start(bf16[528,128]{1,0:T(8,128)(2,1)S(1)} %get-tuple-element.47), channel_id=1, source_target_pairs={{0,3},{1,0},{2,1},{3,2},{4,7},{5,4},{6,5},{7,6},{8,11},{9,8},{10,9... | collective-permute-start | bytes 405512 | tf_op jit(solution)/shard_map/ppermute | solution.py:720
  9.6 1.0 %copy-start.1 = (bf16[32,4096]{1,0:T(8,128)(2,1)S(1)}, bf16[32,4096]{1,0:T(8,128)(2,1)}, u32[]{:S(2)}) copy-start(bf16[32,4096]{1,0:T(8,128)(2,1)} %queries.1) | copy-start | bytes 786436
  10.7 6.1 %collective-permute-start.7 = (bf16[4,384,128]{2,1,0:T(8,128)(2,1)S(1)}, bf16[4,384,128]{2,1,0:T(8,128)(2,1)S(1)}, u32[]{:S(2)}, u32[]{:S(2)}) collective-permute-start(bf16[4,384,128]{2,1,0:T(8,128)(2,1)S(1)} %get-tuple-element.53), channel_id=1, source_target_pairs={{0,4},{4,0},{1,5},{5,1},{2,6},{6,2},{3,7},{7,3},{8,12},{12,8},{9,1... | collective-permute-start | bytes 1179656 | tf_op jit(solution)/shard_map/ppermute | solution.py:725
  16.7 8.0 %collective-permute-start.3 = (bf16[4,272,128]{2,1,0:T(8,128)(2,1)S(1)}, bf16[4,272,128]{2,1,0:T(8,128)(2,1)S(1)}, u32[]{:S(2)}, u32[]{:S(2)}) collective-permute-start(bf16[4,272,128]{2,1,0:T(8,128)(2,1)S(1)} %swap_keys.1), channel_id=1, source_target_pairs={{0,4},{4,0},{1,5},{5,1},{2,6},{6,2},{3,7},{7,3},{8,12},{12,8},{9,1... | collective-permute-start | bytes 835592 | tf_op jit(solution)/shard_map/ppermute | solution.py:725
  16.9 18.1 %collective-permute-start.8 = (bf16[2,256,128]{2,1,0:T(8,128)(2,1)S(1)}, bf16[2,256,128]{2,1,0:T(8,128)(2,1)S(1)}, u32[]{:S(2)}, u32[]{:S(2)}) collective-permute-start(bf16[2,256,128]{2,1,0:T(8,128)(2,1)S(1)} %get-tuple-element.55), channel_id=1, source_target_pairs={{0,2},{1,3},{2,0},{3,1},{4,6},{5,7},{6,4},{7,5},{8,10},{9,11},{10,... | collective-permute-start | bytes 393224 | tf_op jit(solution)/shard_map/ppermute | solution.py:720
  20.9 14.5 %collective-permute-start.9 = (bf16[2,256,128]{2,1,0:T(8,128)(2,1)S(1)}, bf16[2,256,128]{2,1,0:T(8,128)(2,1)S(1)}, u32[]{:S(2)}, u32[]{:S(2)}) collective-permute-start(bf16[2,256,128]{2,1,0:T(8,128)(2,1)S(1)} %get-tuple-element.56), channel_id=1, source_target_pairs={{0,1},{1,2},{2,3},{3,0},{4,5},{5,6},{6,7},{7,4},{8,9},{9,10},{10,1... | collective-permute-start | bytes 393224 | tf_op jit(solution)/shard_map/ppermute | solution.py:720
  20.9 14.5 %collective-permute-start.10 = (bf16[2,256,128]{2,1,0:T(8,128)(2,1)S(1)}, bf16[2,256,128]{2,1,0:T(8,128)(2,1)S(1)}, u32[]{:S(2)}, u32[]{:S(2)}) collective-permute-start(bf16[2,256,128]{2,1,0:T(8,128)(2,1)S(1)} %get-tuple-element.57), channel_id=1, source_target_pairs={{0,3},{1,0},{2,1},{3,2},{4,7},{5,4},{6,5},{7,6},{8,11},{9,8},{10,9... | collective-permute-start | bytes 393224 | tf_op jit(solution)/shard_map/ppermute | solution.py:720
  31.9 7.5 %collective-permute-start.4 = (f32[128,128]{1,0:T(8,128)S(1)}, f32[128,128]{1,0:T(8,128)S(1)}, u32[]{:S(2)}, u32[]{:S(2)}) collective-permute-start(f32[128,128]{1,0:T(8,128)S(1)} %get-tuple-element.49), channel_id=1, source_target_pairs={{0,8},{8,0},{16,24},{24,16},{1,9},{9,1},{17,25},{25,17},{2,10},{10... | collective-permute-start | bytes 196616 | tf_op jit(solution)/shard_map/ppermute | solution.py:595
  33.4 6.4 %collective-permute-start.5 = (f32[128,128]{1,0:T(8,128)S(1)}, f32[128,128]{1,0:T(8,128)S(1)}, u32[]{:S(2)}, u32[]{:S(2)}) collective-permute-start(f32[128,128]{1,0:T(8,128)S(1)} %get-tuple-element.50), channel_id=1, source_target_pairs={{0,16},{8,24},{16,0},{24,8},{1,17},{9,25},{17,1},{25,9},{2,18},{10... | collective-permute-start | bytes 196616 | tf_op jit(solution)/shard_map/ppermute | solution.py:595
  35.0 5.3 %collective-permute-start.6 = (f32[128,128]{1,0:T(8,128)S(1)}, f32[128,128]{1,0:T(8,128)S(1)}, u32[]{:S(2)}, u32[]{:S(2)}) collective-permute-start(f32[128,128]{1,0:T(8,128)S(1)} %get-tuple-element.51), channel_id=1, source_target_pairs={{0,24},{8,16},{16,8},{24,0},{1,25},{9,17},{17,9},{25,1},{2,26},{10... | collective-permute-start | bytes 196616 | tf_op jit(solution)/shard_map/ppermute | solution.py:595
  36.2 4.7 %collective-permute-start.11 = (f32[128,128]{1,0:T(8,128)S(1)}, f32[128,128]{1,0:T(8,128)S(1)}, u32[]{:S(2)}, u32[]{:S(2)}) collective-permute-start(f32[128,128]{1,0:T(8,128)S(1)} %get-tuple-element.61), channel_id=1, source_target_pairs={{0,8},{8,0},{16,24},{24,16},{1,9},{9,1},{17,25},{25,17},{2,10},{10... | collective-permute-start | bytes 196616 | tf_op jit(solution)/shard_map/ppermute | solution.py:595
  37.8 6.3 %collective-permute-start.12 = (f32[128,128]{1,0:T(8,128)S(1)}, f32[128,128]{1,0:T(8,128)S(1)}, u32[]{:S(2)}, u32[]{:S(2)}) collective-permute-start(f32[128,128]{1,0:T(8,128)S(1)} %get-tuple-element.62), channel_id=1, source_target_pairs={{0,16},{8,24},{16,0},{24,8},{1,17},{9,25},{17,1},{25,9},{2,18},{10... | collective-permute-start | bytes 196616 | tf_op jit(solution)/shard_map/ppermute | solution.py:595
  39.3 5.2 %collective-permute-start.13 = (f32[128,128]{1,0:T(8,128)S(1)}, f32[128,128]{1,0:T(8,128)S(1)}, u32[]{:S(2)}, u32[]{:S(2)}) collective-permute-start(f32[128,128]{1,0:T(8,128)S(1)} %get-tuple-element.63), channel_id=1, source_target_pairs={{0,24},{8,16},{16,8},{24,0},{1,25},{9,17},{17,9},{25,1},{2,26},{10... | collective-permute-start | bytes 196616 | tf_op jit(solution)/shard_map/ppermute | solution.py:595
  39.8 7.4 %collective-permute-start.17 = (bf16[2,128,128]{2,1,0:T(8,128)(2,1)S(1)}, bf16[2,128,128]{2,1,0:T(8,128)(2,1)S(1)}, u32[]{:S(2)}, u32[]{:S(2)}) collective-permute-start(bf16[2,128,128]{2,1,0:T(8,128)(2,1)S(1)} %get-tuple-element.69), channel_id=1, source_target_pairs={{0,2},{1,3},{2,0},{3,1},{4,6},{5,7},{6,4},{7,5},{8,10},{9,11},{10,... | collective-permute-start | bytes 196616 | tf_op jit(solution)/shard_map/ppermute | solution.py:720
  40.2 8.2 %collective-permute-start.18 = (bf16[2,128,128]{2,1,0:T(8,128)(2,1)S(1)}, bf16[2,128,128]{2,1,0:T(8,128)(2,1)S(1)}, u32[]{:S(2)}, u32[]{:S(2)}) collective-permute-start(bf16[2,128,128]{2,1,0:T(8,128)(2,1)S(1)} %get-tuple-element.70), channel_id=1, source_target_pairs={{0,1},{1,2},{2,3},{3,0},{4,5},{5,6},{6,7},{7,4},{8,9},{9,10},{10,1... | collective-permute-start | bytes 196616 | tf_op jit(solution)/shard_map/ppermute | solution.py:720
  41.0 7.5 %collective-permute-start.19 = (bf16[2,128,128]{2,1,0:T(8,128)(2,1)S(1)}, bf16[2,128,128]{2,1,0:T(8,128)(2,1)S(1)}, u32[]{:S(2)}, u32[]{:S(2)}) collective-permute-start(bf16[2,128,128]{2,1,0:T(8,128)(2,1)S(1)} %get-tuple-element.71), channel_id=1, source_target_pairs={{0,3},{1,0},{2,1},{3,2},{4,7},{5,4},{6,5},{7,6},{8,11},{9,8},{10,9... | collective-permute-start | bytes 196616 | tf_op jit(solution)/shard_map/ppermute | solution.py:720
  44.9 6.4 %collective-permute-start.14 = (f32[128,128]{1,0:T(8,128)S(1)}, f32[128,128]{1,0:T(8,128)S(1)}, u32[]{:S(2)}, u32[]{:S(2)}) collective-permute-start(f32[128,128]{1,0:T(8,128)S(1)} %get-tuple-element.65), channel_id=1, source_target_pairs={{0,8},{8,0},{16,24},{24,16},{1,9},{9,1},{17,25},{25,17},{2,10},{10... | collective-permute-start | bytes 196616 | tf_op jit(solution)/shard_map/ppermute | solution.py:595
  45.6 5.7 %collective-permute-start.15 = (f32[128,128]{1,0:T(8,128)S(1)}, f32[128,128]{1,0:T(8,128)S(1)}, u32[]{:S(2)}, u32[]{:S(2)}) collective-permute-start(f32[128,128]{1,0:T(8,128)S(1)} %get-tuple-element.66), channel_id=1, source_target_pairs={{0,16},{8,24},{16,0},{24,8},{1,17},{9,25},{17,1},{25,9},{2,18},{10... | collective-permute-start | bytes 196616 | tf_op jit(solution)/shard_map/ppermute | solution.py:595
  47.2 5.2 %collective-permute-start.16 = (f32[128,128]{1,0:T(8,128)S(1)}, f32[128,128]{1,0:T(8,128)S(1)}, u32[]{:S(2)}, u32[]{:S(2)}) collective-permute-start(f32[128,128]{1,0:T(8,128)S(1)} %get-tuple-element.67), channel_id=1, source_target_pairs={{0,24},{8,16},{16,8},{24,0},{1,25},{9,17},{17,9},{25,1},{2,26},{10... | collective-permute-start | bytes 196616 | tf_op jit(solution)/shard_map/ppermute | solution.py:595
  52.9 1.4 %collective-permute-start.20 = (bf16[128,512]{1,0:T(8,128)(2,1)S(1)}, bf16[128,512]{1,0:T(8,128)(2,1)S(1)}, u32[]{:S(2)}, u32[]{:S(2)}) collective-permute-start(bf16[128,512]{1,0:T(8,128)(2,1)S(1)} %get-tuple-element.82), channel_id=1, source_target_pairs={{0,4},{4,0},{1,5},{5,1},{2,6},{6,2},{3,7},{7,3},{8,12},{12,8},{9,1... | collective-permute-start | bytes 393224 | tf_op jit(solution)/shard_map/ppermute | solution.py:725

commit v10 on v7

--- a/solution.py
+++ b/solution.py
@@ -190,18 +190,24 @@
     )
 
 
-def call(kernel, outs, *args, scratch=(), flops=0, far=0, name=None):
+def call(kernel, outs, *args, scratch=(), flops=0, far=0, after=(), name=None):
+    count = len(args)
+
+    def body(*refs):
+        kernel(*refs[:count], *refs[count + len(after) :])
+
     specs = [pl.BlockSpec(memory_space=pltpu.HBM)] * far
-    specs += [pl.BlockSpec(memory_space=pltpu.VMEM)] * (len(args) - far)
+    specs += [pl.BlockSpec(memory_space=pltpu.VMEM)] * (count - far)
+    specs += [pl.BlockSpec(memory_space=pl.ANY)] * len(after)
     return pl.pallas_call(
-        kernel,
+        body,
         out_shape=outs,
         in_specs=specs,
         scratch_shapes=scratch,
         compiler_params=pltpu.CompilerParams(vmem_limit_bytes=24 * 2**20),
         cost_estimate=pl.CostEstimate(flops=flops, bytes_accessed=0, transcendentals=0),
         name=name,
-    )(*args)
+    )(*args, *after)
 
 
 def shape(*sizes, dtype=BF16):
@@ -506,14 +512,14 @@
     return results[:7], results[7:]
 
 
-def value_stage(sizes, pieces, ends, steps):
+def value_stage(sizes, pieces, ends, steps, transitions):
     groups = sizes.groups
 
     def kernel(*refs):
         pieces = refs[:groups]
-        ends, steps, values_out, before_out = refs[groups : groups + 4]
-        totals = refs[groups + 4 : groups + 4 + sizes.heads]
-        blocks, every = refs[groups + 4 + sizes.heads :]
+        ends, steps = refs[groups : groups + 2]
+        transitions = refs[groups + 2 : groups + 2 + sizes.heads]
+        values_out, before_out, *totals, blocks, every = refs[groups + 2 + sizes.heads :]
         gather(sizes, pieces, blocks)
         injects = []
         for unit in range(sizes.units):
@@ -538,36 +544,37 @@
                 every[head] = sums[head]
             chip = axis_index("chip")
             for number in range(sizes.heads):
-                totals[number][...] = every[jnp.bitwise_xor(chip, number)]
+                totals[number][0] = transitions[number][...]
+                totals[number][1] = every[jnp.bitwise_xor(chip, number)]
         else:
             for head in range(sizes.heads):
-                totals[head][...] = sums[head]
+                totals[head][0] = transitions[head][...]
+                totals[head][1] = sums[head]
 
     outs = [shape(sizes.units, REFL, DV), shape(sizes.units, DV, DK, dtype=F32)]
-    outs += [shape(DV, DK, dtype=F32)] * sizes.heads
+    outs += [shape(2, DV, DK, dtype=F32)] * sizes.heads
     scratch = [
         pltpu.VMEM((2 * groups, sizes.heads * KEY_ROWS, DV), BF16),
         pltpu.VMEM((sizes.heads, DV, DK), F32),
     ]
     results = call(
-        kernel, outs, *pieces, ends, steps, scratch=scratch, flops=2_000_000_000, name="value_stage"
+        kernel, outs, *pieces, ends, steps, *transitions, scratch=scratch, name="value_stage"
     )
     return results[0], results[1], results[2:]
 
 
-def scan_states(sizes, transitions, injects):
+def scan_states(sizes, changes):
     chips = sizes.chips
 
     def kernel(*refs):
-        transitions = refs[:chips]
-        injects = refs[chips : 2 * chips]
-        outs = refs[2 * chips : 3 * chips]
-        step, inject, entry = refs[3 * chips :]
+        changes = refs[:chips]
+        outs = refs[chips : 2 * chips]
+        step, inject, entry = refs[2 * chips :]
         chip = axis_index("chip")
         for number in range(chips):
             source = jnp.bitwise_xor(chip, number)
-            step[source] = transitions[number][...]
-            inject[source] = injects[number][...]
+            step[source] = changes[number][0]
+            inject[source] = changes[number][1]
         state = jnp.zeros((DV, DK), F32)
         for index in range(chips):
             entry[index] = state
@@ -582,8 +589,7 @@
     return call(
         kernel,
         [shape(DV, DK, dtype=F32)] * chips,
-        *transitions,
-        *injects,
+        *changes,
         scratch=scratch,
         name="scan_states",
     )
@@ -597,12 +603,11 @@
     ]
 
 
-def entry_states(sizes, transitions, injects):
+def entry_states(sizes, changes):
     if sizes.swapped:
-        arrived = exchanged(sizes, transitions), exchanged(sizes, injects)
-        return exchanged(sizes, scan_states(sizes, *arrived))
-    transition = jnp.stack(transitions)
-    inject = jnp.stack(injects)
+        return exchanged(sizes, scan_states(sizes, exchanged(sizes, changes)))
+    transition = jnp.stack([change[0] for change in changes])
+    inject = jnp.stack([change[1] for change in changes])
     forward = [(chip, chip + 1) for chip in range(sizes.chips - 1)]
 
     def advance(_, entry):
@@ -733,11 +738,11 @@
     (unit_keys, inverse, ends, ratios, rows, steps, prefixes), transitions = key_stage(
         sizes, arrived, other_keys
     )
-    unit_values, before, injects = value_stage(sizes, value_parts, ends, steps)
-    states = entry_states(sizes, transitions, injects)
+    unit_values, before, changes = value_stage(sizes, value_parts, ends, steps, transitions)
     readers, inners = query_stage(
         sizes, query_parts, unit_values, before, unit_keys, inverse, ratios, rows, prefixes
     )
+    states = entry_states(sizes, changes)
     own, other = read_states(sizes, states, readers, inners)
     return join(sizes, own, swapped(other))
 

time: 52.9 us -> 53.4 us (level)
  waiting for transfers between devices: 9.3 us -> 11.3 us
  starting transfers between devices: 28.1 us -> 26.7 us
    ppermute x9 -> x6, starting transfers between devices: 10.7 us -> 7.36 us  [exchanged(): lax.ppermute(part, 'chip', [(chip, chip ^ number) for chip in range(sizes...]
    ppermute x9, starting transfers between devices: 17.2 us -> 19.1 us  [spread(): lax.ppermute(part, 'head', [(z, (z + ahead) % groups) for z in range(grou...]
    ppermute x9, waiting for transfers between devices: 6.33 us -> 7.63 us  [spread(): lax.ppermute(part, 'head', [(z, (z + ahead) % groups) for z in range(grou...]
    ppermute x9 -> x6, waiting for transfers between devices: 1.63 us -> 2.3 us  [exchanged(): lax.ppermute(part, 'chip', [(chip, chip ^ number) for chip in range(sizes...]
  transfers between devices with their start and end apart: 21 -> 18, of which waited for: 5 -> 5; matrix products, arithmetic and copies ran while one was open for 0% -> 0% of each run, Pallas kernels for 22% -> 20%
where the time goes in v10:
time: 53.4 us; the launch traced here: 53.3 us
  starting transfers between devices  26.7 us (50%)
  Pallas kernels  14.3 us (27%)
  waiting for transfers between devices  11.3 us (21%)
  local copies, waits for them, and re-layouts  0.95 us (2%)
    ppermute x9, starting transfers between devices, spread(): lax.ppermute(part, 'head', [(z, (z + ahead) % groups) for z in range(grou...  19.1 us
    pallas_call x10, Pallas kernels, call(): pl.pallas_call(body, out_shape=outs, in_specs=specs, scratch_shapes=scrat...  14.3 us
    ppermute x9, waiting for transfers between devices, spread(): lax.ppermute(part, 'head', [(z, (z + ahead) % groups) for z in range(grou...  7.63 us
    ppermute x6, starting transfers between devices, exchanged(): lax.ppermute(part, 'chip', [(chip, chip ^ number) for chip in range(sizes...  7.36 us
    ppermute x6, waiting for transfers between devices, exchanged(): lax.ppermute(part, 'chip', [(chip, chip ^ number) for chip in range(sizes...  2.3 us
    ppermute x3, waiting for transfers between devices, swapped(): return lax.ppermute(part, 'core', [(0, 1), (1, 0)])  1.34 us
  transfers between devices with their start and end apart: 18, of which 5 were waited for; matrix products, arithmetic and copies ran while one was open for 0% of the time, Pallas kernels for 20%

profile of v10, /device:TPU:0, one launch (start us, length us, event | category | flops | bytes accessed | tf_op | source)
XLA Modules:
  0.0 53.3 jit_solution(14047391546474803422)
XLA Ops:
  0.0 1.6 %pack_keys.1 = (bf16[528,128]{1,0:T(8,128)(2,1)S(1)}, bf16[528,128]{1,0:T(8,128)(2,1)S(1)}, bf16[528,128]{1,0:T(8,128)(2,1)S(1)}, bf16[528,128]{1,0:T(8,128)(2,1)S(1)}) custom-call(bf16[32,8192]{1,0:T(8,128)(2,1)} %refs_0_.3, bf16[32,64]{1,0:T(8,128)(2,1)} %refs_1_.3, bf16[32,32]{1,0:T(8,128)(2,1)} %refs_2_.1, s32[1,128]{1,0:T(1,128)} %bitcast.1), custom_call_target="tpu_custom_call" | custom-call | tf_op jit(solution)/shard_map/pack_keys/pallas_call | solution.py:202
  1.6 3.1 %collective-permute-start.4 = (bf16[528,128]{1,0:T(8,128)(2,1)S(1)}, bf16[528,128]{1,0:T(8,128)(2,1)S(1)}, u32[]{:S(2)}, u32[]{:S(2)}) collective-permute-start(bf16[528,128]{1,0:T(8,128)(2,1)S(1)} %get-tuple-element.51), channel_id=1, source_target_pairs={{0,1},{1,2},{2,3},{3,0},{4,5},{5,6},{6,7},{7,4},{8,9},{9,10},{10,1... | collective-permute-start | bytes 405512 | tf_op jit(solution)/shard_map/ppermute | solution.py:724
  4.7 2.6 %collective-permute-start.5 = (bf16[528,128]{1,0:T(8,128)(2,1)S(1)}, bf16[528,128]{1,0:T(8,128)(2,1)S(1)}, u32[]{:S(2)}, u32[]{:S(2)}) collective-permute-start(bf16[528,128]{1,0:T(8,128)(2,1)S(1)} %get-tuple-element.52), channel_id=1, source_target_pairs={{0,2},{1,3},{2,0},{3,1},{4,6},{5,7},{6,4},{7,5},{8,10},{9,11},{10,... | collective-permute-start | bytes 405512 | tf_op jit(solution)/shard_map/ppermute | solution.py:724
  7.3 1.3 %collective-permute-start.6 = (bf16[528,128]{1,0:T(8,128)(2,1)S(1)}, bf16[528,128]{1,0:T(8,128)(2,1)S(1)}, u32[]{:S(2)}, u32[]{:S(2)}) collective-permute-start(bf16[528,128]{1,0:T(8,128)(2,1)S(1)} %get-tuple-element.53), channel_id=1, source_target_pairs={{0,3},{1,0},{2,1},{3,2},{4,7},{5,4},{6,5},{7,6},{8,11},{9,8},{10,9... | collective-permute-start | bytes 405512 | tf_op jit(solution)/shard_map/ppermute | solution.py:724
  8.7 0.9 %copy-done.1 = bf16[32,4096]{1,0:T(8,128)(2,1)S(1)} copy-done((bf16[32,4096]{1,0:T(8,128)(2,1)S(1)}, bf16[32,4096]{1,0:T(8,128)(2,1)}, u32[]{:S(2)}) %copy-start.1) | copy-done | bytes 262168
  9.6 0.2 pack_reads.1
  9.8 0.1 collective-permute-start
  9.9 1.4 %collective-permute-done.4.refs_1_ = bf16[528,128]{1,0:T(8,128)(2,1)S(1)} collective-permute-done((bf16[528,128]{1,0:T(8,128)(2,1)S(1)}, bf16[528,128]{1,0:T(8,128)(2,1)S(1)}, u32[]{:S(2)}, u32[]{:S(2)}) %collective-permute-start.4) | collective-permute-done | bytes 135200 | tf_op jit(solution)/shard_map/ppermute | solution.py:724
  11.2 5.0 %collective-permute-done.5.refs_2_ = bf16[528,128]{1,0:T(8,128)(2,1)S(1)} collective-permute-done((bf16[528,128]{1,0:T(8,128)(2,1)S(1)}, bf16[528,128]{1,0:T(8,128)(2,1)S(1)}, u32[]{:S(2)}, u32[]{:S(2)}) %collective-permute-start.5) | collective-permute-done | bytes 135200 | tf_op jit(solution)/shard_map/ppermute | solution.py:724
  16.2 0.1 collective-permute-start.7
  16.3 0.1 merge_reads.1
  16.4 3.4 %collective-permute-start.1 = (bf16[2,256,128]{2,1,0:T(8,128)(2,1)S(1)}, bf16[2,256,128]{2,1,0:T(8,128)(2,1)S(1)}, u32[]{:S(2)}, u32[]{:S(2)}) collective-permute-start(bf16[2,256,128]{2,1,0:T(8,128)(2,1)S(1)} %get-tuple-element.47), channel_id=1, source_target_pairs={{0,1},{1,2},{2,3},{3,0},{4,5},{5,6},{6,7},{7,4},{8,9},{9,10},{10,1... | collective-permute-start | bytes 393224 | tf_op jit(solution)/shard_map/ppermute | solution.py:724
  19.8 1.6 %collective-permute-start.2 = (bf16[2,256,128]{2,1,0:T(8,128)(2,1)S(1)}, bf16[2,256,128]{2,1,0:T(8,128)(2,1)S(1)}, u32[]{:S(2)}, u32[]{:S(2)}) collective-permute-start(bf16[2,256,128]{2,1,0:T(8,128)(2,1)S(1)} %get-tuple-element.48), channel_id=1, source_target_pairs={{0,2},{1,3},{2,0},{3,1},{4,6},{5,7},{6,4},{7,5},{8,10},{9,11},{10,... | collective-permute-start | bytes 393224 | tf_op jit(solution)/shard_map/ppermute | solution.py:724
  21.4 0.8 %collective-permute-start.3 = (bf16[2,256,128]{2,1,0:T(8,128)(2,1)S(1)}, bf16[2,256,128]{2,1,0:T(8,128)(2,1)S(1)}, u32[]{:S(2)}, u32[]{:S(2)}) collective-permute-start(bf16[2,256,128]{2,1,0:T(8,128)(2,1)S(1)} %get-tuple-element.49), channel_id=1, source_target_pairs={{0,3},{1,0},{2,1},{3,2},{4,7},{5,4},{6,5},{7,6},{8,11},{9,8},{10,9... | collective-permute-start | bytes 393224 | tf_op jit(solution)/shard_map/ppermute | solution.py:724
  22.3 7.1 %key_stage.1 = (bf16[16,128,128]{2,1,0:T(8,128)(2,1)S(1)}, bf16[16,128,256]{2,1,0:T(8,128)(2,1)S(1)}, bf16[16,128,256]{2,1,0:T(8,128)(2,1)S(1)}, f32[16,64,128]{...) custom-call(bf16[528,128]{1,0:T(8,128)(2,1)S(1)} %get-tuple-element., ...), custom_call_target="tpu_custom_call" | custom-call | flops 6000000000 | tf_op jit(solution)/shard_map/key_stage/pallas_call | solution.py:202
  29.4 1.3 %collective-permute-done.2.refs_2_ = bf16[2,256,128]{2,1,0:T(8,128)(2,1)S(1)} collective-permute-done((bf16[2,256,128]{2,1,0:T(8,128)(2,1)S(1)}, bf16[2,256,128]{2,1,0:T(8,128)(2,1)S(1)}, u32[]{:S(2)}, u32[]{:S(2)}) %collective-permute-start.2) | collective-permute-done | bytes 131104 | tf_op jit(solution)/shard_map/ppermute | solution.py:724
  30.7 0.8 %value_stage.1 = (bf16[16,128,128]{2,1,0:T(8,128)(2,1)S(1)}, f32[16,128,128]{2,1,0:T(8,128)S(1)}, f32[2,128,128]{2,1,0:T(8,128)S(1)}, f32[2,128,128]{2,1,0:T(8,1...) custom-call(bf16[2,256,128]{2,1,0:T(8,128)(2,1)S(1)} %get-tuple-element.46.refs_0_, ...), custom_call_target="tpu_custom_call" | custom-call | tf_op jit(solution)/shard_map/value_stage/pallas_call | solution.py:202
  31.5 1.6 %collective-permute-start.8 = (f32[2,128,128]{2,1,0:T(8,128)S(1)}, f32[2,128,128]{2,1,0:T(8,128)S(1)}, u32[]{:S(2)}, u32[]{:S(2)}) collective-permute-start(f32[2,128,128]{2,1,0:T(8,128)S(1)} %get-tuple-element.61), channel_id=1, source_target_pairs={{0,8},{8,0},{16,24},{24,16},{1,9},{9,1},{17,25},{25,17},{2,10},{10... | collective-permute-start | bytes 393224 | tf_op jit(solution)/shard_map/ppermute | solution.py:600
  33.1 1.5 %collective-permute-start.9 = (f32[2,128,128]{2,1,0:T(8,128)S(1)}, f32[2,128,128]{2,1,0:T(8,128)S(1)}, u32[]{:S(2)}, u32[]{:S(2)}) collective-permute-start(f32[2,128,128]{2,1,0:T(8,128)S(1)} %get-tuple-element.62), channel_id=1, source_target_pairs={{0,16},{8,24},{16,0},{24,8},{1,17},{9,25},{17,1},{25,9},{2,18},{10... | collective-permute-start | bytes 393224 | tf_op jit(solution)/shard_map/ppermute | solution.py:600
  34.6 0.5 collective-permute-start.10
  35.1 3.3 %collective-permute-start.14 = (bf16[2,128,128]{2,1,0:T(8,128)(2,1)S(1)}, bf16[2,128,128]{2,1,0:T(8,128)(2,1)S(1)}, u32[]{:S(2)}, u32[]{:S(2)}) collective-permute-start(bf16[2,128,128]{2,1,0:T(8,128)(2,1)S(1)} %get-tuple-element.69), channel_id=1, source_target_pairs={{0,1},{1,2},{2,3},{3,0},{4,5},{5,6},{6,7},{7,4},{8,9},{9,10},{10,1... | collective-permute-start | bytes 196616 | tf_op jit(solution)/shard_map/ppermute | solution.py:724
  38.4 1.3 %collective-permute-start.15 = (bf16[2,128,128]{2,1,0:T(8,128)(2,1)S(1)}, bf16[2,128,128]{2,1,0:T(8,128)(2,1)S(1)}, u32[]{:S(2)}, u32[]{:S(2)}) collective-permute-start(bf16[2,128,128]{2,1,0:T(8,128)(2,1)S(1)} %get-tuple-element.70), channel_id=1, source_target_pairs={{0,2},{1,3},{2,0},{3,1},{4,6},{5,7},{6,4},{7,5},{8,10},{9,11},{10,... | collective-permute-start | bytes 196616 | tf_op jit(solution)/shard_map/ppermute | solution.py:724
  39.7 1.6 %collective-permute-start.16 = (bf16[2,128,128]{2,1,0:T(8,128)(2,1)S(1)}, bf16[2,128,128]{2,1,0:T(8,128)(2,1)S(1)}, u32[]{:S(2)}, u32[]{:S(2)}) collective-permute-start(bf16[2,128,128]{2,1,0:T(8,128)(2,1)S(1)} %get-tuple-element.71), channel_id=1, source_target_pairs={{0,3},{1,0},{2,1},{3,2},{4,7},{5,4},{6,5},{7,6},{8,11},{9,8},{10,9... | collective-permute-start | bytes 196616 | tf_op jit(solution)/shard_map/ppermute | solution.py:724
  41.3 0.4 scan_states.1
  41.7 2.3 %collective-permute-start.11 = (f32[128,128]{1,0:T(8,128)S(1)}, f32[128,128]{1,0:T(8,128)S(1)}, u32[]{:S(2)}, u32[]{:S(2)}) collective-permute-start(f32[128,128]{1,0:T(8,128)S(1)} %get-tuple-element.65), channel_id=1, source_target_pairs={{0,8},{8,0},{16,24},{24,16},{1,9},{9,1},{17,25},{25,17},{2,10},{10... | collective-permute-start | bytes 196616 | tf_op jit(solution)/shard_map/ppermute | solution.py:600
  43.9 1.6 %collective-permute-start.12 = (f32[128,128]{1,0:T(8,128)S(1)}, f32[128,128]{1,0:T(8,128)S(1)}, u32[]{:S(2)}, u32[]{:S(2)}) collective-permute-start(f32[128,128]{1,0:T(8,128)S(1)} %get-tuple-element.66), channel_id=1, source_target_pairs={{0,16},{8,24},{16,0},{24,8},{1,17},{9,25},{17,1},{25,9},{2,18},{10... | collective-permute-start | bytes 196616 | tf_op jit(solution)/shard_map/ppermute | solution.py:600
  45.5 2.8 %query_stage.1 = (bf16[16,64,256]{2,1,0:T(8,128)(2,1)S(1)}, f32[16,64,128]{2,1,0:T(8,128)S(1)}) custom-call(bf16[2,128,128]{2,1,0:T(8,128)(2,1)S(1)} %get-tuple-element.68.refs_0_, bf16[2,128,128]{2,1,0:T(8,128)(2,1)S(1)} %collective-permute-done.14.refs_1_, bf16[2,128,128]{2,1,0:T(8,128)(2,1)S(1)} %collective-permute-done.15.refs_2_, ...), custom_call_target="tpu_custom_call" | custom-call | flops 3000000000 | tf_op jit(solution)/shard_map/query_stage/pallas_call | solution.py:202
  48.4 2.3 %collective-permute-done.13.refs_3_ = f32[128,128]{1,0:T(8,128)S(1)} collective-permute-done((f32[128,128]{1,0:T(8,128)S(1)}, f32[128,128]{1,0:T(8,128)S(1)}, u32[]{:S(2)}, u32[]{:S(2)}) %collective-permute-start.13) | collective-permute-done | bytes 65568 | tf_op jit(solution)/shard_map/ppermute | solution.py:600
  50.6 0.5 read_states.1
  51.2 0.1 collective-permute-start.17
  51.2 1.3 %collective-permute-done.17.refs_1_ = bf16[128,512]{1,0:T(8,128)(2,1)S(1)} collective-permute-done((bf16[128,512]{1,0:T(8,128)(2,1)S(1)}, bf16[128,512]{1,0:T(8,128)(2,1)S(1)}, u32[]{:S(2)}, u32[]{:S(2)}) %collective-permute-start.17) | collective-permute-done | bytes 131104 | tf_op jit(solution)/shard_map/ppermute | solution.py:730
  52.6 0.7 %join.1 = bf16[128,1024]{1,0:T(8,128)(2,1)} custom-call(bf16[128,512]{1,0:T(8,128)(2,1)S(1)} %get-tuple-element.81.refs_0_, bf16[128,512]{1,0:T(8,128)(2,1)S(1)} %collective-permute-done.17.refs_1_), custom_call_target="tpu_custom_call" | custom-call | tf_op jit(solution)/shard_map/join/pallas_call | solution.py:202
  (18 shorter events, 0.1 us)
Async XLA Ops:
  0.0 8.6 %copy-start = (bf16[32,8192]{1,0:T(8,128)(2,1)S(1)}, bf16[32,8192]{1,0:T(8,128)(2,1)}, u32[]{:S(2)}) copy-start(bf16[32,8192]{1,0:T(8,128)(2,1)} %refs_0_.2) | copy-start | bytes 1572868
  1.6 9.6 %collective-permute-start.4 = (bf16[528,128]{1,0:T(8,128)(2,1)S(1)}, bf16[528,128]{1,0:T(8,128)(2,1)S(1)}, u32[]{:S(2)}, u32[]{:S(2)}) collective-permute-start(bf16[528,128]{1,0:T(8,128)(2,1)S(1)} %get-tuple-element.51), channel_id=1, source_target_pairs={{0,1},{1,2},{2,3},{3,0},{4,5},{5,6},{6,7},{7,4},{8,9},{9,10},{10,1... | collective-permute-start | bytes 405512 | tf_op jit(solution)/shard_map/ppermute | solution.py:724
  4.7 11.5 %collective-permute-start.5 = (bf16[528,128]{1,0:T(8,128)(2,1)S(1)}, bf16[528,128]{1,0:T(8,128)(2,1)S(1)}, u32[]{:S(2)}, u32[]{:S(2)}) collective-permute-start(bf16[528,128]{1,0:T(8,128)(2,1)S(1)} %get-tuple-element.52), channel_id=1, source_target_pairs={{0,2},{1,3},{2,0},{3,1},{4,6},{5,7},{6,4},{7,5},{8,10},{9,11},{10,... | collective-permute-start | bytes 405512 | tf_op jit(solution)/shard_map/ppermute | solution.py:724
  7.3 8.9 %collective-permute-start.6 = (bf16[528,128]{1,0:T(8,128)(2,1)S(1)}, bf16[528,128]{1,0:T(8,128)(2,1)S(1)}, u32[]{:S(2)}, u32[]{:S(2)}) collective-permute-start(bf16[528,128]{1,0:T(8,128)(2,1)S(1)} %get-tuple-element.53), channel_id=1, source_target_pairs={{0,3},{1,0},{2,1},{3,2},{4,7},{5,4},{6,5},{7,6},{8,11},{9,8},{10,9... | collective-permute-start | bytes 405512 | tf_op jit(solution)/shard_map/ppermute | solution.py:724
  8.7 1.0 %copy-start.1 = (bf16[32,4096]{1,0:T(8,128)(2,1)S(1)}, bf16[32,4096]{1,0:T(8,128)(2,1)}, u32[]{:S(2)}) copy-start(bf16[32,4096]{1,0:T(8,128)(2,1)} %refs_1_.2) | copy-start | bytes 786436
  9.8 6.5 %collective-permute-start = (bf16[4,384,128]{2,1,0:T(8,128)(2,1)S(1)}, bf16[4,384,128]{2,1,0:T(8,128)(2,1)S(1)}, u32[]{:S(2)}, u32[]{:S(2)}) collective-permute-start(bf16[4,384,128]{2,1,0:T(8,128)(2,1)S(1)} %get-tuple-element.45), channel_id=1, source_target_pairs={{0,4},{4,0},{1,5},{5,1},{2,6},{6,2},{3,7},{7,3},{8,12},{12,8},{9,1... | collective-permute-start | bytes 1179656 | tf_op jit(solution)/shard_map/ppermute | solution.py:730
  16.2 6.0 %collective-permute-start.7 = (bf16[4,272,128]{2,1,0:T(8,128)(2,1)S(1)}, bf16[4,272,128]{2,1,0:T(8,128)(2,1)S(1)}, u32[]{:S(2)}, u32[]{:S(2)}) collective-permute-start(bf16[4,272,128]{2,1,0:T(8,128)(2,1)S(1)} %swap_keys.1), channel_id=1, source_target_pairs={{0,4},{4,0},{1,5},{5,1},{2,6},{6,2},{3,7},{7,3},{8,12},{12,8},{9,1... | collective-permute-start | bytes 835592 | tf_op jit(solution)/shard_map/ppermute | solution.py:730
  16.4 13.0 %collective-permute-start.1 = (bf16[2,256,128]{2,1,0:T(8,128)(2,1)S(1)}, bf16[2,256,128]{2,1,0:T(8,128)(2,1)S(1)}, u32[]{:S(2)}, u32[]{:S(2)}) collective-permute-start(bf16[2,256,128]{2,1,0:T(8,128)(2,1)S(1)} %get-tuple-element.47), channel_id=1, source_target_pairs={{0,1},{1,2},{2,3},{3,0},{4,5},{5,6},{6,7},{7,4},{8,9},{9,10},{10,1... | collective-permute-start | bytes 393224 | tf_op jit(solution)/shard_map/ppermute | solution.py:724
  19.8 10.9 %collective-permute-start.2 = (bf16[2,256,128]{2,1,0:T(8,128)(2,1)S(1)}, bf16[2,256,128]{2,1,0:T(8,128)(2,1)S(1)}, u32[]{:S(2)}, u32[]{:S(2)}) collective-permute-start(bf16[2,256,128]{2,1,0:T(8,128)(2,1)S(1)} %get-tuple-element.48), channel_id=1, source_target_pairs={{0,2},{1,3},{2,0},{3,1},{4,6},{5,7},{6,4},{7,5},{8,10},{9,11},{10,... | collective-permute-start | bytes 393224 | tf_op jit(solution)/shard_map/ppermute | solution.py:724
  21.4 9.3 %collective-permute-start.3 = (bf16[2,256,128]{2,1,0:T(8,128)(2,1)S(1)}, bf16[2,256,128]{2,1,0:T(8,128)(2,1)S(1)}, u32[]{:S(2)}, u32[]{:S(2)}) collective-permute-start(bf16[2,256,128]{2,1,0:T(8,128)(2,1)S(1)} %get-tuple-element.49), channel_id=1, source_target_pairs={{0,3},{1,0},{2,1},{3,2},{4,7},{5,4},{6,5},{7,6},{8,11},{9,8},{10,9... | collective-permute-start | bytes 393224 | tf_op jit(solution)/shard_map/ppermute | solution.py:724
  31.5 8.2 %collective-permute-start.8 = (f32[2,128,128]{2,1,0:T(8,128)S(1)}, f32[2,128,128]{2,1,0:T(8,128)S(1)}, u32[]{:S(2)}, u32[]{:S(2)}) collective-permute-start(f32[2,128,128]{2,1,0:T(8,128)S(1)} %get-tuple-element.61), channel_id=1, source_target_pairs={{0,8},{8,0},{16,24},{24,16},{1,9},{9,1},{17,25},{25,17},{2,10},{10... | collective-permute-start | bytes 393224 | tf_op jit(solution)/shard_map/ppermute | solution.py:600
  33.1 8.2 %collective-permute-start.9 = (f32[2,128,128]{2,1,0:T(8,128)S(1)}, f32[2,128,128]{2,1,0:T(8,128)S(1)}, u32[]{:S(2)}, u32[]{:S(2)}) collective-permute-start(f32[2,128,128]{2,1,0:T(8,128)S(1)} %get-tuple-element.62), channel_id=1, source_target_pairs={{0,16},{8,24},{16,0},{24,8},{1,17},{9,25},{17,1},{25,9},{2,18},{10... | collective-permute-start | bytes 393224 | tf_op jit(solution)/shard_map/ppermute | solution.py:600
  34.6 6.7 %collective-permute-start.10 = (f32[2,128,128]{2,1,0:T(8,128)S(1)}, f32[2,128,128]{2,1,0:T(8,128)S(1)}, u32[]{:S(2)}, u32[]{:S(2)}) collective-permute-start(f32[2,128,128]{2,1,0:T(8,128)S(1)} %get-tuple-element.63), channel_id=1, source_target_pairs={{0,24},{8,16},{16,8},{24,0},{1,25},{9,17},{17,9},{25,1},{2,26},{10... | collective-permute-start | bytes 393224 | tf_op jit(solution)/shard_map/ppermute | solution.py:600
  35.1 10.4 %collective-permute-start.14 = (bf16[2,128,128]{2,1,0:T(8,128)(2,1)S(1)}, bf16[2,128,128]{2,1,0:T(8,128)(2,1)S(1)}, u32[]{:S(2)}, u32[]{:S(2)}) collective-permute-start(bf16[2,128,128]{2,1,0:T(8,128)(2,1)S(1)} %get-tuple-element.69), channel_id=1, source_target_pairs={{0,1},{1,2},{2,3},{3,0},{4,5},{5,6},{6,7},{7,4},{8,9},{9,10},{10,1... | collective-permute-start | bytes 196616 | tf_op jit(solution)/shard_map/ppermute | solution.py:724
  38.4 7.1 %collective-permute-start.15 = (bf16[2,128,128]{2,1,0:T(8,128)(2,1)S(1)}, bf16[2,128,128]{2,1,0:T(8,128)(2,1)S(1)}, u32[]{:S(2)}, u32[]{:S(2)}) collective-permute-start(bf16[2,128,128]{2,1,0:T(8,128)(2,1)S(1)} %get-tuple-element.70), channel_id=1, source_target_pairs={{0,2},{1,3},{2,0},{3,1},{4,6},{5,7},{6,4},{7,5},{8,10},{9,11},{10,... | collective-permute-start | bytes 196616 | tf_op jit(solution)/shard_map/ppermute | solution.py:724
  39.7 5.8 %collective-permute-start.16 = (bf16[2,128,128]{2,1,0:T(8,128)(2,1)S(1)}, bf16[2,128,128]{2,1,0:T(8,128)(2,1)S(1)}, u32[]{:S(2)}, u32[]{:S(2)}) collective-permute-start(bf16[2,128,128]{2,1,0:T(8,128)(2,1)S(1)} %get-tuple-element.71), channel_id=1, source_target_pairs={{0,3},{1,0},{2,1},{3,2},{4,7},{5,4},{6,5},{7,6},{8,11},{9,8},{10,9... | collective-permute-start | bytes 196616 | tf_op jit(solution)/shard_map/ppermute | solution.py:724
  41.7 6.7 %collective-permute-start.11 = (f32[128,128]{1,0:T(8,128)S(1)}, f32[128,128]{1,0:T(8,128)S(1)}, u32[]{:S(2)}, u32[]{:S(2)}) collective-permute-start(f32[128,128]{1,0:T(8,128)S(1)} %get-tuple-element.65), channel_id=1, source_target_pairs={{0,8},{8,0},{16,24},{24,16},{1,9},{9,1},{17,25},{25,17},{2,10},{10... | collective-permute-start | bytes 196616 | tf_op jit(solution)/shard_map/ppermute | solution.py:600
  43.9 4.4 %collective-permute-start.12 = (f32[128,128]{1,0:T(8,128)S(1)}, f32[128,128]{1,0:T(8,128)S(1)}, u32[]{:S(2)}, u32[]{:S(2)}) collective-permute-start(f32[128,128]{1,0:T(8,128)S(1)} %get-tuple-element.66), channel_id=1, source_target_pairs={{0,16},{8,24},{16,0},{24,8},{1,17},{9,25},{17,1},{25,9},{2,18},{10... | collective-permute-start | bytes 196616 | tf_op jit(solution)/shard_map/ppermute | solution.py:600
  45.5 5.2 %collective-permute-start.13 = (f32[128,128]{1,0:T(8,128)S(1)}, f32[128,128]{1,0:T(8,128)S(1)}, u32[]{:S(2)}, u32[]{:S(2)}) collective-permute-start(f32[128,128]{1,0:T(8,128)S(1)} %get-tuple-element.67), channel_id=1, source_target_pairs={{0,24},{8,16},{16,8},{24,0},{1,25},{9,17},{17,9},{25,1},{2,26},{10... | collective-permute-start | bytes 196616 | tf_op jit(solution)/shard_map/ppermute | solution.py:600
  51.2 1.4 %collective-permute-start.17 = (bf16[128,512]{1,0:T(8,128)(2,1)S(1)}, bf16[128,512]{1,0:T(8,128)(2,1)S(1)}, u32[]{:S(2)}, u32[]{:S(2)}) collective-permute-start(bf16[128,512]{1,0:T(8,128)(2,1)S(1)} %get-tuple-element.82), channel_id=1, source_target_pairs={{0,4},{4,0},{1,5},{5,1},{2,6},{6,2},{3,7},{7,3},{8,12},{12,8},{9,1... | collective-permute-start | bytes 393224 | tf_op jit(solution)/shard_map/ppermute | solution.py:730

commit v11 on v7

--- a/solution.py
+++ b/solution.py
@@ -219,7 +219,7 @@
         self.heads = group_heads // 2
         self.chips = chips
         self.units = self.heads * groups
-        self.swapped = chips == self.heads and chips & (chips - 1) == 0
+        self.swapped = chips == self.heads == 4
 
     def unit(self, number):
         return number // self.groups, number % self.groups
@@ -228,6 +228,14 @@
 def shifted(index, by, size):
     moved = index + by
     return jnp.where(moved >= size, moved - size, moved)
+
+
+def head_distance(core, number, groups):
+    return number if number == 0 else number + (groups - 2 * number) * core
+
+
+def chip_distance(core, number):
+    return number + (3 - 2 * number) * core if number in (1, 2) else number
 
 
 def block_columns(source, first, count):
@@ -271,13 +279,13 @@
         own_starts = jnp.broadcast_to(starts[...].astype(F32), (heads, length)).astype(BF16)
         pieces.append(dot(own_starts, own.astype(BF16)))
         scales = jnp.concatenate(pieces, 1).astype(BF16)
-        for ahead, out in enumerate(outs):
-            target = shifted(z, ahead, sizes.groups)
+        for number, out in enumerate(outs):
+            target = shifted(z, head_distance(core, number, sizes.groups), sizes.groups)
             for side in range(2):
                 owner = jnp.bitwise_xor(core, side)
                 first = ((target * 2 + owner) * sizes.heads) * NH * DK
-                for number, piece in enumerate(block_columns(keys, first, count)):
-                    at = side * rows + number * TOK
+                for part, piece in enumerate(block_columns(keys, first, count)):
+                    at = side * rows + part * TOK
                     out[at : at + TOK, :] = piece
             extent = (SCALE_ROWS, heads)
             pick = (iota(extent, 1) == target * sizes.group_heads + iota(extent, 0)) & (
@@ -304,8 +312,10 @@
     def kernel(*refs):
         out = refs[-1]
         z = axis_index("head")
-        for behind, piece in enumerate(refs[:-1]):
-            source = shifted(z, sizes.groups - behind, sizes.groups) if behind else z
+        core = axis_index("core")
+        for number, piece in enumerate(refs[:-1]):
+            behind = head_distance(core, number, sizes.groups)
+            source = shifted(z, sizes.groups - behind, sizes.groups)
             out[source] = piece[rows:, :]
 
     return call(kernel, shape(sizes.groups, rows + SCALE_ROWS, DK), *arrived, name="swap_keys")
@@ -319,9 +329,10 @@
         z = axis_index("head")
         core = axis_index("core")
         for ahead in range(sizes.groups):
-            target = shifted(z, ahead, sizes.groups)
             for side, out in enumerate((kept, sent)):
-                first = (target * 2 + jnp.bitwise_xor(core, side)) * sizes.heads * DK
+                owner = jnp.bitwise_xor(core, side)
+                target = shifted(z, head_distance(owner, ahead, sizes.groups), sizes.groups)
+                first = (target * 2 + owner) * sizes.heads * DK
                 pieces = block_columns(values, first * NH, sizes.heads * NH)
                 pieces += block_columns(queries, first, sizes.heads)
                 for number, piece in enumerate(pieces):
@@ -350,8 +361,9 @@
 def gather(sizes, pieces, scratch):
     z = axis_index("head")
     core = axis_index("core")
-    for behind, piece in enumerate(pieces):
-        source = shifted(z, sizes.groups - behind, sizes.groups) if behind else z
+    for number, piece in enumerate(pieces):
+        behind = head_distance(core, number, sizes.groups)
+        source = shifted(z, sizes.groups - behind, sizes.groups)
         for side in range(2):
             scratch[jnp.bitwise_xor(core, side) * sizes.groups + source] = piece[side]
 
@@ -382,8 +394,8 @@
         blocks, scales, every = refs[groups + 8 + sizes.heads :]
         z = axis_index("head")
         core = axis_index("core")
-        for behind, piece in enumerate(pieces):
-            source = shifted(z, groups - behind, groups) if behind else z
+        for number, piece in enumerate(pieces):
+            source = shifted(z, groups - head_distance(core, number, groups), groups)
             blocks[core * groups + source] = piece[:rows, :]
             scales[core * groups + source] = piece[2 * rows :, :]
         other = (1 - core) * groups
@@ -480,8 +492,9 @@
             for head in range(sizes.heads):
                 every[head] = prefixes[head]
             chip = axis_index("chip")
+            core = axis_index("core")
             for number in range(sizes.heads):
-                totals[number][...] = every[jnp.bitwise_xor(chip, number)]
+                totals[number][...] = every[jnp.bitwise_xor(chip, chip_distance(core, number))]
         else:
             for head in range(sizes.heads):
                 totals[head][...] = prefixes[head]
@@ -537,8 +550,9 @@
             for head in range(sizes.heads):
                 every[head] = sums[head]
             chip = axis_index("chip")
+            core = axis_index("core")
             for number in range(sizes.heads):
-                totals[number][...] = every[jnp.bitwise_xor(chip, number)]
+                totals[number][...] = every[jnp.bitwise_xor(chip, chip_distance(core, number))]
         else:
             for head in range(sizes.heads):
                 totals[head][...] = sums[head]
@@ -564,8 +578,9 @@
         outs = refs[2 * chips : 3 * chips]
         step, inject, entry = refs[3 * chips :]
         chip = axis_index("chip")
+        core = axis_index("core")
         for number in range(chips):
-            source = jnp.bitwise_xor(chip, number)
+            source = jnp.bitwise_xor(chip, chip_distance(core, number))
             step[source] = transitions[number][...]
             inject[source] = injects[number][...]
         state = jnp.zeros((DV, DK), F32)
@@ -576,7 +591,7 @@
             elif index < chips - 1:
                 state = product(beside(state), factor(step[index])) + inject[index]
         for number in range(chips):
-            outs[number][...] = entry[jnp.bitwise_xor(chip, number)]
+            outs[number][...] = entry[jnp.bitwise_xor(chip, chip_distance(core, number))]
 
     scratch = [pltpu.VMEM((chips, DV, DK), F32)] * 3
     return call(
@@ -590,11 +605,15 @@
 
 
 def exchanged(sizes, parts):
-    return [parts[0]] + [
-        lax.ppermute(part, "chip", [(chip, chip ^ number) for chip in range(sizes.chips)])
-        for number, part in enumerate(parts)
-        if number
-    ]
+    def moved(number, part):
+        pairs = [
+            (chip * 2 + core, (chip ^ chip_distance(core, number)) * 2 + core)
+            for chip in range(sizes.chips)
+            for core in range(2)
+        ]
+        return lax.ppermute(part, ("chip", "core"), pairs)
+
+    return [parts[0]] + [moved(number, part) for number, part in enumerate(parts) if number]
 
 
 def entry_states(sizes, transitions, injects):
@@ -675,7 +694,7 @@
         core = axis_index("core")
         chip = axis_index("chip") if sizes.swapped else 0
         for number in range(sizes.heads):
-            place_ = jnp.bitwise_xor(chip, number) if sizes.swapped else number
+            place_ = jnp.bitwise_xor(chip, chip_distance(core, number)) if sizes.swapped else number
             entry[place_] = states[number][...]
         for head in range(sizes.heads):
             high, low = split(entry[head])
@@ -714,12 +733,16 @@
     groups = lax.axis_size("head")
     sizes = Sizes(groups, log_gates.shape[1] // groups, lax.axis_size("chip"))
 
+    def moved(number, part):
+        pairs = [
+            (core * groups + z, core * groups + (z + head_distance(core, number, groups)) % groups)
+            for core in range(2)
+            for z in range(groups)
+        ]
+        return lax.ppermute(part, ("core", "head"), pairs)
+
     def spread(parts):
-        return [parts[0]] + [
-            lax.ppermute(part, "head", [(z, (z + ahead) % groups) for z in range(groups)])
-            for ahead, part in enumerate(parts)
-            if ahead
-        ]
+        return [parts[0]] + [moved(number, part) for number, part in enumerate(parts) if number]
 
     def swapped(part):
         return lax.ppermute(part, "core", [(0, 1), (1, 0)])

time: 52.9 us -> 54.5 us (1.030)
  waiting for transfers between devices: 9.3 us -> 10.1 us
  starting transfers between devices: 28.1 us -> 28.9 us
    ppermute x18, waiting for transfers between devices: 7.96 us -> 8.75 us  [the longest x9 7.21 us: moved(): return lax.ppermute(part, ('core', 'head'), pairs)]
  transfers between devices with their start and end apart: 21 -> 21, of which waited for: 5 -> 5; matrix products, arithmetic and copies ran while one was open for 0% -> 0% of each run, Pallas kernels for 22% -> 21%
where the time goes in v11:
time: 54.5 us; the launch traced here: 54.3 us
  starting transfers between devices  28.9 us (53%)
  Pallas kernels  14.3 us (26%)
  waiting for transfers between devices  10.1 us (19%)
  local copies, waits for them, and re-layouts  0.95 us (2%)
    ppermute x9, starting transfers between devices, moved(): return lax.ppermute(part, ('core', 'head'), pairs)  17.2 us
    pallas_call x10, Pallas kernels, call(): pl.pallas_call(kernel, out_shape=outs, in_specs=specs, scratch_shapes=scr...  14.3 us
    ppermute x9, starting transfers between devices, moved(): return lax.ppermute(part, ('chip', 'core'), pairs)  11 us
    ppermute x9, waiting for transfers between devices, moved(): return lax.ppermute(part, ('core', 'head'), pairs)  7.21 us
    ppermute x9, waiting for transfers between devices, moved(): return lax.ppermute(part, ('chip', 'core'), pairs)  1.53 us
    ppermute x3, waiting for transfers between devices, swapped(): return lax.ppermute(part, 'core', [(0, 1), (1, 0)])  1.34 us
  transfers between devices with their start and end apart: 21, of which 5 were waited for; matrix products, arithmetic and copies ran while one was open for 0% of the time, Pallas kernels for 21%

profile of v11, /device:TPU:0, one launch (start us, length us, event | category | flops | bytes accessed | tf_op | source)
XLA Modules:
  0.0 54.3 jit_solution(1243258624753920520)
XLA Ops:
  0.0 1.6 %pack_keys.1 = (bf16[528,128]{1,0:T(8,128)(2,1)S(1)}, bf16[528,128]{1,0:T(8,128)(2,1)S(1)}, bf16[528,128]{1,0:T(8,128)(2,1)S(1)}, bf16[528,128]{1,0:T(8,128)(2,1)S(1)}) custom-call(bf16[32,8192]{1,0:T(8,128)(2,1)} %far_keys.1, bf16[32,64]{1,0:T(8,128)(2,1)} %far_betas.1, bf16[32,32]{1,0:T(8,128)(2,1)} %far_gates.1, s32[1,128]{1,0:T(1,128)} %bitcast.1), custom_call_target="tpu_custom_call" | custom-call | tf_op jit(solution)/shard_map/pack_keys/pallas_call | solution.py:196
  1.6 3.1 %collective-permute-start = (bf16[528,128]{1,0:T(8,128)(2,1)S(1)}, bf16[528,128]{1,0:T(8,128)(2,1)S(1)}, u32[]{:S(2)}, u32[]{:S(2)}) collective-permute-start(bf16[528,128]{1,0:T(8,128)(2,1)S(1)} %get-tuple-element.45), channel_id=1, source_target_pairs={{0,1},{1,2},{2,3},{3,0},{4,7},{5,4},{6,5},{7,6},{8,9},{9,10},{10,1... | collective-permute-start | bytes 405512 | tf_op jit(solution)/shard_map/ppermute | solution.py:742
  4.7 2.6 %collective-permute-start.1 = (bf16[528,128]{1,0:T(8,128)(2,1)S(1)}, bf16[528,128]{1,0:T(8,128)(2,1)S(1)}, u32[]{:S(2)}, u32[]{:S(2)}) collective-permute-start(bf16[528,128]{1,0:T(8,128)(2,1)S(1)} %get-tuple-element.46), channel_id=1, source_target_pairs={{0,2},{1,3},{2,0},{3,1},{4,6},{5,7},{6,4},{7,5},{8,10},{9,11},{10,... | collective-permute-start | bytes 405512 | tf_op jit(solution)/shard_map/ppermute | solution.py:742
  7.3 1.3 %collective-permute-start.2 = (bf16[528,128]{1,0:T(8,128)(2,1)S(1)}, bf16[528,128]{1,0:T(8,128)(2,1)S(1)}, u32[]{:S(2)}, u32[]{:S(2)}) collective-permute-start(bf16[528,128]{1,0:T(8,128)(2,1)S(1)} %get-tuple-element.47), channel_id=1, source_target_pairs={{0,3},{1,0},{2,1},{3,2},{4,5},{5,6},{6,7},{7,4},{8,11},{9,8},{10,9... | collective-permute-start | bytes 405512 | tf_op jit(solution)/shard_map/ppermute | solution.py:742
  8.7 0.9 %copy-done.1 = bf16[32,4096]{1,0:T(8,128)(2,1)S(1)} copy-done((bf16[32,4096]{1,0:T(8,128)(2,1)S(1)}, bf16[32,4096]{1,0:T(8,128)(2,1)}, u32[]{:S(2)}) %copy-start.1) | copy-done | bytes 262168
  9.9 1.3 %collective-permute-done.refs_1_ = bf16[528,128]{1,0:T(8,128)(2,1)S(1)} collective-permute-done((bf16[528,128]{1,0:T(8,128)(2,1)S(1)}, bf16[528,128]{1,0:T(8,128)(2,1)S(1)}, u32[]{:S(2)}, u32[]{:S(2)}) %collective-permute-start) | collective-permute-done | bytes 135200 | tf_op jit(solution)/shard_map/ppermute | solution.py:742
  11.2 5.9 %collective-permute-done.1.refs_2_ = bf16[528,128]{1,0:T(8,128)(2,1)S(1)} collective-permute-done((bf16[528,128]{1,0:T(8,128)(2,1)S(1)}, bf16[528,128]{1,0:T(8,128)(2,1)S(1)}, u32[]{:S(2)}, u32[]{:S(2)}) %collective-permute-start.1) | collective-permute-done | bytes 135200 | tf_op jit(solution)/shard_map/ppermute | solution.py:742
  17.1 0.5 collective-permute-start.3
  17.7 2.0 %collective-permute-start.8 = (bf16[2,256,128]{2,1,0:T(8,128)(2,1)S(1)}, bf16[2,256,128]{2,1,0:T(8,128)(2,1)S(1)}, u32[]{:S(2)}, u32[]{:S(2)}) collective-permute-start(bf16[2,256,128]{2,1,0:T(8,128)(2,1)S(1)} %get-tuple-element.55), channel_id=1, source_target_pairs={{0,1},{1,2},{2,3},{3,0},{4,7},{5,4},{6,5},{7,6},{8,9},{9,10},{10,1... | collective-permute-start | bytes 393224 | tf_op jit(solution)/shard_map/ppermute | solution.py:742
  19.7 2.9 %collective-permute-start.9 = (bf16[2,256,128]{2,1,0:T(8,128)(2,1)S(1)}, bf16[2,256,128]{2,1,0:T(8,128)(2,1)S(1)}, u32[]{:S(2)}, u32[]{:S(2)}) collective-permute-start(bf16[2,256,128]{2,1,0:T(8,128)(2,1)S(1)} %get-tuple-element.56), channel_id=1, source_target_pairs={{0,2},{1,3},{2,0},{3,1},{4,6},{5,7},{6,4},{7,5},{8,10},{9,11},{10,... | collective-permute-start | bytes 393224 | tf_op jit(solution)/shard_map/ppermute | solution.py:742
  22.5 1.3 %collective-permute-start.10 = (bf16[2,256,128]{2,1,0:T(8,128)(2,1)S(1)}, bf16[2,256,128]{2,1,0:T(8,128)(2,1)S(1)}, u32[]{:S(2)}, u32[]{:S(2)}) collective-permute-start(bf16[2,256,128]{2,1,0:T(8,128)(2,1)S(1)} %get-tuple-element.57), channel_id=1, source_target_pairs={{0,3},{1,0},{2,1},{3,2},{4,5},{5,6},{6,7},{7,4},{8,11},{9,8},{10,9... | collective-permute-start | bytes 393224 | tf_op jit(solution)/shard_map/ppermute | solution.py:742
  23.8 7.1 %key_stage.1 = (bf16[16,128,128]{2,1,0:T(8,128)(2,1)S(1)}, bf16[16,128,256]{2,1,0:T(8,128)(2,1)S(1)}, bf16[16,128,256]{2,1,0:T(8,128)(2,1)S(1)}, f32[16,64,128]{...) custom-call(bf16[528,128]{1,0:T(8,128)(2,1)S(1)} %get-tuple-element., ...), custom_call_target="tpu_custom_call" | custom-call | flops 6000000000 | tf_op jit(solution)/shard_map/key_stage/pallas_call | solution.py:196
  31.0 1.6 %collective-permute-start.4 = (f32[128,128]{1,0:T(8,128)S(1)}, f32[128,128]{1,0:T(8,128)S(1)}, u32[]{:S(2)}, u32[]{:S(2)}) collective-permute-start(f32[128,128]{1,0:T(8,128)S(1)} %get-tuple-element.49), channel_id=1, source_target_pairs={{0,8},{4,20},{8,0},{12,28},{16,24},{20,4},{24,16},{28,12},{1,9},{5... | collective-permute-start | bytes 196616 | tf_op jit(solution)/shard_map/ppermute | solution.py:614
  32.5 1.5 %collective-permute-start.5 = (f32[128,128]{1,0:T(8,128)S(1)}, f32[128,128]{1,0:T(8,128)S(1)}, u32[]{:S(2)}, u32[]{:S(2)}) collective-permute-start(f32[128,128]{1,0:T(8,128)S(1)} %get-tuple-element.50), channel_id=1, source_target_pairs={{0,16},{4,12},{8,24},{12,4},{16,0},{20,28},{24,8},{28,20},{1,17},{... | collective-permute-start | bytes 196616 | tf_op jit(solution)/shard_map/ppermute | solution.py:614
  34.1 0.5 collective-permute-start.6
  34.6 0.8 %value_stage.1 = (bf16[16,128,128]{2,1,0:T(8,128)(2,1)S(1)}, f32[16,128,128]{2,1,0:T(8,128)S(1)}, f32[128,128]{1,0:T(8,128)S(1)}, f32[128,128]{1,0:T(8,128)S(1)}...) custom-call(bf16[2,256,128]{2,1,0:T(8,128)(2,1)S(1)} %get-tuple-element.54.refs_0_, ...), custom_call_target="tpu_custom_call" | custom-call | flops 2000000000 | tf_op jit(solution)/shard_map/value_stage/pallas_call | solution.py:196
  35.4 1.6 %collective-permute-start.11 = (f32[128,128]{1,0:T(8,128)S(1)}, f32[128,128]{1,0:T(8,128)S(1)}, u32[]{:S(2)}, u32[]{:S(2)}) collective-permute-start(f32[128,128]{1,0:T(8,128)S(1)} %get-tuple-element.61), channel_id=1, source_target_pairs={{0,8},{4,20},{8,0},{12,28},{16,24},{20,4},{24,16},{28,12},{1,9},{5... | collective-permute-start | bytes 196616 | tf_op jit(solution)/shard_map/ppermute | solution.py:614
  36.9 1.5 %collective-permute-start.12 = (f32[128,128]{1,0:T(8,128)S(1)}, f32[128,128]{1,0:T(8,128)S(1)}, u32[]{:S(2)}, u32[]{:S(2)}) collective-permute-start(f32[128,128]{1,0:T(8,128)S(1)} %get-tuple-element.62), channel_id=1, source_target_pairs={{0,16},{4,12},{8,24},{12,4},{16,0},{20,28},{24,8},{28,20},{1,17},{... | collective-permute-start | bytes 196616 | tf_op jit(solution)/shard_map/ppermute | solution.py:614
  38.5 0.4 collective-permute-start.13
  38.9 0.7 %collective-permute-start.17 = (bf16[2,128,128]{2,1,0:T(8,128)(2,1)S(1)}, bf16[2,128,128]{2,1,0:T(8,128)(2,1)S(1)}, u32[]{:S(2)}, u32[]{:S(2)}) collective-permute-start(bf16[2,128,128]{2,1,0:T(8,128)(2,1)S(1)} %get-tuple-element.69), channel_id=1, source_target_pairs={{0,1},{1,2},{2,3},{3,0},{4,7},{5,4},{6,5},{7,6},{8,9},{9,10},{10,1... | collective-permute-start | bytes 196616 | tf_op jit(solution)/shard_map/ppermute | solution.py:742
  39.6 1.3 %collective-permute-start.18 = (bf16[2,128,128]{2,1,0:T(8,128)(2,1)S(1)}, bf16[2,128,128]{2,1,0:T(8,128)(2,1)S(1)}, u32[]{:S(2)}, u32[]{:S(2)}) collective-permute-start(bf16[2,128,128]{2,1,0:T(8,128)(2,1)S(1)} %get-tuple-element.70), channel_id=1, source_target_pairs={{0,2},{1,3},{2,0},{3,1},{4,6},{5,7},{6,4},{7,5},{8,10},{9,11},{10,... | collective-permute-start | bytes 196616 | tf_op jit(solution)/shard_map/ppermute | solution.py:742
  40.9 2.0 %collective-permute-start.19 = (bf16[2,128,128]{2,1,0:T(8,128)(2,1)S(1)}, bf16[2,128,128]{2,1,0:T(8,128)(2,1)S(1)}, u32[]{:S(2)}, u32[]{:S(2)}) collective-permute-start(bf16[2,128,128]{2,1,0:T(8,128)(2,1)S(1)} %get-tuple-element.71), channel_id=1, source_target_pairs={{0,3},{1,0},{2,1},{3,2},{4,5},{5,6},{6,7},{7,4},{8,11},{9,8},{10,9... | collective-permute-start | bytes 196616 | tf_op jit(solution)/shard_map/ppermute | solution.py:742
  43.0 0.6 %collective-permute-done.13.refs_7_ = f32[128,128]{1,0:T(8,128)S(1)} collective-permute-done((f32[128,128]{1,0:T(8,128)S(1)}, f32[128,128]{1,0:T(8,128)S(1)}, u32[]{:S(2)}, u32[]{:S(2)}) %collective-permute-start.13) | collective-permute-done | bytes 65568 | tf_op jit(solution)/shard_map/ppermute | solution.py:614
  43.6 0.4 scan_states.1
  44.0 0.9 %collective-permute-start.14 = (f32[128,128]{1,0:T(8,128)S(1)}, f32[128,128]{1,0:T(8,128)S(1)}, u32[]{:S(2)}, u32[]{:S(2)}) collective-permute-start(f32[128,128]{1,0:T(8,128)S(1)} %get-tuple-element.65), channel_id=1, source_target_pairs={{0,8},{4,20},{8,0},{12,28},{16,24},{20,4},{24,16},{28,12},{1,9},{5... | collective-permute-start | bytes 196616 | tf_op jit(solution)/shard_map/ppermute | solution.py:614
  44.9 1.6 %collective-permute-start.15 = (f32[128,128]{1,0:T(8,128)S(1)}, f32[128,128]{1,0:T(8,128)S(1)}, u32[]{:S(2)}, u32[]{:S(2)}) collective-permute-start(f32[128,128]{1,0:T(8,128)S(1)} %get-tuple-element.66), channel_id=1, source_target_pairs={{0,16},{4,12},{8,24},{12,4},{16,0},{20,28},{24,8},{28,20},{1,17},{... | collective-permute-start | bytes 196616 | tf_op jit(solution)/shard_map/ppermute | solution.py:614
  46.5 1.4 %collective-permute-start.16 = (f32[128,128]{1,0:T(8,128)S(1)}, f32[128,128]{1,0:T(8,128)S(1)}, u32[]{:S(2)}, u32[]{:S(2)}) collective-permute-start(f32[128,128]{1,0:T(8,128)S(1)} %get-tuple-element.67), channel_id=1, source_target_pairs={{0,24},{4,28},{8,16},{12,20},{16,8},{20,12},{24,0},{28,4},{1,25},{... | collective-permute-start | bytes 196616 | tf_op jit(solution)/shard_map/ppermute | solution.py:614
  47.9 2.8 %query_stage.1 = (bf16[16,64,256]{2,1,0:T(8,128)(2,1)S(1)}, f32[16,64,128]{2,1,0:T(8,128)S(1)}) custom-call(bf16[2,128,128]{2,1,0:T(8,128)(2,1)S(1)} %get-tuple-element.68.refs_0_, bf16[2,128,128]{2,1,0:T(8,128)(2,1)S(1)} %collective-permute-done.17.refs_1_, bf16[2,128,128]{2,1,0:T(8,128)(2,1)S(1)} %collective-permute-done.18.refs_2_, ...), custom_call_target="tpu_custom_call" | custom-call | flops 3000000000 | tf_op jit(solution)/shard_map/query_stage/pallas_call | solution.py:196
  50.8 0.9 %collective-permute-done.16.refs_3_ = f32[128,128]{1,0:T(8,128)S(1)} collective-permute-done((f32[128,128]{1,0:T(8,128)S(1)}, f32[128,128]{1,0:T(8,128)S(1)}, u32[]{:S(2)}, u32[]{:S(2)}) %collective-permute-start.16) | collective-permute-done | bytes 65568 | tf_op jit(solution)/shard_map/ppermute | solution.py:614
  51.7 0.5 read_states.1
  52.2 1.3 %collective-permute-done.20.other = bf16[128,512]{1,0:T(8,128)(2,1)S(1)} collective-permute-done((bf16[128,512]{1,0:T(8,128)(2,1)S(1)}, bf16[128,512]{1,0:T(8,128)(2,1)S(1)}, u32[]{:S(2)}, u32[]{:S(2)}) %collective-permute-start.20) | collective-permute-done | bytes 131104 | tf_op jit(solution)/shard_map/ppermute | solution.py:748
  53.6 0.7 %join.1 = bf16[128,1024]{1,0:T(8,128)(2,1)} custom-call(bf16[128,512]{1,0:T(8,128)(2,1)S(1)} %get-tuple-element.81.own, bf16[128,512]{1,0:T(8,128)(2,1)S(1)} %collective-permute-done.20.other), custom_call_target="tpu_custom_call" | custom-call | tf_op jit(solution)/shard_map/join/pallas_call | solution.py:196
  (24 shorter events, 0.5 us)
Async XLA Ops:
  0.0 8.7 %copy-start = (bf16[32,8192]{1,0:T(8,128)(2,1)S(1)}, bf16[32,8192]{1,0:T(8,128)(2,1)}, u32[]{:S(2)}) copy-start(bf16[32,8192]{1,0:T(8,128)(2,1)} %values.1) | copy-start | bytes 1572868
  1.6 9.6 %collective-permute-start = (bf16[528,128]{1,0:T(8,128)(2,1)S(1)}, bf16[528,128]{1,0:T(8,128)(2,1)S(1)}, u32[]{:S(2)}, u32[]{:S(2)}) collective-permute-start(bf16[528,128]{1,0:T(8,128)(2,1)S(1)} %get-tuple-element.45), channel_id=1, source_target_pairs={{0,1},{1,2},{2,3},{3,0},{4,7},{5,4},{6,5},{7,6},{8,9},{9,10},{10,1... | collective-permute-start | bytes 405512 | tf_op jit(solution)/shard_map/ppermute | solution.py:742
  4.7 12.4 %collective-permute-start.1 = (bf16[528,128]{1,0:T(8,128)(2,1)S(1)}, bf16[528,128]{1,0:T(8,128)(2,1)S(1)}, u32[]{:S(2)}, u32[]{:S(2)}) collective-permute-start(bf16[528,128]{1,0:T(8,128)(2,1)S(1)} %get-tuple-element.46), channel_id=1, source_target_pairs={{0,2},{1,3},{2,0},{3,1},{4,6},{5,7},{6,4},{7,5},{8,10},{9,11},{10,... | collective-permute-start | bytes 405512 | tf_op jit(solution)/shard_map/ppermute | solution.py:742
  7.3 9.8 %collective-permute-start.2 = (bf16[528,128]{1,0:T(8,128)(2,1)S(1)}, bf16[528,128]{1,0:T(8,128)(2,1)S(1)}, u32[]{:S(2)}, u32[]{:S(2)}) collective-permute-start(bf16[528,128]{1,0:T(8,128)(2,1)S(1)} %get-tuple-element.47), channel_id=1, source_target_pairs={{0,3},{1,0},{2,1},{3,2},{4,5},{5,6},{6,7},{7,4},{8,11},{9,8},{10,9... | collective-permute-start | bytes 405512 | tf_op jit(solution)/shard_map/ppermute | solution.py:742
  8.7 1.0 %copy-start.1 = (bf16[32,4096]{1,0:T(8,128)(2,1)S(1)}, bf16[32,4096]{1,0:T(8,128)(2,1)}, u32[]{:S(2)}) copy-start(bf16[32,4096]{1,0:T(8,128)(2,1)} %queries.1) | copy-start | bytes 786436
  9.8 7.8 %collective-permute-start.7 = (bf16[4,384,128]{2,1,0:T(8,128)(2,1)S(1)}, bf16[4,384,128]{2,1,0:T(8,128)(2,1)S(1)}, u32[]{:S(2)}, u32[]{:S(2)}) collective-permute-start(bf16[4,384,128]{2,1,0:T(8,128)(2,1)S(1)} %get-tuple-element.53), channel_id=1, source_target_pairs={{0,4},{4,0},{1,5},{5,1},{2,6},{6,2},{3,7},{7,3},{8,12},{12,8},{9,1... | collective-permute-start | bytes 1179656 | tf_op jit(solution)/shard_map/ppermute | solution.py:748
  17.1 6.7 %collective-permute-start.3 = (bf16[4,272,128]{2,1,0:T(8,128)(2,1)S(1)}, bf16[4,272,128]{2,1,0:T(8,128)(2,1)S(1)}, u32[]{:S(2)}, u32[]{:S(2)}) collective-permute-start(bf16[4,272,128]{2,1,0:T(8,128)(2,1)S(1)} %swap_keys.1), channel_id=1, source_target_pairs={{0,4},{4,0},{1,5},{5,1},{2,6},{6,2},{3,7},{7,3},{8,12},{12,8},{9,1... | collective-permute-start | bytes 835592 | tf_op jit(solution)/shard_map/ppermute | solution.py:748
  17.7 16.4 %collective-permute-start.8 = (bf16[2,256,128]{2,1,0:T(8,128)(2,1)S(1)}, bf16[2,256,128]{2,1,0:T(8,128)(2,1)S(1)}, u32[]{:S(2)}, u32[]{:S(2)}) collective-permute-start(bf16[2,256,128]{2,1,0:T(8,128)(2,1)S(1)} %get-tuple-element.55), channel_id=1, source_target_pairs={{0,1},{1,2},{2,3},{3,0},{4,7},{5,4},{6,5},{7,6},{8,9},{9,10},{10,1... | collective-permute-start | bytes 393224 | tf_op jit(solution)/shard_map/ppermute | solution.py:742
  19.7 14.9 %collective-permute-start.9 = (bf16[2,256,128]{2,1,0:T(8,128)(2,1)S(1)}, bf16[2,256,128]{2,1,0:T(8,128)(2,1)S(1)}, u32[]{:S(2)}, u32[]{:S(2)}) collective-permute-start(bf16[2,256,128]{2,1,0:T(8,128)(2,1)S(1)} %get-tuple-element.56), channel_id=1, source_target_pairs={{0,2},{1,3},{2,0},{3,1},{4,6},{5,7},{6,4},{7,5},{8,10},{9,11},{10,... | collective-permute-start | bytes 393224 | tf_op jit(solution)/shard_map/ppermute | solution.py:742
  22.5 12.0 %collective-permute-start.10 = (bf16[2,256,128]{2,1,0:T(8,128)(2,1)S(1)}, bf16[2,256,128]{2,1,0:T(8,128)(2,1)S(1)}, u32[]{:S(2)}, u32[]{:S(2)}) collective-permute-start(bf16[2,256,128]{2,1,0:T(8,128)(2,1)S(1)} %get-tuple-element.57), channel_id=1, source_target_pairs={{0,3},{1,0},{2,1},{3,2},{4,5},{5,6},{6,7},{7,4},{8,11},{9,8},{10,9... | collective-permute-start | bytes 393224 | tf_op jit(solution)/shard_map/ppermute | solution.py:742
  31.0 7.5 %collective-permute-start.4 = (f32[128,128]{1,0:T(8,128)S(1)}, f32[128,128]{1,0:T(8,128)S(1)}, u32[]{:S(2)}, u32[]{:S(2)}) collective-permute-start(f32[128,128]{1,0:T(8,128)S(1)} %get-tuple-element.49), channel_id=1, source_target_pairs={{0,8},{4,20},{8,0},{12,28},{16,24},{20,4},{24,16},{28,12},{1,9},{5... | collective-permute-start | bytes 196616 | tf_op jit(solution)/shard_map/ppermute | solution.py:614
  32.5 6.4 %collective-permute-start.5 = (f32[128,128]{1,0:T(8,128)S(1)}, f32[128,128]{1,0:T(8,128)S(1)}, u32[]{:S(2)}, u32[]{:S(2)}) collective-permute-start(f32[128,128]{1,0:T(8,128)S(1)} %get-tuple-element.50), channel_id=1, source_target_pairs={{0,16},{4,12},{8,24},{12,4},{16,0},{20,28},{24,8},{28,20},{1,17},{... | collective-permute-start | bytes 196616 | tf_op jit(solution)/shard_map/ppermute | solution.py:614
  34.1 5.6 %collective-permute-start.6 = (f32[128,128]{1,0:T(8,128)S(1)}, f32[128,128]{1,0:T(8,128)S(1)}, u32[]{:S(2)}, u32[]{:S(2)}) collective-permute-start(f32[128,128]{1,0:T(8,128)S(1)} %get-tuple-element.51), channel_id=1, source_target_pairs={{0,24},{4,28},{8,16},{12,20},{16,8},{20,12},{24,0},{28,4},{1,25},{... | collective-permute-start | bytes 196616 | tf_op jit(solution)/shard_map/ppermute | solution.py:614
  35.4 5.6 %collective-permute-start.11 = (f32[128,128]{1,0:T(8,128)S(1)}, f32[128,128]{1,0:T(8,128)S(1)}, u32[]{:S(2)}, u32[]{:S(2)}) collective-permute-start(f32[128,128]{1,0:T(8,128)S(1)} %get-tuple-element.61), channel_id=1, source_target_pairs={{0,8},{4,20},{8,0},{12,28},{16,24},{20,4},{24,16},{28,12},{1,9},{5... | collective-permute-start | bytes 196616 | tf_op jit(solution)/shard_map/ppermute | solution.py:614
  36.9 6.1 %collective-permute-start.12 = (f32[128,128]{1,0:T(8,128)S(1)}, f32[128,128]{1,0:T(8,128)S(1)}, u32[]{:S(2)}, u32[]{:S(2)}) collective-permute-start(f32[128,128]{1,0:T(8,128)S(1)} %get-tuple-element.62), channel_id=1, source_target_pairs={{0,16},{4,12},{8,24},{12,4},{16,0},{20,28},{24,8},{28,20},{1,17},{... | collective-permute-start | bytes 196616 | tf_op jit(solution)/shard_map/ppermute | solution.py:614
  38.5 5.2 %collective-permute-start.13 = (f32[128,128]{1,0:T(8,128)S(1)}, f32[128,128]{1,0:T(8,128)S(1)}, u32[]{:S(2)}, u32[]{:S(2)}) collective-permute-start(f32[128,128]{1,0:T(8,128)S(1)} %get-tuple-element.63), channel_id=1, source_target_pairs={{0,24},{4,28},{8,16},{12,20},{16,8},{20,12},{24,0},{28,4},{1,25},{... | collective-permute-start | bytes 196616 | tf_op jit(solution)/shard_map/ppermute | solution.py:614
  38.9 7.6 %collective-permute-start.17 = (bf16[2,128,128]{2,1,0:T(8,128)(2,1)S(1)}, bf16[2,128,128]{2,1,0:T(8,128)(2,1)S(1)}, u32[]{:S(2)}, u32[]{:S(2)}) collective-permute-start(bf16[2,128,128]{2,1,0:T(8,128)(2,1)S(1)} %get-tuple-element.69), channel_id=1, source_target_pairs={{0,1},{1,2},{2,3},{3,0},{4,7},{5,4},{6,5},{7,6},{8,9},{9,10},{10,1... | collective-permute-start | bytes 196616 | tf_op jit(solution)/shard_map/ppermute | solution.py:742
  39.6 8.3 %collective-permute-start.18 = (bf16[2,128,128]{2,1,0:T(8,128)(2,1)S(1)}, bf16[2,128,128]{2,1,0:T(8,128)(2,1)S(1)}, u32[]{:S(2)}, u32[]{:S(2)}) collective-permute-start(bf16[2,128,128]{2,1,0:T(8,128)(2,1)S(1)} %get-tuple-element.70), channel_id=1, source_target_pairs={{0,2},{1,3},{2,0},{3,1},{4,6},{5,7},{6,4},{7,5},{8,10},{9,11},{10,... | collective-permute-start | bytes 196616 | tf_op jit(solution)/shard_map/ppermute | solution.py:742
  40.9 7.0 %collective-permute-start.19 = (bf16[2,128,128]{2,1,0:T(8,128)(2,1)S(1)}, bf16[2,128,128]{2,1,0:T(8,128)(2,1)S(1)}, u32[]{:S(2)}, u32[]{:S(2)}) collective-permute-start(bf16[2,128,128]{2,1,0:T(8,128)(2,1)S(1)} %get-tuple-element.71), channel_id=1, source_target_pairs={{0,3},{1,0},{2,1},{3,2},{4,5},{5,6},{6,7},{7,4},{8,11},{9,8},{10,9... | collective-permute-start | bytes 196616 | tf_op jit(solution)/shard_map/ppermute | solution.py:742
  44.0 6.8 %collective-permute-start.14 = (f32[128,128]{1,0:T(8,128)S(1)}, f32[128,128]{1,0:T(8,128)S(1)}, u32[]{:S(2)}, u32[]{:S(2)}) collective-permute-start(f32[128,128]{1,0:T(8,128)S(1)} %get-tuple-element.65), channel_id=1, source_target_pairs={{0,8},{4,20},{8,0},{12,28},{16,24},{20,4},{24,16},{28,12},{1,9},{5... | collective-permute-start | bytes 196616 | tf_op jit(solution)/shard_map/ppermute | solution.py:614
  44.9 5.9 %collective-permute-start.15 = (f32[128,128]{1,0:T(8,128)S(1)}, f32[128,128]{1,0:T(8,128)S(1)}, u32[]{:S(2)}, u32[]{:S(2)}) collective-permute-start(f32[128,128]{1,0:T(8,128)S(1)} %get-tuple-element.66), channel_id=1, source_target_pairs={{0,16},{4,12},{8,24},{12,4},{16,0},{20,28},{24,8},{28,20},{1,17},{... | collective-permute-start | bytes 196616 | tf_op jit(solution)/shard_map/ppermute | solution.py:614
  46.5 5.2 %collective-permute-start.16 = (f32[128,128]{1,0:T(8,128)S(1)}, f32[128,128]{1,0:T(8,128)S(1)}, u32[]{:S(2)}, u32[]{:S(2)}) collective-permute-start(f32[128,128]{1,0:T(8,128)S(1)} %get-tuple-element.67), channel_id=1, source_target_pairs={{0,24},{4,28},{8,16},{12,20},{16,8},{20,12},{24,0},{28,4},{1,25},{... | collective-permute-start | bytes 196616 | tf_op jit(solution)/shard_map/ppermute | solution.py:614
  52.2 1.4 %collective-permute-start.20 = (bf16[128,512]{1,0:T(8,128)(2,1)S(1)}, bf16[128,512]{1,0:T(8,128)(2,1)S(1)}, u32[]{:S(2)}, u32[]{:S(2)}) collective-permute-start(bf16[128,512]{1,0:T(8,128)(2,1)S(1)} %get-tuple-element.82), channel_id=1, source_target_pairs={{0,4},{4,0},{1,5},{5,1},{2,6},{6,2},{3,7},{7,3},{8,12},{12,8},{9,1... | collective-permute-start | bytes 393224 | tf_op jit(solution)/shard_map/ppermute | solution.py:748

commit v12 on v7

--- a/solution.py
+++ b/solution.py
@@ -589,9 +589,17 @@
     )
 
 
-def exchanged(sizes, parts):
+def exchanged(sizes, parts, needed):
     return [parts[0]] + [
-        lax.ppermute(part, "chip", [(chip, chip ^ number) for chip in range(sizes.chips)])
+        lax.ppermute(
+            part,
+            "chip",
+            [
+                (chip, chip ^ number)
+                for chip in range(sizes.chips)
+                if needed(chip, chip ^ number)
+            ],
+        )
         for number, part in enumerate(parts)
         if number
     ]
@@ -599,8 +607,11 @@
 
 def entry_states(sizes, transitions, injects):
     if sizes.swapped:
-        arrived = exchanged(sizes, transitions), exchanged(sizes, injects)
-        return exchanged(sizes, scan_states(sizes, *arrived))
+        last = sizes.chips - 1
+        transitions = exchanged(sizes, transitions, lambda source, _: 0 < source < last)
+        injects = exchanged(sizes, injects, lambda source, _: source < last)
+        entries = scan_states(sizes, transitions, injects)
+        return exchanged(sizes, entries, lambda _, target: target > 0)
     transition = jnp.stack(transitions)
     inject = jnp.stack(injects)
     forward = [(chip, chip + 1) for chip in range(sizes.chips - 1)]

time: 52.9 us -> 66.4 us (1.26)
  starting transfers between devices: 28.1 us -> 42.7 us
  waiting for transfers between devices: 9.3 us -> 7.7 us
    ppermute x9, starting transfers between devices: 10.7 us -> 25.7 us  [exchanged(): lax.ppermute(part, 'chip', [(chip, chip ^ number) for chip in range(sizes...]
    ppermute x9, waiting for transfers between devices: 1.63 us -> 0.02 us  [exchanged(): lax.ppermute(part, 'chip', [(chip, chip ^ number) for chip in range(sizes...]
  transfers between devices with their start and end apart: 21 -> 21, of which waited for: 5 -> 3; matrix products, arithmetic and copies ran while one was open for 0% -> 0% of each run, Pallas kernels for 22% -> 17%
where the time goes in v12:
time: 66.4 us; the launch traced here: 65.9 us
  starting transfers between devices  42.7 us (64%)
  Pallas kernels  14.3 us (22%)
  waiting for transfers between devices  7.7 us (12%)
  local copies, waits for them, and re-layouts  0.95 us (1%)
    ppermute x9, starting transfers between devices, exchanged(): lax.ppermute(part, 'chip', [(chip, chip ^ number) for chip in range(sizes...  25.7 us
    ppermute x9, starting transfers between devices, spread(): lax.ppermute(part, 'head', [(z, (z + ahead) % groups) for z in range(grou...  16.8 us
    pallas_call x10, Pallas kernels, call(): pl.pallas_call(kernel, out_shape=outs, in_specs=specs, scratch_shapes=scr...  14.3 us
    ppermute x9, waiting for transfers between devices, spread(): lax.ppermute(part, 'head', [(z, (z + ahead) % groups) for z in range(grou...  6.33 us
    ppermute x3, waiting for transfers between devices, swapped(): return lax.ppermute(part, 'core', [(0, 1), (1, 0)])  1.34 us
  transfers between devices with their start and end apart: 21, of which 3 were waited for; matrix products, arithmetic and copies ran while one was open for 0% of the time, Pallas kernels for 17%

profile of v12, /device:TPU:0, one launch (start us, length us, event | category | flops | bytes accessed | tf_op | source)
XLA Modules:
  0.0 65.9 jit_solution(18147361024180893361)
XLA Ops:
  0.0 1.6 %pack_keys.1 = (bf16[528,128]{1,0:T(8,128)(2,1)S(1)}, bf16[528,128]{1,0:T(8,128)(2,1)S(1)}, bf16[528,128]{1,0:T(8,128)(2,1)S(1)}, bf16[528,128]{1,0:T(8,128)(2,1)S(1)}) custom-call(bf16[32,8192]{1,0:T(8,128)(2,1)} %far_keys.1, bf16[32,64]{1,0:T(8,128)(2,1)} %far_betas.1, bf16[32,32]{1,0:T(8,128)(2,1)} %far_gates.1, s32[1,128]{1,0:T(1,128)} %bitcast.1), custom_call_target="tpu_custom_call" | custom-call | tf_op jit(solution)/shard_map/pack_keys/pallas_call | solution.py:196
  1.6 3.1 %collective-permute-start = (bf16[528,128]{1,0:T(8,128)(2,1)S(1)}, bf16[528,128]{1,0:T(8,128)(2,1)S(1)}, u32[]{:S(2)}, u32[]{:S(2)}) collective-permute-start(bf16[528,128]{1,0:T(8,128)(2,1)S(1)} %get-tuple-element.45), channel_id=1, source_target_pairs={{0,1},{1,2},{2,3},{3,0},{4,5},{5,6},{6,7},{7,4},{8,9},{9,10},{10,1... | collective-permute-start | bytes 405512 | tf_op jit(solution)/shard_map/ppermute | solution.py:730
  4.7 2.6 %collective-permute-start.1 = (bf16[528,128]{1,0:T(8,128)(2,1)S(1)}, bf16[528,128]{1,0:T(8,128)(2,1)S(1)}, u32[]{:S(2)}, u32[]{:S(2)}) collective-permute-start(bf16[528,128]{1,0:T(8,128)(2,1)S(1)} %get-tuple-element.46), channel_id=1, source_target_pairs={{0,2},{1,3},{2,0},{3,1},{4,6},{5,7},{6,4},{7,5},{8,10},{9,11},{10,... | collective-permute-start | bytes 405512 | tf_op jit(solution)/shard_map/ppermute | solution.py:730
  7.3 1.3 %collective-permute-start.2 = (bf16[528,128]{1,0:T(8,128)(2,1)S(1)}, bf16[528,128]{1,0:T(8,128)(2,1)S(1)}, u32[]{:S(2)}, u32[]{:S(2)}) collective-permute-start(bf16[528,128]{1,0:T(8,128)(2,1)S(1)} %get-tuple-element.47), channel_id=1, source_target_pairs={{0,3},{1,0},{2,1},{3,2},{4,7},{5,4},{6,5},{7,6},{8,11},{9,8},{10,9... | collective-permute-start | bytes 405512 | tf_op jit(solution)/shard_map/ppermute | solution.py:730
  8.7 0.9 %copy-done.1 = bf16[32,4096]{1,0:T(8,128)(2,1)S(1)} copy-done((bf16[32,4096]{1,0:T(8,128)(2,1)S(1)}, bf16[32,4096]{1,0:T(8,128)(2,1)}, u32[]{:S(2)}) %copy-start.1) | copy-done | bytes 262168
  9.6 0.2 pack_reads.1
  9.9 1.4 %collective-permute-done.refs_1_ = bf16[528,128]{1,0:T(8,128)(2,1)S(1)} collective-permute-done((bf16[528,128]{1,0:T(8,128)(2,1)S(1)}, bf16[528,128]{1,0:T(8,128)(2,1)S(1)}, u32[]{:S(2)}, u32[]{:S(2)}) %collective-permute-start) | collective-permute-done | bytes 135200 | tf_op jit(solution)/shard_map/ppermute | solution.py:730
  11.2 5.0 %collective-permute-done.1.refs_2_ = bf16[528,128]{1,0:T(8,128)(2,1)S(1)} collective-permute-done((bf16[528,128]{1,0:T(8,128)(2,1)S(1)}, bf16[528,128]{1,0:T(8,128)(2,1)S(1)}, u32[]{:S(2)}, u32[]{:S(2)}) %collective-permute-start.1) | collective-permute-done | bytes 135200 | tf_op jit(solution)/shard_map/ppermute | solution.py:730
  16.2 0.1 collective-permute-start.3
  16.4 3.4 %collective-permute-start.8 = (bf16[2,256,128]{2,1,0:T(8,128)(2,1)S(1)}, bf16[2,256,128]{2,1,0:T(8,128)(2,1)S(1)}, u32[]{:S(2)}, u32[]{:S(2)}) collective-permute-start(bf16[2,256,128]{2,1,0:T(8,128)(2,1)S(1)} %get-tuple-element.55), channel_id=1, source_target_pairs={{0,1},{1,2},{2,3},{3,0},{4,5},{5,6},{6,7},{7,4},{8,9},{9,10},{10,1... | collective-permute-start | bytes 393224 | tf_op jit(solution)/shard_map/ppermute | solution.py:730
  19.8 1.6 %collective-permute-start.9 = (bf16[2,256,128]{2,1,0:T(8,128)(2,1)S(1)}, bf16[2,256,128]{2,1,0:T(8,128)(2,1)S(1)}, u32[]{:S(2)}, u32[]{:S(2)}) collective-permute-start(bf16[2,256,128]{2,1,0:T(8,128)(2,1)S(1)} %get-tuple-element.56), channel_id=1, source_target_pairs={{0,2},{1,3},{2,0},{3,1},{4,6},{5,7},{6,4},{7,5},{8,10},{9,11},{10,... | collective-permute-start | bytes 393224 | tf_op jit(solution)/shard_map/ppermute | solution.py:730
  21.4 0.8 %collective-permute-start.10 = (bf16[2,256,128]{2,1,0:T(8,128)(2,1)S(1)}, bf16[2,256,128]{2,1,0:T(8,128)(2,1)S(1)}, u32[]{:S(2)}, u32[]{:S(2)}) collective-permute-start(bf16[2,256,128]{2,1,0:T(8,128)(2,1)S(1)} %get-tuple-element.57), channel_id=1, source_target_pairs={{0,3},{1,0},{2,1},{3,2},{4,7},{5,4},{6,5},{7,6},{8,11},{9,8},{10,9... | collective-permute-start | bytes 393224 | tf_op jit(solution)/shard_map/ppermute | solution.py:730
  22.3 7.1 %key_stage.1 = (bf16[16,128,128]{2,1,0:T(8,128)(2,1)S(1)}, bf16[16,128,256]{2,1,0:T(8,128)(2,1)S(1)}, bf16[16,128,256]{2,1,0:T(8,128)(2,1)S(1)}, f32[16,64,128]{...) custom-call(bf16[528,128]{1,0:T(8,128)(2,1)S(1)} %get-tuple-element., ...), custom_call_target="tpu_custom_call" | custom-call | flops 6000000000 | tf_op jit(solution)/shard_map/key_stage/pallas_call | solution.py:196
  29.4 1.3 %collective-permute-start.4 = (f32[128,128]{1,0:T(8,128)S(1)}, f32[128,128]{1,0:T(8,128)S(1)}, u32[]{:S(2)}, u32[]{:S(2)}) collective-permute-start(f32[128,128]{1,0:T(8,128)S(1)} %get-tuple-element.49), channel_id=1, source_target_pairs={{8,0},{16,24},{9,1},{17,25},{10,2},{18,26},{11,3},{19,27},{12,4},{... | collective-permute-start | bytes 196616 | tf_op jit(solution)/shard_map/ppermute | solution.py:594
  30.7 1.3 %collective-permute-start.5 = (f32[128,128]{1,0:T(8,128)S(1)}, f32[128,128]{1,0:T(8,128)S(1)}, u32[]{:S(2)}, u32[]{:S(2)}) collective-permute-start(f32[128,128]{1,0:T(8,128)S(1)} %get-tuple-element.50), channel_id=1, source_target_pairs={{8,24},{16,0},{9,25},{17,1},{10,26},{18,2},{11,27},{19,3},{12,28},... | collective-permute-start | bytes 196616 | tf_op jit(solution)/shard_map/ppermute | solution.py:594
  32.0 0.7 %collective-permute-start.6 = (f32[128,128]{1,0:T(8,128)S(1)}, f32[128,128]{1,0:T(8,128)S(1)}, u32[]{:S(2)}, u32[]{:S(2)}) collective-permute-start(f32[128,128]{1,0:T(8,128)S(1)} %get-tuple-element.51), channel_id=1, source_target_pairs={{8,16},{16,8},{9,17},{17,9},{10,18},{18,10},{11,19},{19,11},{12,20... | collective-permute-start | bytes 196616 | tf_op jit(solution)/shard_map/ppermute | solution.py:594
  32.7 0.8 %value_stage.1 = (bf16[16,128,128]{2,1,0:T(8,128)(2,1)S(1)}, f32[16,128,128]{2,1,0:T(8,128)S(1)}, f32[128,128]{1,0:T(8,128)S(1)}, f32[128,128]{1,0:T(8,128)S(1)}...) custom-call(bf16[2,256,128]{2,1,0:T(8,128)(2,1)S(1)} %get-tuple-element.54.refs_0_, ...), custom_call_target="tpu_custom_call" | custom-call | flops 2000000000 | tf_op jit(solution)/shard_map/value_stage/pallas_call | solution.py:196
  33.5 8.3 %collective-permute-start.11 = (f32[128,128]{1,0:T(8,128)S(1)}, f32[128,128]{1,0:T(8,128)S(1)}, u32[]{:S(2)}, u32[]{:S(2)}) collective-permute-start(f32[128,128]{1,0:T(8,128)S(1)} %get-tuple-element.61), channel_id=1, source_target_pairs={{0,8},{8,0},{16,24},{1,9},{9,1},{17,25},{2,10},{10,2},{18,26},{3,1... | collective-permute-start | bytes 196616 | tf_op jit(solution)/shard_map/ppermute | solution.py:594
  41.8 1.9 %collective-permute-start.12 = (f32[128,128]{1,0:T(8,128)S(1)}, f32[128,128]{1,0:T(8,128)S(1)}, u32[]{:S(2)}, u32[]{:S(2)}) collective-permute-start(f32[128,128]{1,0:T(8,128)S(1)} %get-tuple-element.62), channel_id=1, source_target_pairs={{0,16},{8,24},{16,0},{1,17},{9,25},{17,1},{2,18},{10,26},{18,2},{3... | collective-permute-start | bytes 196616 | tf_op jit(solution)/shard_map/ppermute | solution.py:594
  43.7 1.3 %collective-permute-start.13 = (f32[128,128]{1,0:T(8,128)S(1)}, f32[128,128]{1,0:T(8,128)S(1)}, u32[]{:S(2)}, u32[]{:S(2)}) collective-permute-start(f32[128,128]{1,0:T(8,128)S(1)} %get-tuple-element.63), channel_id=1, source_target_pairs={{0,24},{8,16},{16,8},{1,25},{9,17},{17,9},{2,26},{10,18},{18,10},{... | collective-permute-start | bytes 196616 | tf_op jit(solution)/shard_map/ppermute | solution.py:594
  45.0 1.3 %collective-permute-start.17 = (bf16[2,128,128]{2,1,0:T(8,128)(2,1)S(1)}, bf16[2,128,128]{2,1,0:T(8,128)(2,1)S(1)}, u32[]{:S(2)}, u32[]{:S(2)}) collective-permute-start(bf16[2,128,128]{2,1,0:T(8,128)(2,1)S(1)} %get-tuple-element.69), channel_id=1, source_target_pairs={{0,1},{1,2},{2,3},{3,0},{4,5},{5,6},{6,7},{7,4},{8,9},{9,10},{10,1... | collective-permute-start | bytes 196616 | tf_op jit(solution)/shard_map/ppermute | solution.py:730
  46.3 1.3 %collective-permute-start.18 = (bf16[2,128,128]{2,1,0:T(8,128)(2,1)S(1)}, bf16[2,128,128]{2,1,0:T(8,128)(2,1)S(1)}, u32[]{:S(2)}, u32[]{:S(2)}) collective-permute-start(bf16[2,128,128]{2,1,0:T(8,128)(2,1)S(1)} %get-tuple-element.70), channel_id=1, source_target_pairs={{0,2},{1,3},{2,0},{3,1},{4,6},{5,7},{6,4},{7,5},{8,10},{9,11},{10,... | collective-permute-start | bytes 196616 | tf_op jit(solution)/shard_map/ppermute | solution.py:730
  47.6 1.4 %collective-permute-start.19 = (bf16[2,128,128]{2,1,0:T(8,128)(2,1)S(1)}, bf16[2,128,128]{2,1,0:T(8,128)(2,1)S(1)}, u32[]{:S(2)}, u32[]{:S(2)}) collective-permute-start(bf16[2,128,128]{2,1,0:T(8,128)(2,1)S(1)} %get-tuple-element.71), channel_id=1, source_target_pairs={{0,3},{1,0},{2,1},{3,2},{4,7},{5,4},{6,5},{7,6},{8,11},{9,8},{10,9... | collective-permute-start | bytes 196616 | tf_op jit(solution)/shard_map/ppermute | solution.py:730
  49.0 0.4 scan_states.1
  49.3 6.0 %collective-permute-start.14 = (f32[128,128]{1,0:T(8,128)S(1)}, f32[128,128]{1,0:T(8,128)S(1)}, u32[]{:S(2)}, u32[]{:S(2)}) collective-permute-start(f32[128,128]{1,0:T(8,128)S(1)} %get-tuple-element.65), channel_id=1, source_target_pairs={{0,8},{16,24},{24,16},{1,9},{17,25},{25,17},{2,10},{18,26},{26,18}... | collective-permute-start | bytes 196616 | tf_op jit(solution)/shard_map/ppermute | solution.py:594
  55.3 1.6 %collective-permute-start.15 = (f32[128,128]{1,0:T(8,128)S(1)}, f32[128,128]{1,0:T(8,128)S(1)}, u32[]{:S(2)}, u32[]{:S(2)}) collective-permute-start(f32[128,128]{1,0:T(8,128)S(1)} %get-tuple-element.66), channel_id=1, source_target_pairs={{0,16},{8,24},{24,8},{1,17},{9,25},{25,9},{2,18},{10,26},{26,10},{... | collective-permute-start | bytes 196616 | tf_op jit(solution)/shard_map/ppermute | solution.py:594
  57.0 3.4 %collective-permute-start.16 = (f32[128,128]{1,0:T(8,128)S(1)}, f32[128,128]{1,0:T(8,128)S(1)}, u32[]{:S(2)}, u32[]{:S(2)}) collective-permute-start(f32[128,128]{1,0:T(8,128)S(1)} %get-tuple-element.67), channel_id=1, source_target_pairs={{0,24},{8,16},{16,8},{1,25},{9,17},{17,9},{2,26},{10,18},{18,10},{... | collective-permute-start | bytes 196616 | tf_op jit(solution)/shard_map/ppermute | solution.py:594
  60.4 2.8 %query_stage.1 = (bf16[16,64,256]{2,1,0:T(8,128)(2,1)S(1)}, f32[16,64,128]{2,1,0:T(8,128)S(1)}) custom-call(bf16[2,128,128]{2,1,0:T(8,128)(2,1)S(1)} %get-tuple-element.68.refs_0_, bf16[2,128,128]{2,1,0:T(8,128)(2,1)S(1)} %collective-permute-done.17.refs_1_, bf16[2,128,128]{2,1,0:T(8,128)(2,1)S(1)} %collective-permute-done.18.refs_2_, ...), custom_call_target="tpu_custom_call" | custom-call | flops 3000000000 | tf_op jit(solution)/shard_map/query_stage/pallas_call | solution.py:196
  63.3 0.5 read_states.1
  63.8 0.1 collective-permute-start.20
  63.9 1.3 %collective-permute-done.20.other = bf16[128,512]{1,0:T(8,128)(2,1)S(1)} collective-permute-done((bf16[128,512]{1,0:T(8,128)(2,1)S(1)}, bf16[128,512]{1,0:T(8,128)(2,1)S(1)}, u32[]{:S(2)}, u32[]{:S(2)}) %collective-permute-start.20) | collective-permute-done | bytes 131104 | tf_op jit(solution)/shard_map/ppermute | solution.py:736
  65.2 0.7 %join.1 = bf16[128,1024]{1,0:T(8,128)(2,1)} custom-call(bf16[128,512]{1,0:T(8,128)(2,1)S(1)} %get-tuple-element.81.own, bf16[128,512]{1,0:T(8,128)(2,1)S(1)} %collective-permute-done.20.other), custom_call_target="tpu_custom_call" | custom-call | tf_op jit(solution)/shard_map/join/pallas_call | solution.py:196
  (24 shorter events, 0.2 us)
Async XLA Ops:
  0.0 8.6 %copy-start = (bf16[32,8192]{1,0:T(8,128)(2,1)S(1)}, bf16[32,8192]{1,0:T(8,128)(2,1)}, u32[]{:S(2)}) copy-start(bf16[32,8192]{1,0:T(8,128)(2,1)} %values.1) | copy-start | bytes 1572868
  1.6 9.6 %collective-permute-start = (bf16[528,128]{1,0:T(8,128)(2,1)S(1)}, bf16[528,128]{1,0:T(8,128)(2,1)S(1)}, u32[]{:S(2)}, u32[]{:S(2)}) collective-permute-start(bf16[528,128]{1,0:T(8,128)(2,1)S(1)} %get-tuple-element.45), channel_id=1, source_target_pairs={{0,1},{1,2},{2,3},{3,0},{4,5},{5,6},{6,7},{7,4},{8,9},{9,10},{10,1... | collective-permute-start | bytes 405512 | tf_op jit(solution)/shard_map/ppermute | solution.py:730
  4.7 11.5 %collective-permute-start.1 = (bf16[528,128]{1,0:T(8,128)(2,1)S(1)}, bf16[528,128]{1,0:T(8,128)(2,1)S(1)}, u32[]{:S(2)}, u32[]{:S(2)}) collective-permute-start(bf16[528,128]{1,0:T(8,128)(2,1)S(1)} %get-tuple-element.46), channel_id=1, source_target_pairs={{0,2},{1,3},{2,0},{3,1},{4,6},{5,7},{6,4},{7,5},{8,10},{9,11},{10,... | collective-permute-start | bytes 405512 | tf_op jit(solution)/shard_map/ppermute | solution.py:730
  7.3 8.9 %collective-permute-start.2 = (bf16[528,128]{1,0:T(8,128)(2,1)S(1)}, bf16[528,128]{1,0:T(8,128)(2,1)S(1)}, u32[]{:S(2)}, u32[]{:S(2)}) collective-permute-start(bf16[528,128]{1,0:T(8,128)(2,1)S(1)} %get-tuple-element.47), channel_id=1, source_target_pairs={{0,3},{1,0},{2,1},{3,2},{4,7},{5,4},{6,5},{7,6},{8,11},{9,8},{10,9... | collective-permute-start | bytes 405512 | tf_op jit(solution)/shard_map/ppermute | solution.py:730
  8.7 1.0 %copy-start.1 = (bf16[32,4096]{1,0:T(8,128)(2,1)S(1)}, bf16[32,4096]{1,0:T(8,128)(2,1)}, u32[]{:S(2)}) copy-start(bf16[32,4096]{1,0:T(8,128)(2,1)} %queries.1) | copy-start | bytes 786436
  9.8 6.5 %collective-permute-start.7 = (bf16[4,384,128]{2,1,0:T(8,128)(2,1)S(1)}, bf16[4,384,128]{2,1,0:T(8,128)(2,1)S(1)}, u32[]{:S(2)}, u32[]{:S(2)}) collective-permute-start(bf16[4,384,128]{2,1,0:T(8,128)(2,1)S(1)} %get-tuple-element.53), channel_id=1, source_target_pairs={{0,4},{4,0},{1,5},{5,1},{2,6},{6,2},{3,7},{7,3},{8,12},{12,8},{9,1... | collective-permute-start | bytes 1179656 | tf_op jit(solution)/shard_map/ppermute | solution.py:736
  16.2 6.0 %collective-permute-start.3 = (bf16[4,272,128]{2,1,0:T(8,128)(2,1)S(1)}, bf16[4,272,128]{2,1,0:T(8,128)(2,1)S(1)}, u32[]{:S(2)}, u32[]{:S(2)}) collective-permute-start(bf16[4,272,128]{2,1,0:T(8,128)(2,1)S(1)} %swap_keys.1), channel_id=1, source_target_pairs={{0,4},{4,0},{1,5},{5,1},{2,6},{6,2},{3,7},{7,3},{8,12},{12,8},{9,1... | collective-permute-start | bytes 835592 | tf_op jit(solution)/shard_map/ppermute | solution.py:736
  16.4 15.6 %collective-permute-start.8 = (bf16[2,256,128]{2,1,0:T(8,128)(2,1)S(1)}, bf16[2,256,128]{2,1,0:T(8,128)(2,1)S(1)}, u32[]{:S(2)}, u32[]{:S(2)}) collective-permute-start(bf16[2,256,128]{2,1,0:T(8,128)(2,1)S(1)} %get-tuple-element.55), channel_id=1, source_target_pairs={{0,1},{1,2},{2,3},{3,0},{4,5},{5,6},{6,7},{7,4},{8,9},{9,10},{10,1... | collective-permute-start | bytes 393224 | tf_op jit(solution)/shard_map/ppermute | solution.py:730
  19.8 12.9 %collective-permute-start.9 = (bf16[2,256,128]{2,1,0:T(8,128)(2,1)S(1)}, bf16[2,256,128]{2,1,0:T(8,128)(2,1)S(1)}, u32[]{:S(2)}, u32[]{:S(2)}) collective-permute-start(bf16[2,256,128]{2,1,0:T(8,128)(2,1)S(1)} %get-tuple-element.56), channel_id=1, source_target_pairs={{0,2},{1,3},{2,0},{3,1},{4,6},{5,7},{6,4},{7,5},{8,10},{9,11},{10,... | collective-permute-start | bytes 393224 | tf_op jit(solution)/shard_map/ppermute | solution.py:730
  21.4 11.3 %collective-permute-start.10 = (bf16[2,256,128]{2,1,0:T(8,128)(2,1)S(1)}, bf16[2,256,128]{2,1,0:T(8,128)(2,1)S(1)}, u32[]{:S(2)}, u32[]{:S(2)}) collective-permute-start(bf16[2,256,128]{2,1,0:T(8,128)(2,1)S(1)} %get-tuple-element.57), channel_id=1, source_target_pairs={{0,3},{1,0},{2,1},{3,2},{4,7},{5,4},{6,5},{7,6},{8,11},{9,8},{10,9... | collective-permute-start | bytes 393224 | tf_op jit(solution)/shard_map/ppermute | solution.py:730
  29.4 14.3 %collective-permute-start.4 = (f32[128,128]{1,0:T(8,128)S(1)}, f32[128,128]{1,0:T(8,128)S(1)}, u32[]{:S(2)}, u32[]{:S(2)}) collective-permute-start(f32[128,128]{1,0:T(8,128)S(1)} %get-tuple-element.49), channel_id=1, source_target_pairs={{8,0},{16,24},{9,1},{17,25},{10,2},{18,26},{11,3},{19,27},{12,4},{... | collective-permute-start | bytes 196616 | tf_op jit(solution)/shard_map/ppermute | solution.py:594
  30.7 14.3 %collective-permute-start.5 = (f32[128,128]{1,0:T(8,128)S(1)}, f32[128,128]{1,0:T(8,128)S(1)}, u32[]{:S(2)}, u32[]{:S(2)}) collective-permute-start(f32[128,128]{1,0:T(8,128)S(1)} %get-tuple-element.50), channel_id=1, source_target_pairs={{8,24},{16,0},{9,25},{17,1},{10,26},{18,2},{11,27},{19,3},{12,28},... | collective-permute-start | bytes 196616 | tf_op jit(solution)/shard_map/ppermute | solution.py:594
  32.0 14.3 %collective-permute-start.6 = (f32[128,128]{1,0:T(8,128)S(1)}, f32[128,128]{1,0:T(8,128)S(1)}, u32[]{:S(2)}, u32[]{:S(2)}) collective-permute-start(f32[128,128]{1,0:T(8,128)S(1)} %get-tuple-element.51), channel_id=1, source_target_pairs={{8,16},{16,8},{9,17},{17,9},{10,18},{18,10},{11,19},{19,11},{12,20... | collective-permute-start | bytes 196616 | tf_op jit(solution)/shard_map/ppermute | solution.py:594
  33.5 14.1 %collective-permute-start.11 = (f32[128,128]{1,0:T(8,128)S(1)}, f32[128,128]{1,0:T(8,128)S(1)}, u32[]{:S(2)}, u32[]{:S(2)}) collective-permute-start(f32[128,128]{1,0:T(8,128)S(1)} %get-tuple-element.61), channel_id=1, source_target_pairs={{0,8},{8,0},{16,24},{1,9},{9,1},{17,25},{2,10},{10,2},{18,26},{3,1... | collective-permute-start | bytes 196616 | tf_op jit(solution)/shard_map/ppermute | solution.py:594
  41.8 7.2 %collective-permute-start.12 = (f32[128,128]{1,0:T(8,128)S(1)}, f32[128,128]{1,0:T(8,128)S(1)}, u32[]{:S(2)}, u32[]{:S(2)}) collective-permute-start(f32[128,128]{1,0:T(8,128)S(1)} %get-tuple-element.62), channel_id=1, source_target_pairs={{0,16},{8,24},{16,0},{1,17},{9,25},{17,1},{2,18},{10,26},{18,2},{3... | collective-permute-start | bytes 196616 | tf_op jit(solution)/shard_map/ppermute | solution.py:594
  43.7 5.3 %collective-permute-start.13 = (f32[128,128]{1,0:T(8,128)S(1)}, f32[128,128]{1,0:T(8,128)S(1)}, u32[]{:S(2)}, u32[]{:S(2)}) collective-permute-start(f32[128,128]{1,0:T(8,128)S(1)} %get-tuple-element.63), channel_id=1, source_target_pairs={{0,24},{8,16},{16,8},{1,25},{9,17},{17,9},{2,26},{10,18},{18,10},{... | collective-permute-start | bytes 196616 | tf_op jit(solution)/shard_map/ppermute | solution.py:594
  45.0 12.0 %collective-permute-start.17 = (bf16[2,128,128]{2,1,0:T(8,128)(2,1)S(1)}, bf16[2,128,128]{2,1,0:T(8,128)(2,1)S(1)}, u32[]{:S(2)}, u32[]{:S(2)}) collective-permute-start(bf16[2,128,128]{2,1,0:T(8,128)(2,1)S(1)} %get-tuple-element.69), channel_id=1, source_target_pairs={{0,1},{1,2},{2,3},{3,0},{4,5},{5,6},{6,7},{7,4},{8,9},{9,10},{10,1... | collective-permute-start | bytes 196616 | tf_op jit(solution)/shard_map/ppermute | solution.py:730
  46.3 14.1 %collective-permute-start.18 = (bf16[2,128,128]{2,1,0:T(8,128)(2,1)S(1)}, bf16[2,128,128]{2,1,0:T(8,128)(2,1)S(1)}, u32[]{:S(2)}, u32[]{:S(2)}) collective-permute-start(bf16[2,128,128]{2,1,0:T(8,128)(2,1)S(1)} %get-tuple-element.70), channel_id=1, source_target_pairs={{0,2},{1,3},{2,0},{3,1},{4,6},{5,7},{6,4},{7,5},{8,10},{9,11},{10,... | collective-permute-start | bytes 196616 | tf_op jit(solution)/shard_map/ppermute | solution.py:730
  47.6 12.8 %collective-permute-start.19 = (bf16[2,128,128]{2,1,0:T(8,128)(2,1)S(1)}, bf16[2,128,128]{2,1,0:T(8,128)(2,1)S(1)}, u32[]{:S(2)}, u32[]{:S(2)}) collective-permute-start(bf16[2,128,128]{2,1,0:T(8,128)(2,1)S(1)} %get-tuple-element.71), channel_id=1, source_target_pairs={{0,3},{1,0},{2,1},{3,2},{4,7},{5,4},{6,5},{7,6},{8,11},{9,8},{10,9... | collective-permute-start | bytes 196616 | tf_op jit(solution)/shard_map/ppermute | solution.py:730
  49.3 13.9 %collective-permute-start.14 = (f32[128,128]{1,0:T(8,128)S(1)}, f32[128,128]{1,0:T(8,128)S(1)}, u32[]{:S(2)}, u32[]{:S(2)}) collective-permute-start(f32[128,128]{1,0:T(8,128)S(1)} %get-tuple-element.65), channel_id=1, source_target_pairs={{0,8},{16,24},{24,16},{1,9},{17,25},{25,17},{2,10},{18,26},{26,18}... | collective-permute-start | bytes 196616 | tf_op jit(solution)/shard_map/ppermute | solution.py:594
  55.3 7.9 %collective-permute-start.15 = (f32[128,128]{1,0:T(8,128)S(1)}, f32[128,128]{1,0:T(8,128)S(1)}, u32[]{:S(2)}, u32[]{:S(2)}) collective-permute-start(f32[128,128]{1,0:T(8,128)S(1)} %get-tuple-element.66), channel_id=1, source_target_pairs={{0,16},{8,24},{24,8},{1,17},{9,25},{25,9},{2,18},{10,26},{26,10},{... | collective-permute-start | bytes 196616 | tf_op jit(solution)/shard_map/ppermute | solution.py:594
  57.0 6.3 %collective-permute-start.16 = (f32[128,128]{1,0:T(8,128)S(1)}, f32[128,128]{1,0:T(8,128)S(1)}, u32[]{:S(2)}, u32[]{:S(2)}) collective-permute-start(f32[128,128]{1,0:T(8,128)S(1)} %get-tuple-element.67), channel_id=1, source_target_pairs={{0,24},{8,16},{16,8},{1,25},{9,17},{17,9},{2,26},{10,18},{18,10},{... | collective-permute-start | bytes 196616 | tf_op jit(solution)/shard_map/ppermute | solution.py:594
  63.8 1.4 %collective-permute-start.20 = (bf16[128,512]{1,0:T(8,128)(2,1)S(1)}, bf16[128,512]{1,0:T(8,128)(2,1)S(1)}, u32[]{:S(2)}, u32[]{:S(2)}) collective-permute-start(bf16[128,512]{1,0:T(8,128)(2,1)S(1)} %get-tuple-element.82), channel_id=1, source_target_pairs={{0,4},{4,0},{1,5},{5,1},{2,6},{6,2},{3,7},{7,3},{8,12},{12,8},{9,1... | collective-permute-start | bytes 393224 | tf_op jit(solution)/shard_map/ppermute | solution.py:736

commit v13 on v7

--- a/solution.py
+++ b/solution.py
@@ -254,7 +254,7 @@
         ]
         for copy in copies:
             copy.start()
-        for copy in copies:
+        for copy in copies[:3]:
             copy.wait()
         z = axis_index("head")
         core = axis_index("core")
@@ -271,6 +271,8 @@
         own_starts = jnp.broadcast_to(starts[...].astype(F32), (heads, length)).astype(BF16)
         pieces.append(dot(own_starts, own.astype(BF16)))
         scales = jnp.concatenate(pieces, 1).astype(BF16)
+        for copy in copies[3:]:
+            copy.wait()
         for ahead, out in enumerate(outs):
             target = shifted(z, ahead, sizes.groups)
             for side in range(2):
@@ -665,13 +667,13 @@
     )
 
 
-def read_states(sizes, states, readers, inners):
+def read_states(sizes, states, readers, inners, side):
     groups = sizes.groups
     half = groups // 2
 
     def kernel(*refs):
         states = refs[: sizes.heads]
-        readers, inners, own, other, entry = refs[sizes.heads :]
+        readers, inners, out, entry = refs[sizes.heads :]
         core = axis_index("core")
         chip = axis_index("chip") if sizes.swapped else 0
         for number in range(sizes.heads):
@@ -686,17 +688,16 @@
                 ],
                 0,
             )
-            for side, out in enumerate((own, other)):
-                first = head * groups + jnp.bitwise_xor(core, side) * half
-                pair = readers[pl.ds(first, half)].reshape(half * CHUNK, 2 * DK)
-                both = dot_nt(pair, stack)
-                inner = inners[pl.ds(first, half)].reshape(half * CHUNK, DV)
-                result = inner + both[:, :DV] + both[:, DV:]
-                out[:, head * DV : (head + 1) * DV] = result.astype(BF16)
-
-    outs = [shape(half * CHUNK, sizes.heads * DV)] * 2
+            first = head * groups + jnp.bitwise_xor(core, side) * half
+            pair = readers[pl.ds(first, half)].reshape(half * CHUNK, 2 * DK)
+            both = dot_nt(pair, stack)
+            inner = inners[pl.ds(first, half)].reshape(half * CHUNK, DV)
+            result = inner + both[:, :DV] + both[:, DV:]
+            out[:, head * DV : (head + 1) * DV] = result.astype(BF16)
+
+    out = shape(half * CHUNK, sizes.heads * DV)
     scratch = [pltpu.VMEM((sizes.heads, DV, DK), F32)]
-    return call(kernel, outs, *states, readers, inners, scratch=scratch, name="read_states")
+    return call(kernel, out, *states, readers, inners, scratch=scratch, name="read_states")
 
 
 def join(sizes, own, other):
@@ -738,8 +739,9 @@
     readers, inners = query_stage(
         sizes, query_parts, unit_values, before, unit_keys, inverse, ratios, rows, prefixes
     )
-    own, other = read_states(sizes, states, readers, inners)
-    return join(sizes, own, swapped(other))
+    other = swapped(read_states(sizes, states, readers, inners, 1))
+    own = read_states(sizes, states, readers, inners, 0)
+    return join(sizes, own, other)
 
 
 def solution(mesh):

time: 52.9 us -> 52.5 us (level)
    pallas_call x10 -> x11, Pallas kernels: 14.3 us -> 14.2 us  [call(): pl.pallas_call(kernel, out_shape=outs, in_specs=specs, scratch_shapes=scr...]
where the time goes in v13:
time: 52.5 us; the launch traced here: 52.3 us
  starting transfers between devices  28.1 us (54%)
  Pallas kernels  14.2 us (27%)
  waiting for transfers between devices  8.95 us (17%)
  local copies, waits for them, and re-layouts  0.95 us (2%)
    ppermute x9, starting transfers between devices, spread(): lax.ppermute(part, 'head', [(z, (z + ahead) % groups) for z in range(grou...  17.2 us
    pallas_call x11, Pallas kernels, call(): pl.pallas_call(kernel, out_shape=outs, in_specs=specs, scratch_shapes=scr...  14.2 us
    ppermute x9, starting transfers between devices, exchanged(): lax.ppermute(part, 'chip', [(chip, chip ^ number) for chip in range(sizes...  10.7 us
    ppermute x9, waiting for transfers between devices, spread(): lax.ppermute(part, 'head', [(z, (z + ahead) % groups) for z in range(grou...  6.33 us
    ppermute x9, waiting for transfers between devices, exchanged(): lax.ppermute(part, 'chip', [(chip, chip ^ number) for chip in range(sizes...  1.63 us
  transfers between devices with their start and end apart: 21, of which 5 were waited for; matrix products, arithmetic and copies ran while one was open for 0% of the time, Pallas kernels for 22%

profile of v13, /device:TPU:0, one launch (start us, length us, event | category | flops | bytes accessed | tf_op | source)
XLA Modules:
  0.0 52.3 jit_solution(12962709612141460347)
XLA Ops:
  0.0 1.4 %pack_keys.1 = (bf16[528,128]{1,0:T(8,128)(2,1)S(1)}, bf16[528,128]{1,0:T(8,128)(2,1)S(1)}, bf16[528,128]{1,0:T(8,128)(2,1)S(1)}, bf16[528,128]{1,0:T(8,128)(2,1)S(1)}) custom-call(bf16[32,8192]{1,0:T(8,128)(2,1)} %far_keys.1, bf16[32,64]{1,0:T(8,128)(2,1)} %far_betas.1, bf16[32,32]{1,0:T(8,128)(2,1)} %far_gates.1, s32[1,128]{1,0:T(1,128)} %bitcast.1), custom_call_target="tpu_custom_call" | custom-call | tf_op jit(solution)/shard_map/pack_keys/pallas_call | solution.py:196
  1.4 3.1 %collective-permute-start = (bf16[528,128]{1,0:T(8,128)(2,1)S(1)}, bf16[528,128]{1,0:T(8,128)(2,1)S(1)}, u32[]{:S(2)}, u32[]{:S(2)}) collective-permute-start(bf16[528,128]{1,0:T(8,128)(2,1)S(1)} %get-tuple-element.43), channel_id=1, source_target_pairs={{0,1},{1,2},{2,3},{3,0},{4,5},{5,6},{6,7},{7,4},{8,9},{9,10},{10,1... | collective-permute-start | bytes 405512 | tf_op jit(solution)/shard_map/ppermute | solution.py:720
  4.5 2.6 %collective-permute-start.1 = (bf16[528,128]{1,0:T(8,128)(2,1)S(1)}, bf16[528,128]{1,0:T(8,128)(2,1)S(1)}, u32[]{:S(2)}, u32[]{:S(2)}) collective-permute-start(bf16[528,128]{1,0:T(8,128)(2,1)S(1)} %get-tuple-element.44), channel_id=1, source_target_pairs={{0,2},{1,3},{2,0},{3,1},{4,6},{5,7},{6,4},{7,5},{8,10},{9,11},{10,... | collective-permute-start | bytes 405512 | tf_op jit(solution)/shard_map/ppermute | solution.py:720
  7.1 1.3 %collective-permute-start.2 = (bf16[528,128]{1,0:T(8,128)(2,1)S(1)}, bf16[528,128]{1,0:T(8,128)(2,1)S(1)}, u32[]{:S(2)}, u32[]{:S(2)}) collective-permute-start(bf16[528,128]{1,0:T(8,128)(2,1)S(1)} %get-tuple-element.45), channel_id=1, source_target_pairs={{0,3},{1,0},{2,1},{3,2},{4,7},{5,4},{6,5},{7,6},{8,11},{9,8},{10,9... | collective-permute-start | bytes 405512 | tf_op jit(solution)/shard_map/ppermute | solution.py:720
  8.5 0.9 %copy-done.1 = bf16[32,4096]{1,0:T(8,128)(2,1)S(1)} copy-done((bf16[32,4096]{1,0:T(8,128)(2,1)S(1)}, bf16[32,4096]{1,0:T(8,128)(2,1)}, u32[]{:S(2)}) %copy-start.1) | copy-done | bytes 262168
  9.7 1.4 %collective-permute-done.refs_1_ = bf16[528,128]{1,0:T(8,128)(2,1)S(1)} collective-permute-done((bf16[528,128]{1,0:T(8,128)(2,1)S(1)}, bf16[528,128]{1,0:T(8,128)(2,1)S(1)}, u32[]{:S(2)}, u32[]{:S(2)}) %collective-permute-start) | collective-permute-done | bytes 135200 | tf_op jit(solution)/shard_map/ppermute | solution.py:720
  11.0 5.0 %collective-permute-done.1.refs_2_ = bf16[528,128]{1,0:T(8,128)(2,1)S(1)} collective-permute-done((bf16[528,128]{1,0:T(8,128)(2,1)S(1)}, bf16[528,128]{1,0:T(8,128)(2,1)S(1)}, u32[]{:S(2)}, u32[]{:S(2)}) %collective-permute-start.1) | collective-permute-done | bytes 135200 | tf_op jit(solution)/shard_map/ppermute | solution.py:720
  16.2 3.4 %collective-permute-start.8 = (bf16[2,256,128]{2,1,0:T(8,128)(2,1)S(1)}, bf16[2,256,128]{2,1,0:T(8,128)(2,1)S(1)}, u32[]{:S(2)}, u32[]{:S(2)}) collective-permute-start(bf16[2,256,128]{2,1,0:T(8,128)(2,1)S(1)} %get-tuple-element.53), channel_id=1, source_target_pairs={{0,1},{1,2},{2,3},{3,0},{4,5},{5,6},{6,7},{7,4},{8,9},{9,10},{10,1... | collective-permute-start | bytes 393224 | tf_op jit(solution)/shard_map/ppermute | solution.py:720
  19.6 1.6 %collective-permute-start.9 = (bf16[2,256,128]{2,1,0:T(8,128)(2,1)S(1)}, bf16[2,256,128]{2,1,0:T(8,128)(2,1)S(1)}, u32[]{:S(2)}, u32[]{:S(2)}) collective-permute-start(bf16[2,256,128]{2,1,0:T(8,128)(2,1)S(1)} %get-tuple-element.54), channel_id=1, source_target_pairs={{0,2},{1,3},{2,0},{3,1},{4,6},{5,7},{6,4},{7,5},{8,10},{9,11},{10,... | collective-permute-start | bytes 393224 | tf_op jit(solution)/shard_map/ppermute | solution.py:720
  21.2 0.8 %collective-permute-start.10 = (bf16[2,256,128]{2,1,0:T(8,128)(2,1)S(1)}, bf16[2,256,128]{2,1,0:T(8,128)(2,1)S(1)}, u32[]{:S(2)}, u32[]{:S(2)}) collective-permute-start(bf16[2,256,128]{2,1,0:T(8,128)(2,1)S(1)} %get-tuple-element.55), channel_id=1, source_target_pairs={{0,3},{1,0},{2,1},{3,2},{4,7},{5,4},{6,5},{7,6},{8,11},{9,8},{10,9... | collective-permute-start | bytes 393224 | tf_op jit(solution)/shard_map/ppermute | solution.py:720
  22.1 7.1 %key_stage.1 = (bf16[16,128,128]{2,1,0:T(8,128)(2,1)S(1)}, bf16[16,128,256]{2,1,0:T(8,128)(2,1)S(1)}, bf16[16,128,256]{2,1,0:T(8,128)(2,1)S(1)}, f32[16,64,128]{...) custom-call(bf16[528,128]{1,0:T(8,128)(2,1)S(1)} %get-tuple-element., ...), custom_call_target="tpu_custom_call" | custom-call | flops 6000000000 | tf_op jit(solution)/shard_map/key_stage/pallas_call | solution.py:196
  29.2 1.6 %collective-permute-start.4 = (f32[128,128]{1,0:T(8,128)S(1)}, f32[128,128]{1,0:T(8,128)S(1)}, u32[]{:S(2)}, u32[]{:S(2)}) collective-permute-start(f32[128,128]{1,0:T(8,128)S(1)} %get-tuple-element.47), channel_id=1, source_target_pairs={{0,8},{8,0},{16,24},{24,16},{1,9},{9,1},{17,25},{25,17},{2,10},{10... | collective-permute-start | bytes 196616 | tf_op jit(solution)/shard_map/ppermute | solution.py:596
  30.8 1.5 %collective-permute-start.5 = (f32[128,128]{1,0:T(8,128)S(1)}, f32[128,128]{1,0:T(8,128)S(1)}, u32[]{:S(2)}, u32[]{:S(2)}) collective-permute-start(f32[128,128]{1,0:T(8,128)S(1)} %get-tuple-element.48), channel_id=1, source_target_pairs={{0,16},{8,24},{16,0},{24,8},{1,17},{9,25},{17,1},{25,9},{2,18},{10... | collective-permute-start | bytes 196616 | tf_op jit(solution)/shard_map/ppermute | solution.py:596
  32.3 0.5 collective-permute-start.6
  32.8 0.8 %value_stage.1 = (bf16[16,128,128]{2,1,0:T(8,128)(2,1)S(1)}, f32[16,128,128]{2,1,0:T(8,128)S(1)}, f32[128,128]{1,0:T(8,128)S(1)}, f32[128,128]{1,0:T(8,128)S(1)}...) custom-call(bf16[2,256,128]{2,1,0:T(8,128)(2,1)S(1)} %get-tuple-element.52.refs_0_, ...), custom_call_target="tpu_custom_call" | custom-call | flops 2000000000 | tf_op jit(solution)/shard_map/value_stage/pallas_call | solution.py:196
  33.6 1.6 %collective-permute-start.11 = (f32[128,128]{1,0:T(8,128)S(1)}, f32[128,128]{1,0:T(8,128)S(1)}, u32[]{:S(2)}, u32[]{:S(2)}) collective-permute-start(f32[128,128]{1,0:T(8,128)S(1)} %get-tuple-element.59), channel_id=1, source_target_pairs={{0,8},{8,0},{16,24},{24,16},{1,9},{9,1},{17,25},{25,17},{2,10},{10... | collective-permute-start | bytes 196616 | tf_op jit(solution)/shard_map/ppermute | solution.py:596
  35.1 1.5 %collective-permute-start.12 = (f32[128,128]{1,0:T(8,128)S(1)}, f32[128,128]{1,0:T(8,128)S(1)}, u32[]{:S(2)}, u32[]{:S(2)}) collective-permute-start(f32[128,128]{1,0:T(8,128)S(1)} %get-tuple-element.60), channel_id=1, source_target_pairs={{0,16},{8,24},{16,0},{24,8},{1,17},{9,25},{17,1},{25,9},{2,18},{10... | collective-permute-start | bytes 196616 | tf_op jit(solution)/shard_map/ppermute | solution.py:596
  36.7 0.5 collective-permute-start.13
  37.1 1.2 %collective-permute-start.17 = (bf16[2,128,128]{2,1,0:T(8,128)(2,1)S(1)}, bf16[2,128,128]{2,1,0:T(8,128)(2,1)S(1)}, u32[]{:S(2)}, u32[]{:S(2)}) collective-permute-start(bf16[2,128,128]{2,1,0:T(8,128)(2,1)S(1)} %get-tuple-element.67), channel_id=1, source_target_pairs={{0,1},{1,2},{2,3},{3,0},{4,5},{5,6},{6,7},{7,4},{8,9},{9,10},{10,1... | collective-permute-start | bytes 196616 | tf_op jit(solution)/shard_map/ppermute | solution.py:720
  38.3 1.3 %collective-permute-start.18 = (bf16[2,128,128]{2,1,0:T(8,128)(2,1)S(1)}, bf16[2,128,128]{2,1,0:T(8,128)(2,1)S(1)}, u32[]{:S(2)}, u32[]{:S(2)}) collective-permute-start(bf16[2,128,128]{2,1,0:T(8,128)(2,1)S(1)} %get-tuple-element.68), channel_id=1, source_target_pairs={{0,2},{1,3},{2,0},{3,1},{4,6},{5,7},{6,4},{7,5},{8,10},{9,11},{10,... | collective-permute-start | bytes 196616 | tf_op jit(solution)/shard_map/ppermute | solution.py:720
  39.6 1.8 %collective-permute-start.19 = (bf16[2,128,128]{2,1,0:T(8,128)(2,1)S(1)}, bf16[2,128,128]{2,1,0:T(8,128)(2,1)S(1)}, u32[]{:S(2)}, u32[]{:S(2)}) collective-permute-start(bf16[2,128,128]{2,1,0:T(8,128)(2,1)S(1)} %get-tuple-element.69), channel_id=1, source_target_pairs={{0,3},{1,0},{2,1},{3,2},{4,7},{5,4},{6,5},{7,6},{8,11},{9,8},{10,9... | collective-permute-start | bytes 196616 | tf_op jit(solution)/shard_map/ppermute | solution.py:720
  41.5 0.4 collective-permute-done.13.refs_7_
  41.8 0.4 scan_states.1
  42.2 0.9 %collective-permute-start.14 = (f32[128,128]{1,0:T(8,128)S(1)}, f32[128,128]{1,0:T(8,128)S(1)}, u32[]{:S(2)}, u32[]{:S(2)}) collective-permute-start(f32[128,128]{1,0:T(8,128)S(1)} %get-tuple-element.63), channel_id=1, source_target_pairs={{0,8},{8,0},{16,24},{24,16},{1,9},{9,1},{17,25},{25,17},{2,10},{10... | collective-permute-start | bytes 196616 | tf_op jit(solution)/shard_map/ppermute | solution.py:596
  43.1 1.6 %collective-permute-start.15 = (f32[128,128]{1,0:T(8,128)S(1)}, f32[128,128]{1,0:T(8,128)S(1)}, u32[]{:S(2)}, u32[]{:S(2)}) collective-permute-start(f32[128,128]{1,0:T(8,128)S(1)} %get-tuple-element.64), channel_id=1, source_target_pairs={{0,16},{8,24},{16,0},{24,8},{1,17},{9,25},{17,1},{25,9},{2,18},{10... | collective-permute-start | bytes 196616 | tf_op jit(solution)/shard_map/ppermute | solution.py:596
  44.7 1.1 %collective-permute-start.16 = (f32[128,128]{1,0:T(8,128)S(1)}, f32[128,128]{1,0:T(8,128)S(1)}, u32[]{:S(2)}, u32[]{:S(2)}) collective-permute-start(f32[128,128]{1,0:T(8,128)S(1)} %get-tuple-element.65), channel_id=1, source_target_pairs={{0,24},{8,16},{16,8},{24,0},{1,25},{9,17},{17,9},{25,1},{2,26},{10... | collective-permute-start | bytes 196616 | tf_op jit(solution)/shard_map/ppermute | solution.py:596
  45.8 2.8 %query_stage.1 = (bf16[16,64,256]{2,1,0:T(8,128)(2,1)S(1)}, f32[16,64,128]{2,1,0:T(8,128)S(1)}) custom-call(bf16[2,128,128]{2,1,0:T(8,128)(2,1)S(1)} %get-tuple-element.66.refs_0_, bf16[2,128,128]{2,1,0:T(8,128)(2,1)S(1)} %collective-permute-done.17.refs_1_, bf16[2,128,128]{2,1,0:T(8,128)(2,1)S(1)} %collective-permute-done.18.refs_2_, ...), custom_call_target="tpu_custom_call" | custom-call | flops 3000000000 | tf_op jit(solution)/shard_map/query_stage/pallas_call | solution.py:196
  48.6 1.2 %collective-permute-done.16.refs_3_ = f32[128,128]{1,0:T(8,128)S(1)} collective-permute-done((f32[128,128]{1,0:T(8,128)S(1)}, f32[128,128]{1,0:T(8,128)S(1)}, u32[]{:S(2)}, u32[]{:S(2)}) %collective-permute-start.16) | collective-permute-done | bytes 65568 | tf_op jit(solution)/shard_map/ppermute | solution.py:596
  49.9 0.3 read_states.3
  50.3 0.3 read_states.2.own
  50.6 1.0 %collective-permute-done.20.other = bf16[128,512]{1,0:T(8,128)(2,1)S(1)} collective-permute-done((bf16[128,512]{1,0:T(8,128)(2,1)S(1)}, bf16[128,512]{1,0:T(8,128)(2,1)S(1)}, u32[]{:S(2)}, u32[]{:S(2)}) %collective-permute-start.20) | collective-permute-done | bytes 131104 | tf_op jit(solution)/shard_map/ppermute | solution.py:726
  51.6 0.7 %join.1 = bf16[128,1024]{1,0:T(8,128)(2,1)} custom-call(bf16[128,512]{1,0:T(8,128)(2,1)S(1)} %read_states.2.own, bf16[128,512]{1,0:T(8,128)(2,1)S(1)} %collective-permute-done.20.other), custom_call_target="tpu_custom_call" | custom-call | tf_op jit(solution)/shard_map/join/pallas_call | solution.py:196
  (25 shorter events, 0.5 us)
Async XLA Ops:
  0.0 8.5 %copy-start = (bf16[32,8192]{1,0:T(8,128)(2,1)S(1)}, bf16[32,8192]{1,0:T(8,128)(2,1)}, u32[]{:S(2)}) copy-start(bf16[32,8192]{1,0:T(8,128)(2,1)} %values.1) | copy-start | bytes 1572868
  1.4 9.6 %collective-permute-start = (bf16[528,128]{1,0:T(8,128)(2,1)S(1)}, bf16[528,128]{1,0:T(8,128)(2,1)S(1)}, u32[]{:S(2)}, u32[]{:S(2)}) collective-permute-start(bf16[528,128]{1,0:T(8,128)(2,1)S(1)} %get-tuple-element.43), channel_id=1, source_target_pairs={{0,1},{1,2},{2,3},{3,0},{4,5},{5,6},{6,7},{7,4},{8,9},{9,10},{10,1... | collective-permute-start | bytes 405512 | tf_op jit(solution)/shard_map/ppermute | solution.py:720
  4.5 11.5 %collective-permute-start.1 = (bf16[528,128]{1,0:T(8,128)(2,1)S(1)}, bf16[528,128]{1,0:T(8,128)(2,1)S(1)}, u32[]{:S(2)}, u32[]{:S(2)}) collective-permute-start(bf16[528,128]{1,0:T(8,128)(2,1)S(1)} %get-tuple-element.44), channel_id=1, source_target_pairs={{0,2},{1,3},{2,0},{3,1},{4,6},{5,7},{6,4},{7,5},{8,10},{9,11},{10,... | collective-permute-start | bytes 405512 | tf_op jit(solution)/shard_map/ppermute | solution.py:720
  7.1 8.9 %collective-permute-start.2 = (bf16[528,128]{1,0:T(8,128)(2,1)S(1)}, bf16[528,128]{1,0:T(8,128)(2,1)S(1)}, u32[]{:S(2)}, u32[]{:S(2)}) collective-permute-start(bf16[528,128]{1,0:T(8,128)(2,1)S(1)} %get-tuple-element.45), channel_id=1, source_target_pairs={{0,3},{1,0},{2,1},{3,2},{4,7},{5,4},{6,5},{7,6},{8,11},{9,8},{10,9... | collective-permute-start | bytes 405512 | tf_op jit(solution)/shard_map/ppermute | solution.py:720
  8.5 1.0 %copy-start.1 = (bf16[32,4096]{1,0:T(8,128)(2,1)S(1)}, bf16[32,4096]{1,0:T(8,128)(2,1)}, u32[]{:S(2)}) copy-start(bf16[32,4096]{1,0:T(8,128)(2,1)} %queries.1) | copy-start | bytes 786436
  9.6 6.5 %collective-permute-start.7 = (bf16[4,384,128]{2,1,0:T(8,128)(2,1)S(1)}, bf16[4,384,128]{2,1,0:T(8,128)(2,1)S(1)}, u32[]{:S(2)}, u32[]{:S(2)}) collective-permute-start(bf16[4,384,128]{2,1,0:T(8,128)(2,1)S(1)} %get-tuple-element.51), channel_id=1, source_target_pairs={{0,4},{4,0},{1,5},{5,1},{2,6},{6,2},{3,7},{7,3},{8,12},{12,8},{9,1... | collective-permute-start | bytes 1179656 | tf_op jit(solution)/shard_map/ppermute | solution.py:726
  16.0 6.0 %collective-permute-start.3 = (bf16[4,272,128]{2,1,0:T(8,128)(2,1)S(1)}, bf16[4,272,128]{2,1,0:T(8,128)(2,1)S(1)}, u32[]{:S(2)}, u32[]{:S(2)}) collective-permute-start(bf16[4,272,128]{2,1,0:T(8,128)(2,1)S(1)} %swap_keys.1), channel_id=1, source_target_pairs={{0,4},{4,0},{1,5},{5,1},{2,6},{6,2},{3,7},{7,3},{8,12},{12,8},{9,1... | collective-permute-start | bytes 835592 | tf_op jit(solution)/shard_map/ppermute | solution.py:726
  16.2 16.1 %collective-permute-start.8 = (bf16[2,256,128]{2,1,0:T(8,128)(2,1)S(1)}, bf16[2,256,128]{2,1,0:T(8,128)(2,1)S(1)}, u32[]{:S(2)}, u32[]{:S(2)}) collective-permute-start(bf16[2,256,128]{2,1,0:T(8,128)(2,1)S(1)} %get-tuple-element.53), channel_id=1, source_target_pairs={{0,1},{1,2},{2,3},{3,0},{4,5},{5,6},{6,7},{7,4},{8,9},{9,10},{10,1... | collective-permute-start | bytes 393224 | tf_op jit(solution)/shard_map/ppermute | solution.py:720
  19.6 13.2 %collective-permute-start.9 = (bf16[2,256,128]{2,1,0:T(8,128)(2,1)S(1)}, bf16[2,256,128]{2,1,0:T(8,128)(2,1)S(1)}, u32[]{:S(2)}, u32[]{:S(2)}) collective-permute-start(bf16[2,256,128]{2,1,0:T(8,128)(2,1)S(1)} %get-tuple-element.54), channel_id=1, source_target_pairs={{0,2},{1,3},{2,0},{3,1},{4,6},{5,7},{6,4},{7,5},{8,10},{9,11},{10,... | collective-permute-start | bytes 393224 | tf_op jit(solution)/shard_map/ppermute | solution.py:720
  21.2 11.5 %collective-permute-start.10 = (bf16[2,256,128]{2,1,0:T(8,128)(2,1)S(1)}, bf16[2,256,128]{2,1,0:T(8,128)(2,1)S(1)}, u32[]{:S(2)}, u32[]{:S(2)}) collective-permute-start(bf16[2,256,128]{2,1,0:T(8,128)(2,1)S(1)} %get-tuple-element.55), channel_id=1, source_target_pairs={{0,3},{1,0},{2,1},{3,2},{4,7},{5,4},{6,5},{7,6},{8,11},{9,8},{10,9... | collective-permute-start | bytes 393224 | tf_op jit(solution)/shard_map/ppermute | solution.py:720
  29.2 7.5 %collective-permute-start.4 = (f32[128,128]{1,0:T(8,128)S(1)}, f32[128,128]{1,0:T(8,128)S(1)}, u32[]{:S(2)}, u32[]{:S(2)}) collective-permute-start(f32[128,128]{1,0:T(8,128)S(1)} %get-tuple-element.47), channel_id=1, source_target_pairs={{0,8},{8,0},{16,24},{24,16},{1,9},{9,1},{17,25},{25,17},{2,10},{10... | collective-permute-start | bytes 196616 | tf_op jit(solution)/shard_map/ppermute | solution.py:596
  30.8 6.4 %collective-permute-start.5 = (f32[128,128]{1,0:T(8,128)S(1)}, f32[128,128]{1,0:T(8,128)S(1)}, u32[]{:S(2)}, u32[]{:S(2)}) collective-permute-start(f32[128,128]{1,0:T(8,128)S(1)} %get-tuple-element.48), channel_id=1, source_target_pairs={{0,16},{8,24},{16,0},{24,8},{1,17},{9,25},{17,1},{25,9},{2,18},{10... | collective-permute-start | bytes 196616 | tf_op jit(solution)/shard_map/ppermute | solution.py:596
  32.3 6.1 %collective-permute-start.6 = (f32[128,128]{1,0:T(8,128)S(1)}, f32[128,128]{1,0:T(8,128)S(1)}, u32[]{:S(2)}, u32[]{:S(2)}) collective-permute-start(f32[128,128]{1,0:T(8,128)S(1)} %get-tuple-element.49), channel_id=1, source_target_pairs={{0,24},{8,16},{16,8},{24,0},{1,25},{9,17},{17,9},{25,1},{2,26},{10... | collective-permute-start | bytes 196616 | tf_op jit(solution)/shard_map/ppermute | solution.py:596
  33.6 6.1 %collective-permute-start.11 = (f32[128,128]{1,0:T(8,128)S(1)}, f32[128,128]{1,0:T(8,128)S(1)}, u32[]{:S(2)}, u32[]{:S(2)}) collective-permute-start(f32[128,128]{1,0:T(8,128)S(1)} %get-tuple-element.59), channel_id=1, source_target_pairs={{0,8},{8,0},{16,24},{24,16},{1,9},{9,1},{17,25},{25,17},{2,10},{10... | collective-permute-start | bytes 196616 | tf_op jit(solution)/shard_map/ppermute | solution.py:596
  35.1 6.3 %collective-permute-start.12 = (f32[128,128]{1,0:T(8,128)S(1)}, f32[128,128]{1,0:T(8,128)S(1)}, u32[]{:S(2)}, u32[]{:S(2)}) collective-permute-start(f32[128,128]{1,0:T(8,128)S(1)} %get-tuple-element.60), channel_id=1, source_target_pairs={{0,16},{8,24},{16,0},{24,8},{1,17},{9,25},{17,1},{25,9},{2,18},{10... | collective-permute-start | bytes 196616 | tf_op jit(solution)/shard_map/ppermute | solution.py:596
  36.7 5.2 %collective-permute-start.13 = (f32[128,128]{1,0:T(8,128)S(1)}, f32[128,128]{1,0:T(8,128)S(1)}, u32[]{:S(2)}, u32[]{:S(2)}) collective-permute-start(f32[128,128]{1,0:T(8,128)S(1)} %get-tuple-element.61), channel_id=1, source_target_pairs={{0,24},{8,16},{16,8},{24,0},{1,25},{9,17},{17,9},{25,1},{2,26},{10... | collective-permute-start | bytes 196616 | tf_op jit(solution)/shard_map/ppermute | solution.py:596
  37.1 7.6 %collective-permute-start.17 = (bf16[2,128,128]{2,1,0:T(8,128)(2,1)S(1)}, bf16[2,128,128]{2,1,0:T(8,128)(2,1)S(1)}, u32[]{:S(2)}, u32[]{:S(2)}) collective-permute-start(bf16[2,128,128]{2,1,0:T(8,128)(2,1)S(1)} %get-tuple-element.67), channel_id=1, source_target_pairs={{0,1},{1,2},{2,3},{3,0},{4,5},{5,6},{6,7},{7,4},{8,9},{9,10},{10,1... | collective-permute-start | bytes 196616 | tf_op jit(solution)/shard_map/ppermute | solution.py:720
  38.3 7.4 %collective-permute-start.18 = (bf16[2,128,128]{2,1,0:T(8,128)(2,1)S(1)}, bf16[2,128,128]{2,1,0:T(8,128)(2,1)S(1)}, u32[]{:S(2)}, u32[]{:S(2)}) collective-permute-start(bf16[2,128,128]{2,1,0:T(8,128)(2,1)S(1)} %get-tuple-element.68), channel_id=1, source_target_pairs={{0,2},{1,3},{2,0},{3,1},{4,6},{5,7},{6,4},{7,5},{8,10},{9,11},{10,... | collective-permute-start | bytes 196616 | tf_op jit(solution)/shard_map/ppermute | solution.py:720
  39.6 6.1 %collective-permute-start.19 = (bf16[2,128,128]{2,1,0:T(8,128)(2,1)S(1)}, bf16[2,128,128]{2,1,0:T(8,128)(2,1)S(1)}, u32[]{:S(2)}, u32[]{:S(2)}) collective-permute-start(bf16[2,128,128]{2,1,0:T(8,128)(2,1)S(1)} %get-tuple-element.69), channel_id=1, source_target_pairs={{0,3},{1,0},{2,1},{3,2},{4,7},{5,4},{6,5},{7,6},{8,11},{9,8},{10,9... | collective-permute-start | bytes 196616 | tf_op jit(solution)/shard_map/ppermute | solution.py:720
  42.2 6.4 %collective-permute-start.14 = (f32[128,128]{1,0:T(8,128)S(1)}, f32[128,128]{1,0:T(8,128)S(1)}, u32[]{:S(2)}, u32[]{:S(2)}) collective-permute-start(f32[128,128]{1,0:T(8,128)S(1)} %get-tuple-element.63), channel_id=1, source_target_pairs={{0,8},{8,0},{16,24},{24,16},{1,9},{9,1},{17,25},{25,17},{2,10},{10... | collective-permute-start | bytes 196616 | tf_op jit(solution)/shard_map/ppermute | solution.py:596
  43.1 5.5 %collective-permute-start.15 = (f32[128,128]{1,0:T(8,128)S(1)}, f32[128,128]{1,0:T(8,128)S(1)}, u32[]{:S(2)}, u32[]{:S(2)}) collective-permute-start(f32[128,128]{1,0:T(8,128)S(1)} %get-tuple-element.64), channel_id=1, source_target_pairs={{0,16},{8,24},{16,0},{24,8},{1,17},{9,25},{17,1},{25,9},{2,18},{10... | collective-permute-start | bytes 196616 | tf_op jit(solution)/shard_map/ppermute | solution.py:596
  44.7 5.2 %collective-permute-start.16 = (f32[128,128]{1,0:T(8,128)S(1)}, f32[128,128]{1,0:T(8,128)S(1)}, u32[]{:S(2)}, u32[]{:S(2)}) collective-permute-start(f32[128,128]{1,0:T(8,128)S(1)} %get-tuple-element.65), channel_id=1, source_target_pairs={{0,24},{8,16},{16,8},{24,0},{1,25},{9,17},{17,9},{25,1},{2,26},{10... | collective-permute-start | bytes 196616 | tf_op jit(solution)/shard_map/ppermute | solution.py:596
  50.2 1.4 %collective-permute-start.20 = (bf16[128,512]{1,0:T(8,128)(2,1)S(1)}, bf16[128,512]{1,0:T(8,128)(2,1)S(1)}, u32[]{:S(2)}, u32[]{:S(2)}) collective-permute-start(bf16[128,512]{1,0:T(8,128)(2,1)S(1)} %read_states.3), channel_id=1, source_target_pairs={{0,4},{4,0},{1,5},{5,1},{2,6},{6,2},{3,7},{7,3},{8,12},{12,8},{9,1... | collective-permute-start | bytes 393224 | tf_op jit(solution)/shard_map/ppermute | solution.py:726
